TPU v7x, 32 devices: a whole 2x2x4 slice. The times are simulated.
32 devices in a mesh: dp: 16 (over z, x, core), rep: 2 (over y).
Axes of the slice: x: 2, y: 2, z: 4, core: 2. Of those that a mesh axis runs over, the one named last changes fastest.
Arguments:
- hidden_states: bfloat16 [512, 64, 768], P(('dp', 'rep')), may hold values from -6 to 6
- image_features: bfloat16 [512, 257, 1408], P(('dp', 'rep')), may hold values from -6 to 6
- caption_lengths: int32 [512, 2], P(('dp', 'rep')), may hold values from 4 to 16
- attn_weights: bfloat16 [6, 768, 768], replicated, may hold values from -0.21875 to 0.21875
- cross_kv: bfloat16 [2, 768, 1408], replicated, may hold values from -0.15625 to 0.15625
- ffn_in: bfloat16 [2, 768, 3072], replicated, may hold values from -0.21875 to 0.21875
- ffn_out: bfloat16 [2, 3072, 768], replicated, may hold values from -0.109375 to 0.109375
- projections: bfloat16 [2, 768, 256], replicated, may hold values from -0.21875 to 0.21875
- norm_gains: float32 [4, 768], replicated, may hold values from 0.25 to 1.75
- biases: float32 [12, 768], replicated, may hold values from -1.8 to 1.8
- ffn_bias: float32 [2, 3072], replicated, may hold values from -1.8 to 1.8
- proj_bias: float32 [2, 256], replicated, may hold values from -1.8 to 1.8
- out_grad: bfloat16 [512, 64, 768], P(('dp', 'rep')), may hold values from -6 to 6
Outputs:
- layer_out: bfloat16 [512, 64, 768], P(('dp', 'rep'))
- row_loss: float32 [512], P(('dp', 'rep'))
- input_grad: float32 [512, 64, 768], P(('dp', 'rep'))
- attn_grad: float32 [6, 768, 768], P('rep', 'dp')
- cross_grad: float32 [2, 768, 1408], P('rep', 'dp')
- ffn_in_grad: float32 [2, 768, 3072], P('rep', 'dp')
- ffn_out_grad: float32 [2, 3072, 768], P('rep', 'dp')
- proj_grad: float32 [2, 768, 256], P('rep', 'dp')
- gain_grad: float32 [4, 768], P('rep', 'dp')
- bias_grad: float32 [12, 768], P('rep', 'dp')
- ffn_bias_grad: float32 [2, 3072], P('rep', 'dp')
- proj_bias_grad: float32 [2, 256], P('rep', 'dp')
Inputs may be any that keep to these rules, and one draw needn't show every extreme that they name: `caption_lengths`: caption 1 starts where caption 0 ends; the slots after both captions are padding.
All inputs are finite; a program needn't handle non-finite values.
Results may differ from a plain program's by a relative error of at most 0.018.
Values may be sent and summed in bfloat16 or wider, within the bound.
No kernel may reach another device: no remote copies, remote signals or barrier semaphores. Data moves between devices by JAX's collectives and lax.ppermute only.
A program may use at most 320 MiB of HBM per device.

v0:
```python
import jax
import jax.numpy as jnp
from jax import lax
from jax.sharding import PartitionSpec as P

HEADS = 12
HEAD_DIM = 64
QUERIES = 32
TEXT = 32


blocked = -1000000000.0
epsilon = 1e-06
sharpness = 14.0
loss_weight = 16.0


def matmul(left, right):
    return jnp.einsum("...k,kn->...n", left, right, preferred_element_type=jnp.float32)


def matmul_back(grad_rows, right):
    return jnp.einsum("...n,kn->...k", grad_rows, right, preferred_element_type=jnp.float32)


def weight_grad(left, grad_rows):
    flat_left = left.reshape(-1, left.shape[-1])
    flat_grad = grad_rows.reshape(-1, grad_rows.shape[-1])
    return jnp.einsum("tk,tn->kn", flat_left, flat_grad, preferred_element_type=jnp.float32)


def bias_sum(grad_rows):
    return jnp.sum(grad_rows.reshape(-1, grad_rows.shape[-1]), 0, dtype=jnp.float32)


def layer_norm(values, gain_row, shift_row):
    center = values - jnp.mean(values, -1, keepdims=True)
    spread = jnp.mean(center * center, -1, keepdims=True)
    return center * lax.rsqrt(spread + epsilon) * gain_row + shift_row


def norm_back(values, gain_row, shift_row, grad_rows):
    unused, pullback = jax.vjp(layer_norm, values, gain_row, shift_row)
    return pullback(grad_rows)


def unit_rows(values):
    return values * lax.rsqrt(jnp.sum(values * values, -1, keepdims=True) + epsilon)


def unit_back(values, grad_rows):
    unused, pullback = jax.vjp(unit_rows, values)
    return pullback(grad_rows)[0]


def smooth_gate(values):
    return jax.nn.gelu(values, approximate=False)


def gate_back(values, grad_rows):
    unused, pullback = jax.vjp(smooth_gate, values)
    return pullback(grad_rows)[0]


def split_heads(values):
    return values.reshape(values.shape[:-1] + (HEADS, HEAD_DIM))


def join_heads(values):
    return values.reshape(values.shape[:-2] + (-1,))


def caption_layout(length_rows):
    row_count = length_rows.shape[0]
    first_len = length_rows[:, 0:1]
    second_end = first_len + length_rows[:, 1:2]
    slot_index = lax.broadcasted_iota(jnp.int32, (row_count, TEXT), 1)
    text_group = (slot_index >= first_len).astype(jnp.int32) + (slot_index >= second_end).astype(
        jnp.int32
    )
    group_ids = jnp.concatenate([jnp.full((row_count, QUERIES), -1, jnp.int32), text_group], 1)
    allowed = group_ids[:, :, None] == group_ids[:, None, :]
    head_starts = jnp.concatenate([jnp.zeros_like(first_len), first_len], 1)
    pick_mask = slot_index[:, None, :] == head_starts[:, :, None]
    return (allowed, pick_mask)


def attn_scores(queries, key_rows, allowed):
    scores = jnp.einsum(
        "rqhe,rkhe->rhqk",
        split_heads(queries),
        split_heads(key_rows),
        preferred_element_type=jnp.float32,
    ) * HEAD_DIM ** (-0.5)
    if allowed is None:
        return scores
    return jnp.where(allowed[:, None], scores, blocked)


def attn_forward(queries, key_rows, value_rows, allowed):
    scores = attn_scores(queries, key_rows, allowed)
    maximum = jnp.max(scores, -1, keepdims=True)
    log_total = maximum + jnp.log(jnp.sum(jnp.exp(scores - maximum), -1, keepdims=True))
    weights = jnp.exp(scores - log_total).astype(jnp.bfloat16)
    mixture = jnp.einsum(
        "rhqk,rkhe->rqhe", weights, split_heads(value_rows), preferred_element_type=jnp.float32
    )
    return (join_heads(mixture).astype(jnp.bfloat16), log_total)


def attn_backward(queries, key_rows, value_rows, allowed, log_total, grad_mix):
    scores = attn_scores(queries, key_rows, allowed)
    prob_rows = jnp.exp(scores - log_total)
    grad_heads = split_heads(grad_mix)
    grad_prob = jnp.einsum(
        "rqhe,rkhe->rhqk", grad_heads, split_heads(value_rows), preferred_element_type=jnp.float32
    )
    grad_values = jnp.einsum(
        "rhqk,rqhe->rkhe",
        prob_rows.astype(jnp.bfloat16),
        grad_heads,
        preferred_element_type=jnp.float32,
    )
    grad_scores = (
        prob_rows * (grad_prob - jnp.sum(grad_prob * prob_rows, -1, keepdims=True))
    ).astype(jnp.bfloat16)
    score_scale = HEAD_DIM ** (-0.5)
    grad_queries = (
        jnp.einsum(
            "rhqk,rkhe->rqhe",
            grad_scores,
            split_heads(key_rows),
            preferred_element_type=jnp.float32,
        )
        * score_scale
    )
    grad_keys = (
        jnp.einsum(
            "rhqk,rqhe->rkhe", grad_scores, split_heads(queries), preferred_element_type=jnp.float32
        )
        * score_scale
    )
    return (
        join_heads(grad_queries).astype(jnp.bfloat16),
        join_heads(grad_keys).astype(jnp.bfloat16),
        join_heads(grad_values).astype(jnp.bfloat16),
    )


def shards(
    hidden_states,
    image_features,
    caption_lengths,
    attn_weights,
    cross_kv,
    ffn_in,
    ffn_out,
    projections,
    norm_gains,
    biases,
    ffn_bias,
    proj_bias,
    out_grad,
):
    row_count = hidden_states.shape[0]
    captions_here = 2 * row_count
    allowed, pick_mask = caption_layout(caption_lengths)
    pick_low = pick_mask.astype(jnp.bfloat16)
    pick_full = pick_mask.astype(jnp.float32)
    inputs_full = hidden_states.astype(jnp.float32)
    self_q = (matmul(hidden_states, attn_weights[0]) + biases[0]).astype(jnp.bfloat16)
    self_k = matmul(hidden_states, attn_weights[1]).astype(jnp.bfloat16)
    self_v = (matmul(hidden_states, attn_weights[2]) + biases[1]).astype(jnp.bfloat16)
    self_mix, self_total = attn_forward(self_q, self_k, self_v, allowed)
    first_sum = inputs_full + matmul(self_mix, attn_weights[3]) + biases[2]
    first_norm = layer_norm(first_sum, norm_gains[0], biases[8])
    first_low = first_norm.astype(jnp.bfloat16)
    query_low = first_low[:, :QUERIES]
    text_low = first_low[:, QUERIES:]
    cross_q = (matmul(query_low, attn_weights[4]) + biases[3]).astype(jnp.bfloat16)
    cross_k = jnp.einsum(
        "rjc,dc->rjd", image_features, cross_kv[0], preferred_element_type=jnp.float32
    ).astype(jnp.bfloat16)
    cross_v = (
        jnp.einsum("rjc,dc->rjd", image_features, cross_kv[1], preferred_element_type=jnp.float32)
        + biases[4]
    ).astype(jnp.bfloat16)
    cross_mix, cross_total = attn_forward(cross_q, cross_k, cross_v, None)
    second_sum = first_norm[:, :QUERIES] + matmul(cross_mix, attn_weights[5]) + biases[5]
    second_norm = layer_norm(second_sum, norm_gains[1], biases[9])
    second_low = second_norm.astype(jnp.bfloat16)
    query_pre = matmul(second_low, ffn_in[0]) + ffn_bias[0]
    query_act = smooth_gate(query_pre).astype(jnp.bfloat16)
    third_sum = second_norm + matmul(query_act, ffn_out[0]) + biases[6]
    query_out = layer_norm(third_sum, norm_gains[2], biases[10])
    text_pre = matmul(text_low, ffn_in[1]) + ffn_bias[1]
    text_act = smooth_gate(text_pre).astype(jnp.bfloat16)
    fourth_sum = first_norm[:, QUERIES:] + matmul(text_act, ffn_out[1]) + biases[7]
    text_out = layer_norm(fourth_sum, norm_gains[3], biases[11])
    layer_out = jnp.concatenate([query_out, text_out], 1).astype(jnp.bfloat16)
    query_out_low = query_out.astype(jnp.bfloat16)
    text_out_low = text_out.astype(jnp.bfloat16)
    query_raw = matmul(query_out_low, projections[0]) + proj_bias[0]
    query_embed = unit_rows(query_raw).astype(jnp.bfloat16)
    caption_heads = jnp.einsum(
        "rkt,rtd->rkd", pick_low, text_out_low, preferred_element_type=jnp.float32
    ).astype(jnp.bfloat16)
    caption_raw = matmul(caption_heads, projections[1]) + proj_bias[1]
    caption_embed = unit_rows(caption_raw).astype(jnp.bfloat16).reshape(captions_here, -1)
    every_caption = lax.all_gather(caption_embed, ("dp", "rep"), axis=0, tiled=True)
    sims = jnp.einsum("rqp,cp->rqc", query_embed, every_caption, preferred_element_type=jnp.float32)
    expo = jnp.exp(sharpness * (sims - 1.0))
    affinity = jnp.mean(expo, 1)
    offset = lax.axis_index(("dp", "rep")) * captions_here
    own_block = lax.dynamic_slice_in_dim(affinity, offset, captions_here, 1).reshape(
        row_count, row_count, 2
    )
    diagonal = (
        lax.broadcasted_iota(jnp.int32, (row_count, row_count), 0)
        == lax.broadcasted_iota(jnp.int32, (row_count, row_count), 1)
    ).astype(jnp.float32)
    positive = jnp.sum(own_block * diagonal[:, :, None], 1)
    row_total = jnp.sum(affinity, 1)
    partial_cols = jnp.sum(affinity, 0)
    all_cols = lax.psum(partial_cols, ("dp", "rep"))
    own_cols = lax.dynamic_slice_in_dim(all_cols, offset, captions_here, 0).reshape(row_count, 2)
    inverse_all = 1.0 / all_cols
    row_loss = (
        jnp.log(row_total)
        - jnp.log(positive[:, 0])
        + jnp.sum(jnp.log(own_cols) - jnp.log(positive), 1)
    )
    grad_affinity = loss_weight * (1.0 / row_total[:, None] + inverse_all[None, :])
    pair_weight = jnp.array([2.0, 1.0], jnp.float32)
    correction = (loss_weight * diagonal[:, :, None] * pair_weight / own_block).reshape(
        row_count, captions_here
    )
    own_grad = lax.dynamic_slice_in_dim(grad_affinity, offset, captions_here, 1) - correction
    grad_affinity = lax.dynamic_update_slice_in_dim(grad_affinity, own_grad, offset, 1)
    grad_sims = (grad_affinity[:, None, :] * expo * (sharpness / QUERIES)).astype(jnp.bfloat16)
    grad_query_embed = jnp.einsum(
        "rqc,cp->rqp", grad_sims, every_caption, preferred_element_type=jnp.float32
    )
    grad_caption_embed = lax.psum_scatter(
        jnp.einsum("rqc,rqp->cp", grad_sims, query_embed, preferred_element_type=jnp.float32),
        ("dp", "rep"),
        scatter_dimension=0,
        tiled=True,
    )
    query_raw_grad = unit_back(query_raw, grad_query_embed).astype(jnp.bfloat16)
    caption_raw_grad = unit_back(caption_raw, grad_caption_embed.reshape(row_count, 2, -1)).astype(
        jnp.bfloat16
    )
    query_proj_grad = weight_grad(query_out_low, query_raw_grad)
    caption_proj_grad = weight_grad(caption_heads, caption_raw_grad)
    grad_heads = matmul_back(caption_raw_grad, projections[1])
    grad_full = out_grad.astype(jnp.float32)
    grad_query_out = grad_full[:, :QUERIES] + matmul_back(query_raw_grad, projections[0])
    grad_text_out = grad_full[:, QUERIES:] + jnp.sum(
        pick_full[:, :, :, None] * grad_heads[:, :, None, :], 1
    )
    grad_fourth, gain_four, shift_four = norm_back(
        fourth_sum, norm_gains[3], biases[11], grad_text_out
    )
    text_branch_grad = grad_fourth.astype(jnp.bfloat16)
    text_pre_grad = gate_back(text_pre, matmul_back(text_branch_grad, ffn_out[1])).astype(
        jnp.bfloat16
    )
    grad_third, gain_three, shift_three = norm_back(
        third_sum, norm_gains[2], biases[10], grad_query_out
    )
    query_branch_grad = grad_third.astype(jnp.bfloat16)
    query_pre_grad = gate_back(query_pre, matmul_back(query_branch_grad, ffn_out[0])).astype(
        jnp.bfloat16
    )
    ffn_in_grad = jnp.stack(
        [weight_grad(second_low, query_pre_grad), weight_grad(text_low, text_pre_grad)]
    )
    ffn_out_grad = jnp.stack(
        [weight_grad(query_act, query_branch_grad), weight_grad(text_act, text_branch_grad)]
    )
    proj_grad = jnp.stack([query_proj_grad, caption_proj_grad])
    ffn_bias_grad = jnp.stack([bias_sum(query_pre_grad), bias_sum(text_pre_grad)])
    proj_bias_grad = jnp.stack([bias_sum(query_raw_grad), bias_sum(caption_raw_grad)])
    grad_second_norm = grad_third + matmul_back(query_pre_grad, ffn_in[0])
    grad_second, gain_two, shift_two = norm_back(
        second_sum, norm_gains[1], biases[9], grad_second_norm
    )
    cross_branch_grad = grad_second.astype(jnp.bfloat16)
    cross_mix_grad = matmul_back(cross_branch_grad, attn_weights[5]).astype(jnp.bfloat16)
    cross_q_grad, cross_k_grad, cross_v_grad = attn_backward(
        cross_q, cross_k, cross_v, None, cross_total, cross_mix_grad
    )
    grad_first_norm = jnp.concatenate(
        [
            grad_second + matmul_back(cross_q_grad, attn_weights[4]),
            grad_fourth + matmul_back(text_pre_grad, ffn_in[1]),
        ],
        1,
    )
    grad_first, gain_one, shift_one = norm_back(
        first_sum, norm_gains[0], biases[8], grad_first_norm
    )
    self_branch_grad = grad_first.astype(jnp.bfloat16)
    self_mix_grad = matmul_back(self_branch_grad, attn_weights[3]).astype(jnp.bfloat16)
    self_q_grad, self_k_grad, self_v_grad = attn_backward(
        self_q, self_k, self_v, allowed, self_total, self_mix_grad
    )
    input_grad = (
        grad_first
        + matmul_back(self_q_grad, attn_weights[0])
        + matmul_back(self_k_grad, attn_weights[1])
        + matmul_back(self_v_grad, attn_weights[2])
    )
    attn_grad = jnp.stack(
        [
            weight_grad(hidden_states, self_q_grad),
            weight_grad(hidden_states, self_k_grad),
            weight_grad(hidden_states, self_v_grad),
            weight_grad(self_mix, self_branch_grad),
            weight_grad(query_low, cross_q_grad),
            weight_grad(cross_mix, cross_branch_grad),
        ]
    )
    cross_grad = jnp.stack(
        [
            jnp.einsum(
                "rjd,rjc->dc", cross_k_grad, image_features, preferred_element_type=jnp.float32
            ),
            jnp.einsum(
                "rjd,rjc->dc", cross_v_grad, image_features, preferred_element_type=jnp.float32
            ),
        ]
    )
    gain_grad = jnp.stack([gain_one, gain_two, gain_three, gain_four])
    bias_grad = jnp.stack(
        [
            bias_sum(self_q_grad),
            bias_sum(self_v_grad),
            bias_sum(self_branch_grad),
            bias_sum(cross_q_grad),
            bias_sum(cross_v_grad),
            bias_sum(cross_branch_grad),
            bias_sum(query_branch_grad),
            bias_sum(text_branch_grad),
            shift_one,
            shift_two,
            shift_three,
            shift_four,
        ]
    )
    feature_sums = (
        lax.psum_scatter(attn_grad, "dp", scatter_dimension=1, tiled=True),
        lax.psum_scatter(cross_grad, "dp", scatter_dimension=1, tiled=True),
        lax.psum_scatter(ffn_in_grad, "dp", scatter_dimension=1, tiled=True),
        lax.psum_scatter(ffn_out_grad, "dp", scatter_dimension=1, tiled=True),
        lax.psum_scatter(proj_grad, "dp", scatter_dimension=1, tiled=True),
        lax.psum_scatter(gain_grad, "dp", scatter_dimension=1, tiled=True),
        lax.psum_scatter(bias_grad, "dp", scatter_dimension=1, tiled=True),
        lax.psum_scatter(ffn_bias_grad, "dp", scatter_dimension=1, tiled=True),
        lax.psum_scatter(proj_bias_grad, "dp", scatter_dimension=1, tiled=True),
    )
    summed = (
        lax.psum_scatter(
            feature_sums[0].astype(jnp.bfloat16), "rep", scatter_dimension=0, tiled=True
        ).astype(jnp.float32),
        lax.psum_scatter(
            feature_sums[1].astype(jnp.bfloat16), "rep", scatter_dimension=0, tiled=True
        ).astype(jnp.float32),
        lax.psum_scatter(
            feature_sums[2].astype(jnp.bfloat16), "rep", scatter_dimension=0, tiled=True
        ).astype(jnp.float32),
        lax.psum_scatter(
            feature_sums[3].astype(jnp.bfloat16), "rep", scatter_dimension=0, tiled=True
        ).astype(jnp.float32),
        lax.psum_scatter(
            feature_sums[4].astype(jnp.bfloat16), "rep", scatter_dimension=0, tiled=True
        ).astype(jnp.float32),
        lax.psum_scatter(
            feature_sums[5].astype(jnp.bfloat16), "rep", scatter_dimension=0, tiled=True
        ).astype(jnp.float32),
        lax.psum_scatter(
            feature_sums[6].astype(jnp.bfloat16), "rep", scatter_dimension=0, tiled=True
        ).astype(jnp.float32),
        lax.psum_scatter(
            feature_sums[7].astype(jnp.bfloat16), "rep", scatter_dimension=0, tiled=True
        ).astype(jnp.float32),
        lax.psum_scatter(
            feature_sums[8].astype(jnp.bfloat16), "rep", scatter_dimension=0, tiled=True
        ).astype(jnp.float32),
    )
    return (
        layer_out,
        row_loss,
        input_grad,
        summed[0],
        summed[1],
        summed[2],
        summed[3],
        summed[4],
        summed[5],
        summed[6],
        summed[7],
        summed[8],
    )


def solution(mesh):
    placed = (
        P(("dp", "rep"), None, None),
        P(("dp", "rep"), None, None),
        P(("dp", "rep"), None),
        P(),
        P(),
        P(),
        P(),
        P(),
        P(),
        P(),
        P(),
        P(),
        P(("dp", "rep"), None, None),
    )
    return jax.shard_map(
        shards,
        mesh=mesh,
        in_specs=placed,
        out_specs=(
            P(("dp", "rep"), None, None),
            P(("dp", "rep")),
            P(("dp", "rep"), None, None),
            P("rep", "dp", None),
            P("rep", "dp", None),
            P("rep", "dp", None),
            P("rep", "dp", None),
            P("rep", "dp", None),
            P("rep", "dp"),
            P("rep", "dp"),
            P("rep", "dp"),
            P("rep", "dp"),
        ),
        check_vma=False,
    )
```

profile of v0, /device:TPU:0, one launch (start us, length us, event | category | flops | bytes accessed | tf_op | source)
XLA Modules:
  0.0 1617.1 jit_solution(11769059240615198048)
XLA Ops:
  66.2 17.3 %fusion.7 = bf16[16,257,768]{2,1,0:T(8,128)(2,1)} fusion(bf16[16,257,1408]{2,0,1:T(8,128)(2,1)} %param.15, bf16[2,768,1408]{2,1,0:T(8,128)(2,1)} %param.18), kind=kOutput, calls=%fused_computation.20 | convolution fusion | flops 8896131072 | bytes 20058112 | tf_op jit(solution)/shard_map/rjc,dc->rjd/dot_general | solution.py:181
  83.5 16.8 %add_convert_fusion = bf16[16,257,768]{2,1,0:T(8,128)(2,1)} fusion(bf16[16,257,1408]{2,0,1:T(8,128)(2,1)} %param.15, f32[768]{0:T(1024)S(1)} %get-tuple-element.70, bf16[2,768,1408]{2,1,0:T(8,128)(2,1)} %param.18), kind=kOutput, calls=%fused_computation.4 | convolution fusion | flops 8899289088 | bytes 20061184 | tf_op jit(solution)/shard_map/rjc,dc->rjd/dot_general | solution.py:185
  100.3 11.1 copy.249
  111.5 11.2 copy.251
  128.9 15.3 multiply_convert_fusion.5
  149.2 77.3 %all_gather.3 = bf16[1024,256]{1,0:T(8,128)(2,1)} all-gather(bf16[32,256]{1,0:T(8,128)(2,1)S(1)} %reshape.413), channel_id=1, replica_groups=mesh['dp'=16,'rep'=2] {'dp','rep'}, dimensions={0}, use_global_device_ids=true | all-gather | bytes 540672 | tf_op jit(solution)/shard_map/all_gather | solution.py:210
  236.5 9.8 fusion.80
  261.7 15.7 multiply_convert_fusion.6
  285.0 36.9 %psum.7 = f32[1024]{0:T(1024)S(1)} all-reduce(f32[1024]{0:T(1024)S(1)} %get-tuple-element.64), channel_id=1, replica_groups=mesh['dp'=16,'rep'=2] {'dp','rep'}, use_global_device_ids=true, to_apply=%region_18.19 | all-reduce | flops 1024 | bytes 8192 | tf_op jit(solution)/shard_map/psum | solution.py:225
  336.7 127.9 %reduce-scatter.24.cloned.1.call-done = f32[32,256]{1,0:T(8,128)} async-done(((f32[1024,256]{1,0:T(8,128)}), f32[32,256]{1,0:T(8,128)}) %reduce-scatter.24.cloned.1.call-update) | async-done | bytes 32784 | tf_op jit(solution)/shard_map/reduce_scatter | solution.py:244
  474.9 8.5 convert_reduce_fusion.2
  495.5 11.9 multiply_reduce_fusion
  507.5 7.1 convert_reduce_fusion
  516.0 18.2 %fusion.51 = f32[1,768,1408]{2,1,0:T(8,128)} fusion(bf16[16,257,768]{1,2,0:T(8,128)(2,1)} %bitcast.298, bf16[16,257,1408]{2,0,1:T(8,128)(2,1)} %param.15), kind=kOutput, calls=%fused_computation.104 | convolution fusion | flops 8892973056 | bytes 22220800 | tf_op jit(solution)/shard_map/rjd,rjc->dc/dot_general | solution.py:330
  542.7 14.7 fusion.48
  563.7 9.1 convert_reduce_fusion.5
  585.1 9.1 convert_reduce_fusion.1
  613.3 9.2 multiply_reduce_fusion.2
  688.7 17.5 %copy.280 = f32[6,768,768]{2,0,1:T(8,128)} copy(f32[6,768,768]{1,2,0:T(8,128)} %bitcast_dynamic-update-slice_fusion.3) | data formatting | bytes 28311552 | tf_op jit(solution)/shard_map/stack | solution.py:315
  715.0 10.6 pad_maximum_fusion.1
  734.0 7.2 pad_maximum_fusion
  751.2 146.0 %reduce-scatter.26.cloned.1.call-done = f32[6,48,768]{2,0,1:T(8,128)} async-done(((f32[6,768,768]{2,0,1:T(8,128)}), f32[6,48,768]{2,0,1:T(8,128)}) %reduce-scatter.26.cloned.1.call-update) | async-done | bytes 884752 | tf_op jit(solution)/shard_map/reduce_scatter | solution.py:353
  902.5 192.7 %reduce-scatter.38.cloned.1.call-done = f32[2,192,768]{2,1,0:T(8,128)} async-done(((f32[2,3072,768]{2,1,0:T(8,128)}), f32[2,192,768]{2,1,0:T(8,128)}) %reduce-scatter.38.cloned.1.call-update) | async-done | bytes 1179664 | tf_op jit(solution)/shard_map/reduce_scatter | solution.py:356
  1108.3 184.8 %reduce-scatter.34.cloned.1.call-done = f32[2,48,3072]{2,1,0:T(8,128)} async-done(((f32[2,768,3072]{2,1,0:T(8,128)}), f32[2,48,3072]{2,1,0:T(8,128)}) %reduce-scatter.34.cloned.1.call-update) | async-done | bytes 1179664 | tf_op jit(solution)/shard_map/reduce_scatter | solution.py:355
  1302.1 48.7 %reduce-scatter.52.cloned.1.call-done = f32[16,2]{1,0:T(8,128)} async-done(((f32[256,2]{1,0:T(8,128)}), f32[16,2]{1,0:T(8,128)}) %reduce-scatter.52.cloned.1.call-update) | async-done | bytes 144
  1351.6 57.4 %reduce-scatter.46.cloned.1.call-done = f32[48,4]{1,0:T(8,128)} async-done(((f32[768,4]{1,0:T(8,128)}), f32[48,4]{1,0:T(8,128)}) %reduce-scatter.46.cloned.1.call-update) | async-done | bytes 784
  1409.8 61.8 %reduce-scatter.50.cloned.1.call-done = f32[192,2]{1,0:T(8,128)} async-done(((f32[3072,2]{1,0:T(8,128)}), f32[192,2]{1,0:T(8,128)}) %reduce-scatter.50.cloned.1.call-update) | async-done | bytes 1552
  1472.6 57.0 %reduce-scatter.48.cloned.1.call-done = f32[48,12]{1,0:T(8,128)} async-done(((f32[768,12]{1,0:T(8,128)}), f32[48,12]{1,0:T(8,128)}) %reduce-scatter.48.cloned.1.call-update) | async-done | bytes 2320
  1542.7 13.2 reduce-scatter.32.cloned.1.call-done
  1557.6 14.9 reduce-scatter.28.cloned.1.call-done
  1574.2 16.4 %reduce-scatter.40.cloned.1.call-done = bf16[1,192,768]{2,1,0:T(8,128)(2,1)} async-done(((bf16[2,192,768]{2,1,0:T(8,128)(2,1)}), bf16[1,192,768]{2,1,0:T(8,128)(2,1)}) %reduce-scatter.40.cloned.1.call-update) | async-done | bytes 294928 | tf_op jit(solution)/shard_map/reduce_scatter | solution.py:373
  1592.3 16.2 reduce-scatter.36.cloned.1.call-done
  (560 shorter events, 327.7 us)
Async XLA Ops:
  7.2 457.4 %reduce-scatter.24.cloned.1.call-start = ((), (), s32[]{:S(2)}) async-start(), calls=%async_computation.15 | async-start | bytes 1081344 | tf_op jit(solution)/shard_map/reduce_scatter | solution.py:244
  11.8 135.4 %copy-start.90 = (f32[768]{0:T(1024)}, f32[768]{0:T(1024)S(1)}, u32[]{:S(2)}) copy-start(f32[768]{0:T(1024)S(1)} %get-tuple-element.80) | copy-start | bytes 9220
  11.8 265.6 %copy-start.113 = (f32[768]{0:T(1024)}, f32[768]{0:T(1024)S(1)}, u32[]{:S(2)}) copy-start(f32[768]{0:T(1024)S(1)} %get-tuple-element.78) | copy-start | bytes 9220
  11.8 321.0 %copy-start.88 = (f32[768]{0:T(1024)}, f32[768]{0:T(1024)S(1)}, u32[]{:S(2)}) copy-start(f32[768]{0:T(1024)S(1)} %get-tuple-element.77) | copy-start | bytes 9220
  12.7 249.0 %copy-start.94 = (f32[1,3072]{1,0:T(1,128)}, f32[1,3072]{1,0:T(1,128)S(1)}, u32[]{:S(2)}) copy-start(f32[1,3072]{1,0:T(1,128)S(1)} %get-tuple-element.115) | copy-start | bytes 36868
  13.9 263.5 %copy-start.129 = (f32[768]{0:T(1024)}, f32[768]{0:T(1024)S(1)}, u32[]{:S(2)}) copy-start(f32[768]{0:T(1024)S(1)} %get-tuple-element.67) | copy-start | bytes 9220
  146.9 322.5 %copy-start.7 = (f32[16,32,768]{2,1,0:T(8,128)}, f32[16,32,768]{2,1,0:T(8,128)S(1)}, u32[]{:S(2)}) copy-start(f32[16,32,768]{2,1,0:T(8,128)S(1)} %get-tuple-element.128) | copy-start | bytes 4718596
  328.8 418.7 %reduce-scatter.42.cloned.1.call-start = ((), (), s32[]{:S(2)}) async-start(), calls=%async_computation.24 | async-start | bytes 1671168 | tf_op jit(solution)/shard_map/reduce_scatter | solution.py:357
  332.8 132.7 %copy-start.120 = (f32[16,2]{0,1:T(2,128)S(1)}, f32[16,2]{0,1:T(2,128)}, u32[]{:S(2)}) copy-start(f32[16,2]{0,1:T(2,128)} %copy-done.119) | copy-start | bytes 388
  335.4 134.0 %copy-start.89 = (f32[768]{0:T(1024)S(1)}, f32[768]{0:T(1024)}, u32[]{:S(2)}) copy-start(f32[768]{0:T(1024)} %copy-done.88) | copy-start | bytes 9220
  335.4 134.0 %copy-start.91 = (f32[768]{0:T(1024)S(1)}, f32[768]{0:T(1024)}, u32[]{:S(2)}) copy-start(f32[768]{0:T(1024)} %copy-done.90) | copy-start | bytes 9220
  515.9 233.3 %reduce-scatter.30.cloned.1.call-start = ((), (), s32[]{:S(2)}) async-start(), calls=%async_computation.18 | async-start | bytes 9191424 | tf_op jit(solution)/shard_map/reduce_scatter | solution.py:354
  563.7 333.5 %reduce-scatter.26.cloned.1.call-start = ((), (), s32[]{:S(2)}) async-start(), calls=%async_computation.16 | async-start | bytes 20054016 | tf_op jit(solution)/shard_map/reduce_scatter | solution.py:353
  706.3 389.0 %reduce-scatter.38.cloned.1.call-start = ((), (), s32[]{:S(2)}) async-start(), calls=%async_computation.22 | async-start | bytes 20054016 | tf_op jit(solution)/shard_map/reduce_scatter | solution.py:356
  725.6 567.5 %reduce-scatter.34.cloned.1.call-start = ((), (), s32[]{:S(2)}) async-start(), calls=%async_computation.20 | async-start | bytes 20054016 | tf_op jit(solution)/shard_map/reduce_scatter | solution.py:355
  741.4 609.4 %reduce-scatter.52.cloned.1.call-start = ((), (), s32[]{:S(2)}) async-start(), calls=%async_computation.29 | async-start | bytes 139264
  742.7 156.8 %copy-start.133 = (u32[32]{0:T(128)S(1)}, u32[32]{0:T(128)}, u32[]{:S(2)}) copy-start(u32[32]{0:T(128)} %constant.150) | copy-start | bytes 388
  742.8 159.6 %copy-start.103 = (f32[16,32]{1,0:T(8,128)S(1)}, f32[16,32]{1,0:T(8,128)}, u32[]{:S(2)}) copy-start(f32[16,32]{1,0:T(8,128)} %get-tuple-element.113) | copy-start | bytes 6148
  742.8 666.2 %reduce-scatter.46.cloned.1.call-start = ((), (), s32[]{:S(2)}) async-start(), calls=%async_computation.26 | async-start | bytes 417792
  743.8 727.8 %reduce-scatter.50.cloned.1.call-start = ((), (), s32[]{:S(2)}) async-start(), calls=%async_computation.28 | async-start | bytes 1671168
  745.6 351.9 %copy-start.19 = (bf16[16,32,768]{2,1,0:T(8,128)(2,1)S(1)}, bf16[16,32,768]{2,1,0:T(8,128)(2,1)}, u32[]{:S(2)}) copy-start(bf16[16,32,768]{2,1,0:T(8,128)(2,1)} %copy-done.18) | copy-start | bytes 2359300
  745.6 351.9 %copy-start.40 = (bf16[16,32,768]{2,1,0:T(8,128)(2,1)S(1)}, bf16[16,32,768]{2,1,0:T(8,128)(2,1)}, u32[]{:S(2)}) copy-start(bf16[16,32,768]{2,1,0:T(8,128)(2,1)} %copy-done.38) | copy-start | bytes 2359300
  745.6 784.0 %reduce-scatter.48.cloned.1.call-start = ((), (), s32[]{:S(2)}) async-start(), calls=%async_computation.27 | async-start | bytes 417792
  747.5 793.9 %reduce-scatter.44.cloned.1.call-start = ((), (), s32[]{:S(2)}) async-start(), calls=%async_computation.25 | async-start | bytes 73728 | tf_op jit(solution)/shard_map/reduce_scatter | solution.py:376
  749.1 349.6 %copy-start.132 = (f32[16]{0:T(128)S(1)}, f32[16]{0:T(128)}, u32[]{:S(2)}) copy-start(f32[16]{0:T(128)} %copy-done.131) | copy-start | bytes 196
  749.1 350.2 %copy-start.57 = (bf16[16,64,768]{2,1,0:T(8,128)(2,1)S(1)}, bf16[16,64,768]{2,1,0:T(8,128)(2,1)}, u32[]{:S(2)}) copy-start(bf16[16,64,768]{2,1,0:T(8,128)(2,1)} %convert_element_type.361) | copy-start | bytes 4718596
  749.1 806.8 %reduce-scatter.32.cloned.1.call-start = ((), (), s32[]{:S(2)}) async-start(), calls=%async_computation.19 | async-start | bytes 405504 | tf_op jit(solution)/shard_map/reduce_scatter | solution.py:367
  751.1 821.3 %reduce-scatter.28.cloned.1.call-start = ((), (), s32[]{:S(2)}) async-start(), calls=%async_computation.17 | async-start | bytes 663552 | tf_op jit(solution)/shard_map/reduce_scatter | solution.py:364
  899.5 691.0 %reduce-scatter.40.cloned.1.call-start = ((), (), s32[]{:S(2)}) async-start(), calls=%async_computation.23 | async-start | bytes 884736 | tf_op jit(solution)/shard_map/reduce_scatter | solution.py:373
  1097.4 511.1 %reduce-scatter.36.cloned.1.call-start = ((), (), s32[]{:S(2)}) async-start(), calls=%async_computation.21 | async-start | bytes 884736 | tf_op jit(solution)/shard_map/reduce_scatter | solution.py:370
  1103.6 191.6 %copy-start.6 = (f32[16,64,768]{2,1,0:T(8,128)S(1)}, f32[16,64,768]{2,1,0:T(8,128)}, u32[]{:S(2)}) copy-start(f32[16,64,768]{2,1,0:T(8,128)} %copy-done.5) | copy-start | bytes 9437188
  1103.6 191.7 %copy-start.76 = (f32[16,64]{1,0:T(8,128)S(1)}, f32[16,64]{1,0:T(8,128)}, u32[]{:S(2)}) copy-start(f32[16,64]{1,0:T(8,128)} %copy-done.75) | copy-start | bytes 12292
  (146 other events, 1611.8 us)
Sparse Core Ops, SparseCore 0:
  329.0 135.6 reduce-scatter.23
  516.0 55.5 reduce-scatter.41
  575.7 106.1 reduce-scatter.29
  706.4 190.7 reduce-scatter.25
  901.1 194.0 reduce-scatter.37
  1099.2 193.8 reduce-scatter.33
  1296.5 54.1 reduce-scatter.51
  1354.3 54.6 reduce-scatter.45
  1413.1 58.4 reduce-scatter.49
  1475.0 54.5 reduce-scatter.47
  1532.4 8.8 reduce-scatter.43
  1544.1 11.7 reduce-scatter.31
  1558.8 13.6 reduce-scatter.27
  1575.2 15.2 reduce-scatter.39
  1593.2 15.2 reduce-scatter.35
where the time goes:
time: 1620 us
  waiting for transfers between devices  940 us (58%)
  matrix products  286 us (18%)
  local copies, waits for them, and re-layouts  141 us (9%)
  blocking collectives  119 us (7%)
  other arithmetic  113 us (7%)
  between operations  17.8 us (1%)
    unnamed x19, waiting for transfers between devices  225 us
    reduce_scatter x1, waiting for transfers between devices, shards(): lax.psum_scatter(ffn_out_grad, 'dp', scatter_dimension=1, tiled=True)  193 us
    reduce_scatter x1, waiting for transfers between devices, shards(): lax.psum_scatter(ffn_in_grad, 'dp', scatter_dimension=1, tiled=True)  185 us
    reduce_scatter x1, waiting for transfers between devices, shards(): lax.psum_scatter(attn_grad, 'dp', scatter_dimension=1, tiled=True)  146 us
    reduce_scatter x1, waiting for transfers between devices, shards(): lax.psum_scatter(jnp.einsum('rqc,rqp->cp', grad_sims, query_embed, prefer...  128 us
    all_gather x1, blocking collectives, shards(): lax.all_gather(caption_embed, ('dp', 'rep'), axis=0, tiled=True)  77.3 us
    dot_general x12, matrix products, matmul_back(): jnp.einsum('...n,kn->...k', grad_rows, right, preferred_element_type=jnp....  55.2 us
    dot_general x12, matrix products, matmul(): jnp.einsum('...k,kn->...n', left, right, preferred_element_type=jnp.float32)  42.2 us
  transfers between devices with their start and end apart: 15, of which 13 were waited for; matrix products, arithmetic and copies ran while one was open for 17% of the time, Pallas kernels for 0%

commit v1 on v0

--- a/solution.py
+++ b/solution.py
@@ -1,3 +1,5 @@
+import functools
+
 import jax
 import jax.numpy as jnp
 from jax import lax
@@ -145,6 +147,107 @@
         join_heads(grad_keys).astype(jnp.bfloat16),
         join_heads(grad_values).astype(jnp.bfloat16),
     )
+
+
+def own_bit(stage):
+    axis, bit = stage
+    return (lax.axis_index(axis) >> bit) & 1
+
+
+def swap(values, stage, sizes):
+    axis, bit = stage
+    return lax.ppermute(values, axis, [(i, i ^ (1 << bit)) for i in range(sizes[axis])])
+
+
+def bit_stages(sizes):
+    depth = sizes["dp"].bit_length() - 1
+    return [("dp", bit) for bit in range(depth)]
+
+
+def pick(term, places):
+    array, fixed = term
+    starts = [0] * array.ndim
+    extent = list(array.shape)
+    for dim, place in fixed.items():
+        starts[dim] = place
+        extent[dim] = 1
+    for dim, place in places.items():
+        starts[dim] = place
+        extent[dim] = 1
+    return lax.dynamic_slice(array, starts, extent)
+
+
+def total(terms, places):
+    return sum(pick(term, places).astype(jnp.float32) for term in terms)
+
+
+def halve(terms, stage, dim, sizes):
+    mine = own_bit(stage)
+    send = total(terms, {dim: 1 - mine}).astype(jnp.bfloat16)
+    arrived = swap(send, stage, sizes)
+    kept = [(array, {**fixed, dim: mine}) for array, fixed in terms]
+    return kept + [(arrived, {})]
+
+
+def pair_scatter(first, second, order, sizes):
+    depth = sizes["dp"].bit_length() - 1
+
+    def spread(array):
+        rows, cols = array.shape
+        return array.reshape((2,) * depth + (rows // sizes["dp"], cols))
+
+    streams = [[(spread(first), {})], [(spread(second), {})]]
+    for stage in order:
+        if stage[0] == "rep":
+            mine = own_bit(stage)
+            sums = [total(terms, {}) for terms in streams]
+            send = jnp.where(mine == 0, sums[1], sums[0]).astype(jnp.bfloat16)
+            keep = jnp.where(mine == 0, sums[0], sums[1])
+            streams = [[(keep, {}), (swap(send, stage, sizes), {})]]
+        else:
+            dim = depth - 1 - stage[1]
+            streams = [halve(terms, stage, dim, sizes) for terms in streams]
+    result = total(streams[0], {})
+    return result.reshape(result.shape[-2:])
+
+
+def orders(sizes):
+    stages = bit_stages(sizes)
+    head, mid, tail = stages[:1], stages[1:3], stages[3:]
+    ring = mid + [("rep", 0)]
+    return [head + ring[k:] + ring[:k] + tail for k in range(3)]
+
+
+def scatter_parts(first, second, sizes):
+    cols = first.shape[1]
+    lanes = cols // 128
+    cuts = [0, 128 * ((lanes + 2) // 3), 128 * ((2 * lanes + 2) // 3), cols]
+    done = [
+        pair_scatter(first[:, a:b], second[:, a:b], order, sizes)
+        for a, b, order in zip(cuts[:-1], cuts[1:], orders(sizes))
+    ]
+    return jnp.concatenate(done, 1)
+
+
+def gather_rows(values, sizes):
+    stages = [("rep", 0)] + bit_stages(sizes)
+    for stage in stages:
+        other = swap(values, stage, sizes)
+        low = own_bit(stage) == 0
+        values = jnp.concatenate([jnp.where(low, values, other), jnp.where(low, other, values)], 0)
+    return values
+
+
+def scatter_rows(values, sizes):
+    stages = bit_stages(sizes)
+    depth = len(stages)
+    count = values.shape[0] // (2 * sizes["dp"])
+    terms = [(values.reshape((2,) * (depth + 1) + (count, values.shape[1])), {})]
+    for stage in stages:
+        terms = halve(terms, stage, depth - 1 - stage[1], sizes)
+    terms = halve(terms, ("rep", 0), depth, sizes)
+    result = total(terms, {})
+    return result.reshape(result.shape[-2:])
 
 
 def shards(
@@ -161,6 +264,7 @@
     ffn_bias,
     proj_bias,
     out_grad,
+    sizes,
 ):
     row_count = hidden_states.shape[0]
     captions_here = 2 * row_count
@@ -177,6 +281,17 @@
     first_low = first_norm.astype(jnp.bfloat16)
     query_low = first_low[:, :QUERIES]
     text_low = first_low[:, QUERIES:]
+    text_pre = matmul(text_low, ffn_in[1]) + ffn_bias[1]
+    text_act = smooth_gate(text_pre).astype(jnp.bfloat16)
+    fourth_sum = first_norm[:, QUERIES:] + matmul(text_act, ffn_out[1]) + biases[7]
+    text_out = layer_norm(fourth_sum, norm_gains[3], biases[11])
+    text_out_low = text_out.astype(jnp.bfloat16)
+    caption_heads = jnp.einsum(
+        "rkt,rtd->rkd", pick_low, text_out_low, preferred_element_type=jnp.float32
+    ).astype(jnp.bfloat16)
+    caption_raw = matmul(caption_heads, projections[1]) + proj_bias[1]
+    caption_embed = unit_rows(caption_raw).astype(jnp.bfloat16).reshape(captions_here, -1)
+    every_caption = gather_rows(caption_embed, sizes)
     cross_q = (matmul(query_low, attn_weights[4]) + biases[3]).astype(jnp.bfloat16)
     cross_k = jnp.einsum(
         "rjc,dc->rjd", image_features, cross_kv[0], preferred_element_type=jnp.float32
@@ -193,21 +308,10 @@
     query_act = smooth_gate(query_pre).astype(jnp.bfloat16)
     third_sum = second_norm + matmul(query_act, ffn_out[0]) + biases[6]
     query_out = layer_norm(third_sum, norm_gains[2], biases[10])
-    text_pre = matmul(text_low, ffn_in[1]) + ffn_bias[1]
-    text_act = smooth_gate(text_pre).astype(jnp.bfloat16)
-    fourth_sum = first_norm[:, QUERIES:] + matmul(text_act, ffn_out[1]) + biases[7]
-    text_out = layer_norm(fourth_sum, norm_gains[3], biases[11])
     layer_out = jnp.concatenate([query_out, text_out], 1).astype(jnp.bfloat16)
     query_out_low = query_out.astype(jnp.bfloat16)
-    text_out_low = text_out.astype(jnp.bfloat16)
     query_raw = matmul(query_out_low, projections[0]) + proj_bias[0]
     query_embed = unit_rows(query_raw).astype(jnp.bfloat16)
-    caption_heads = jnp.einsum(
-        "rkt,rtd->rkd", pick_low, text_out_low, preferred_element_type=jnp.float32
-    ).astype(jnp.bfloat16)
-    caption_raw = matmul(caption_heads, projections[1]) + proj_bias[1]
-    caption_embed = unit_rows(caption_raw).astype(jnp.bfloat16).reshape(captions_here, -1)
-    every_caption = lax.all_gather(caption_embed, ("dp", "rep"), axis=0, tiled=True)
     sims = jnp.einsum("rqp,cp->rqc", query_embed, every_caption, preferred_element_type=jnp.float32)
     expo = jnp.exp(sharpness * (sims - 1.0))
     affinity = jnp.mean(expo, 1)
@@ -222,7 +326,17 @@
     positive = jnp.sum(own_block * diagonal[:, :, None], 1)
     row_total = jnp.sum(affinity, 1)
     partial_cols = jnp.sum(affinity, 0)
-    all_cols = lax.psum(partial_cols, ("dp", "rep"))
+    world = sizes["dp"] * sizes["rep"]
+    all_cols = jnp.sum(
+        lax.all_to_all(
+            jnp.broadcast_to(partial_cols[None], (world,) + partial_cols.shape),
+            ("dp", "rep"),
+            0,
+            0,
+            tiled=True,
+        ),
+        0,
+    )
     own_cols = lax.dynamic_slice_in_dim(all_cols, offset, captions_here, 0).reshape(row_count, 2)
     inverse_all = 1.0 / all_cols
     row_loss = (
@@ -241,11 +355,11 @@
     grad_query_embed = jnp.einsum(
         "rqc,cp->rqp", grad_sims, every_caption, preferred_element_type=jnp.float32
     )
-    grad_caption_embed = lax.psum_scatter(
-        jnp.einsum("rqc,rqp->cp", grad_sims, query_embed, preferred_element_type=jnp.float32),
-        ("dp", "rep"),
-        scatter_dimension=0,
-        tiled=True,
+    grad_caption_embed = scatter_rows(
+        jnp.einsum("rqc,rqp->cp", grad_sims, query_embed, preferred_element_type=jnp.float32).astype(
+            jnp.bfloat16
+        ),
+        sizes,
     )
     query_raw_grad = unit_back(query_raw, grad_query_embed).astype(jnp.bfloat16)
     caption_raw_grad = unit_back(caption_raw, grad_caption_embed.reshape(row_count, 2, -1)).astype(
@@ -273,13 +387,20 @@
     query_pre_grad = gate_back(query_pre, matmul_back(query_branch_grad, ffn_out[0])).astype(
         jnp.bfloat16
     )
-    ffn_in_grad = jnp.stack(
-        [weight_grad(second_low, query_pre_grad), weight_grad(text_low, text_pre_grad)]
-    )
-    ffn_out_grad = jnp.stack(
-        [weight_grad(query_act, query_branch_grad), weight_grad(text_act, text_branch_grad)]
-    )
-    proj_grad = jnp.stack([query_proj_grad, caption_proj_grad])
+    low = jnp.bfloat16
+    ffn_in_grad = scatter_parts(
+        weight_grad(second_low, query_pre_grad).astype(low),
+        weight_grad(text_low, text_pre_grad).astype(low),
+        sizes,
+    )
+    ffn_out_grad = scatter_parts(
+        weight_grad(query_act, query_branch_grad).astype(low),
+        weight_grad(text_act, text_branch_grad).astype(low),
+        sizes,
+    )
+    proj_grad = pair_scatter(
+        query_proj_grad.astype(low), caption_proj_grad.astype(low), orders(sizes)[0], sizes
+    )
     ffn_bias_grad = jnp.stack([bias_sum(query_pre_grad), bias_sum(text_pre_grad)])
     proj_bias_grad = jnp.stack([bias_sum(query_raw_grad), bias_sum(caption_raw_grad)])
     grad_second_norm = grad_third + matmul_back(query_pre_grad, ffn_in[0])
@@ -312,25 +433,25 @@
         + matmul_back(self_k_grad, attn_weights[1])
         + matmul_back(self_v_grad, attn_weights[2])
     )
+    attn_pairs = (
+        (weight_grad(hidden_states, self_q_grad), weight_grad(self_mix, self_branch_grad)),
+        (weight_grad(hidden_states, self_k_grad), weight_grad(query_low, cross_q_grad)),
+        (weight_grad(hidden_states, self_v_grad), weight_grad(cross_mix, cross_branch_grad)),
+    )
     attn_grad = jnp.stack(
         [
-            weight_grad(hidden_states, self_q_grad),
-            weight_grad(hidden_states, self_k_grad),
-            weight_grad(hidden_states, self_v_grad),
-            weight_grad(self_mix, self_branch_grad),
-            weight_grad(query_low, cross_q_grad),
-            weight_grad(cross_mix, cross_branch_grad),
+            pair_scatter(one.astype(low), two.astype(low), order, sizes)
+            for (one, two), order in zip(attn_pairs, orders(sizes))
         ]
     )
-    cross_grad = jnp.stack(
-        [
-            jnp.einsum(
-                "rjd,rjc->dc", cross_k_grad, image_features, preferred_element_type=jnp.float32
-            ),
-            jnp.einsum(
-                "rjd,rjc->dc", cross_v_grad, image_features, preferred_element_type=jnp.float32
-            ),
-        ]
+    cross_grad = scatter_parts(
+        jnp.einsum(
+            "rjd,rjc->dc", cross_k_grad, image_features, preferred_element_type=jnp.float32
+        ).astype(low),
+        jnp.einsum(
+            "rjd,rjc->dc", cross_v_grad, image_features, preferred_element_type=jnp.float32
+        ).astype(low),
+        sizes,
     )
     gain_grad = jnp.stack([gain_one, gain_two, gain_three, gain_four])
     bias_grad = jnp.stack(
@@ -349,59 +470,34 @@
             shift_four,
         ]
     )
-    feature_sums = (
-        lax.psum_scatter(attn_grad, "dp", scatter_dimension=1, tiled=True),
-        lax.psum_scatter(cross_grad, "dp", scatter_dimension=1, tiled=True),
-        lax.psum_scatter(ffn_in_grad, "dp", scatter_dimension=1, tiled=True),
-        lax.psum_scatter(ffn_out_grad, "dp", scatter_dimension=1, tiled=True),
-        lax.psum_scatter(proj_grad, "dp", scatter_dimension=1, tiled=True),
-        lax.psum_scatter(gain_grad, "dp", scatter_dimension=1, tiled=True),
-        lax.psum_scatter(bias_grad, "dp", scatter_dimension=1, tiled=True),
-        lax.psum_scatter(ffn_bias_grad, "dp", scatter_dimension=1, tiled=True),
-        lax.psum_scatter(proj_bias_grad, "dp", scatter_dimension=1, tiled=True),
-    )
-    summed = (
-        lax.psum_scatter(
-            feature_sums[0].astype(jnp.bfloat16), "rep", scatter_dimension=0, tiled=True
-        ).astype(jnp.float32),
-        lax.psum_scatter(
-            feature_sums[1].astype(jnp.bfloat16), "rep", scatter_dimension=0, tiled=True
-        ).astype(jnp.float32),
-        lax.psum_scatter(
-            feature_sums[2].astype(jnp.bfloat16), "rep", scatter_dimension=0, tiled=True
-        ).astype(jnp.float32),
-        lax.psum_scatter(
-            feature_sums[3].astype(jnp.bfloat16), "rep", scatter_dimension=0, tiled=True
-        ).astype(jnp.float32),
-        lax.psum_scatter(
-            feature_sums[4].astype(jnp.bfloat16), "rep", scatter_dimension=0, tiled=True
-        ).astype(jnp.float32),
-        lax.psum_scatter(
-            feature_sums[5].astype(jnp.bfloat16), "rep", scatter_dimension=0, tiled=True
-        ).astype(jnp.float32),
-        lax.psum_scatter(
-            feature_sums[6].astype(jnp.bfloat16), "rep", scatter_dimension=0, tiled=True
-        ).astype(jnp.float32),
-        lax.psum_scatter(
-            feature_sums[7].astype(jnp.bfloat16), "rep", scatter_dimension=0, tiled=True
-        ).astype(jnp.float32),
-        lax.psum_scatter(
-            feature_sums[8].astype(jnp.bfloat16), "rep", scatter_dimension=0, tiled=True
-        ).astype(jnp.float32),
-    )
+    vectors = (gain_grad, bias_grad, ffn_bias_grad, proj_bias_grad)
+
+    def deal(array):
+        mats, cols = array.shape
+        cut = array.reshape(sizes["rep"], mats // sizes["rep"], sizes["dp"], cols // sizes["dp"])
+        return cut.transpose(2, 0, 1, 3).reshape(world, -1)
+
+    dealt = jnp.concatenate([deal(array) for array in vectors], 1)
+    arrived = jnp.sum(lax.all_to_all(dealt, ("dp", "rep"), 0, 0, tiled=True), 0)
+    small = []
+    start = 0
+    for array in vectors:
+        mats, cols = array.shape[0] // sizes["rep"], array.shape[1] // sizes["dp"]
+        small.append(arrived[start : start + mats * cols].reshape(mats, cols))
+        start += mats * cols
     return (
         layer_out,
         row_loss,
         input_grad,
-        summed[0],
-        summed[1],
-        summed[2],
-        summed[3],
-        summed[4],
-        summed[5],
-        summed[6],
-        summed[7],
-        summed[8],
+        attn_grad,
+        cross_grad[None],
+        ffn_in_grad[None],
+        ffn_out_grad[None],
+        proj_grad[None],
+        small[0],
+        small[1],
+        small[2],
+        small[3],
     )
 
 
@@ -421,8 +517,9 @@
         P(),
         P(("dp", "rep"), None, None),
     )
+    sizes = dict(mesh.shape)
     return jax.shard_map(
-        shards,
+        functools.partial(shards, sizes=sizes),
         mesh=mesh,
         in_specs=placed,
         out_specs=(

time: 1620 us -> 874 us (0.54)
  waiting for transfers between devices: 940 us -> 195 us
  blocking collectives: 119 us -> 0 us
  starting transfers between devices: 1.09 us -> 111 us
  local copies, waits for them, and re-layouts: 141 us -> 166 us
    reduce_scatter x11 -> x0, waiting for transfers between devices: 714 us -> none  [the longest x1 193 us: shards(): lax.psum_scatter(ffn_out_grad, 'dp', scatter_dimension=1, tiled=True)]
    unnamed x19 -> x0, waiting for transfers between devices: 225 us -> none
    ppermute x0 -> x102, waiting for transfers between devices: none -> 190 us  [swap(): lax.ppermute(values, axis, [(i, i ^ 1 << bit) for i in range(sizes[axis])])]
    ppermute x0 -> x102, starting transfers between devices: none -> 102 us  [swap(): lax.ppermute(values, axis, [(i, i ^ 1 << bit) for i in range(sizes[axis])])]
    all_gather x1 -> x0, blocking collectives: 77.3 us -> none  [shards(): lax.all_gather(caption_embed, ('dp', 'rep'), axis=0, tiled=True)]
    psum x1 -> x0, blocking collectives: 36.9 us -> none  [shards(): all_cols = lax.psum(partial_cols, ('dp', 'rep'))]
    dynamic_slice x0 -> x27, local copies, waits for them, and re-layouts: none -> 25 us  [pick(): return lax.dynamic_slice(array, starts, extent)]
    another operation x7, other arithmetic: 25.9 us -> 3.05 us  [the longest x1 10.6 us: shards(): jnp.stack([weight_grad(query_act, query_branch_grad), weight_grad(text_ac...]
  transfers between devices with their start and end apart: 15 -> 104, of which waited for: 13 -> 46; matrix products, arithmetic and copies ran while one was open for 17% -> 49% of each run, Pallas kernels for 0% -> 0%
where the time goes in v1:
time: 874 us; the launch traced here: 867 us
  matrix products  290 us (33%)
  waiting for transfers between devices  195 us (22%)
  local copies, waits for them, and re-layouts  166 us (19%)
  starting transfers between devices  111 us (13%)
  other arithmetic  102 us (12%)
    ppermute x102, waiting for transfers between devices, swap(): lax.ppermute(values, axis, [(i, i ^ 1 << bit) for i in range(sizes[axis])])  190 us
    ppermute x102, starting transfers between devices, swap(): lax.ppermute(values, axis, [(i, i ^ 1 << bit) for i in range(sizes[axis])])  102 us
    dot_general x12, matrix products, matmul_back(): jnp.einsum('...n,kn->...k', grad_rows, right, preferred_element_type=jnp....  50.6 us
    dot_general x12, matrix products, matmul(): jnp.einsum('...k,kn->...n', left, right, preferred_element_type=jnp.float32)  45.6 us
    dot_general x12, matrix products, weight_grad(): jnp.einsum('tk,tn->kn', flat_left, flat_grad, preferred_element_type=jnp....  37.6 us
    reshape x6, local copies, waits for them, and re-layouts, split_heads(): return values.reshape(values.shape[:-1] + (HEADS, HEAD_DIM))  27.5 us
    dynamic_slice x27, local copies, waits for them, and re-layouts, pick(): return lax.dynamic_slice(array, starts, extent)  25 us
    dot_general x2, matrix products, attn_backward(): jnp.einsum('rqhe,rkhe->rhqk', grad_heads, split_heads(value_rows), prefer...  23.7 us
  transfers between devices with their start and end apart: 104, of which 46 were waited for; matrix products, arithmetic and copies ran while one was open for 49% of the time, Pallas kernels for 0%

profile of v1, /device:TPU:0, one launch (start us, length us, event | category | flops | bytes accessed | tf_op | source)
XLA Modules:
  0.0 867.3 jit_solution(6066827373484622185)
XLA Ops:
  23.1 5.9 reshape.565
  51.5 7.9 fusion.58
  59.4 15.3 %multiply_convert_fusion.5 = (bf16[16,32,3072]{2,1,0:T(8,128)(2,1)S(1)}, f32[16,32,3072]{2,1,0:T(8,128)}) fusion(f32[16,32,3072]{2,1,0:T(8,128)S(1)} %get-tuple-element.138, f32[3072]{0:T(1024)S(1)} %bitcast.454, u16[32,3072]{1,0:T(8,128)(2,1)S(1)} %get-tuple-element.15, u16[32,3072]{1,0:T(8,128)(2,1)S(1)} %get-tuple-element.14), kind=kLoop, calls=%fused_computation.44 | loop fusion | flops 111673344 | bytes 16134144 | tf_op jit(solution)/shard_map/convert_element_type | solution.py:285
  88.4 17.6 %fusion.7 = bf16[16,257,768]{2,1,0:T(8,128)(2,1)} fusion(bf16[16,257,1408]{2,0,1:T(8,128)(2,1)} %param.15, bf16[2,768,1408]{2,1,0:T(8,128)(2,1)} %param.18), kind=kOutput, calls=%fused_computation.21 | convolution fusion | flops 8896131072 | bytes 20058112 | tf_op jit(solution)/shard_map/rjc,dc->rjd/dot_general | solution.py:296
  106.0 16.8 %add_convert_fusion = bf16[16,257,768]{2,1,0:T(8,128)(2,1)} fusion(bf16[16,257,1408]{2,0,1:T(8,128)(2,1)} %param.15, f32[768]{0:T(1024)S(1)} %get-tuple-element.34, bf16[2,768,1408]{2,1,0:T(8,128)(2,1)} %param.18), kind=kOutput, calls=%fused_computation.2 | convolution fusion | flops 8899289088 | bytes 20061184 | tf_op jit(solution)/shard_map/rjc,dc->rjd/dot_general | solution.py:300
  122.8 11.1 %copy.232 = bf16[16,257,768]{1,2,0:T(8,128)(2,1)} copy(bf16[16,257,768]{2,1,0:T(8,128)(2,1)} %add_convert_fusion) | data formatting | bytes 12632064 | tf_op jit(solution)/shard_map/convert_element_type | solution.py:302
  134.0 11.1 %copy.234 = bf16[16,257,768]{1,2,0:T(8,128)(2,1)} copy(bf16[16,257,768]{2,1,0:T(8,128)(2,1)} %fusion.7) | data formatting | bytes 12632064 | tf_op jit(solution)/shard_map/convert_element_type | solution.py:298
  153.8 11.0 %fusion.78 = bf16[16,32,12,64]{3,1,2,0:T(8,128)(2,1)} fusion(bf16[16,257,12,64]{1,3,2,0:T(8,128)(2,1)} %bitcast.338, f32[16,12,32,257]{3,2,1,0:T(8,128)} %copy-done, f32[16,12,32]{2,1,0:T(8,128)S(1)} %log_add_fusion), kind=kOutput, calls=%fused_computation.183 | convolution fusion | flops 207243264 | bytes 13443072 | tf_op jit(solution)/shard_map/rhqk,rkhe->rqhe/dot_general | solution.py:107
  172.2 6.9 fusion.57
  179.1 15.2 %multiply_convert_fusion.6 = (bf16[16,32,3072]{2,1,0:T(8,128)(2,1)S(1)}, f32[16,32,3072]{2,1,0:T(8,128)}) fusion(f32[16,32,3072]{2,1,0:T(8,128)S(1)} %get-tuple-element.145, f32[3072]{0:T(1024)S(1)} %bitcast.457, u16[32,3072]{1,0:T(8,128)(2,1)S(1)} %get-tuple-element.13, u16[32,3072]{1,0:T(8,128)(2,1)S(1)} %get-tuple-element.12), kind=kLoop, calls=%fused_computation.57 | loop fusion | flops 111673344 | bytes 16134144 | tf_op jit(solution)/shard_map/convert_element_type | solution.py:308
  214.6 9.6 %collective-permute-done.4 = bf16[512,256]{1,0:T(8,128)(2,1)S(1)} collective-permute-done((bf16[512,256]{1,0:T(8,128)(2,1)S(1)}, bf16[512,256]{1,0:T(8,128)(2,1)S(1)}, u32[]{:S(2)}, u32[]{:S(2)}) %collective-permute-start.4) | collective-permute-done | bytes 262176 | tf_op jit(solution)/shard_map/ppermute | solution.py:159
  251.5 6.5 convert_reduce_fusion.2
  258.0 7.1 multiply_reduce_fusion.9
  338.7 14.6 %multiply_reduce_fusion = (f32[16,12,32]{2,1,0:T(8,128)S(1)}, f32[16,12,32,257]{3,2,1,0:T(8,128)}) fusion(f32[16,12,32,257]{3,2,1,0:T(8,128)} %copy-done, f32[16,12,32]{2,1,0:T(8,128)S(1)} %log_add_fusion, bf16[16,257,12,64]{1,3,2,0:T(8,128)(2,1)} %bitcast.339, bf16[16,32,12,64]{3,2,1,0:T(8,128)(2,1)} %reshape.571), kind=kOutput, calls=%fused_computation.10 | convolution fusion | flops 208422912 | bytes 19783680 | tf_op jit(solution)/shard_map/rqhe,rkhe->rhqk/dot_general | solution.py:117
  353.3 8.3 convert_reduce_fusion
  361.6 17.3 %bitcast_convert_fusion.4 = bf16[768,1408]{1,0:T(8,128)(2,1)} fusion(bf16[16,257,768]{1,2,0:T(8,128)(2,1)} %bitcast.348, bf16[16,257,1408]{2,0,1:T(8,128)(2,1)} %param.15), kind=kOutput, calls=%fused_computation.92 | convolution fusion | flops 8894054400 | bytes 20058112 | tf_op jit(solution)/shard_map/rjd,rjc->dc/dot_general | solution.py:451
  387.7 8.6 convert_reduce_fusion.5
  413.0 6.4 convert_reduce_fusion.1
  440.9 6.0 reshape.573
  447.0 9.1 %multiply_reduce_fusion.2 = (f32[16,12,64]{2,1,0:T(8,128)S(1)}, f32[16,12,64,64]{2,3,1,0:T(8,128)S(1)}) fusion(f32[16,12,64,64]{2,3,1,0:T(8,128)} %copy-done.3, f32[16,12,64]{2,1,0:T(8,128)S(1)} %copy-done.77, pred[16,64,64]{1,2,0:T(8,128)(4,1)S(1)} %copy-done.67, bf16[16,64,12,64]{3,2,1,0:T(8,128)(2,1)} %reshape.563, bf16[16,64,12,64]{3,2,1,0:T(8,128)(2,1)} %reshape.573), kind=kOutput, calls=%fused_computation.41 | convolution fusion | flops 104583168 | bytes 9601024 | tf_op jit(solution)/shard_map/rqhe,rkhe->rhqk/dot_general | solution.py:117
  456.1 6.2 convert_reduce_fusion.3
  477.1 6.2 convert_element_type.1385
  502.1 6.1 convert_element_type.1382
  540.4 15.9 %bitcast_convert_fusion.5 = bf16[768,1408]{1,0:T(8,128)(2,1)S(1)} fusion(bf16[16,257,768]{1,2,0:T(8,128)(2,1)} %bitcast.349, bf16[16,257,1408]{2,0,1:T(8,128)(2,1)} %param.15), kind=kOutput, calls=%fused_computation.93 | convolution fusion | flops 8894054400 | bytes 20058112 | tf_op jit(solution)/shard_map/rjd,rjc->dc/dot_general | solution.py:448
  640.8 13.2 %collective-permute-done.35 = bf16[2,2,1,1,48,512]{5,4,3,2,1,0:T(8,128)(2,1)S(1)} collective-permute-done((bf16[2,2,1,1,48,512]{5,4,3,2,1,0:T(8,128)(2,1)S(1)}, bf16[2,2,1,1,48,512]{5,4,3,2,1,0:T(8,128)(2,1)S(1)}, u32[]{:S(2)}, u32[]{:S(2)}) %collective-permute-start.35) | collective-permute-done | bytes 196640 | tf_op jit(solution)/shard_map/ppermute | solution.py:159
  685.7 17.6 %collective-permute-done.50 = bf16[2,1,1,1,48,384]{5,4,3,2,1,0:T(8,128)(2,1)S(1)} collective-permute-done((bf16[2,1,1,1,48,384]{5,4,3,2,1,0:T(8,128)(2,1)S(1)}, bf16[2,1,1,1,48,384]{5,4,3,2,1,0:T(8,128)(2,1)S(1)}, u32[]{:S(2)}, u32[]{:S(2)}) %collective-permute-start.50) | collective-permute-done | bytes 73760 | tf_op jit(solution)/shard_map/ppermute | solution.py:159
  715.8 7.5 collective-permute-done.14
  754.2 9.4 %collective-permute-done.22 = bf16[2,1,2,1,48,768]{5,4,3,2,1,0:T(8,128)(2,1)S(1)} collective-permute-done((bf16[2,1,2,1,48,768]{5,4,3,2,1,0:T(8,128)(2,1)S(1)}, bf16[2,1,2,1,48,768]{5,4,3,2,1,0:T(8,128)(2,1)S(1)}, u32[]{:S(2)}, u32[]{:S(2)}) %collective-permute-start.22) | collective-permute-done | bytes 294944 | tf_op jit(solution)/shard_map/ppermute | solution.py:159
  797.2 13.7 %collective-permute-done.85 = bf16[2,1,2,1,192,256]{5,4,3,2,1,0:T(8,128)(2,1)S(1)} collective-permute-done((bf16[2,1,2,1,192,256]{5,4,3,2,1,0:T(8,128)(2,1)S(1)}, bf16[2,1,2,1,192,256]{5,4,3,2,1,0:T(8,128)(2,1)S(1)}, u32[]{:S(2)}, u32[]{:S(2)}) %collective-permute-start.85) | collective-permute-done | bytes 393248 | tf_op jit(solution)/shard_map/ppermute | solution.py:159
  829.2 6.2 collective-permute-done.59
  835.5 6.0 collective-permute-done.30
  845.5 6.5 collective-permute-done.87
  (915 shorter events, 536.4 us)
Async XLA Ops:
  79.7 119.2 %collective-permute-start = (bf16[32,256]{1,0:T(8,128)(2,1)S(1)}, bf16[32,256]{1,0:T(8,128)(2,1)S(1)}, u32[]{:S(2)}, u32[]{:S(2)}) collective-permute-start(bf16[32,256]{1,0:T(8,128)(2,1)S(1)} %reshape.569), channel_id=1, source_target_pairs={{0,1},{1,0},{2,3},{3,2},{4,5},{5,4},{6,7},{7,6},{8,9},{9,8},{10,11... | collective-permute-start | bytes 49160 | tf_op jit(solution)/shard_map/ppermute | solution.py:159
  276.6 27.8 %collective-permute-start.94 = (bf16[2,2,2,1,48,256]{5,4,3,2,1,0:T(8,128)(2,1)}, bf16[2,2,2,1,48,256]{5,4,3,2,1,0:T(8,128)(2,1)}, u32[]{:S(2)}, u32[]{:S(2)}) collective-permute-start(bf16[2,2,2,1,48,256]{5,4,3,2,1,0:T(8,128)(2,1)} %constant_dynamic-slice_fusion.46), channel_id=1, source_target_pairs={{0,2},{2,0},{4,6},{6,4},{8,10},{10,8},{12,14},{14,12},{16,18},{18,... | collective-permute-start | bytes 589832 | tf_op jit(solution)/shard_map/ppermute | solution.py:159
  285.1 305.4 %collective-permute-start.60 = (bf16[2,2,2,1,48,1024]{5,4,3,2,1,0:T(8,128)(2,1)}, bf16[2,2,2,1,48,1024]{5,4,3,2,1,0:T(8,128)(2,1)}, u32[]{:S(2)}, u32[]{:S(2)}) collective-permute-start(bf16[2,2,2,1,48,1024]{5,4,3,2,1,0:T(8,128)(2,1)} %constant_dynamic-slice_fusion), channel_id=1, source_target_pairs={{0,2},{2,0},{4,6},{6,4},{8,10},{10,8},{12,14},{14,12},{16,18},{18,... | collective-permute-start | bytes 2359304 | tf_op jit(solution)/shard_map/ppermute | solution.py:159
  289.4 302.5 %collective-permute-start.52 = (bf16[2,2,2,1,48,1024]{5,4,3,2,1,0:T(8,128)(2,1)}, bf16[2,2,2,1,48,1024]{5,4,3,2,1,0:T(8,128)(2,1)}, u32[]{:S(2)}, u32[]{:S(2)}) collective-permute-start(bf16[2,2,2,1,48,1024]{5,4,3,2,1,0:T(8,128)(2,1)} %constant_dynamic-slice_fusion.7), channel_id=1, source_target_pairs={{0,2},{2,0},{4,6},{6,4},{8,10},{10,8},{12,14},{14,12},{16,18},{18,... | collective-permute-start | bytes 2359304 | tf_op jit(solution)/shard_map/ppermute | solution.py:159
  303.1 290.6 %collective-permute-start.81 = (bf16[2,2,2,1,192,256]{5,4,3,2,1,0:T(8,128)(2,1)}, bf16[2,2,2,1,192,256]{5,4,3,2,1,0:T(8,128)(2,1)}, u32[]{:S(2)}, u32[]{:S(2)}) collective-permute-start(bf16[2,2,2,1,192,256]{5,4,3,2,1,0:T(8,128)(2,1)} %constant_dynamic-slice_fusion.49), channel_id=1, source_target_pairs={{0,2},{2,0},{4,6},{6,4},{8,10},{10,8},{12,14},{14,12},{16,18},{18,... | collective-permute-start | bytes 2359304 | tf_op jit(solution)/shard_map/ppermute | solution.py:159
  303.1 292.1 %collective-permute-start.73 = (bf16[2,2,2,1,192,256]{5,4,3,2,1,0:T(8,128)(2,1)}, bf16[2,2,2,1,192,256]{5,4,3,2,1,0:T(8,128)(2,1)}, u32[]{:S(2)}, u32[]{:S(2)}) collective-permute-start(bf16[2,2,2,1,192,256]{5,4,3,2,1,0:T(8,128)(2,1)} %constant_dynamic-slice_fusion.2), channel_id=1, source_target_pairs={{0,2},{2,0},{4,6},{6,4},{8,10},{10,8},{12,14},{14,12},{16,18},{18,... | collective-permute-start | bytes 2359304 | tf_op jit(solution)/shard_map/ppermute | solution.py:159
  517.6 70.2 %collective-permute-start.97 = (bf16[2,2,2,1,48,256]{5,4,3,2,1,0:T(8,128)(2,1)}, bf16[2,2,2,1,48,256]{5,4,3,2,1,0:T(8,128)(2,1)}, u32[]{:S(2)}, u32[]{:S(2)}) collective-permute-start(bf16[2,2,2,1,48,256]{5,4,3,2,1,0:T(8,128)(2,1)} %constant_dynamic-slice_fusion.51), channel_id=1, source_target_pairs={{0,2},{2,0},{4,6},{6,4},{8,10},{10,8},{12,14},{14,12},{16,18},{18,... | collective-permute-start | bytes 589832 | tf_op jit(solution)/shard_map/ppermute | solution.py:159
  536.1 48.2 %all-to-all-start.1 = ((f32[32,1,592]{2,1,0:T(1,128)}), f32[32,1,592]{2,1,0:T(1,128)}, u32[]{:S(2)}, u32[]{:S(2)}) async-start(f32[32,1,592]{2,1,0:T(1,128)} %copy.270), calls=%async_computation.1 | async-start | bytes 163840 | tf_op jit(solution)/shard_map/all_to_all | solution.py:481
  590.5 27.1 %collective-permute-start.26 = (bf16[2,2,2,1,48,768]{5,4,3,2,1,0:T(8,128)(2,1)}, bf16[2,2,2,1,48,768]{5,4,3,2,1,0:T(8,128)(2,1)S(1)}, u32[]{:S(2)}, u32[]{:S(2)}) collective-permute-start(bf16[2,2,2,1,48,768]{5,4,3,2,1,0:T(8,128)(2,1)} %constant_dynamic-slice_fusion.36), channel_id=1, source_target_pairs={{0,2},{2,0},{4,6},{6,4},{8,10},{10,8},{12,14},{14,12},{16,18},{18,... | collective-permute-start | bytes 1769480 | tf_op jit(solution)/shard_map/ppermute | solution.py:159
  625.3 32.5 %collective-permute-start.88 = (bf16[2,2,2,1,192,256]{5,4,3,2,1,0:T(8,128)(2,1)S(1)}, bf16[2,2,2,1,192,256]{5,4,3,2,1,0:T(8,128)(2,1)S(1)}, u32[]{:S(2)}, u32[]{:S(2)}) collective-permute-start(bf16[2,2,2,1,192,256]{5,4,3,2,1,0:T(8,128)(2,1)S(1)} %copy-done.93), channel_id=1, source_target_pairs={{0,2},{2,0},{4,6},{6,4},{8,10},{10,8},{12,14},{14,12},{16,18},{18,... | collective-permute-start | bytes 2359304 | tf_op jit(solution)/shard_map/ppermute | solution.py:159
  629.3 29.1 %collective-permute-start.53 = (bf16[2,2,1,1,48,1024]{5,4,3,2,1,0:T(8,128)(2,1)S(1)}, bf16[2,2,1,1,48,1024]{5,4,3,2,1,0:T(8,128)(2,1)S(1)}, u32[]{:S(2)}, u32[]{:S(2)}) collective-permute-start(bf16[2,2,1,1,48,1024]{5,4,3,2,1,0:T(8,128)(2,1)S(1)} %add_convert_fusion.21), channel_id=1, source_target_pairs={{0,4},{2,6},{4,0},{6,2},{8,12},{10,14},{12,8},{14,10},{16,20},{18,... | collective-permute-start | bytes 1179656 | tf_op jit(solution)/shard_map/ppermute | solution.py:159
  632.8 25.9 %collective-permute-start.74 = (bf16[2,2,1,1,192,256]{5,4,3,2,1,0:T(8,128)(2,1)S(1)}, bf16[2,2,1,1,192,256]{5,4,3,2,1,0:T(8,128)(2,1)S(1)}, u32[]{:S(2)}, u32[]{:S(2)}) collective-permute-start(bf16[2,2,1,1,192,256]{5,4,3,2,1,0:T(8,128)(2,1)S(1)} %add_convert_fusion.16), channel_id=1, source_target_pairs={{0,4},{2,6},{4,0},{6,2},{8,12},{10,14},{12,8},{14,10},{16,20},{18,... | collective-permute-start | bytes 1179656 | tf_op jit(solution)/shard_map/ppermute | solution.py:159
  633.5 20.4 %collective-permute-start.35 = (bf16[2,2,1,1,48,512]{5,4,3,2,1,0:T(8,128)(2,1)S(1)}, bf16[2,2,1,1,48,512]{5,4,3,2,1,0:T(8,128)(2,1)S(1)}, u32[]{:S(2)}, u32[]{:S(2)}) collective-permute-start(bf16[2,2,1,1,48,512]{5,4,3,2,1,0:T(8,128)(2,1)S(1)} %add_convert_fusion.37), channel_id=1, source_target_pairs={{0,4},{2,6},{4,0},{6,2},{8,12},{10,14},{12,8},{14,10},{16,20},{18,... | collective-permute-start | bytes 589832 | tf_op jit(solution)/shard_map/ppermute | solution.py:159
  669.5 79.5 %collective-permute-start.61 = (bf16[2,1,2,1,48,1024]{5,4,3,2,1,0:T(8,128)(2,1)S(1)}, bf16[2,1,2,1,48,1024]{5,4,3,2,1,0:T(8,128)(2,1)S(1)}, u32[]{:S(2)}, u32[]{:S(2)}) collective-permute-start(bf16[2,1,2,1,48,1024]{5,4,3,2,1,0:T(8,128)(2,1)S(1)} %add_convert_fusion.19), channel_id=1, source_target_pairs={{0,8},{2,10},{4,12},{6,14},{8,0},{10,2},{12,4},{14,6},{16,24},{18,... | collective-permute-start | bytes 1179656 | tf_op jit(solution)/shard_map/ppermute | solution.py:159
  670.4 73.4 %collective-permute-start.82 = (bf16[2,1,2,1,192,256]{5,4,3,2,1,0:T(8,128)(2,1)S(1)}, bf16[2,1,2,1,192,256]{5,4,3,2,1,0:T(8,128)(2,1)S(1)}, u32[]{:S(2)}, u32[]{:S(2)}) collective-permute-start(bf16[2,1,2,1,192,256]{5,4,3,2,1,0:T(8,128)(2,1)S(1)} %add_convert_fusion.14), channel_id=1, source_target_pairs={{0,8},{2,10},{4,12},{6,14},{8,0},{10,2},{12,4},{14,6},{16,24},{18,... | collective-permute-start | bytes 1179656 | tf_op jit(solution)/shard_map/ppermute | solution.py:159
  672.2 42.8 %collective-permute-start.21 = (bf16[2,1,2,1,48,768]{5,4,3,2,1,0:T(8,128)(2,1)S(1)}, bf16[2,1,2,1,48,768]{5,4,3,2,1,0:T(8,128)(2,1)S(1)}, u32[]{:S(2)}, u32[]{:S(2)}) collective-permute-start(bf16[2,1,2,1,48,768]{5,4,3,2,1,0:T(8,128)(2,1)S(1)} %add_convert_fusion.23), channel_id=1, source_target_pairs={{0,8},{2,10},{4,12},{6,14},{8,0},{10,2},{12,4},{14,6},{16,24},{18,... | collective-permute-start | bytes 884744 | tf_op jit(solution)/shard_map/ppermute | solution.py:159
  675.1 40.5 %collective-permute-start.19 = (bf16[2,1,2,1,48,768]{5,4,3,2,1,0:T(8,128)(2,1)S(1)}, bf16[2,1,2,1,48,768]{5,4,3,2,1,0:T(8,128)(2,1)S(1)}, u32[]{:S(2)}, u32[]{:S(2)}) collective-permute-start(bf16[2,1,2,1,48,768]{5,4,3,2,1,0:T(8,128)(2,1)S(1)} %add_convert_fusion.24), channel_id=1, source_target_pairs={{0,8},{2,10},{4,12},{6,14},{8,0},{10,2},{12,4},{14,6},{16,24},{18,... | collective-permute-start | bytes 884744 | tf_op jit(solution)/shard_map/ppermute | solution.py:159
  684.0 19.3 %collective-permute-start.50 = (bf16[2,1,1,1,48,384]{5,4,3,2,1,0:T(8,128)(2,1)S(1)}, bf16[2,1,1,1,48,384]{5,4,3,2,1,0:T(8,128)(2,1)S(1)}, u32[]{:S(2)}, u32[]{:S(2)}) collective-permute-start(bf16[2,1,1,1,48,384]{5,4,3,2,1,0:T(8,128)(2,1)S(1)} %add_convert_fusion.56), channel_id=1, source_target_pairs={{0,8},{2,10},{4,12},{6,14},{8,0},{10,2},{12,4},{14,6},{16,24},{18,... | collective-permute-start | bytes 221192 | tf_op jit(solution)/shard_map/ppermute | solution.py:159
  715.5 29.8 %collective-permute-start.84 = (bf16[2,1,2,1,192,256]{5,4,3,2,1,0:T(8,128)(2,1)S(1)}, bf16[2,1,2,1,192,256]{5,4,3,2,1,0:T(8,128)(2,1)S(1)}, u32[]{:S(2)}, u32[]{:S(2)}) collective-permute-start(bf16[2,1,2,1,192,256]{5,4,3,2,1,0:T(8,128)(2,1)S(1)} %add_convert_fusion.13), channel_id=1, source_target_pairs={{0,8},{2,10},{4,12},{6,14},{8,0},{10,2},{12,4},{14,6},{16,24},{18,... | collective-permute-start | bytes 1179656 | tf_op jit(solution)/shard_map/ppermute | solution.py:159
  743.8 26.7 %collective-permute-start.27 = (bf16[2,2,2,1,48,768]{5,4,3,2,1,0:T(8,128)(2,1)S(1)}, bf16[2,2,2,1,48,768]{5,4,3,2,1,0:T(8,128)(2,1)S(1)}, u32[]{:S(2)}, u32[]{:S(2)}) collective-permute-start(bf16[2,2,2,1,48,768]{5,4,3,2,1,0:T(8,128)(2,1)S(1)} %get-tuple-element.102), channel_id=1, source_target_pairs={{0,1},{1,0},{2,3},{3,2},{4,5},{5,4},{6,7},{7,6},{8,9},{9,8},{10,11... | collective-permute-start | bytes 1769480 | tf_op jit(solution)/shard_map/ppermute | solution.py:159
  745.3 19.9 %collective-permute-start.56 = (bf16[2,2,1,1,48,1024]{5,4,3,2,1,0:T(8,128)(2,1)S(1)}, bf16[2,2,1,1,48,1024]{5,4,3,2,1,0:T(8,128)(2,1)S(1)}, u32[]{:S(2)}, u32[]{:S(2)}) collective-permute-start(bf16[2,2,1,1,48,1024]{5,4,3,2,1,0:T(8,128)(2,1)S(1)} %add_convert_fusion.20), channel_id=1, source_target_pairs={{0,4},{2,6},{4,0},{6,2},{8,12},{10,14},{12,8},{14,10},{16,20},{18,... | collective-permute-start | bytes 1179656 | tf_op jit(solution)/shard_map/ppermute | solution.py:159
  749.0 38.3 %collective-permute-start.54 = (bf16[2,1,1,1,48,1024]{5,4,3,2,1,0:T(8,128)(2,1)S(1)}, bf16[2,1,1,1,48,1024]{5,4,3,2,1,0:T(8,128)(2,1)S(1)}, u32[]{:S(2)}, u32[]{:S(2)}) collective-permute-start(bf16[2,1,1,1,48,1024]{5,4,3,2,1,0:T(8,128)(2,1)S(1)} %add_convert_fusion.34), channel_id=1, source_target_pairs={{0,8},{2,10},{4,12},{6,14},{8,0},{10,2},{12,4},{14,6},{16,24},{18,... | collective-permute-start | bytes 589832 | tf_op jit(solution)/shard_map/ppermute | solution.py:159
  751.8 31.2 %collective-permute-start.75 = (bf16[2,1,1,1,192,256]{5,4,3,2,1,0:T(8,128)(2,1)S(1)}, bf16[2,1,1,1,192,256]{5,4,3,2,1,0:T(8,128)(2,1)S(1)}, u32[]{:S(2)}, u32[]{:S(2)}) collective-permute-start(bf16[2,1,1,1,192,256]{5,4,3,2,1,0:T(8,128)(2,1)S(1)} %add_convert_fusion.30), channel_id=1, source_target_pairs={{0,8},{2,10},{4,12},{6,14},{8,0},{10,2},{12,4},{14,6},{16,24},{18,... | collective-permute-start | bytes 589832 | tf_op jit(solution)/shard_map/ppermute | solution.py:159
  765.2 47.1 %collective-permute-start.90 = (bf16[2,2,2,1,192,256]{5,4,3,2,1,0:T(8,128)(2,1)S(1)}, bf16[2,2,2,1,192,256]{5,4,3,2,1,0:T(8,128)(2,1)S(1)}, u32[]{:S(2)}, u32[]{:S(2)}) collective-permute-start(bf16[2,2,2,1,192,256]{5,4,3,2,1,0:T(8,128)(2,1)S(1)} %get-tuple-element.88), channel_id=1, source_target_pairs={{0,1},{1,0},{2,3},{3,2},{4,5},{5,4},{6,7},{7,6},{8,9},{9,8},{10,11... | collective-permute-start | bytes 2359304 | tf_op jit(solution)/shard_map/ppermute | solution.py:159
  781.6 32.3 %collective-permute-start.69 = (bf16[2,2,2,1,48,1024]{5,4,3,2,1,0:T(8,128)(2,1)S(1)}, bf16[2,2,2,1,48,1024]{5,4,3,2,1,0:T(8,128)(2,1)S(1)}, u32[]{:S(2)}, u32[]{:S(2)}) collective-permute-start(bf16[2,2,2,1,48,1024]{5,4,3,2,1,0:T(8,128)(2,1)S(1)} %get-tuple-element.96), channel_id=1, source_target_pairs={{0,1},{1,0},{2,3},{3,2},{4,5},{5,4},{6,7},{7,6},{8,9},{9,8},{10,11... | collective-permute-start | bytes 2359304 | tf_op jit(solution)/shard_map/ppermute | solution.py:159
  783.0 27.9 %collective-permute-start.85 = (bf16[2,1,2,1,192,256]{5,4,3,2,1,0:T(8,128)(2,1)S(1)}, bf16[2,1,2,1,192,256]{5,4,3,2,1,0:T(8,128)(2,1)S(1)}, u32[]{:S(2)}, u32[]{:S(2)}) collective-permute-start(bf16[2,1,2,1,192,256]{5,4,3,2,1,0:T(8,128)(2,1)S(1)} %get-tuple-element.78), channel_id=1, source_target_pairs={{0,1},{1,0},{2,3},{3,2},{4,5},{5,4},{6,7},{7,6},{8,9},{9,8},{10,11... | collective-permute-start | bytes 1179656 | tf_op jit(solution)/shard_map/ppermute | solution.py:159
  795.0 20.6 %collective-permute-start.64 = (bf16[2,1,2,1,48,1024]{5,4,3,2,1,0:T(8,128)(2,1)S(1)}, bf16[2,1,2,1,48,1024]{5,4,3,2,1,0:T(8,128)(2,1)S(1)}, u32[]{:S(2)}, u32[]{:S(2)}) collective-permute-start(bf16[2,1,2,1,48,1024]{5,4,3,2,1,0:T(8,128)(2,1)S(1)} %get-tuple-element.80), channel_id=1, source_target_pairs={{0,1},{1,0},{2,3},{3,2},{4,5},{5,4},{6,7},{7,6},{8,9},{9,8},{10,11... | collective-permute-start | bytes 1179656 | tf_op jit(solution)/shard_map/ppermute | solution.py:159
  796.6 20.7 %collective-permute-start.79 = (bf16[2,1,1,1,192,256]{5,4,3,2,1,0:T(8,128)(2,1)S(1)}, bf16[2,1,1,1,192,256]{5,4,3,2,1,0:T(8,128)(2,1)S(1)}, u32[]{:S(2)}, u32[]{:S(2)}) collective-permute-start(bf16[2,1,1,1,192,256]{5,4,3,2,1,0:T(8,128)(2,1)S(1)} %get-tuple-element.74), channel_id=1, source_target_pairs={{0,1},{1,0},{2,3},{3,2},{4,5},{5,4},{6,7},{7,6},{8,9},{9,8},{10,11... | collective-permute-start | bytes 589832 | tf_op jit(solution)/shard_map/ppermute | solution.py:159
  813.9 28.4 %collective-permute-start.86 = (bf16[2,1,1,1,192,256]{5,4,3,2,1,0:T(8,128)(2,1)S(1)}, bf16[2,1,1,1,192,256]{5,4,3,2,1,0:T(8,128)(2,1)S(1)}, u32[]{:S(2)}, u32[]{:S(2)}) collective-permute-start(bf16[2,1,1,1,192,256]{5,4,3,2,1,0:T(8,128)(2,1)S(1)} %add_convert_fusion.28), channel_id=1, source_target_pairs={{0,4},{2,6},{4,0},{6,2},{8,12},{10,14},{12,8},{14,10},{16,20},{18,... | collective-permute-start | bytes 589832 | tf_op jit(solution)/shard_map/ppermute | solution.py:159
  815.6 36.4 %collective-permute-start.91 = (bf16[2,2,1,1,192,256]{5,4,3,2,1,0:T(8,128)(2,1)S(1)}, bf16[2,2,1,1,192,256]{5,4,3,2,1,0:T(8,128)(2,1)S(1)}, u32[]{:S(2)}, u32[]{:S(2)}) collective-permute-start(bf16[2,2,1,1,192,256]{5,4,3,2,1,0:T(8,128)(2,1)S(1)} %add_convert_fusion.12), channel_id=1, source_target_pairs={{0,4},{2,6},{4,0},{6,2},{8,12},{10,14},{12,8},{14,10},{16,20},{18,... | collective-permute-start | bytes 1179656 | tf_op jit(solution)/shard_map/ppermute | solution.py:159
  817.2 25.2 %collective-permute-start.65 = (bf16[2,1,1,1,48,1024]{5,4,3,2,1,0:T(8,128)(2,1)S(1)}, bf16[2,1,1,1,48,1024]{5,4,3,2,1,0:T(8,128)(2,1)S(1)}, u32[]{:S(2)}, u32[]{:S(2)}) collective-permute-start(bf16[2,1,1,1,48,1024]{5,4,3,2,1,0:T(8,128)(2,1)S(1)} %add_convert_fusion.32), channel_id=1, source_target_pairs={{0,4},{2,6},{4,0},{6,2},{8,12},{10,14},{12,8},{14,10},{16,20},{18,... | collective-permute-start | bytes 589832 | tf_op jit(solution)/shard_map/ppermute | solution.py:159
  819.3 32.9 %collective-permute-start.70 = (bf16[2,2,1,1,48,1024]{5,4,3,2,1,0:T(8,128)(2,1)S(1)}, bf16[2,2,1,1,48,1024]{5,4,3,2,1,0:T(8,128)(2,1)S(1)}, u32[]{:S(2)}, u32[]{:S(2)}) collective-permute-start(bf16[2,2,1,1,48,1024]{5,4,3,2,1,0:T(8,128)(2,1)S(1)} %add_convert_fusion.17), channel_id=1, source_target_pairs={{0,4},{2,6},{4,0},{6,2},{8,12},{10,14},{12,8},{14,10},{16,20},{18,... | collective-permute-start | bytes 1179656 | tf_op jit(solution)/shard_map/ppermute | solution.py:159
  (269 other events, 3653.3 us)

commit v2 on v1

v2 whole, which is shorter than its diff:
```python
import functools

import jax
import jax.numpy as jnp
from jax import lax
from jax.experimental import pallas as pl
from jax.experimental.pallas import tpu as pltpu
from jax.sharding import PartitionSpec as P

HEADS = 12
QUERIES = 32
TEXT = 32
SLOTS = QUERIES + TEXT


blocked = -1000000000.0
epsilon = 1e-06
sharpness = 14.0
loss_weight = 16.0


def unit_rows(values):
    return values * lax.rsqrt(jnp.sum(values * values, -1, keepdims=True) + epsilon)


def unit_back(values, grad_rows):
    unused, pullback = jax.vjp(unit_rows, values)
    return pullback(grad_rows)[0]


def caption_layout(length_rows):
    row_count = length_rows.shape[0]
    first_len = length_rows[:, 0:1]
    second_end = first_len + length_rows[:, 1:2]
    slot_index = lax.broadcasted_iota(jnp.int32, (row_count, TEXT), 1)
    text_group = (slot_index >= first_len).astype(jnp.int32) + (slot_index >= second_end).astype(
        jnp.int32
    )
    group_ids = jnp.concatenate([jnp.full((row_count, QUERIES), -1, jnp.int32), text_group], 1)
    allowed = group_ids[:, :, None] == group_ids[:, None, :]
    head_starts = jnp.concatenate([jnp.zeros_like(first_len), first_len], 1)
    pick_mask = slot_index[:, None, :] == head_starts[:, :, None]
    return (allowed, pick_mask)


f32 = jnp.float32
bf16 = jnp.bfloat16
ROOT_HALF = 0.7071067811865476
ROOT_TAU = 0.3989422804014327
MIB = 1024 * 1024


def dot_nn(a, b):
    return lax.dot_general(a, b, (((1,), (0,)), ((), ())), preferred_element_type=f32)


def dot_nt(a, b):
    return lax.dot_general(a, b, (((1,), (1,)), ((), ())), preferred_element_type=f32)


def dot_tn(a, b):
    return lax.dot_general(a, b, (((0,), (0,)), ((), ())), preferred_element_type=f32)


def whole(shape):
    return pl.BlockSpec(shape, lambda *_: (0,) * len(shape))


def held(shape, index):
    return pl.BlockSpec(shape, index, pipeline_mode=pl.Buffered(1))


def params(mib):
    return pltpu.CompilerParams(vmem_limit_bytes=mib * MIB, dimension_semantics=("arbitrary",))


def norm_parts(values):
    center = values - jnp.mean(values, -1, keepdims=True)
    scale = lax.rsqrt(jnp.mean(center * center, -1, keepdims=True) + epsilon)
    return center * scale, scale


def norm_grads(values, gain_row, grad):
    unit, scale = norm_parts(values)
    inner = grad * gain_row
    first = jnp.mean(inner, -1, keepdims=True)
    second = jnp.mean(inner * unit, -1, keepdims=True)
    return (
        scale * (inner - first - unit * second),
        jnp.sum(grad * unit, 0, keepdims=True),
        jnp.sum(grad, 0, keepdims=True),
    )


def gate_parts(u):
    size = jnp.abs(u) * ROOT_HALF
    t = 1.0 / (1.0 + 0.3275911 * size)
    bell = jnp.exp(-size * size)
    poly = t * (
        0.127414796
        + t * (-0.142248368 + t * (0.7107068705 + t * (-0.7265760135 + t * 0.5307027145)))
    )
    tail = poly * bell
    cdf = jnp.where(u > 0, 1.0 - tail, tail)
    return u * cdf, cdf + (ROOT_TAU * u) * bell


def half_lanes(rows):
    low = (lax.broadcasted_iota(jnp.int32, (rows, 128), 1) < 64).astype(f32)
    return low.astype(bf16), (1.0 - low).astype(bf16)


def spread_heads(x, low, high):
    left, right = x[:, :128], x[:, 128:]
    none = jnp.zeros_like(left)
    return jnp.concatenate(
        [
            jnp.concatenate([left * low, none], 1),
            jnp.concatenate([left * high, none], 1),
            jnp.concatenate([none, right * low], 1),
            jnp.concatenate([none, right * high], 1),
        ],
        0,
    )


def collect_heads(o, n):
    low = lax.broadcasted_iota(jnp.int32, (n, 128), 1) < 64
    left = jnp.where(low, o[:n, :128], o[n : 2 * n, :128])
    right = jnp.where(low, o[2 * n : 3 * n, 128:], o[3 * n :, 128:])
    return jnp.concatenate([left, right], 1)


def columns_softmax(scores):
    raised = jnp.exp(scores - jnp.max(scores, 0, keepdims=True))
    return raised * (1.0 / jnp.sum(raised, 0, keepdims=True))


GROUPS = HEADS // 4


def self_forward_kernel(
    x_ref, w_ref, bias_ref, gain_ref, mask_ref, q_ref, k_ref, v_ref, mix_ref, sum_ref, norm_ref
):
    x = x_ref[...]
    q_ref[...] = (dot_nn(x, w_ref[0]) + bias_ref[0:1]).astype(bf16)
    k_ref[...] = dot_nn(x, w_ref[1]).astype(bf16)
    v_ref[...] = (dot_nn(x, w_ref[2]) + bias_ref[1:2]).astype(bf16)
    low, high = half_lanes(SLOTS)

    def one_row(r, carry):
        rows = pl.ds(pl.multiple_of(r * SLOTS, SLOTS), SLOTS)
        allowed = mask_ref[r] > 0.0
        for g in range(GROUPS):
            cols = slice(g * 256, (g + 1) * 256)
            queries = spread_heads(q_ref[rows, cols] * bf16(0.125), low, high)
            scores = jnp.where(allowed, dot_nt(k_ref[rows, cols], queries), blocked)
            prob = columns_softmax(scores).astype(bf16)
            mixed = dot_tn(prob, v_ref[rows, cols])
            mix_ref[rows, cols] = collect_heads(mixed, SLOTS).astype(bf16)
        return carry

    lax.fori_loop(0, x_ref.shape[0] // SLOTS, one_row, 0)
    total = x.astype(f32) + dot_nn(mix_ref[...], w_ref[3]) + bias_ref[2:3]
    sum_ref[...] = total
    unit, _ = norm_parts(total)
    norm_ref[...] = unit * gain_ref[0:1] + bias_ref[8:9]


def self_forward(x, weights, biases, gains, mask):
    tokens, width = x.shape
    step = 4 * SLOTS
    tile = pl.BlockSpec((step, width), lambda i: (i, 0))
    low, full = jax.ShapeDtypeStruct(x.shape, bf16), jax.ShapeDtypeStruct(x.shape, f32)
    return pl.pallas_call(
        self_forward_kernel,
        grid=(tokens // step,),
        in_specs=[
            tile,
            held((4, width, width), lambda i: (0, 0, 0)),
            whole(biases.shape),
            whole(gains.shape),
            pl.BlockSpec((4,) + mask.shape[1:], lambda i: (i, 0, 0)),
        ],
        out_specs=[tile] * 6,
        out_shape=[low, low, low, low, full, full],
        compiler_params=params(40),
        name="self_forward",
    )(x, weights, biases, gains, mask)


def self_backward_kernel(
    x_ref,
    w_ref,
    gain_ref,
    mask_ref,
    q_ref,
    k_ref,
    v_ref,
    mix_ref,
    sum_ref,
    top_ref,
    low_ref,
    dx_ref,
    dw_ref,
    side_ref,
    dq_all,
    dk_all,
    dv_all,
    branch_all,
    dmix_all,
):
    step = pl.program_id(0)
    count = sum_ref.shape[0]
    steps = x_ref.shape[0] // count
    low, high = half_lanes(SLOTS)

    @pl.when(step == 0)
    def _():
        side_ref[...] = jnp.zeros_like(side_ref)

    @pl.when(step < steps)
    def _():
        base = pl.multiple_of(step * count, count)
        here = pl.ds(base, count)
        grad = jnp.concatenate([top_ref[...], low_ref[...]], 1).reshape(count, -1)
        down, dgain, dshift = norm_grads(sum_ref[...], gain_ref[0:1], grad)
        branch = down.astype(bf16)
        branch_all[here] = branch
        dmix_all[...] = dot_nt(branch, w_ref[3]).astype(bf16)

        def one_row(r, carry):
            local = pl.ds(pl.multiple_of(r * SLOTS, SLOTS), SLOTS)
            rows = pl.ds(pl.multiple_of(base + r * SLOTS, SLOTS), SLOTS)
            allowed = mask_ref[r] > 0.0
            for g in range(GROUPS):
                cols = slice(g * 256, (g + 1) * 256)
                keys = k_ref[local, cols]
                queries = spread_heads(q_ref[local, cols] * bf16(0.125), low, high)
                outs = spread_heads(dmix_all[local, cols], low, high)
                prob = columns_softmax(jnp.where(allowed, dot_nt(keys, queries), blocked))
                dprob = dot_nt(v_ref[local, cols], outs)
                dscore = (prob * (dprob - jnp.sum(dprob * prob, 0, keepdims=True))).astype(bf16)
                dv_all[rows, cols] = dot_nn(prob.astype(bf16), outs).astype(bf16)
                dk_all[rows, cols] = dot_nn(dscore, queries).astype(bf16)
                dq_all[rows, cols] = (collect_heads(dot_tn(dscore, keys), SLOTS) * 0.125).astype(bf16)
            return carry

        lax.fori_loop(0, count // SLOTS, one_row, 0)
        dq, dk, dv = dq_all[here], dk_all[here], dv_all[here]
        dx_ref[...] = down + dot_nt(dq, w_ref[0]) + dot_nt(dk, w_ref[1]) + dot_nt(dv, w_ref[2])
        side_ref[0:1] += dgain
        side_ref[1:2] += dshift
        for place, rows in enumerate((dq, dv, branch)):
            side_ref[2 + place : 3 + place] += jnp.sum(rows.astype(f32), 0, keepdims=True)

    for place, right in enumerate((dq_all, dk_all, dv_all, branch_all)):

        @pl.when(step == steps + place)
        def _():
            left = mix_ref if place == 3 else x_ref
            dw_ref[0] = dot_tn(left[...], right[...]).astype(bf16)


def self_backward(x, weights, gains, mask, q, k, v, mix, total, top, text):
    tokens, width = x.shape
    count = 4 * SLOTS
    steps = tokens // count

    def near(i):
        return jnp.minimum(i, steps - 1)

    tile = pl.BlockSpec((count, width), lambda i: (near(i), 0))
    part = pl.BlockSpec((4, QUERIES, width), lambda i: (near(i), 0, 0))
    scratch = pltpu.VMEM((tokens, width), bf16)
    return pl.pallas_call(
        self_backward_kernel,
        grid=(steps + 4,),
        in_specs=[
            held(x.shape, lambda i: (0, 0)),
            held((4, width, width), lambda i: (0, 0, 0)),
            whole(gains.shape),
            pl.BlockSpec((4,) + mask.shape[1:], lambda i: (near(i), 0, 0)),
            tile,
            tile,
            tile,
            held(x.shape, lambda i: (0, 0)),
            tile,
            part,
            part,
        ],
        out_specs=[
            tile,
            pl.BlockSpec((1, width, width), lambda i: (jnp.maximum(i - steps, 0), 0, 0)),
            whole((8, width)),
        ],
        out_shape=[
            jax.ShapeDtypeStruct(x.shape, f32),
            jax.ShapeDtypeStruct((4, width, width), bf16),
            jax.ShapeDtypeStruct((8, width), f32),
        ],
        scratch_shapes=[scratch] * 4 + [pltpu.VMEM((count, width), bf16)],
        compiler_params=params(48),
        name="self_backward",
    )(x, weights, gains, mask, q, k, v, mix, total, top, text)


TAIL = 16


def cross_forward_kernel(
    image_ref,
    end_ref,
    kv_ref,
    w_ref,
    bias_ref,
    gain_ref,
    norm_ref,
    key_ref,
    value_ref,
    key_end_ref,
    value_end_ref,
    q_ref,
    mix_ref,
    sum_ref,
    out_ref,
):
    rows_here = image_ref.shape[0]
    main = image_ref.shape[1] - 1
    width = norm_ref.shape[-1]
    end = end_ref[...].reshape(rows_here * TAIL, -1)
    key_end_ref[...] = dot_nt(end, kv_ref[0]).astype(bf16)
    value_end_ref[...] = (dot_nt(end, kv_ref[1]) + bias_ref[4:5]).astype(bf16)
    residual = norm_ref[...].reshape(rows_here * QUERIES, width)
    q_ref[...] = (dot_nn(residual.astype(bf16), w_ref[0]) + bias_ref[3:4]).astype(bf16)
    low, high = half_lanes(QUERIES)
    shown = lax.broadcasted_iota(jnp.int32, (main + TAIL, 128), 0) <= main

    def one_row(r, carry):
        span = pl.ds(pl.multiple_of(r * main, main), main)
        last = pl.ds(pl.multiple_of(r * TAIL, TAIL), TAIL)
        mine = pl.ds(pl.multiple_of(r * QUERIES, QUERIES), QUERIES)
        tokens = image_ref[r, :main]
        key_ref[span] = dot_nt(tokens, kv_ref[0]).astype(bf16)
        value_ref[span] = (dot_nt(tokens, kv_ref[1]) + bias_ref[4:5]).astype(bf16)
        for g in range(GROUPS):
            cols = slice(g * 256, (g + 1) * 256)
            keys = jnp.concatenate([key_ref[span, cols], key_end_ref[last, cols]], 0)
            values = jnp.concatenate([value_ref[span, cols], value_end_ref[last, cols]], 0)
            queries = spread_heads(q_ref[mine, cols] * bf16(0.125), low, high)
            prob = columns_softmax(jnp.where(shown, dot_nt(keys, queries), blocked)).astype(bf16)
            mix_ref[mine, cols] = collect_heads(dot_tn(prob, values), QUERIES).astype(bf16)
        return carry

    lax.fori_loop(0, rows_here, one_row, 0)
    total = residual + dot_nn(mix_ref[...], w_ref[1]) + bias_ref[5:6]
    sum_ref[...] = total
    unit, _ = norm_parts(total)
    out_ref[...] = unit * gain_ref[1:2] + bias_ref[9:10]


def cross_forward(images, ends, kv, weights, biases, gains, norm):
    rows, patches, vis = images.shape
    main = patches - 1
    width = norm.shape[-1]
    take = 4
    keys = pl.BlockSpec((take * main, width), lambda i: (i, 0))
    tails = pl.BlockSpec((take * TAIL, width), lambda i: (i, 0))
    tile = pl.BlockSpec((take * QUERIES, width), lambda i: (i, 0))

    def shape(count, dtype):
        return jax.ShapeDtypeStruct((rows * count, width), dtype)

    return pl.pallas_call(
        cross_forward_kernel,
        grid=(rows // take,),
        in_specs=[
            pl.BlockSpec((take, patches, vis), lambda i: (i, 0, 0)),
            pl.BlockSpec((take, TAIL, vis), lambda i: (i, 0, 0)),
            held(kv.shape, lambda i: (0, 0, 0)),
            held((2, width, width), lambda i: (2, 0, 0)),
            whole(biases.shape),
            whole(gains.shape),
            pl.BlockSpec((take, QUERIES, width), lambda i: (i, 0, 0)),
        ],
        out_specs=[keys, keys, tails, tails, tile, tile, tile, tile],
        out_shape=[
            shape(main, bf16),
            shape(main, bf16),
            shape(TAIL, bf16),
            shape(TAIL, bf16),
            shape(QUERIES, bf16),
            shape(QUERIES, bf16),
            shape(QUERIES, f32),
            shape(QUERIES, f32),
        ],
        compiler_params=params(48),
        name="cross_forward",
    )(images, ends, kv, weights, biases, gains, norm)


def cross_backward_kernel(
    image_ref,
    end_ref,
    w_ref,
    norm_ref,
    key_ref,
    value_ref,
    key_end_ref,
    value_end_ref,
    q_ref,
    mix_ref,
    down_ref,
    dnorm_ref,
    dkey_w_ref,
    dvalue_w_ref,
    dw_ref,
    side_ref,
    key_sum,
    value_sum,
    w_sum,
    dkey,
    dvalue,
    dkey_end,
    dvalue_end,
    dq_all,
    dmix_all,
):
    step = pl.program_id(0)
    rows_here = image_ref.shape[0]
    main = image_ref.shape[1] - 1
    width = norm_ref.shape[-1]
    low, high = half_lanes(QUERIES)
    shown = lax.broadcasted_iota(jnp.int32, (main + TAIL, 128), 0) <= main

    @pl.when(step == 0)
    def _():
        side_ref[...] = jnp.zeros_like(side_ref)
        key_sum[...] = jnp.zeros_like(key_sum)
        value_sum[...] = jnp.zeros_like(value_sum)
        w_sum[...] = jnp.zeros_like(w_sum)

    down = down_ref[...]
    branch = down.astype(bf16)
    dmix_all[...] = dot_nt(branch, w_ref[1]).astype(bf16)

    def one_row(r, carry):
        span = pl.ds(pl.multiple_of(r * main, main), main)
        last = pl.ds(pl.multiple_of(r * TAIL, TAIL), TAIL)
        mine = pl.ds(pl.multiple_of(r * QUERIES, QUERIES), QUERIES)
        for g in range(GROUPS):
            cols = slice(g * 256, (g + 1) * 256)
            keys = jnp.concatenate([key_ref[span, cols], key_end_ref[last, cols]], 0)
            values = jnp.concatenate([value_ref[span, cols], value_end_ref[last, cols]], 0)
            queries = spread_heads(q_ref[mine, cols] * bf16(0.125), low, high)
            outs = spread_heads(dmix_all[mine, cols], low, high)
            prob = columns_softmax(jnp.where(shown, dot_nt(keys, queries), blocked))
            dprob = dot_nt(values, outs)
            dscore = (prob * (dprob - jnp.sum(dprob * prob, 0, keepdims=True))).astype(bf16)
            dv = dot_nn(prob.astype(bf16), outs).astype(bf16)
            dk = dot_nn(dscore, queries).astype(bf16)
            dvalue[span, cols] = dv[:main]
            dvalue_end[last, cols] = dv[main:]
            dkey[span, cols] = dk[:main]
            dkey_end[last, cols] = dk[main:]
            dq_all[mine, cols] = (collect_heads(dot_tn(dscore, keys), QUERIES) * 0.125).astype(bf16)
        return carry

    lax.fori_loop(0, rows_here, one_row, 0)
    end = end_ref[...].reshape(rows_here * TAIL, -1)
    for grads, grads_end, gathered in ((dkey, dkey_end, key_sum), (dvalue, dvalue_end, value_sum)):
        gathered[...] += dot_tn(grads_end[...], end)

        def add_row(r, carry):
            span = pl.ds(pl.multiple_of(r * main, main), main)
            gathered[...] += dot_tn(grads[span], image_ref[r, :main])
            return carry

        lax.fori_loop(0, rows_here, add_row, 0)
    dq = dq_all[...]
    dnorm_ref[...] = (down + dot_nt(dq, w_ref[0])).reshape(rows_here, QUERIES, width)
    low_norm = norm_ref[...].reshape(rows_here * QUERIES, width).astype(bf16)
    w_sum[0] += dot_tn(low_norm, dq)
    w_sum[1] += dot_tn(mix_ref[...], branch)
    side_ref[0:1] += jnp.sum(dq.astype(f32), 0, keepdims=True)
    side_ref[1:2] += jnp.sum(dvalue[...].astype(f32), 0, keepdims=True) + jnp.sum(
        dvalue_end[...].astype(f32), 0, keepdims=True
    )
    side_ref[2:3] += jnp.sum(branch.astype(f32), 0, keepdims=True)

    @pl.when(step == pl.num_programs(0) - 1)
    def _():
        dkey_w_ref[...] = key_sum[...].astype(bf16)
        dvalue_w_ref[...] = value_sum[...].astype(bf16)
        dw_ref[...] = w_sum[...].astype(bf16)


def cross_backward(images, ends, weights, norm, keys, values, key_ends, value_ends, q, mix, down):
    rows, patches, vis = images.shape
    main = patches - 1
    width = norm.shape[-1]
    take = 2
    span = pl.BlockSpec((take * main, width), lambda i: (i, 0))
    tails = pl.BlockSpec((take * TAIL, width), lambda i: (i, 0))
    tile = pl.BlockSpec((take * QUERIES, width), lambda i: (i, 0))
    part = pl.BlockSpec((take, QUERIES, width), lambda i: (i, 0, 0))
    return pl.pallas_call(
        cross_backward_kernel,
        grid=(rows // take,),
        in_specs=[
            pl.BlockSpec((take, patches, vis), lambda i: (i, 0, 0)),
            pl.BlockSpec((take, TAIL, vis), lambda i: (i, 0, 0)),
            held((2, width, width), lambda i: (2, 0, 0)),
            part,
            span,
            span,
            tails,
            tails,
            tile,
            tile,
            tile,
        ],
        out_specs=[
            part,
            held((width, vis), lambda i: (0, 0)),
            held((width, vis), lambda i: (0, 0)),
            held((2, width, width), lambda i: (0, 0, 0)),
            whole((8, width)),
        ],
        out_shape=[
            jax.ShapeDtypeStruct((rows, QUERIES, width), f32),
            jax.ShapeDtypeStruct((width, vis), bf16),
            jax.ShapeDtypeStruct((width, vis), bf16),
            jax.ShapeDtypeStruct((2, width, width), bf16),
            jax.ShapeDtypeStruct((8, width), f32),
        ],
        scratch_shapes=[
            pltpu.VMEM((width, vis), f32),
            pltpu.VMEM((width, vis), f32),
            pltpu.VMEM((2, width, width), f32),
            pltpu.VMEM((take * main, width), bf16),
            pltpu.VMEM((take * main, width), bf16),
            pltpu.VMEM((take * TAIL, width), bf16),
            pltpu.VMEM((take * TAIL, width), bf16),
            pltpu.VMEM((take * QUERIES, width), bf16),
            pltpu.VMEM((take * QUERIES, width), bf16),
        ],
        compiler_params=params(52),
        name="cross_backward",
    )(images, ends, weights, norm, keys, values, key_ends, value_ends, q, mix, down)


def ffn_forward_kernel(
    which,
    norm_ref,
    in_ref,
    in_bias_ref,
    out_ref,
    proj_ref,
    proj_bias_ref,
    bias_ref,
    gain_ref,
    *rest,
):
    act_ref, slope_ref, sum_ref, low_ref, raw_ref, embed_ref, rows_low = rest[-7:]
    step = pl.program_id(0)
    tokens, width = sum_ref.shape

    @pl.when(step == 0)
    def _():
        full = norm_ref[...].reshape(tokens, width)
        rows_low[...] = full.astype(bf16)
        sum_ref[...] = full + bias_ref[6 + which : 7 + which]

    u = dot_nn(rows_low[...], in_ref[0]) + in_bias_ref[which : which + 1]
    act, slope = gate_parts(u)
    act = act.astype(bf16)
    act_ref[...] = act
    slope_ref[...] = slope.astype(bf16)
    sum_ref[...] += dot_nn(act, out_ref[0])

    @pl.when(step == pl.num_programs(0) - 1)
    def _():
        unit, _ = norm_parts(sum_ref[...])
        low = (unit * gain_ref[2 + which : 3 + which] + bias_ref[10 + which : 11 + which]).astype(bf16)
        low_ref[...] = low.reshape(low_ref.shape)
        raw = dot_nn(low, proj_ref[0]) + proj_bias_ref[which : which + 1]
        raw_ref[...] = raw
        size = lax.rsqrt(jnp.sum(raw * raw, -1, keepdims=True) + epsilon)
        embed_ref[...] = (raw * size).astype(bf16)


def ffn_forward(which, part, norm, ffn_in, ffn_bias, ffn_out, projections, proj_bias, biases, gains, layer):
    rows, width = norm.shape[0], norm.shape[-1]
    tokens = rows * QUERIES
    hidden = ffn_in.shape[2]
    embed = projections.shape[2]
    chunk = 512
    cols = pl.BlockSpec((tokens, chunk), lambda j: (0, j))
    halves = [] if layer is None else [layer]
    return pl.pallas_call(
        functools.partial(ffn_forward_kernel, which),
        grid=(hidden // chunk,),
        in_specs=[
            held((rows, QUERIES, width), lambda j: (0, part, 0)),
            pl.BlockSpec((1, width, chunk), lambda j: (which, 0, j)),
            pl.BlockSpec((2, chunk), lambda j: (0, j)),
            pl.BlockSpec((1, chunk, width), lambda j: (which, j, 0)),
            held((1, width, embed), lambda j: (which, 0, 0)),
            whole(proj_bias.shape),
            whole(biases.shape),
            whole(gains.shape),
        ]
        + [pl.BlockSpec(memory_space=pl.ANY)] * len(halves),
        out_specs=[
            cols,
            cols,
            whole((tokens, width)),
            pl.BlockSpec((rows, QUERIES, width), lambda j: (0, which, 0)),
            whole((tokens, embed)),
            whole((tokens, embed)),
        ],
        out_shape=[
            jax.ShapeDtypeStruct((tokens, hidden), bf16),
            jax.ShapeDtypeStruct((tokens, hidden), bf16),
            jax.ShapeDtypeStruct((tokens, width), f32),
            jax.ShapeDtypeStruct((rows, SLOTS, width), bf16),
            jax.ShapeDtypeStruct((tokens, embed), f32),
            jax.ShapeDtypeStruct((tokens, embed), bf16),
        ],
        scratch_shapes=[pltpu.VMEM((tokens, width), bf16)],
        input_output_aliases={8: 3} if halves else {},
        compiler_params=params(48),
        name="ffn_forward",
    )(norm, ffn_in, ffn_bias, ffn_out, projections, proj_bias, biases, gains, *halves)


def ffn_backward_kernel(
    which,
    norm_ref,
    sum_ref,
    before_ref,
    layer_ref,
    grad_ref,
    raw_ref,
    proj_ref,
    gain_ref,
    in_ref,
    out_ref,
    act_ref,
    slope_ref,
    down_ref,
    din_ref,
    dout_ref,
    dproj_ref,
    side_ref,
    dbias_ref,
    dproj_bias_ref,
    branch_all,
    low_turned,
    rest,
):
    step = pl.program_id(0)
    tokens, width = sum_ref.shape

    @pl.when(step == 0)
    def _():
        raw = raw_ref[...]
        grad = grad_ref[...].reshape(tokens, width).astype(f32) + dot_nt(raw, proj_ref[0])
        down, dgain, dshift = norm_grads(sum_ref[...], gain_ref[2 + which : 3 + which], grad)
        branch = down.astype(bf16)
        branch_all[...] = branch
        rest[...] = down
        side_ref[...] = jnp.zeros_like(side_ref)
        side_ref[0:1] = dgain
        side_ref[1:2] = dshift
        side_ref[2:3] = jnp.sum(branch.astype(f32), 0, keepdims=True)
        dproj_ref[...] = dot_tn(layer_ref[...].reshape(tokens, width), raw).astype(bf16)
        dproj_bias_ref[...] = jnp.broadcast_to(
            jnp.sum(raw.astype(f32), 0, keepdims=True), dproj_bias_ref.shape
        )
        low_turned[...] = norm_ref[...].reshape(tokens, width).astype(bf16).T

    branch = branch_all[...]
    du = (dot_nt(branch, out_ref[0]) * slope_ref[...].astype(f32)).astype(bf16)
    rest[...] += dot_nt(du, in_ref[0])
    dout_ref[...] = dot_tn(act_ref[...], branch).astype(bf16)
    din_ref[...] = dot_nn(low_turned[...], du).astype(bf16)
    dbias_ref[...] = jnp.broadcast_to(jnp.sum(du.astype(f32), 0, keepdims=True), dbias_ref.shape)

    @pl.when(step == pl.num_programs(0) - 1)
    def _():
        if which == 0:
            down, dgain, dshift = norm_grads(before_ref[...], gain_ref[1:2], rest[...])
            side_ref[3:4] = dgain
            side_ref[4:5] = dshift
            down_ref[...] = down.reshape(down_ref.shape)
        else:
            down_ref[...] = rest[...].reshape(down_ref.shape)


def ffn_backward(
    which, part, norm, total, before, layer, grad, raw, projections, gains, ffn_in, ffn_out, act, slope
):
    rows = layer.shape[0]
    tokens, width = total.shape
    hidden = ffn_in.shape[2]
    embed = projections.shape[2]
    chunk = 512
    cols = pl.BlockSpec((tokens, chunk), lambda j: (0, j))
    before_spec = held(before.shape, lambda j: (0, 0))
    return pl.pallas_call(
        functools.partial(ffn_backward_kernel, which),
        grid=(hidden // chunk,),
        in_specs=[
            held((rows, QUERIES, width), lambda j: (0, part, 0)),
            held((tokens, width), lambda j: (0, 0)),
            before_spec,
            held((rows, QUERIES, width), lambda j: (0, which, 0)),
            held((rows, QUERIES, width), lambda j: (0, which, 0)),
            held((tokens, embed), lambda j: (0, 0)),
            held((1, width, embed), lambda j: (which, 0, 0)),
            whole(gains.shape),
            pl.BlockSpec((1, width, chunk), lambda j: (which, 0, j)),
            pl.BlockSpec((1, chunk, width), lambda j: (which, j, 0)),
            cols,
            cols,
        ],
        out_specs=[
            whole((rows, QUERIES, width)),
            pl.BlockSpec((width, chunk), lambda j: (0, j)),
            pl.BlockSpec((chunk, width), lambda j: (j, 0)),
            whole((width, embed)),
            whole((8, width)),
            pl.BlockSpec((8, chunk), lambda j: (0, j)),
            whole((8, embed)),
        ],
        out_shape=[
            jax.ShapeDtypeStruct((rows, QUERIES, width), f32),
            jax.ShapeDtypeStruct((width, hidden), bf16),
            jax.ShapeDtypeStruct((hidden, width), bf16),
            jax.ShapeDtypeStruct((width, embed), bf16),
            jax.ShapeDtypeStruct((8, width), f32),
            jax.ShapeDtypeStruct((8, hidden), f32),
            jax.ShapeDtypeStruct((8, embed), f32),
        ],
        scratch_shapes=[
            pltpu.VMEM((tokens, width), bf16),
            pltpu.VMEM((width, tokens), bf16),
            pltpu.VMEM((tokens, width), f32),
        ],
        compiler_params=params(52),
        name="ffn_backward",
    )(norm, total, before, layer, grad, raw, projections, gains, ffn_in, ffn_out, act, slope)


def own_bit(stage):
    axis, bit = stage
    return (lax.axis_index(axis) >> bit) & 1


def swap(values, stage, sizes):
    axis, bit = stage
    return lax.ppermute(values, axis, [(i, i ^ (1 << bit)) for i in range(sizes[axis])])


def bit_stages(sizes):
    depth = sizes["dp"].bit_length() - 1
    return [("dp", bit) for bit in range(depth)]


def pick(term, places):
    array, fixed = term
    starts = [0] * array.ndim
    extent = list(array.shape)
    for dim, place in fixed.items():
        starts[dim] = place
        extent[dim] = 1
    for dim, place in places.items():
        starts[dim] = place
        extent[dim] = 1
    return lax.dynamic_slice(array, starts, extent)


def total(terms, places):
    return sum(pick(term, places).astype(jnp.float32) for term in terms)


def halve(terms, stage, dim, sizes):
    mine = own_bit(stage)
    send = total(terms, {dim: 1 - mine}).astype(jnp.bfloat16)
    arrived = swap(send, stage, sizes)
    kept = [(array, {**fixed, dim: mine}) for array, fixed in terms]
    return kept + [(arrived, {})]


def pair_scatter(first, second, order, sizes):
    depth = sizes["dp"].bit_length() - 1

    def spread(array):
        rows, cols = array.shape
        return array.reshape((2,) * depth + (rows // sizes["dp"], cols))

    streams = [[(spread(first), {})], [(spread(second), {})]]
    for stage in order:
        if stage[0] == "rep":
            mine = own_bit(stage)
            sums = [total(terms, {}) for terms in streams]
            send = jnp.where(mine == 0, sums[1], sums[0]).astype(jnp.bfloat16)
            keep = jnp.where(mine == 0, sums[0], sums[1])
            streams = [[(keep, {}), (swap(send, stage, sizes), {})]]
        else:
            dim = depth - 1 - stage[1]
            streams = [halve(terms, stage, dim, sizes) for terms in streams]
    result = total(streams[0], {})
    return result.reshape(result.shape[-2:])


def orders(sizes):
    stages = bit_stages(sizes)
    head, mid, tail = stages[:1], stages[1:3], stages[3:]
    ring = mid + [("rep", 0)]
    return [head + ring[k:] + ring[:k] + tail for k in range(3)]


def scatter_parts(first, second, sizes):
    cols = first.shape[1]
    lanes = cols // 128
    cuts = [0, 128 * ((lanes + 2) // 3), 128 * ((2 * lanes + 2) // 3), cols]
    done = [
        pair_scatter(first[:, a:b], second[:, a:b], order, sizes)
        for a, b, order in zip(cuts[:-1], cuts[1:], orders(sizes))
    ]
    return jnp.concatenate(done, 1)


def gather_rows(values, sizes):
    stages = [("rep", 0)] + bit_stages(sizes)
    for stage in stages:
        other = swap(values, stage, sizes)
        low = own_bit(stage) == 0
        values = jnp.concatenate([jnp.where(low, values, other), jnp.where(low, other, values)], 0)
    return values


def scatter_rows(values, sizes):
    stages = bit_stages(sizes)
    depth = len(stages)
    count = values.shape[0] // (2 * sizes["dp"])
    terms = [(values.reshape((2,) * (depth + 1) + (count, values.shape[1])), {})]
    for stage in stages:
        terms = halve(terms, stage, depth - 1 - stage[1], sizes)
    terms = halve(terms, ("rep", 0), depth, sizes)
    result = total(terms, {})
    return result.reshape(result.shape[-2:])


def shards(
    hidden_states,
    image_features,
    caption_lengths,
    attn_weights,
    cross_kv,
    ffn_in,
    ffn_out,
    projections,
    norm_gains,
    biases,
    ffn_bias,
    proj_bias,
    out_grad,
    sizes,
):
    row_count, slots, width = hidden_states.shape
    captions_here = 2 * row_count
    world = sizes["dp"] * sizes["rep"]
    allowed, pick_mask = caption_layout(caption_lengths)
    pick_low = pick_mask.astype(bf16)
    pick_full = pick_mask.astype(f32)
    mask = jnp.tile(allowed.astype(f32), (1, 1, 4))
    inputs = hidden_states.reshape(row_count * slots, width)
    self_q, self_k, self_v, self_mix, first_sum, first_norm = self_forward(
        inputs, attn_weights, biases, norm_gains, mask
    )
    first_norm = first_norm.reshape(row_count, slots, width)
    text_act, text_slope, fourth_sum, layer_half, caption_raw, caption_all = ffn_forward(
        1, 1, first_norm, ffn_in, ffn_bias, ffn_out, projections, proj_bias, biases, norm_gains, None
    )
    caption_embed = (
        jnp.einsum(
            "rkt,rtd->rkd",
            pick_low,
            caption_all.reshape(row_count, TEXT, -1),
            preferred_element_type=f32,
        )
        .astype(bf16)
        .reshape(captions_here, -1)
    )
    every_caption = gather_rows(caption_embed, sizes)
    image_ends = jnp.pad(image_features[:, -1:], ((0, 0), (0, TAIL - 1), (0, 0)))
    keys, values, key_ends, value_ends, cross_q, cross_mix, second_sum, second_norm = cross_forward(
        image_features, image_ends, cross_kv, attn_weights, biases, norm_gains, first_norm
    )
    second_norm = second_norm.reshape(row_count, QUERIES, width)
    query_act, query_slope, third_sum, layer_out, query_raw, query_embed = ffn_forward(
        0,
        0,
        second_norm,
        ffn_in,
        ffn_bias,
        ffn_out,
        projections,
        proj_bias,
        biases,
        norm_gains,
        layer_half,
    )
    query_raw = query_raw.reshape(row_count, QUERIES, -1)
    query_embed = query_embed.reshape(row_count, QUERIES, -1)
    sims = jnp.einsum("rqp,cp->rqc", query_embed, every_caption, preferred_element_type=f32)
    expo = jnp.exp(sharpness * (sims - 1.0))
    affinity = jnp.mean(expo, 1)
    offset = lax.axis_index(("dp", "rep")) * captions_here
    own_block = lax.dynamic_slice_in_dim(affinity, offset, captions_here, 1).reshape(
        row_count, row_count, 2
    )
    diagonal = (
        lax.broadcasted_iota(jnp.int32, (row_count, row_count), 0)
        == lax.broadcasted_iota(jnp.int32, (row_count, row_count), 1)
    ).astype(f32)
    positive = jnp.sum(own_block * diagonal[:, :, None], 1)
    row_total = jnp.sum(affinity, 1)
    partial_cols = jnp.sum(affinity, 0)
    all_cols = jnp.sum(
        lax.all_to_all(
            jnp.broadcast_to(partial_cols[None], (world,) + partial_cols.shape),
            ("dp", "rep"),
            0,
            0,
            tiled=True,
        ),
        0,
    )
    own_cols = lax.dynamic_slice_in_dim(all_cols, offset, captions_here, 0).reshape(row_count, 2)
    inverse_all = 1.0 / all_cols
    row_loss = (
        jnp.log(row_total)
        - jnp.log(positive[:, 0])
        + jnp.sum(jnp.log(own_cols) - jnp.log(positive), 1)
    )
    grad_affinity = loss_weight * (1.0 / row_total[:, None] + inverse_all[None, :])
    pair_weight = jnp.array([2.0, 1.0], f32)
    correction = (loss_weight * diagonal[:, :, None] * pair_weight / own_block).reshape(
        row_count, captions_here
    )
    own_grad = lax.dynamic_slice_in_dim(grad_affinity, offset, captions_here, 1) - correction
    grad_affinity = lax.dynamic_update_slice_in_dim(grad_affinity, own_grad, offset, 1)
    grad_sims = (grad_affinity[:, None, :] * expo * (sharpness / QUERIES)).astype(bf16)
    grad_query_embed = jnp.einsum(
        "rqc,cp->rqp", grad_sims, every_caption, preferred_element_type=f32
    )
    grad_caption_embed = scatter_rows(
        jnp.einsum("rqc,rqp->cp", grad_sims, query_embed, preferred_element_type=f32).astype(bf16),
        sizes,
    )
    query_raw_grad = unit_back(query_raw, grad_query_embed).astype(bf16)
    head_raw = jnp.sum(
        pick_full[:, :, :, None] * caption_raw.reshape(row_count, 1, TEXT, -1), 2
    )
    head_raw_grad = unit_back(head_raw, grad_caption_embed.reshape(row_count, 2, -1)).astype(bf16)
    caption_raw_grad = jnp.einsum(
        "rkt,rkd->rtd", pick_low, head_raw_grad, preferred_element_type=f32
    ).astype(bf16)
    grad_second, query_din, query_dout, query_dproj, query_side, query_dbias, query_dproj_bias = (
        ffn_backward(
            0,
            0,
            second_norm,
            third_sum,
            second_sum,
            layer_out,
            out_grad,
            query_raw_grad.reshape(row_count * QUERIES, -1),
            projections,
            norm_gains,
            ffn_in,
            ffn_out,
            query_act,
            query_slope,
        )
    )
    text_first, text_din, text_dout, text_dproj, text_side, text_dbias, text_dproj_bias = (
        ffn_backward(
            1,
            1,
            first_norm,
            fourth_sum,
            fourth_sum,
            layer_out,
            out_grad,
            caption_raw_grad.reshape(row_count * TEXT, -1),
            projections,
            norm_gains,
            ffn_in,
            ffn_out,
            text_act,
            text_slope,
        )
    )
    ffn_in_grad = scatter_parts(query_din, text_din, sizes)
    ffn_out_grad = scatter_parts(query_dout, text_dout, sizes)
    proj_grad = pair_scatter(query_dproj, text_dproj, orders(sizes)[0], sizes)
    query_first, key_grad, value_grad, cross_dw, cross_side = cross_backward(
        image_features,
        image_ends,
        attn_weights,
        first_norm,
        keys,
        values,
        key_ends,
        value_ends,
        cross_q,
        cross_mix,
        grad_second.reshape(row_count * QUERIES, width),
    )
    cross_grad = scatter_parts(key_grad, value_grad, sizes)
    input_grad, self_dw, self_side = self_backward(
        inputs,
        attn_weights,
        norm_gains,
        mask,
        self_q,
        self_k,
        self_v,
        self_mix,
        first_sum,
        query_first,
        text_first,
    )
    attn_pairs = ((self_dw[0], self_dw[3]), (self_dw[1], cross_dw[0]), (self_dw[2], cross_dw[1]))
    attn_grad = jnp.stack(
        [
            pair_scatter(one, two, order, sizes)
            for (one, two), order in zip(attn_pairs, orders(sizes))
        ]
    )
    gain_grad = jnp.stack([self_side[0], query_side[3], query_side[0], text_side[0]])
    bias_grad = jnp.stack(
        [
            self_side[2],
            self_side[3],
            self_side[4],
            cross_side[0],
            cross_side[1],
            cross_side[2],
            query_side[2],
            text_side[2],
            self_side[1],
            query_side[4],
            query_side[1],
            text_side[1],
        ]
    )
    vectors = (
        gain_grad,
        bias_grad,
        jnp.stack([query_dbias[0], text_dbias[0]]),
        jnp.stack([query_dproj_bias[0], text_dproj_bias[0]]),
    )

    def deal(array):
        mats, cols = array.shape
        cut = array.reshape(sizes["rep"], mats // sizes["rep"], sizes["dp"], cols // sizes["dp"])
        return cut.transpose(2, 0, 1, 3).reshape(world, -1)

    dealt = jnp.concatenate([deal(array) for array in vectors], 1)
    arrived = jnp.sum(lax.all_to_all(dealt, ("dp", "rep"), 0, 0, tiled=True), 0)
    small = []
    start = 0
    for array in vectors:
        mats, cols = array.shape[0] // sizes["rep"], array.shape[1] // sizes["dp"]
        small.append(arrived[start : start + mats * cols].reshape(mats, cols))
        start += mats * cols
    return (
        layer_out,
        row_loss,
        input_grad.reshape(hidden_states.shape),
        attn_grad,
        cross_grad[None],
        ffn_in_grad[None],
        ffn_out_grad[None],
        proj_grad[None],
        small[0],
        small[1],
        small[2],
        small[3],
    )


def solution(mesh):
    placed = (
        P(("dp", "rep"), None, None),
        P(("dp", "rep"), None, None),
        P(("dp", "rep"), None),
        P(),
        P(),
        P(),
        P(),
        P(),
        P(),
        P(),
        P(),
        P(),
        P(("dp", "rep"), None, None),
    )
    sizes = dict(mesh.shape)
    return jax.shard_map(
        functools.partial(shards, sizes=sizes),
        mesh=mesh,
        in_specs=placed,
        out_specs=(
            P(("dp", "rep"), None, None),
            P(("dp", "rep")),
            P(("dp", "rep"), None, None),
            P("rep", "dp", None),
            P("rep", "dp", None),
            P("rep", "dp", None),
            P("rep", "dp", None),
            P("rep", "dp", None),
            P("rep", "dp"),
            P("rep", "dp"),
            P("rep", "dp"),
            P("rep", "dp"),
        ),
        check_vma=False,
    )
```

time: 874 us -> 737 us (0.84)
  matrix products: 290 us -> 6.66 us
  Pallas kernels: 0 us -> 269 us
  local copies, waits for them, and re-layouts: 166 us -> 77.6 us
  other arithmetic: 102 us -> 46.6 us
  waiting for transfers between devices: 195 us -> 218 us
    dot_general x53 -> x2, matrix products: 283 us -> 0.63 us  [the longest x1 0.42 us: shards(): jnp.einsum('rkt,rkd->rtd', pick_low, head_raw_grad, preferred_element_typ...]
    pallas_call x0 -> x8, Pallas kernels: none -> 269 us  [the longest x1 79.8 us: cross_backward(): pl.pallas_call(cross_backward_kernel, grid=(rows // take,), in_specs=[pl....]
    convert_element_type x13 -> x0, local copies, waits for them, and re-layouts: 63.8 us -> none  [the longest x4 16.3 us: attn_backward(): join_heads(grad_queries).astype(jnp.bfloat16)]
    convert_element_type x8 -> x3, other arithmetic: 42.7 us -> 0.5 us  [the longest x1 0.22 us: shards(): query_raw_grad = unit_back(query_raw, grad_query_embed).astype(bf16)]
    reshape x7 -> x1, local copies, waits for them, and re-layouts: 27.5 us -> 0.01 us  [shards(): caption_embed = jnp.einsum('rkt,rtd->rkd', pick_low, caption_all.reshape(...]
    ppermute x102, waiting for transfers between devices: 190 us -> 210 us  [swap(): lax.ppermute(values, axis, [(i, i ^ 1 << bit) for i in range(sizes[axis])])]
    reduce_sum x19 -> x3, other arithmetic: 19.7 us -> 0.52 us  [the longest x1 0.29 us: shards(): jnp.sum(pick_full[:, :, :, None] * caption_raw.reshape(row_count, 1, TEXT...]
    unnamed x395 -> x226, local copies, waits for them, and re-layouts: 16.9 us -> 28.7 us
  transfers between devices with their start and end apart: 104 -> 104, of which waited for: 46 -> 53; matrix products, arithmetic and copies ran while one was open for 49% -> 11% of each run, Pallas kernels for 0% -> 17%
where the time goes in v2:
time: 737 us; the launch traced here: 728 us
  Pallas kernels  269 us (36%)
  waiting for transfers between devices  218 us (30%)
  starting transfers between devices  107 us (15%)
  local copies, waits for them, and re-layouts  77.6 us (11%)
  other arithmetic  46.6 us (6%)
    ppermute x102, waiting for transfers between devices, swap(): lax.ppermute(values, axis, [(i, i ^ 1 << bit) for i in range(sizes[axis])])  210 us
    ppermute x102, starting transfers between devices, swap(): lax.ppermute(values, axis, [(i, i ^ 1 << bit) for i in range(sizes[axis])])  98.1 us
    pallas_call x1, Pallas kernels, cross_backward(): pl.pallas_call(cross_backward_kernel, grid=(rows // take,), in_specs=[pl....  79.8 us
    pallas_call x1, Pallas kernels, cross_forward(): pl.pallas_call(cross_forward_kernel, grid=(rows // take,), in_specs=[pl.B...  55.4 us
    pallas_call x2, Pallas kernels, ffn_backward(): pl.pallas_call(functools.partial(ffn_backward_kernel, which), grid=(hidde...  40.4 us
    pallas_call x1, Pallas kernels, self_backward(): pl.pallas_call(self_backward_kernel, grid=(steps + 4,), in_specs=[held(x....  36.7 us
    pallas_call x2, Pallas kernels, ffn_forward(): pl.pallas_call(functools.partial(ffn_forward_kernel, which), grid=(hidden...  29.7 us
    unnamed x226, local copies, waits for them, and re-layouts  28.7 us
  transfers between devices with their start and end apart: 104, of which 53 were waited for; matrix products, arithmetic and copies ran while one was open for 11% of the time, Pallas kernels for 17%

profile of v2, /device:TPU:0, one launch (start us, length us, event | category | flops | bytes accessed | tf_op | source)
XLA Modules:
  0.0 727.8 jit_solution(13074680136379887865)
XLA Ops:
  6.3 27.3 %self_forward.1 = (bf16[1024,768]{1,0:T(8,128)(2,1)S(1)}, bf16[1024,768]{1,0:T(8,128)(2,1)S(1)}, bf16[1024,768]{1,0:T(8,128)(2,1)S(1)}, bf16[1024,768]{1,0:T(8,1...) custom-call(bf16[1024,768]{1,0:T(8,128)(2,1)S(1)} %bitcast.119, bf16[6,768,768]{2,1,0:T(8,128)(2,1)} %w_ref.7, ...), custom_call_target="tpu_custom_call" | custom-call | tf_op jit(solution)/shard_map/self_forward/pallas_call | solution.py:175
  39.9 15.1 %ffn_forward.2 = (bf16[512,3072]{1,0:T(8,128)(2,1)}, bf16[512,3072]{1,0:T(8,128)(2,1)}, f32[512,768]{1,0:T(8,128)S(1)}, bf16[16,64,768]{2,1,0:T(8,128)(2,1)}, f3...) custom-call(f32[16,64,768]{2,1,0:T(8,128)} %bitcast.136, bf16[2,768,3072]{2,1,0:T(8,128)(2,1)} %in_ref.7, ...), custom_call_target="tpu_custom_call" | custom-call | tf_op jit(solution)/shard_map/ffn_forward/pallas_call | solution.py:601
  62.1 7.6 %copy.65.image_ref = bf16[16,257,1408]{2,1,0:T(8,128)(2,1)S(1)} copy(bf16[16,257,1408]{2,0,1:T(8,128)(2,1)} %param.15) | data formatting | bytes 23158784 | tf_op args[1]
  69.7 4.3 copy-done.24
  74.1 55.4 %cross_forward.1 = (bf16[4096,768]{1,0:T(8,128)(2,1)}, bf16[4096,768]{1,0:T(8,128)(2,1)}, bf16[256,768]{1,0:T(8,128)(2,1)S(1)}, bf16[256,768]{1,0:T(8,128)(2,1)S...) custom-call(bf16[16,257,1408]{2,1,0:T(8,128)(2,1)} %copy-done.24, ...), custom_call_target="tpu_custom_call" | custom-call | tf_op jit(solution)/shard_map/cross_forward/pallas_call | solution.py:374
  135.3 14.7 %ffn_forward.3 = (bf16[512,3072]{1,0:T(8,128)(2,1)}, bf16[512,3072]{1,0:T(8,128)(2,1)}, f32[512,768]{1,0:T(8,128)S(1)}, bf16[16,64,768]{2,1,0:T(8,128)(2,1)}, f3...) custom-call(f32[16,32,768]{2,1,0:T(8,128)S(1)} %bitcast.118, ...), custom_call_target="tpu_custom_call", output_to_operand_aliasing={{3}: (8, {})} | custom-call | tf_op jit(solution)/shard_map/ffn_forward/pallas_call | solution.py:601
  166.3 11.4 %collective-permute-done.4 = bf16[512,256]{1,0:T(8,128)(2,1)} collective-permute-done((bf16[512,256]{1,0:T(8,128)(2,1)}, bf16[512,256]{1,0:T(8,128)(2,1)}, u32[]{:S(2)}, u32[]{:S(2)}) %collective-permute-start.4) | collective-permute-done | bytes 262176 | tf_op jit(solution)/shard_map/ppermute | solution.py:764
  182.3 5.7 all-to-all-start
  189.0 7.6 %all-to-all-done = f32[32,1,1024]{2,1,0:T(1,128)} async-done(((f32[32,1,1024]{2,1,0:T(1,128)}), f32[32,1,1024]{2,1,0:T(1,128)}, u32[]{:S(2)}, u32[]{:S(2)}) %all-to-all-start) | async-done | bytes 131104 | tf_op jit(solution)/shard_map/all_to_all | solution.py:935
  204.1 20.3 %ffn_backward.2 = (f32[16,32,768]{2,1,0:T(8,128)}, bf16[768,3072]{1,0:T(8,128)(2,1)}, bf16[3072,768]{1,0:T(8,128)(2,1)}, bf16[768,256]{1,0:T(8,128)(2,1)S(1)}, f...) custom-call(f32[16,32,768]{2,1,0:T(8,128)} %bitcast.117, f32[512,768]{1,0:T(8,128)} %copy-done.7, ...), custom_call_target="tpu_custom_call" | custom-call | tf_op jit(solution)/shard_map/ffn_backward/pallas_call | solution.py:712
  224.4 79.8 %cross_backward.1 = (f32[16,32,768]{2,1,0:T(8,128)}, bf16[768,1408]{1,0:T(8,128)(2,1)}, bf16[768,1408]{1,0:T(8,128)(2,1)}, bf16[2,768,768]{2,1,0:T(8,128)(2,1)}, f32[8,768]{1,0:T(8,128)S(1)}) custom-call(bf16[16,257,1408]{2,1,0:T(8,128)(2,1)} %copy-done.24, bf16[16,16,1408]{2,1,0:T(8,128)(2,1)S(1)} %pad.6.end_ref, bf16[6,768,768]{2,1,0:T(8,128)(2,1)} %w_ref.7, ...), custom_call_target="tpu_custom_call" | custom-call | tf_op jit(solution)/shard_map/cross_backward/pallas_call | solution.py:507
  345.7 4.0 collective-permute-done.8
  356.3 20.1 %ffn_backward.3 = (f32[16,32,768]{2,1,0:T(8,128)}, bf16[768,3072]{1,0:T(8,128)(2,1)}, bf16[3072,768]{1,0:T(8,128)(2,1)}, bf16[768,256]{1,0:T(8,128)(2,1)S(1)}, f...) custom-call(f32[16,64,768]{2,1,0:T(8,128)} %bitcast.139, f32[512,768]{1,0:T(8,128)} %copy-done.4, ...), custom_call_target="tpu_custom_call" | custom-call | tf_op jit(solution)/shard_map/ffn_backward/pallas_call | solution.py:712
  376.5 36.7 %self_backward.1 = (f32[1024,768]{1,0:T(8,128)}, bf16[4,768,768]{2,1,0:T(8,128)(2,1)}, f32[8,768]{1,0:T(8,128)S(1)}) custom-call(bf16[1024,768]{1,0:T(8,128)(2,1)S(1)} %bitcast.120, bf16[6,768,768]{2,1,0:T(8,128)(2,1)} %w_ref.7, f32[4,768]{1,0:T(4,128)S(1)} %copy-done.17, f32[16,64,256]{2,1,0:T(8,128)S(1)} %tile.10.mask_ref, ...), custom_call_target="tpu_custom_call" | custom-call | tf_op jit(solution)/shard_map/self_backward/pallas_call | solution.py:276
  472.7 4.0 collective-permute-done.43
  487.0 3.7 collective-permute-done.50
  496.1 3.9 collective-permute-done.99
  528.3 8.8 %collective-permute-done.53 = bf16[2,2,1,1,48,1024]{5,4,3,2,1,0:T(8,128)(2,1)S(1)} collective-permute-done((bf16[2,2,1,1,48,1024]{5,4,3,2,1,0:T(8,128)(2,1)S(1)}, bf16[2,2,1,1,48,1024]{5,4,3,2,1,0:T(8,128)(2,1)S(1)}, u32[]{:S(2)}, u32[]{:S(2)}) %collective-permute-start.53) | collective-permute-done | bytes 393248 | tf_op jit(solution)/shard_map/ppermute | solution.py:764
  538.3 6.4 collective-permute-done.74
  551.8 7.2 collective-permute-done.11
  559.1 5.1 collective-permute-done.14
  566.4 4.6 collective-permute-done.19
  572.5 18.6 %collective-permute-done.12 = bf16[2,1,1,1,48,768]{5,4,3,2,1,0:T(8,128)(2,1)S(1)} collective-permute-done((bf16[2,1,1,1,48,768]{5,4,3,2,1,0:T(8,128)(2,1)S(1)}, bf16[2,1,1,1,48,768]{5,4,3,2,1,0:T(8,128)(2,1)S(1)}, u32[]{:S(2)}, u32[]{:S(2)}) %collective-permute-start.12) | collective-permute-done | bytes 147488 | tf_op jit(solution)/shard_map/ppermute | solution.py:764
  598.9 4.3 collective-permute-done.56
  608.4 7.1 collective-permute-done.22
  617.7 4.6 collective-permute-done.16
  646.7 17.7 %collective-permute-done.64 = bf16[2,1,2,1,48,1024]{5,4,3,2,1,0:T(8,128)(2,1)S(1)} collective-permute-done((bf16[2,1,2,1,48,1024]{5,4,3,2,1,0:T(8,128)(2,1)S(1)}, bf16[2,1,2,1,48,1024]{5,4,3,2,1,0:T(8,128)(2,1)S(1)}, u32[]{:S(2)}, u32[]{:S(2)}) %collective-permute-start.64) | collective-permute-done | bytes 393248 | tf_op jit(solution)/shard_map/ppermute | solution.py:764
  682.6 5.5 collective-permute-done.59
  688.5 7.5 %collective-permute-done.80 = bf16[1,1,1,1,192,256]{5,4,3,2,1,0:T(8,128)(2,1)S(1)} collective-permute-done((bf16[1,1,1,1,192,256]{5,4,3,2,1,0:T(8,128)(2,1)S(1)}, bf16[1,1,1,1,192,256]{5,4,3,2,1,0:T(8,128)(2,1)S(1)}, u32[]{:S(2)}, u32[]{:S(2)}) %collective-permute-start.80) | collective-permute-done | bytes 98336 | tf_op jit(solution)/shard_map/ppermute | solution.py:764
  696.1 7.1 collective-permute-done.30
  707.2 3.6 collective-permute-done.66
  713.2 4.7 collective-permute-done.71
  (627 shorter events, 290.3 us)
Async XLA Ops:
  61.7 89.4 %collective-permute-start.1 = (bf16[64,256]{1,0:T(8,128)(2,1)}, bf16[64,256]{1,0:T(8,128)(2,1)}, u32[]{:S(2)}, u32[]{:S(2)}) collective-permute-start(bf16[64,256]{1,0:T(8,128)(2,1)} %pad_maximum_fusion.4), channel_id=1, source_target_pairs={{0,2},{2,0},{4,6},{6,4},{8,10},{10,8},{12,14},{14,12},{16,18},{18,... | collective-permute-start | bytes 98312 | tf_op jit(solution)/shard_map/ppermute | solution.py:764
  338.9 106.3 %collective-permute-start.20 = (bf16[2,2,2,1,48,768]{5,4,3,2,1,0:T(8,128)(2,1)}, bf16[2,2,2,1,48,768]{5,4,3,2,1,0:T(8,128)(2,1)}, u32[]{:S(2)}, u32[]{:S(2)}) collective-permute-start(bf16[2,2,2,1,48,768]{5,4,3,2,1,0:T(8,128)(2,1)} %constant_dynamic-slice_fusion.42), channel_id=1, source_target_pairs={{0,2},{2,0},{4,6},{6,4},{8,10},{10,8},{12,14},{14,12},{16,18},{18,... | collective-permute-start | bytes 1769480 | tf_op jit(solution)/shard_map/ppermute | solution.py:764
  339.0 125.9 %collective-permute-start.60 = (bf16[2,2,2,1,48,1024]{5,4,3,2,1,0:T(8,128)(2,1)}, bf16[2,2,2,1,48,1024]{5,4,3,2,1,0:T(8,128)(2,1)}, u32[]{:S(2)}, u32[]{:S(2)}) collective-permute-start(bf16[2,2,2,1,48,1024]{5,4,3,2,1,0:T(8,128)(2,1)} %constant_dynamic-slice_fusion), channel_id=1, source_target_pairs={{0,2},{2,0},{4,6},{6,4},{8,10},{10,8},{12,14},{14,12},{16,18},{18,... | collective-permute-start | bytes 2359304 | tf_op jit(solution)/shard_map/ppermute | solution.py:764
  344.6 122.1 %collective-permute-start.52 = (bf16[2,2,2,1,48,1024]{5,4,3,2,1,0:T(8,128)(2,1)}, bf16[2,2,2,1,48,1024]{5,4,3,2,1,0:T(8,128)(2,1)}, u32[]{:S(2)}, u32[]{:S(2)}) collective-permute-start(bf16[2,2,2,1,48,1024]{5,4,3,2,1,0:T(8,128)(2,1)} %constant_dynamic-slice_fusion.7), channel_id=1, source_target_pairs={{0,2},{2,0},{4,6},{6,4},{8,10},{10,8},{12,14},{14,12},{16,18},{18,... | collective-permute-start | bytes 2359304 | tf_op jit(solution)/shard_map/ppermute | solution.py:764
  349.7 82.6 %collective-permute-start.40 = (bf16[2,1,2,1,48,512]{5,4,3,2,1,0:T(8,128)(2,1)}, bf16[2,1,2,1,48,512]{5,4,3,2,1,0:T(8,128)(2,1)S(1)}, u32[]{:S(2)}, u32[]{:S(2)}) collective-permute-start(bf16[2,1,2,1,48,512]{5,4,3,2,1,0:T(8,128)(2,1)} %add_convert_fusion.24), channel_id=1, source_target_pairs={{0,8},{2,10},{4,12},{6,14},{8,0},{10,2},{12,4},{14,6},{16,24},{18,... | collective-permute-start | bytes 589832 | tf_op jit(solution)/shard_map/ppermute | solution.py:764
  353.5 80.5 %collective-permute-start.42 = (bf16[2,1,2,1,48,512]{5,4,3,2,1,0:T(8,128)(2,1)}, bf16[2,1,2,1,48,512]{5,4,3,2,1,0:T(8,128)(2,1)}, u32[]{:S(2)}, u32[]{:S(2)}) collective-permute-start(bf16[2,1,2,1,48,512]{5,4,3,2,1,0:T(8,128)(2,1)} %add_convert_fusion.23), channel_id=1, source_target_pairs={{0,8},{2,10},{4,12},{6,14},{8,0},{10,2},{12,4},{14,6},{16,24},{18,... | collective-permute-start | bytes 589832 | tf_op jit(solution)/shard_map/ppermute | solution.py:764
  414.9 35.1 %all-to-all-start.1 = ((f32[32,1,592]{2,1,0:T(1,128)}), f32[32,1,592]{2,1,0:T(1,128)S(1)}, u32[]{:S(2)}, u32[]{:S(2)}) async-start(f32[32,1,592]{2,1,0:T(1,128)} %copy.76), calls=%async_computation.1 | async-start | bytes 163840 | tf_op jit(solution)/shard_map/all_to_all | solution.py:1077
  443.5 26.2 %collective-permute-start.81 = (bf16[2,2,2,1,192,256]{5,4,3,2,1,0:T(8,128)(2,1)}, bf16[2,2,2,1,192,256]{5,4,3,2,1,0:T(8,128)(2,1)}, u32[]{:S(2)}, u32[]{:S(2)}) collective-permute-start(bf16[2,2,2,1,192,256]{5,4,3,2,1,0:T(8,128)(2,1)} %constant_dynamic-slice_fusion.49), channel_id=1, source_target_pairs={{0,2},{2,0},{4,6},{6,4},{8,10},{10,8},{12,14},{14,12},{16,18},{18,... | collective-permute-start | bytes 2359304 | tf_op jit(solution)/shard_map/ppermute | solution.py:764
  463.9 59.4 %collective-permute-start.26 = (bf16[2,2,2,1,48,768]{5,4,3,2,1,0:T(8,128)(2,1)}, bf16[2,2,2,1,48,768]{5,4,3,2,1,0:T(8,128)(2,1)S(1)}, u32[]{:S(2)}, u32[]{:S(2)}) collective-permute-start(bf16[2,2,2,1,48,768]{5,4,3,2,1,0:T(8,128)(2,1)} %constant_dynamic-slice_fusion.36), channel_id=1, source_target_pairs={{0,2},{2,0},{4,6},{6,4},{8,10},{10,8},{12,14},{14,12},{16,18},{18,... | collective-permute-start | bytes 1769480 | tf_op jit(solution)/shard_map/ppermute | solution.py:764
  464.9 59.8 %collective-permute-start.67 = (bf16[2,2,2,1,48,1024]{5,4,3,2,1,0:T(8,128)(2,1)}, bf16[2,2,2,1,48,1024]{5,4,3,2,1,0:T(8,128)(2,1)S(1)}, u32[]{:S(2)}, u32[]{:S(2)}) collective-permute-start(bf16[2,2,2,1,48,1024]{5,4,3,2,1,0:T(8,128)(2,1)} %constant_dynamic-slice_fusion.30), channel_id=1, source_target_pairs={{0,2},{2,0},{4,6},{6,4},{8,10},{10,8},{12,14},{14,12},{16,18},{18,... | collective-permute-start | bytes 2359304 | tf_op jit(solution)/shard_map/ppermute | solution.py:764
  466.7 29.2 %collective-permute-start.96 = (bf16[2,1,1,1,48,256]{5,4,3,2,1,0:T(8,128)(2,1)S(1)}, bf16[2,1,1,1,48,256]{5,4,3,2,1,0:T(8,128)(2,1)S(1)}, u32[]{:S(2)}, u32[]{:S(2)}) collective-permute-start(bf16[2,1,1,1,48,256]{5,4,3,2,1,0:T(8,128)(2,1)S(1)} %copy-done.98), channel_id=1, source_target_pairs={{0,8},{2,10},{4,12},{6,14},{8,0},{10,2},{12,4},{14,6},{16,24},{18,... | collective-permute-start | bytes 147464 | tf_op jit(solution)/shard_map/ppermute | solution.py:764
  472.4 52.2 %collective-permute-start.10 = (bf16[2,2,2,1,48,768]{5,4,3,2,1,0:T(8,128)(2,1)}, bf16[2,2,2,1,48,768]{5,4,3,2,1,0:T(8,128)(2,1)S(1)}, u32[]{:S(2)}, u32[]{:S(2)}) collective-permute-start(bf16[2,2,2,1,48,768]{5,4,3,2,1,0:T(8,128)(2,1)} %constant_dynamic-slice_fusion.53), channel_id=1, source_target_pairs={{0,2},{2,0},{4,6},{6,4},{8,10},{10,8},{12,14},{14,12},{16,18},{18,... | collective-permute-start | bytes 1769480 | tf_op jit(solution)/shard_map/ppermute | solution.py:764
  496.0 29.2 %collective-permute-start.25 = (bf16[2,2,2,1,48,768]{5,4,3,2,1,0:T(8,128)(2,1)}, bf16[2,2,2,1,48,768]{5,4,3,2,1,0:T(8,128)(2,1)S(1)}, u32[]{:S(2)}, u32[]{:S(2)}) collective-permute-start(bf16[2,2,2,1,48,768]{5,4,3,2,1,0:T(8,128)(2,1)} %constant_dynamic-slice_fusion.37), channel_id=1, source_target_pairs={{0,2},{2,0},{4,6},{6,4},{8,10},{10,8},{12,14},{14,12},{16,18},{18,... | collective-permute-start | bytes 1769480 | tf_op jit(solution)/shard_map/ppermute | solution.py:764
  524.7 20.7 %collective-permute-start.68 = (bf16[2,2,2,1,48,1024]{5,4,3,2,1,0:T(8,128)(2,1)}, bf16[2,2,2,1,48,1024]{5,4,3,2,1,0:T(8,128)(2,1)S(1)}, u32[]{:S(2)}, u32[]{:S(2)}) collective-permute-start(bf16[2,2,2,1,48,1024]{5,4,3,2,1,0:T(8,128)(2,1)} %constant_dynamic-slice_fusion.29), channel_id=1, source_target_pairs={{0,2},{2,0},{4,6},{6,4},{8,10},{10,8},{12,14},{14,12},{16,18},{18,... | collective-permute-start | bytes 2359304 | tf_op jit(solution)/shard_map/ppermute | solution.py:764
  546.5 47.7 %collective-permute-start.61 = (bf16[2,1,2,1,48,1024]{5,4,3,2,1,0:T(8,128)(2,1)S(1)}, bf16[2,1,2,1,48,1024]{5,4,3,2,1,0:T(8,128)(2,1)S(1)}, u32[]{:S(2)}, u32[]{:S(2)}) collective-permute-start(bf16[2,1,2,1,48,1024]{5,4,3,2,1,0:T(8,128)(2,1)S(1)} %add_convert_fusion.7), channel_id=1, source_target_pairs={{0,8},{2,10},{4,12},{6,14},{8,0},{10,2},{12,4},{14,6},{16,24},{18,... | collective-permute-start | bytes 1179656 | tf_op jit(solution)/shard_map/ppermute | solution.py:764
  559.0 45.7 %collective-permute-start.82 = (bf16[2,1,2,1,192,256]{5,4,3,2,1,0:T(8,128)(2,1)S(1)}, bf16[2,1,2,1,192,256]{5,4,3,2,1,0:T(8,128)(2,1)S(1)}, u32[]{:S(2)}, u32[]{:S(2)}) collective-permute-start(bf16[2,1,2,1,192,256]{5,4,3,2,1,0:T(8,128)(2,1)S(1)} %add_convert_fusion.2), channel_id=1, source_target_pairs={{0,8},{2,10},{4,12},{6,14},{8,0},{10,2},{12,4},{14,6},{16,24},{18,... | collective-permute-start | bytes 1179656 | tf_op jit(solution)/shard_map/ppermute | solution.py:764
  564.3 31.6 %collective-permute-start.63 = (bf16[2,1,2,1,48,1024]{5,4,3,2,1,0:T(8,128)(2,1)S(1)}, bf16[2,1,2,1,48,1024]{5,4,3,2,1,0:T(8,128)(2,1)S(1)}, u32[]{:S(2)}, u32[]{:S(2)}) collective-permute-start(bf16[2,1,2,1,48,1024]{5,4,3,2,1,0:T(8,128)(2,1)S(1)} %add_convert_fusion.6), channel_id=1, source_target_pairs={{0,8},{2,10},{4,12},{6,14},{8,0},{10,2},{12,4},{14,6},{16,24},{18,... | collective-permute-start | bytes 1179656 | tf_op jit(solution)/shard_map/ppermute | solution.py:764
  564.7 26.4 %collective-permute-start.12 = (bf16[2,1,1,1,48,768]{5,4,3,2,1,0:T(8,128)(2,1)S(1)}, bf16[2,1,1,1,48,768]{5,4,3,2,1,0:T(8,128)(2,1)S(1)}, u32[]{:S(2)}, u32[]{:S(2)}) collective-permute-start(bf16[2,1,1,1,48,768]{5,4,3,2,1,0:T(8,128)(2,1)S(1)} %add_convert_fusion.31), channel_id=1, source_target_pairs={{0,8},{2,10},{4,12},{6,14},{8,0},{10,2},{12,4},{14,6},{16,24},{18,... | collective-permute-start | bytes 442376 | tf_op jit(solution)/shard_map/ppermute | solution.py:764
  571.0 22.7 %collective-permute-start.15 = (bf16[2,1,1,1,48,768]{5,4,3,2,1,0:T(8,128)(2,1)S(1)}, bf16[2,1,1,1,48,768]{5,4,3,2,1,0:T(8,128)(2,1)S(1)}, u32[]{:S(2)}, u32[]{:S(2)}) collective-permute-start(bf16[2,1,1,1,48,768]{5,4,3,2,1,0:T(8,128)(2,1)S(1)} %add_convert_fusion.30), channel_id=1, source_target_pairs={{0,8},{2,10},{4,12},{6,14},{8,0},{10,2},{12,4},{14,6},{16,24},{18,... | collective-permute-start | bytes 442376 | tf_op jit(solution)/shard_map/ppermute | solution.py:764
  594.3 29.5 %collective-permute-start.27 = (bf16[2,2,2,1,48,768]{5,4,3,2,1,0:T(8,128)(2,1)S(1)}, bf16[2,2,2,1,48,768]{5,4,3,2,1,0:T(8,128)(2,1)S(1)}, u32[]{:S(2)}, u32[]{:S(2)}) collective-permute-start(bf16[2,2,2,1,48,768]{5,4,3,2,1,0:T(8,128)(2,1)S(1)} %get-tuple-element.146), channel_id=1, source_target_pairs={{0,1},{1,0},{2,3},{3,2},{4,5},{5,4},{6,7},{7,6},{8,9},{9,8},{10,11... | collective-permute-start | bytes 1769480 | tf_op jit(solution)/shard_map/ppermute | solution.py:764
  595.8 21.2 %collective-permute-start.77 = (bf16[2,2,1,1,192,256]{5,4,3,2,1,0:T(8,128)(2,1)S(1)}, bf16[2,2,1,1,192,256]{5,4,3,2,1,0:T(8,128)(2,1)S(1)}, u32[]{:S(2)}, u32[]{:S(2)}) collective-permute-start(bf16[2,2,1,1,192,256]{5,4,3,2,1,0:T(8,128)(2,1)S(1)} %add_convert_fusion.3), channel_id=1, source_target_pairs={{0,4},{2,6},{4,0},{6,2},{8,12},{10,14},{12,8},{14,10},{16,20},{18,... | collective-permute-start | bytes 1179656 | tf_op jit(solution)/shard_map/ppermute | solution.py:764
  604.7 28.4 %collective-permute-start.54 = (bf16[2,1,1,1,48,1024]{5,4,3,2,1,0:T(8,128)(2,1)S(1)}, bf16[2,1,1,1,48,1024]{5,4,3,2,1,0:T(8,128)(2,1)S(1)}, u32[]{:S(2)}, u32[]{:S(2)}) collective-permute-start(bf16[2,1,1,1,48,1024]{5,4,3,2,1,0:T(8,128)(2,1)S(1)} %add_convert_fusion.22), channel_id=1, source_target_pairs={{0,8},{2,10},{4,12},{6,14},{8,0},{10,2},{12,4},{14,6},{16,24},{18,... | collective-permute-start | bytes 589832 | tf_op jit(solution)/shard_map/ppermute | solution.py:764
  605.3 33.3 %collective-permute-start.75 = (bf16[2,1,1,1,192,256]{5,4,3,2,1,0:T(8,128)(2,1)S(1)}, bf16[2,1,1,1,192,256]{5,4,3,2,1,0:T(8,128)(2,1)S(1)}, u32[]{:S(2)}, u32[]{:S(2)}) collective-permute-start(bf16[2,1,1,1,192,256]{5,4,3,2,1,0:T(8,128)(2,1)S(1)} %add_convert_fusion.18), channel_id=1, source_target_pairs={{0,8},{2,10},{4,12},{6,14},{8,0},{10,2},{12,4},{14,6},{16,24},{18,... | collective-permute-start | bytes 589832 | tf_op jit(solution)/shard_map/ppermute | solution.py:764
  617.0 48.9 %collective-permute-start.69 = (bf16[2,2,2,1,48,1024]{5,4,3,2,1,0:T(8,128)(2,1)S(1)}, bf16[2,2,2,1,48,1024]{5,4,3,2,1,0:T(8,128)(2,1)S(1)}, u32[]{:S(2)}, u32[]{:S(2)}) collective-permute-start(bf16[2,2,2,1,48,1024]{5,4,3,2,1,0:T(8,128)(2,1)S(1)} %get-tuple-element.136), channel_id=1, source_target_pairs={{0,1},{1,0},{2,3},{3,2},{4,5},{5,4},{6,7},{7,6},{8,9},{9,8},{10,11... | collective-permute-start | bytes 2359304 | tf_op jit(solution)/shard_map/ppermute | solution.py:764
  631.3 36.4 %collective-permute-start.90 = (bf16[2,2,2,1,192,256]{5,4,3,2,1,0:T(8,128)(2,1)S(1)}, bf16[2,2,2,1,192,256]{5,4,3,2,1,0:T(8,128)(2,1)S(1)}, u32[]{:S(2)}, u32[]{:S(2)}) collective-permute-start(bf16[2,2,2,1,192,256]{5,4,3,2,1,0:T(8,128)(2,1)S(1)} %get-tuple-element.128), channel_id=1, source_target_pairs={{0,1},{1,0},{2,3},{3,2},{4,5},{5,4},{6,7},{7,6},{8,9},{9,8},{10,11... | collective-permute-start | bytes 2359304 | tf_op jit(solution)/shard_map/ppermute | solution.py:764
  635.7 28.7 %collective-permute-start.64 = (bf16[2,1,2,1,48,1024]{5,4,3,2,1,0:T(8,128)(2,1)S(1)}, bf16[2,1,2,1,48,1024]{5,4,3,2,1,0:T(8,128)(2,1)S(1)}, u32[]{:S(2)}, u32[]{:S(2)}) collective-permute-start(bf16[2,1,2,1,48,1024]{5,4,3,2,1,0:T(8,128)(2,1)S(1)} %get-tuple-element.120), channel_id=1, source_target_pairs={{0,1},{1,0},{2,3},{3,2},{4,5},{5,4},{6,7},{7,6},{8,9},{9,8},{10,11... | collective-permute-start | bytes 1179656 | tf_op jit(solution)/shard_map/ppermute | solution.py:764
  644.5 28.3 %collective-permute-start.85 = (bf16[2,1,2,1,192,256]{5,4,3,2,1,0:T(8,128)(2,1)S(1)}, bf16[2,1,2,1,192,256]{5,4,3,2,1,0:T(8,128)(2,1)S(1)}, u32[]{:S(2)}, u32[]{:S(2)}) collective-permute-start(bf16[2,1,2,1,192,256]{5,4,3,2,1,0:T(8,128)(2,1)S(1)} %get-tuple-element.118), channel_id=1, source_target_pairs={{0,1},{1,0},{2,3},{3,2},{4,5},{5,4},{6,7},{7,6},{8,9},{9,8},{10,11... | collective-permute-start | bytes 1179656 | tf_op jit(solution)/shard_map/ppermute | solution.py:764
  645.4 31.3 %collective-permute-start.58 = (bf16[2,1,1,1,48,1024]{5,4,3,2,1,0:T(8,128)(2,1)S(1)}, bf16[2,1,1,1,48,1024]{5,4,3,2,1,0:T(8,128)(2,1)S(1)}, u32[]{:S(2)}, u32[]{:S(2)}) collective-permute-start(bf16[2,1,1,1,48,1024]{5,4,3,2,1,0:T(8,128)(2,1)S(1)} %get-tuple-element.116), channel_id=1, source_target_pairs={{0,1},{1,0},{2,3},{3,2},{4,5},{5,4},{6,7},{7,6},{8,9},{9,8},{10,11... | collective-permute-start | bytes 589832 | tf_op jit(solution)/shard_map/ppermute | solution.py:764
  667.7 36.4 %collective-permute-start.65 = (bf16[2,1,1,1,48,1024]{5,4,3,2,1,0:T(8,128)(2,1)S(1)}, bf16[2,1,1,1,48,1024]{5,4,3,2,1,0:T(8,128)(2,1)S(1)}, u32[]{:S(2)}, u32[]{:S(2)}) collective-permute-start(bf16[2,1,1,1,48,1024]{5,4,3,2,1,0:T(8,128)(2,1)S(1)} %add_convert_fusion.20), channel_id=1, source_target_pairs={{0,4},{2,6},{4,0},{6,2},{8,12},{10,14},{12,8},{14,10},{16,20},{18,... | collective-permute-start | bytes 589832 | tf_op jit(solution)/shard_map/ppermute | solution.py:764
  672.8 38.1 %collective-permute-start.70 = (bf16[2,2,1,1,48,1024]{5,4,3,2,1,0:T(8,128)(2,1)S(1)}, bf16[2,2,1,1,48,1024]{5,4,3,2,1,0:T(8,128)(2,1)S(1)}, u32[]{:S(2)}, u32[]{:S(2)}) collective-permute-start(bf16[2,2,1,1,48,1024]{5,4,3,2,1,0:T(8,128)(2,1)S(1)} %add_convert_fusion.5), channel_id=1, source_target_pairs={{0,4},{2,6},{4,0},{6,2},{8,12},{10,14},{12,8},{14,10},{16,20},{18,... | collective-permute-start | bytes 1179656 | tf_op jit(solution)/shard_map/ppermute | solution.py:764
  676.7 27.4 %collective-permute-start.86 = (bf16[2,1,1,1,192,256]{5,4,3,2,1,0:T(8,128)(2,1)S(1)}, bf16[2,1,1,1,192,256]{5,4,3,2,1,0:T(8,128)(2,1)S(1)}, u32[]{:S(2)}, u32[]{:S(2)}) collective-permute-start(bf16[2,1,1,1,192,256]{5,4,3,2,1,0:T(8,128)(2,1)S(1)} %add_convert_fusion.16), channel_id=1, source_target_pairs={{0,4},{2,6},{4,0},{6,2},{8,12},{10,14},{12,8},{14,10},{16,20},{18,... | collective-permute-start | bytes 589832 | tf_op jit(solution)/shard_map/ppermute | solution.py:764
  678.8 32.6 %collective-permute-start.91 = (bf16[2,2,1,1,192,256]{5,4,3,2,1,0:T(8,128)(2,1)S(1)}, bf16[2,2,1,1,192,256]{5,4,3,2,1,0:T(8,128)(2,1)S(1)}, u32[]{:S(2)}, u32[]{:S(2)}) collective-permute-start(bf16[2,2,1,1,192,256]{5,4,3,2,1,0:T(8,128)(2,1)S(1)} %add_convert_fusion), channel_id=1, source_target_pairs={{0,4},{2,6},{4,0},{6,2},{8,12},{10,14},{12,8},{14,10},{16,20},{18,... | collective-permute-start | bytes 1179656 | tf_op jit(solution)/shard_map/ppermute | solution.py:764
  (184 other events, 1820.4 us)

commit v3 on v2

--- a/solution.py
+++ b/solution.py
@@ -68,6 +68,15 @@
 
 def held(shape, index):
     return pl.BlockSpec(shape, index, pipeline_mode=pl.Buffered(1))
+
+
+def cost(micros):
+    return pl.CostEstimate(flops=int(micros * 1.1e9), bytes_accessed=0, transcendentals=0)
+
+
+def store_units(ref, values):
+    for place in range(values.shape[1] // 128):
+        ref[place] = values[:, place * 128 : (place + 1) * 128].astype(ref.dtype)
 
 
 def params(mib):
@@ -186,6 +195,7 @@
         out_shape=[low, low, low, low, full, full],
         compiler_params=params(40),
         name="self_forward",
+        cost_estimate=cost(27),
     )(x, weights, biases, gains, mask)
 
 
@@ -259,7 +269,7 @@
         @pl.when(step == steps + place)
         def _():
             left = mix_ref if place == 3 else x_ref
-            dw_ref[0] = dot_tn(left[...], right[...]).astype(bf16)
+            store_units(dw_ref.at[0], dot_tn(left[...], right[...]))
 
 
 def self_backward(x, weights, gains, mask, q, k, v, mix, total, top, text):
@@ -291,17 +301,18 @@
         ],
         out_specs=[
             tile,
-            pl.BlockSpec((1, width, width), lambda i: (jnp.maximum(i - steps, 0), 0, 0)),
+            pl.BlockSpec((1, width // 128, width, 128), lambda i: (jnp.maximum(i - steps, 0), 0, 0, 0)),
             whole((8, width)),
         ],
         out_shape=[
             jax.ShapeDtypeStruct(x.shape, f32),
-            jax.ShapeDtypeStruct((4, width, width), bf16),
+            jax.ShapeDtypeStruct((4, width // 128, width, 128), bf16),
             jax.ShapeDtypeStruct((8, width), f32),
         ],
         scratch_shapes=[scratch] * 4 + [pltpu.VMEM((count, width), bf16)],
         compiler_params=params(48),
         name="self_backward",
+        cost_estimate=cost(37),
     )(x, weights, gains, mask, q, k, v, mix, total, top, text)
 
 
@@ -396,6 +407,7 @@
         ],
         compiler_params=params(48),
         name="cross_forward",
+        cost_estimate=cost(55),
     )(images, ends, kv, weights, biases, gains, norm)
 
 
@@ -411,6 +423,7 @@
     q_ref,
     mix_ref,
     down_ref,
+    order_ref,
     dnorm_ref,
     dkey_w_ref,
     dvalue_w_ref,
@@ -426,6 +439,7 @@
     dq_all,
     dmix_all,
 ):
+    del order_ref
     step = pl.program_id(0)
     rows_here = image_ref.shape[0]
     main = image_ref.shape[1] - 1
@@ -490,12 +504,13 @@
 
     @pl.when(step == pl.num_programs(0) - 1)
     def _():
-        dkey_w_ref[...] = key_sum[...].astype(bf16)
-        dvalue_w_ref[...] = value_sum[...].astype(bf16)
-        dw_ref[...] = w_sum[...].astype(bf16)
-
-
-def cross_backward(images, ends, weights, norm, keys, values, key_ends, value_ends, q, mix, down):
+        store_units(dkey_w_ref, key_sum[...])
+        store_units(dvalue_w_ref, value_sum[...])
+        store_units(dw_ref.at[0], w_sum[0])
+        store_units(dw_ref.at[1], w_sum[1])
+
+
+def cross_backward(images, ends, weights, norm, keys, values, key_ends, value_ends, q, mix, down, order):
     rows, patches, vis = images.shape
     main = patches - 1
     width = norm.shape[-1]
@@ -519,19 +534,20 @@
             tile,
             tile,
             tile,
+            pl.BlockSpec(memory_space=pl.ANY),
         ],
         out_specs=[
             part,
-            held((width, vis), lambda i: (0, 0)),
-            held((width, vis), lambda i: (0, 0)),
-            held((2, width, width), lambda i: (0, 0, 0)),
+            held((vis // 128, width, 128), lambda i: (0, 0, 0)),
+            held((vis // 128, width, 128), lambda i: (0, 0, 0)),
+            held((2, width // 128, width, 128), lambda i: (0, 0, 0, 0)),
             whole((8, width)),
         ],
         out_shape=[
             jax.ShapeDtypeStruct((rows, QUERIES, width), f32),
-            jax.ShapeDtypeStruct((width, vis), bf16),
-            jax.ShapeDtypeStruct((width, vis), bf16),
-            jax.ShapeDtypeStruct((2, width, width), bf16),
+            jax.ShapeDtypeStruct((vis // 128, width, 128), bf16),
+            jax.ShapeDtypeStruct((vis // 128, width, 128), bf16),
+            jax.ShapeDtypeStruct((2, width // 128, width, 128), bf16),
             jax.ShapeDtypeStruct((8, width), f32),
         ],
         scratch_shapes=[
@@ -547,7 +563,8 @@
         ],
         compiler_params=params(52),
         name="cross_backward",
-    )(images, ends, weights, norm, keys, values, key_ends, value_ends, q, mix, down)
+        cost_estimate=cost(79),
+    )(images, ends, weights, norm, keys, values, key_ends, value_ends, q, mix, down, order)
 
 
 def ffn_forward_kernel(
@@ -632,6 +649,7 @@
         input_output_aliases={8: 3} if halves else {},
         compiler_params=params(48),
         name="ffn_forward",
+        cost_estimate=cost(15),
     )(norm, ffn_in, ffn_bias, ffn_out, projections, proj_bias, biases, gains, *halves)
 
 
@@ -675,7 +693,7 @@
         side_ref[0:1] = dgain
         side_ref[1:2] = dshift
         side_ref[2:3] = jnp.sum(branch.astype(f32), 0, keepdims=True)
-        dproj_ref[...] = dot_tn(layer_ref[...].reshape(tokens, width), raw).astype(bf16)
+        store_units(dproj_ref, dot_tn(layer_ref[...].reshape(tokens, width), raw))
         dproj_bias_ref[...] = jnp.broadcast_to(
             jnp.sum(raw.astype(f32), 0, keepdims=True), dproj_bias_ref.shape
         )
@@ -684,8 +702,8 @@
     branch = branch_all[...]
     du = (dot_nt(branch, out_ref[0]) * slope_ref[...].astype(f32)).astype(bf16)
     rest[...] += dot_nt(du, in_ref[0])
-    dout_ref[...] = dot_tn(act_ref[...], branch).astype(bf16)
-    din_ref[...] = dot_nn(low_turned[...], du).astype(bf16)
+    store_units(dout_ref, dot_tn(act_ref[...], branch))
+    store_units(din_ref, dot_nn(low_turned[...], du))
     dbias_ref[...] = jnp.broadcast_to(jnp.sum(du.astype(f32), 0, keepdims=True), dbias_ref.shape)
 
     @pl.when(step == pl.num_programs(0) - 1)
@@ -728,18 +746,18 @@
         ],
         out_specs=[
             whole((rows, QUERIES, width)),
-            pl.BlockSpec((width, chunk), lambda j: (0, j)),
-            pl.BlockSpec((chunk, width), lambda j: (j, 0)),
-            whole((width, embed)),
+            pl.BlockSpec((chunk // 128, width, 128), lambda j: (j, 0, 0)),
+            pl.BlockSpec((width // 128, chunk, 128), lambda j: (0, j, 0)),
+            whole((embed // 128, width, 128)),
             whole((8, width)),
             pl.BlockSpec((8, chunk), lambda j: (0, j)),
             whole((8, embed)),
         ],
         out_shape=[
             jax.ShapeDtypeStruct((rows, QUERIES, width), f32),
-            jax.ShapeDtypeStruct((width, hidden), bf16),
-            jax.ShapeDtypeStruct((hidden, width), bf16),
-            jax.ShapeDtypeStruct((width, embed), bf16),
+            jax.ShapeDtypeStruct((hidden // 128, width, 128), bf16),
+            jax.ShapeDtypeStruct((width // 128, hidden, 128), bf16),
+            jax.ShapeDtypeStruct((embed // 128, width, 128), bf16),
             jax.ShapeDtypeStruct((8, width), f32),
             jax.ShapeDtypeStruct((8, hidden), f32),
             jax.ShapeDtypeStruct((8, embed), f32),
@@ -751,6 +769,7 @@
         ],
         compiler_params=params(52),
         name="ffn_backward",
+        cost_estimate=cost(20),
     )(norm, total, before, layer, grad, raw, projections, gains, ffn_in, ffn_out, act, slope)
 
 
@@ -762,97 +781,102 @@
 def swap(values, stage, sizes):
     axis, bit = stage
     return lax.ppermute(values, axis, [(i, i ^ (1 << bit)) for i in range(sizes[axis])])
-
-
-def bit_stages(sizes):
-    depth = sizes["dp"].bit_length() - 1
-    return [("dp", bit) for bit in range(depth)]
 
 
 def pick(term, places):
     array, fixed = term
     starts = [0] * array.ndim
     extent = list(array.shape)
-    for dim, place in fixed.items():
-        starts[dim] = place
-        extent[dim] = 1
-    for dim, place in places.items():
+    for dim, place in (fixed | places).items():
         starts[dim] = place
         extent[dim] = 1
     return lax.dynamic_slice(array, starts, extent)
 
 
 def total(terms, places):
-    return sum(pick(term, places).astype(jnp.float32) for term in terms)
-
-
-def halve(terms, stage, dim, sizes):
-    mine = own_bit(stage)
-    send = total(terms, {dim: 1 - mine}).astype(jnp.bfloat16)
-    arrived = swap(send, stage, sizes)
-    kept = [(array, {**fixed, dim: mine}) for array, fixed in terms]
-    return kept + [(arrived, {})]
-
-
-def pair_scatter(first, second, order, sizes):
+    return sum(pick(term, places).astype(f32) for term in terms)
+
+
+def swap_all(pieces, stage, sizes):
+    flat = [piece.reshape(-1, 128) for piece in pieces]
+    sent = flat[0] if len(flat) == 1 else jnp.concatenate(flat, 0)
+    arrived = swap(sent, stage, sizes)
+    start, got = 0, []
+    for piece, rows in zip(pieces, flat):
+        got.append(arrived[start : start + rows.shape[0]].reshape(piece.shape))
+        start += rows.shape[0]
+    return got
+
+
+def scatter_pairs(pairs, order, sizes):
     depth = sizes["dp"].bit_length() - 1
 
     def spread(array):
-        rows, cols = array.shape
-        return array.reshape((2,) * depth + (rows // sizes["dp"], cols))
-
-    streams = [[(spread(first), {})], [(spread(second), {})]]
+        units, rows, lanes = array.shape
+        return array.reshape((units,) + (2,) * depth + (rows // sizes["dp"], lanes))
+
+    streams = [[[(spread(array), {})] for array in pair] for pair in pairs]
     for stage in order:
+        mine = own_bit(stage)
         if stage[0] == "rep":
-            mine = own_bit(stage)
-            sums = [total(terms, {}) for terms in streams]
-            send = jnp.where(mine == 0, sums[1], sums[0]).astype(jnp.bfloat16)
-            keep = jnp.where(mine == 0, sums[0], sums[1])
-            streams = [[(keep, {}), (swap(send, stage, sizes), {})]]
+            sums = [[total(terms, {}) for terms in pair] for pair in streams]
+            sent = [jnp.where(mine == 0, two, one).astype(bf16) for one, two in sums]
+            kept = [jnp.where(mine == 0, one, two).astype(bf16) for one, two in sums]
+            got = swap_all(sent, stage, sizes)
+            streams = [[[(keep, {}), (piece, {})]] for keep, piece in zip(kept, got)]
         else:
-            dim = depth - 1 - stage[1]
-            streams = [halve(terms, stage, dim, sizes) for terms in streams]
-    result = total(streams[0], {})
-    return result.reshape(result.shape[-2:])
+            dim = depth - stage[1]
+            sent = [total(terms, {dim: 1 - mine}).astype(bf16) for pair in streams for terms in pair]
+            got = iter(swap_all(sent, stage, sizes))
+            streams = [
+                [
+                    [(array, fixed | {dim: mine}) for array, fixed in terms] + [(next(got), {})]
+                    for terms in pair
+                ]
+                for pair in streams
+            ]
+    results = []
+    for (terms,) in streams:
+        result = total(terms, {})
+        results.append(result.reshape(result.shape[0], result.shape[-2], 128))
+    return results
 
 
 def orders(sizes):
-    stages = bit_stages(sizes)
+    stages = [("dp", bit) for bit in range(sizes["dp"].bit_length() - 1)]
     head, mid, tail = stages[:1], stages[1:3], stages[3:]
     ring = mid + [("rep", 0)]
     return [head + ring[k:] + ring[:k] + tail for k in range(3)]
 
 
-def scatter_parts(first, second, sizes):
-    cols = first.shape[1]
-    lanes = cols // 128
-    cuts = [0, 128 * ((lanes + 2) // 3), 128 * ((2 * lanes + 2) // 3), cols]
-    done = [
-        pair_scatter(first[:, a:b], second[:, a:b], order, sizes)
-        for a, b, order in zip(cuts[:-1], cuts[1:], orders(sizes))
+def cut_units(array, part):
+    units = array.shape[0]
+    edges = [(units * k + 1) // 3 for k in range(4)]
+    return array[edges[part] : edges[part + 1]]
+
+
+def scatter_group(pairs, sizes):
+    parts = [
+        scatter_pairs([tuple(cut_units(array, part) for array in pair) for pair in pairs], order, sizes)
+        for part, order in enumerate(orders(sizes))
     ]
-    return jnp.concatenate(done, 1)
+    joined = [jnp.concatenate(pieces, 0) for pieces in zip(*parts)]
+    return [array.transpose(1, 0, 2).reshape(array.shape[1], -1) for array in joined]
+
+
+def exchange(values, sizes):
+    return lax.all_to_all(values, ("dp", "rep"), 0, 0, tiled=True)
 
 
 def gather_rows(values, sizes):
-    stages = [("rep", 0)] + bit_stages(sizes)
-    for stage in stages:
-        other = swap(values, stage, sizes)
-        low = own_bit(stage) == 0
-        values = jnp.concatenate([jnp.where(low, values, other), jnp.where(low, other, values)], 0)
-    return values
+    world = sizes["dp"] * sizes["rep"]
+    return exchange(jnp.tile(values, (world, 1)), sizes)
 
 
 def scatter_rows(values, sizes):
-    stages = bit_stages(sizes)
-    depth = len(stages)
-    count = values.shape[0] // (2 * sizes["dp"])
-    terms = [(values.reshape((2,) * (depth + 1) + (count, values.shape[1])), {})]
-    for stage in stages:
-        terms = halve(terms, stage, depth - 1 - stage[1], sizes)
-    terms = halve(terms, ("rep", 0), depth, sizes)
-    result = total(terms, {})
-    return result.reshape(result.shape[-2:])
+    world = sizes["dp"] * sizes["rep"]
+    arrived = exchange(values, sizes)
+    return jnp.sum(arrived.reshape(world, -1, values.shape[1]).astype(f32), 0)
 
 
 def shards(
@@ -932,14 +956,7 @@
     row_total = jnp.sum(affinity, 1)
     partial_cols = jnp.sum(affinity, 0)
     all_cols = jnp.sum(
-        lax.all_to_all(
-            jnp.broadcast_to(partial_cols[None], (world,) + partial_cols.shape),
-            ("dp", "rep"),
-            0,
-            0,
-            tiled=True,
-        ),
-        0,
+        exchange(jnp.broadcast_to(partial_cols[None], (world,) + partial_cols.shape), sizes), 0
     )
     own_cols = lax.dynamic_slice_in_dim(all_cols, offset, captions_here, 0).reshape(row_count, 2)
     inverse_all = 1.0 / all_cols
@@ -1007,9 +1024,9 @@
             text_slope,
         )
     )
-    ffn_in_grad = scatter_parts(query_din, text_din, sizes)
-    ffn_out_grad = scatter_parts(query_dout, text_dout, sizes)
-    proj_grad = pair_scatter(query_dproj, text_dproj, orders(sizes)[0], sizes)
+    ffn_in_grad, ffn_out_grad, proj_grad = scatter_group(
+        [(query_din, text_din), (query_dout, text_dout), (query_dproj, text_dproj)], sizes
+    )
     query_first, key_grad, value_grad, cross_dw, cross_side = cross_backward(
         image_features,
         image_ends,
@@ -1022,8 +1039,9 @@
         cross_q,
         cross_mix,
         grad_second.reshape(row_count * QUERIES, width),
-    )
-    cross_grad = scatter_parts(key_grad, value_grad, sizes)
+        text_first,
+    )
+    (cross_grad,) = scatter_group([(key_grad, value_grad)], sizes)
     input_grad, self_dw, self_side = self_backward(
         inputs,
         attn_weights,
@@ -1038,12 +1056,7 @@
         text_first,
     )
     attn_pairs = ((self_dw[0], self_dw[3]), (self_dw[1], cross_dw[0]), (self_dw[2], cross_dw[1]))
-    attn_grad = jnp.stack(
-        [
-            pair_scatter(one, two, order, sizes)
-            for (one, two), order in zip(attn_pairs, orders(sizes))
-        ]
-    )
+    attn_grad = jnp.stack(scatter_group(attn_pairs, sizes))
     gain_grad = jnp.stack([self_side[0], query_side[3], query_side[0], text_side[0]])
     bias_grad = jnp.stack(
         [
@@ -1074,7 +1087,7 @@
         return cut.transpose(2, 0, 1, 3).reshape(world, -1)
 
     dealt = jnp.concatenate([deal(array) for array in vectors], 1)
-    arrived = jnp.sum(lax.all_to_all(dealt, ("dp", "rep"), 0, 0, tiled=True), 0)
+    arrived = jnp.sum(exchange(dealt, sizes), 0)
     small = []
     start = 0
     for array in vectors:

time: 737 us -> 693 us (0.940)
  waiting for transfers between devices: 218 us -> 119 us
  local copies, waits for them, and re-layouts: 77.6 us -> 146 us
  starting transfers between devices: 107 us -> 74.9 us
  other arithmetic: 46.6 us -> 63.4 us
    ppermute x102 -> x45, waiting for transfers between devices: 210 us -> 111 us  [swap(): lax.ppermute(values, axis, [(i, i ^ 1 << bit) for i in range(sizes[axis])])]
    ppermute x102 -> x45, starting transfers between devices: 98.1 us -> 51.7 us  [swap(): lax.ppermute(values, axis, [(i, i ^ 1 << bit) for i in range(sizes[axis])])]
    slice x10 -> x55, local copies, waits for them, and re-layouts: 16.2 us -> 39.9 us  [the longest x11 22.3 us: cut_units(): return array[edges[part]:edges[part + 1]]]
    unnamed x226 -> x362, local copies, waits for them, and re-layouts: 28.7 us -> 51.2 us
    concatenate x4 -> x26, other arithmetic: 1.36 us -> 23.7 us  [swap_all(): sent = flat[0] if len(flat) == 1 else jnp.concatenate(flat, 0)]
    all_to_all x2 -> x4, starting transfers between devices: 8.51 us -> 23.2 us  [exchange(): return lax.all_to_all(values, ('dp', 'rep'), 0, 0, tiled=True)]
    dynamic_slice x27 -> x50, local copies, waits for them, and re-layouts: 20.9 us -> 30.4 us  [pick(): return lax.dynamic_slice(array, starts, extent)]
    convert_element_type x70 -> x86, other arithmetic: 32.9 us -> 30.5 us  [the longest x66 23.6 us: scatter_pairs(): total(terms, {dim: 1 - mine}).astype(bf16)]
  transfers between devices with their start and end apart: 104 -> 49, of which waited for: 53 -> 26; matrix products, arithmetic and copies ran while one was open for 11% -> 20% of each run, Pallas kernels for 17% -> 13%
where the time goes in v3:
time: 693 us; the launch traced here: 686 us
  Pallas kernels  269 us (39%)
  local copies, waits for them, and re-layouts  146 us (21%)
  waiting for transfers between devices  119 us (17%)
  starting transfers between devices  74.9 us (11%)
  other arithmetic  63.4 us (9%)
  matrix products  8.65 us (1%)
    ppermute x45, waiting for transfers between devices, swap(): lax.ppermute(values, axis, [(i, i ^ 1 << bit) for i in range(sizes[axis])])  111 us
    pallas_call x1, Pallas kernels, cross_backward(): pl.pallas_call(cross_backward_kernel, grid=(rows // take,), in_specs=[pl....  79.8 us
    pallas_call x1, Pallas kernels, cross_forward(): pl.pallas_call(cross_forward_kernel, grid=(rows // take,), in_specs=[pl.B...  55.3 us
    ppermute x45, starting transfers between devices, swap(): lax.ppermute(values, axis, [(i, i ^ 1 << bit) for i in range(sizes[axis])])  51.7 us
    unnamed x362, local copies, waits for them, and re-layouts  51.2 us
    pallas_call x2, Pallas kernels, ffn_backward(): pl.pallas_call(functools.partial(ffn_backward_kernel, which), grid=(hidde...  40 us
    pallas_call x1, Pallas kernels, self_backward(): pl.pallas_call(self_backward_kernel, grid=(steps + 4,), in_specs=[held(x....  37.2 us
    dynamic_slice x50, local copies, waits for them, and re-layouts, pick(): return lax.dynamic_slice(array, starts, extent)  30.4 us
  transfers between devices with their start and end apart: 49, of which 26 were waited for; matrix products, arithmetic and copies ran while one was open for 20% of the time, Pallas kernels for 13%

profile of v3, /device:TPU:0, one launch (start us, length us, event | category | flops | bytes accessed | tf_op | source)
XLA Modules:
  0.0 685.6 jit_solution(5491929650733639540)
XLA Ops:
  6.3 27.6 %self_forward.1 = (bf16[1024,768]{1,0:T(8,128)(2,1)S(1)}, bf16[1024,768]{1,0:T(8,128)(2,1)S(1)}, bf16[1024,768]{1,0:T(8,128)(2,1)S(1)}, bf16[1024,768]{1,0:T(8,1...) custom-call(bf16[1024,768]{1,0:T(8,128)(2,1)S(1)} %bitcast.962, bf16[6,768,768]{2,1,0:T(8,128)(2,1)} %w_ref.7, ...), custom_call_target="tpu_custom_call" | custom-call | flops 29699999744 | tf_op jit(solution)/shard_map/self_forward/pallas_call | solution.py:184
  40.2 15.0 %ffn_forward.2 = (bf16[512,3072]{1,0:T(8,128)(2,1)}, bf16[512,3072]{1,0:T(8,128)(2,1)}, f32[512,768]{1,0:T(8,128)S(1)}, bf16[16,64,768]{2,1,0:T(8,128)(2,1)}, f3...) custom-call(f32[16,64,768]{2,1,0:T(8,128)} %bitcast.1478, bf16[2,768,3072]{2,1,0:T(8,128)(2,1)} %in_ref.7, ...), custom_call_target="tpu_custom_call" | custom-call | flops 16499999744 | tf_op jit(solution)/shard_map/ffn_forward/pallas_call | solution.py:618
  57.5 7.6 %all-to-all-start = ((bf16[32,32,256]{2,1,0:T(8,128)(2,1)}), bf16[32,32,256]{2,1,0:T(8,128)(2,1)}, u32[]{:S(2)}, u32[]{:S(2)}) async-start(bf16[32,32,256]{2,1,0:T(8,128)(2,1)} %tile.20), calls=%async_computation | async-start | bytes 1048576 | tf_op jit(solution)/shard_map/all_to_all | solution.py:868
  65.1 7.6 %copy.1325.image_ref = bf16[16,257,1408]{2,1,0:T(8,128)(2,1)S(1)} copy(bf16[16,257,1408]{2,0,1:T(8,128)(2,1)} %param.15) | data formatting | bytes 23158784 | tf_op args[1]
  72.7 4.2 copy-done.24
  77.0 55.3 %cross_forward.1 = (bf16[4096,768]{1,0:T(8,128)(2,1)}, bf16[4096,768]{1,0:T(8,128)(2,1)}, bf16[256,768]{1,0:T(8,128)(2,1)S(1)}, bf16[256,768]{1,0:T(8,128)(2,1)S...) custom-call(bf16[16,257,1408]{2,1,0:T(8,128)(2,1)} %copy-done.24, ...), custom_call_target="tpu_custom_call" | custom-call | flops 60500000768 | tf_op jit(solution)/shard_map/cross_forward/pallas_call | solution.py:385
  137.5 14.4 %ffn_forward.3 = (bf16[512,3072]{1,0:T(8,128)(2,1)}, bf16[512,3072]{1,0:T(8,128)(2,1)}, f32[512,768]{1,0:T(8,128)S(1)}, bf16[16,64,768]{2,1,0:T(8,128)(2,1)}, f3...) custom-call(f32[16,32,768]{2,1,0:T(8,128)S(1)} %bitcast.965, ...), custom_call_target="tpu_custom_call", output_to_operand_aliasing={{3}: (8, {})} | custom-call | flops 16499999744 | tf_op jit(solution)/shard_map/ffn_forward/pallas_call | solution.py:618
  157.5 5.9 all-to-all-start.1
  163.8 8.3 %all-to-all-done.1 = f32[32,1,1024]{2,1,0:T(1,128)S(1)} async-done(((f32[32,1,1024]{2,1,0:T(1,128)}), f32[32,1,1024]{2,1,0:T(1,128)S(1)}, u32[]{:S(2)}, u32[]{:S(2)}) %all-to-all-start.1) | async-done | bytes 131104 | tf_op jit(solution)/shard_map/all_to_all | solution.py:868
  172.9 3.3 fusion.1
  177.9 3.6 all-to-all-start.2
  181.8 20.1 %ffn_backward.2 = (f32[16,32,768]{2,1,0:T(8,128)}, bf16[24,768,128]{2,1,0:T(8,128)(2,1)}, bf16[6,3072,128]{2,1,0:T(8,128)(2,1)}, bf16[2,768,128]{2,1,0:T(8,128)(...) custom-call(f32[16,32,768]{2,1,0:T(8,128)} %bitcast.964, f32[512,768]{1,0:T(8,128)} %copy-done.11, ...), custom_call_target="tpu_custom_call" | custom-call | flops 22000001024 | tf_op jit(solution)/shard_map/ffn_backward/pallas_call | solution.py:730
  202.6 4.2 fusion.94
  217.1 20.0 %ffn_backward.3 = (f32[16,32,768]{2,1,0:T(8,128)}, bf16[24,768,128]{2,1,0:T(8,128)(2,1)}, bf16[6,3072,128]{2,1,0:T(8,128)(2,1)}, bf16[2,768,128]{2,1,0:T(8,128)(...) custom-call(f32[16,64,768]{2,1,0:T(8,128)} %bitcast.1480, f32[512,768]{1,0:T(8,128)} %copy-done.10, ...), custom_call_target="tpu_custom_call" | custom-call | flops 22000001024 | tf_op jit(solution)/shard_map/ffn_backward/pallas_call | solution.py:730
  237.1 79.8 %cross_backward.1 = (f32[16,32,768]{2,1,0:T(8,128)}, bf16[11,768,128]{2,1,0:T(8,128)(2,1)}, bf16[11,768,128]{2,1,0:T(8,128)(2,1)}, bf16[2,6,768,128]{3,2,1,0:T(8,128)(2,1)}, f32[8,768]{1,0:T(8,128)S(1)}) custom-call(bf16[16,257,1408]{2,1,0:T(8,128)(2,1)} %copy-done.24, bf16[16,16,1408]{2,1,0:T(8,128)(2,1)S(1)} %pad.6.end_ref, bf16[6,768,768]{2,1,0:T(8,128)(2,1)} %w_ref.7, ...), custom_call_target="tpu_custom_call" | custom-call | flops 86899998720 | tf_op jit(solution)/shard_map/cross_backward/pallas_call | solution.py:522
  326.3 37.2 %self_backward.1 = (f32[1024,768]{1,0:T(8,128)}, bf16[4,6,768,128]{3,2,1,0:T(8,128)(2,1)}, f32[8,768]{1,0:T(8,128)S(1)}) custom-call(bf16[1024,768]{1,0:T(8,128)(2,1)S(1)} %bitcast.963, bf16[6,768,768]{2,1,0:T(8,128)(2,1)} %w_ref.7, f32[4,768]{1,0:T(4,128)S(1)} %copy-done.7, f32[16,64,256]{2,1,0:T(8,128)S(1)} %copy-done.1, bf16[1024,768]{1,0:T(8,128)(2,1)S(1)} %copy-done.15, ...), custom_call_target="tpu_custom_call" | custom-call | flops 40699998208 | tf_op jit(solution)/shard_map/self_backward/pallas_call | solution.py:286
  363.5 4.0 fusion.95
  385.3 6.1 all-to-all-start.3
  407.8 18.7 %pad_maximum_fusion = bf16[12288,128]{1,0:T(8,128)(2,1)} fusion(bf16[3072,128]{1,0:T(8,128)(2,1)S(1)} %bitcast.1011, bf16[3072,128]{1,0:T(8,128)(2,1)S(1)} %bitcast.1009, bf16[3072,128]{1,0:T(8,128)(2,1)S(1)} %bitcast.1010, bf16[3072,128]{1,0:T(8,128)(2,1)S(1)} %bitcast.1008), kind=kLoop, calls=%fused_computation | loop fusion | flops 12582912 | bytes 6291456 | tf_op jit(solution)/shard_map/concatenate | solution.py:802
  506.8 12.9 %collective-permute-done.18 = bf16[384,128]{1,0:T(8,128)(2,1)S(1)} collective-permute-done((bf16[384,128]{1,0:T(8,128)(2,1)S(1)}, bf16[384,128]{1,0:T(8,128)(2,1)S(1)}, u32[]{:S(2)}, u32[]{:S(2)}) %collective-permute-start.18) | collective-permute-done | bytes 98336 | tf_op jit(solution)/shard_map/ppermute | solution.py:783
  520.1 4.2 collective-permute-done.28
  524.3 3.1 collective-permute-start.19
  541.1 5.5 collective-permute-done.6
  559.5 3.3 collective-permute-done.2
  568.0 3.1 collective-permute-start.14
  601.5 13.1 %collective-permute-done.36 = bf16[6144,128]{1,0:T(8,128)(2,1)S(1)} collective-permute-done((bf16[6144,128]{1,0:T(8,128)(2,1)S(1)}, bf16[6144,128]{1,0:T(8,128)(2,1)S(1)}, u32[]{:S(2)}, u32[]{:S(2)}) %collective-permute-start.36) | collective-permute-done | bytes 1572896 | tf_op jit(solution)/shard_map/ppermute | solution.py:783
  617.8 5.6 collective-permute-done.31
  624.8 13.3 %collective-permute-done.41 = bf16[6528,128]{1,0:T(8,128)(2,1)S(1)} collective-permute-done((bf16[6528,128]{1,0:T(8,128)(2,1)S(1)}, bf16[6528,128]{1,0:T(8,128)(2,1)S(1)}, u32[]{:S(2)}, u32[]{:S(2)}) %collective-permute-start.41) | collective-permute-done | bytes 1671200 | tf_op jit(solution)/shard_map/ppermute | solution.py:783
  639.1 11.9 %collective-permute-done.37 = bf16[3072,128]{1,0:T(8,128)(2,1)S(1)} collective-permute-done((bf16[3072,128]{1,0:T(8,128)(2,1)S(1)}, bf16[3072,128]{1,0:T(8,128)(2,1)S(1)}, u32[]{:S(2)}, u32[]{:S(2)}) %collective-permute-start.37) | collective-permute-done | bytes 786464 | tf_op jit(solution)/shard_map/ppermute | solution.py:783
  654.2 4.9 collective-permute-done.38
  661.2 7.6 %collective-permute-done.39 = bf16[768,128]{1,0:T(8,128)(2,1)S(1)} collective-permute-done((bf16[768,128]{1,0:T(8,128)(2,1)S(1)}, bf16[768,128]{1,0:T(8,128)(2,1)S(1)}, u32[]{:S(2)}, u32[]{:S(2)}) %collective-permute-start.39) | collective-permute-done | bytes 196640 | tf_op jit(solution)/shard_map/ppermute | solution.py:783
  673.1 6.3 collective-permute-done.34
  (821 shorter events, 243.3 us)
Async XLA Ops:
  57.5 96.2 %all-to-all-start = ((bf16[32,32,256]{2,1,0:T(8,128)(2,1)}), bf16[32,32,256]{2,1,0:T(8,128)(2,1)}, u32[]{:S(2)}, u32[]{:S(2)}) async-start(bf16[32,32,256]{2,1,0:T(8,128)(2,1)} %tile.20), calls=%async_computation | async-start | bytes 1048576 | tf_op jit(solution)/shard_map/all_to_all | solution.py:868
  157.5 14.6 %all-to-all-start.1 = ((f32[32,1,1024]{2,1,0:T(1,128)}), f32[32,1,1024]{2,1,0:T(1,128)S(1)}, u32[]{:S(2)}, u32[]{:S(2)}) async-start(f32[32,1,1024]{2,1,0:T(1,128)} %broadcast_in_dim.6), calls=%async_computation.1 | async-start | bytes 262144 | tf_op jit(solution)/shard_map/all_to_all | solution.py:868
  177.9 37.5 %all-to-all-start.2 = ((bf16[32,32,256]{2,1,0:T(8,128)(2,1)}), bf16[32,32,256]{2,1,0:T(8,128)(2,1)}, u32[]{:S(2)}, u32[]{:S(2)}) async-start(bf16[32,32,256]{2,1,0:T(8,128)(2,1)} %bitcast.17), calls=%async_computation.2 | async-start | bytes 1048576 | tf_op jit(solution)/shard_map/all_to_all | solution.py:868
  385.3 62.1 %all-to-all-start.3 = ((f32[32,1,592]{2,1,0:T(1,128)}), f32[32,1,592]{2,1,0:T(1,128)S(1)}, u32[]{:S(2)}, u32[]{:S(2)}) async-start(f32[32,1,592]{2,1,0:T(1,128)} %copy.1646), calls=%async_computation.3 | async-start | bytes 163840 | tf_op jit(solution)/shard_map/all_to_all | solution.py:868
  395.7 51.8 %collective-permute-start.20 = (bf16[2304,128]{1,0:T(8,128)(2,1)}, bf16[2304,128]{1,0:T(8,128)(2,1)}, u32[]{:S(2)}, u32[]{:S(2)}) collective-permute-start(bf16[2304,128]{1,0:T(8,128)(2,1)} %pad_maximum_fusion.8), channel_id=1, source_target_pairs={{0,2},{2,0},{4,6},{6,4},{8,10},{10,8},{12,14},{14,12},{16,18},{18,... | collective-permute-start | bytes 1769480 | tf_op jit(solution)/shard_map/ppermute | solution.py:783
  397.4 54.1 %collective-permute-start.15 = (bf16[3072,128]{1,0:T(8,128)(2,1)}, bf16[3072,128]{1,0:T(8,128)(2,1)}, u32[]{:S(2)}, u32[]{:S(2)}) collective-permute-start(bf16[3072,128]{1,0:T(8,128)(2,1)} %pad_maximum_fusion.4), channel_id=1, source_target_pairs={{0,2},{2,0},{4,6},{6,4},{8,10},{10,8},{12,14},{14,12},{16,18},{18,... | collective-permute-start | bytes 2359304 | tf_op jit(solution)/shard_map/ppermute | solution.py:783
  398.8 62.2 %collective-permute-start.25 = (bf16[3072,128]{1,0:T(8,128)(2,1)}, bf16[3072,128]{1,0:T(8,128)(2,1)}, u32[]{:S(2)}, u32[]{:S(2)}) collective-permute-start(bf16[3072,128]{1,0:T(8,128)(2,1)} %pad_maximum_fusion.5), channel_id=1, source_target_pairs={{0,2},{2,0},{4,6},{6,4},{8,10},{10,8},{12,14},{14,12},{16,18},{18,... | collective-permute-start | bytes 2359304 | tf_op jit(solution)/shard_map/ppermute | solution.py:783
  426.6 155.2 %collective-permute-start.35 = (bf16[12288,128]{1,0:T(8,128)(2,1)}, bf16[12288,128]{1,0:T(8,128)(2,1)}, u32[]{:S(2)}, u32[]{:S(2)}) collective-permute-start(bf16[12288,128]{1,0:T(8,128)(2,1)} %pad_maximum_fusion), channel_id=1, source_target_pairs={{0,2},{2,0},{4,6},{6,4},{8,10},{10,8},{12,14},{14,12},{16,18},{18,... | collective-permute-start | bytes 9437192 | tf_op jit(solution)/shard_map/ppermute | solution.py:783
  432.2 49.4 %collective-permute-start = (bf16[4608,128]{1,0:T(8,128)(2,1)}, bf16[4608,128]{1,0:T(8,128)(2,1)}, u32[]{:S(2)}, u32[]{:S(2)}) collective-permute-start(bf16[4608,128]{1,0:T(8,128)(2,1)} %constant_dynamic-update-slice_fusion), channel_id=1, source_target_pairs={{0,2},{2,0},{4,6},{6,4},{8,10},{10,8},{12,14},{14,12},{16,18},{18,... | collective-permute-start | bytes 3538952 | tf_op jit(solution)/shard_map/ppermute | solution.py:783
  454.9 23.1 %collective-permute-start.16 = (bf16[1536,128]{1,0:T(8,128)(2,1)}, bf16[1536,128]{1,0:T(8,128)(2,1)}, u32[]{:S(2)}, u32[]{:S(2)}) collective-permute-start(bf16[1536,128]{1,0:T(8,128)(2,1)} %pad_maximum_fusion.12), channel_id=1, source_target_pairs={{0,4},{2,6},{4,0},{6,2},{8,12},{10,14},{12,8},{14,10},{16,20},{18,... | collective-permute-start | bytes 1179656 | tf_op jit(solution)/shard_map/ppermute | solution.py:783
  467.3 9.7 %collective-permute-start.26 = (bf16[1536,128]{1,0:T(8,128)(2,1)}, bf16[1536,128]{1,0:T(8,128)(2,1)}, u32[]{:S(2)}, u32[]{:S(2)}) collective-permute-start(bf16[1536,128]{1,0:T(8,128)(2,1)} %bitcast.239), channel_id=1, source_target_pairs={{0,1},{1,0},{2,3},{3,2},{4,5},{5,4},{6,7},{7,6},{8,9},{9,8},{10,11... | collective-permute-start | bytes 1179656 | tf_op jit(solution)/shard_map/ppermute | solution.py:783
  474.8 115.2 %collective-permute-start.30 = (bf16[13056,128]{1,0:T(8,128)(2,1)}, bf16[13056,128]{1,0:T(8,128)(2,1)}, u32[]{:S(2)}, u32[]{:S(2)}) collective-permute-start(bf16[13056,128]{1,0:T(8,128)(2,1)} %constant_dynamic-update-slice_fusion.36), channel_id=1, source_target_pairs={{0,2},{2,0},{4,6},{6,4},{8,10},{10,8},{12,14},{14,12},{16,18},{18,... | collective-permute-start | bytes 10027016 | tf_op jit(solution)/shard_map/ppermute | solution.py:783
  478.0 117.3 %collective-permute-start.40 = (bf16[13056,128]{1,0:T(8,128)(2,1)}, bf16[13056,128]{1,0:T(8,128)(2,1)}, u32[]{:S(2)}, u32[]{:S(2)}) collective-permute-start(bf16[13056,128]{1,0:T(8,128)(2,1)} %copy-done.142), channel_id=1, source_target_pairs={{0,2},{2,0},{4,6},{6,4},{8,10},{10,8},{12,14},{14,12},{16,18},{18,... | collective-permute-start | bytes 10027016 | tf_op jit(solution)/shard_map/ppermute | solution.py:783
  481.6 10.3 %collective-permute-start.10 = (bf16[4608,128]{1,0:T(8,128)(2,1)S(1)}, bf16[4608,128]{1,0:T(8,128)(2,1)S(1)}, u32[]{:S(2)}, u32[]{:S(2)}) collective-permute-start(bf16[4608,128]{1,0:T(8,128)(2,1)S(1)} %copy-done.146), channel_id=1, source_target_pairs={{0,2},{2,0},{4,6},{6,4},{8,10},{10,8},{12,14},{14,12},{16,18},{18,... | collective-permute-start | bytes 3538952 | tf_op jit(solution)/shard_map/ppermute | solution.py:783
  484.6 17.9 %collective-permute-start.17 = (bf16[768,128]{1,0:T(8,128)(2,1)S(1)}, bf16[768,128]{1,0:T(8,128)(2,1)S(1)}, u32[]{:S(2)}, u32[]{:S(2)}) collective-permute-start(bf16[768,128]{1,0:T(8,128)(2,1)S(1)} %pad_maximum_fusion.19), channel_id=1, source_target_pairs={{0,8},{2,10},{4,12},{6,14},{8,0},{10,2},{12,4},{14,6},{16,24},{18,... | collective-permute-start | bytes 589832 | tf_op jit(solution)/shard_map/ppermute | solution.py:783
  491.9 13.2 %collective-permute-start.27 = (bf16[768,128]{1,0:T(8,128)(2,1)S(1)}, bf16[768,128]{1,0:T(8,128)(2,1)S(1)}, u32[]{:S(2)}, u32[]{:S(2)}) collective-permute-start(bf16[768,128]{1,0:T(8,128)(2,1)S(1)} %bitcast.1394), channel_id=1, source_target_pairs={{0,4},{2,6},{4,0},{6,2},{8,12},{10,14},{12,8},{14,10},{16,20},{18,... | collective-permute-start | bytes 589832 | tf_op jit(solution)/shard_map/ppermute | solution.py:783
  502.6 34.6 %collective-permute-start.11 = (bf16[2304,128]{1,0:T(8,128)(2,1)}, bf16[2304,128]{1,0:T(8,128)(2,1)}, u32[]{:S(2)}, u32[]{:S(2)}) collective-permute-start(bf16[2304,128]{1,0:T(8,128)(2,1)} %pad_maximum_fusion.7), channel_id=1, source_target_pairs={{0,1},{1,0},{2,3},{3,2},{4,5},{5,4},{6,7},{7,6},{8,9},{9,8},{10,11... | collective-permute-start | bytes 1769480 | tf_op jit(solution)/shard_map/ppermute | solution.py:783
  505.2 14.5 %collective-permute-start.18 = (bf16[384,128]{1,0:T(8,128)(2,1)S(1)}, bf16[384,128]{1,0:T(8,128)(2,1)S(1)}, u32[]{:S(2)}, u32[]{:S(2)}) collective-permute-start(bf16[384,128]{1,0:T(8,128)(2,1)S(1)} %bitcast.1465), channel_id=1, source_target_pairs={{0,1},{1,0},{2,3},{3,2},{4,5},{5,4},{6,7},{7,6},{8,9},{9,8},{10,11... | collective-permute-start | bytes 294920 | tf_op jit(solution)/shard_map/ppermute | solution.py:783
  535.4 11.2 %collective-permute-start.6 = (bf16[2304,128]{1,0:T(8,128)(2,1)}, bf16[2304,128]{1,0:T(8,128)(2,1)}, u32[]{:S(2)}, u32[]{:S(2)}) collective-permute-start(bf16[2304,128]{1,0:T(8,128)(2,1)} %constant_dynamic-update-slice_fusion.24), channel_id=1, source_target_pairs={{0,8},{2,10},{4,12},{6,14},{8,0},{10,2},{12,4},{14,6},{16,24},{18,... | collective-permute-start | bytes 1769480 | tf_op jit(solution)/shard_map/ppermute | solution.py:783
  537.2 13.6 %collective-permute-start.1 = (bf16[2304,128]{1,0:T(8,128)(2,1)}, bf16[2304,128]{1,0:T(8,128)(2,1)S(1)}, u32[]{:S(2)}, u32[]{:S(2)}) collective-permute-start(bf16[2304,128]{1,0:T(8,128)(2,1)} %copy-done.148), channel_id=1, source_target_pairs={{0,4},{2,6},{4,0},{6,2},{8,12},{10,14},{12,8},{14,10},{16,20},{18,... | collective-permute-start | bytes 1769480 | tf_op jit(solution)/shard_map/ppermute | solution.py:783
  546.6 9.4 %collective-permute-start.12 = (bf16[1152,128]{1,0:T(8,128)(2,1)S(1)}, bf16[1152,128]{1,0:T(8,128)(2,1)S(1)}, u32[]{:S(2)}, u32[]{:S(2)}) collective-permute-start(bf16[1152,128]{1,0:T(8,128)(2,1)S(1)} %pad_maximum_fusion.15), channel_id=1, source_target_pairs={{0,4},{2,6},{4,0},{6,2},{8,12},{10,14},{12,8},{14,10},{16,20},{18,... | collective-permute-start | bytes 884744 | tf_op jit(solution)/shard_map/ppermute | solution.py:783
  586.9 27.6 %collective-permute-start.36 = (bf16[6144,128]{1,0:T(8,128)(2,1)S(1)}, bf16[6144,128]{1,0:T(8,128)(2,1)S(1)}, u32[]{:S(2)}, u32[]{:S(2)}) collective-permute-start(bf16[6144,128]{1,0:T(8,128)(2,1)S(1)} %pad_maximum_fusion.2), channel_id=1, source_target_pairs={{0,8},{2,10},{4,12},{6,14},{8,0},{10,2},{12,4},{14,6},{16,24},{18,... | collective-permute-start | bytes 4718600 | tf_op jit(solution)/shard_map/ppermute | solution.py:783
  595.3 28.1 %collective-permute-start.31 = (bf16[6528,128]{1,0:T(8,128)(2,1)S(1)}, bf16[6528,128]{1,0:T(8,128)(2,1)S(1)}, u32[]{:S(2)}, u32[]{:S(2)}) collective-permute-start(bf16[6528,128]{1,0:T(8,128)(2,1)S(1)} %constant_dynamic-update-slice_fusion.42), channel_id=1, source_target_pairs={{0,4},{2,6},{4,0},{6,2},{8,12},{10,14},{12,8},{14,10},{16,20},{18,... | collective-permute-start | bytes 5013512 | tf_op jit(solution)/shard_map/ppermute | solution.py:783
  601.4 36.7 %collective-permute-start.41 = (bf16[6528,128]{1,0:T(8,128)(2,1)S(1)}, bf16[6528,128]{1,0:T(8,128)(2,1)S(1)}, u32[]{:S(2)}, u32[]{:S(2)}) collective-permute-start(bf16[6528,128]{1,0:T(8,128)(2,1)S(1)} %pad_maximum_fusion.1), channel_id=1, source_target_pairs={{0,1},{1,0},{2,3},{3,2},{4,5},{5,4},{6,7},{7,6},{8,9},{9,8},{10,11... | collective-permute-start | bytes 5013512 | tf_op jit(solution)/shard_map/ppermute | solution.py:783
  616.2 34.7 %collective-permute-start.37 = (bf16[3072,128]{1,0:T(8,128)(2,1)S(1)}, bf16[3072,128]{1,0:T(8,128)(2,1)S(1)}, u32[]{:S(2)}, u32[]{:S(2)}) collective-permute-start(bf16[3072,128]{1,0:T(8,128)(2,1)S(1)} %pad_maximum_fusion.6), channel_id=1, source_target_pairs={{0,1},{1,0},{2,3},{3,2},{4,5},{5,4},{6,7},{7,6},{8,9},{9,8},{10,11... | collective-permute-start | bytes 2359304 | tf_op jit(solution)/shard_map/ppermute | solution.py:783
  624.1 27.6 %collective-permute-start.32 = (bf16[3264,128]{1,0:T(8,128)(2,1)S(1)}, bf16[3264,128]{1,0:T(8,128)(2,1)S(1)}, u32[]{:S(2)}, u32[]{:S(2)}) collective-permute-start(bf16[3264,128]{1,0:T(8,128)(2,1)S(1)} %constant_dynamic-update-slice_fusion.48), channel_id=1, source_target_pairs={{0,8},{2,10},{4,12},{6,14},{8,0},{10,2},{12,4},{14,6},{16,24},{18,... | collective-permute-start | bytes 2506760 | tf_op jit(solution)/shard_map/ppermute | solution.py:783
  638.6 15.2 %collective-permute-start.42 = (bf16[3264,128]{1,0:T(8,128)(2,1)S(1)}, bf16[3264,128]{1,0:T(8,128)(2,1)S(1)}, u32[]{:S(2)}, u32[]{:S(2)}) collective-permute-start(bf16[3264,128]{1,0:T(8,128)(2,1)S(1)} %pad_maximum_fusion.3), channel_id=1, source_target_pairs={{0,4},{2,6},{4,0},{6,2},{8,12},{10,14},{12,8},{14,10},{16,20},{18,... | collective-permute-start | bytes 2506760 | tf_op jit(solution)/shard_map/ppermute | solution.py:783
  652.4 16.5 %collective-permute-start.33 = (bf16[1632,128]{1,0:T(8,128)(2,1)S(1)}, bf16[1632,128]{1,0:T(8,128)(2,1)S(1)}, u32[]{:S(2)}, u32[]{:S(2)}) collective-permute-start(bf16[1632,128]{1,0:T(8,128)(2,1)S(1)} %pad_maximum_fusion.10), channel_id=1, source_target_pairs={{0,1},{1,0},{2,3},{3,2},{4,5},{5,4},{6,7},{7,6},{8,9},{9,8},{10,11... | collective-permute-start | bytes 1253384 | tf_op jit(solution)/shard_map/ppermute | solution.py:783
  659.3 9.5 %collective-permute-start.39 = (bf16[768,128]{1,0:T(8,128)(2,1)S(1)}, bf16[768,128]{1,0:T(8,128)(2,1)S(1)}, u32[]{:S(2)}, u32[]{:S(2)}) collective-permute-start(bf16[768,128]{1,0:T(8,128)(2,1)S(1)} %pad_maximum_fusion.20), channel_id=1, source_target_pairs={{0,16},{2,18},{4,20},{6,22},{8,24},{10,26},{12,28},{14,30},{16,0},... | collective-permute-start | bytes 589832 | tf_op jit(solution)/shard_map/ppermute | solution.py:783
  659.4 11.6 %collective-permute-start.43 = (bf16[1632,128]{1,0:T(8,128)(2,1)S(1)}, bf16[1632,128]{1,0:T(8,128)(2,1)S(1)}, u32[]{:S(2)}, u32[]{:S(2)}) collective-permute-start(bf16[1632,128]{1,0:T(8,128)(2,1)S(1)} %pad_maximum_fusion.11), channel_id=1, source_target_pairs={{0,8},{2,10},{4,12},{6,14},{8,0},{10,2},{12,4},{14,6},{16,24},{18,... | collective-permute-start | bytes 1253384 | tf_op jit(solution)/shard_map/ppermute | solution.py:783
  669.1 10.3 %collective-permute-start.34 = (bf16[816,128]{1,0:T(8,128)(2,1)S(1)}, bf16[816,128]{1,0:T(8,128)(2,1)S(1)}, u32[]{:S(2)}, u32[]{:S(2)}) collective-permute-start(bf16[816,128]{1,0:T(8,128)(2,1)S(1)} %pad_maximum_fusion.17), channel_id=1, source_target_pairs={{0,16},{2,18},{4,20},{6,22},{8,24},{10,26},{12,28},{14,30},{16,0},... | collective-permute-start | bytes 626696 | tf_op jit(solution)/shard_map/ppermute | solution.py:783
  671.2 10.4 %collective-permute-start.44 = (bf16[816,128]{1,0:T(8,128)(2,1)S(1)}, bf16[816,128]{1,0:T(8,128)(2,1)S(1)}, u32[]{:S(2)}, u32[]{:S(2)}) collective-permute-start(bf16[816,128]{1,0:T(8,128)(2,1)S(1)} %pad_maximum_fusion.18), channel_id=1, source_target_pairs={{0,16},{2,18},{4,20},{6,22},{8,24},{10,26},{12,28},{14,30},{16,0},... | collective-permute-start | bytes 626696 | tf_op jit(solution)/shard_map/ppermute | solution.py:783
  (172 other events, 1252.1 us)

commit v4 on v3

--- a/solution.py
+++ b/solution.py
@@ -77,6 +77,17 @@
 def store_units(ref, values):
     for place in range(values.shape[1] // 128):
         ref[place] = values[:, place * 128 : (place + 1) * 128].astype(ref.dtype)
+
+
+def ordered(kernel, inputs, count):
+    def run(*refs):
+        kernel(*refs[:inputs], *refs[inputs + count :])
+
+    return run
+
+
+def unread(count):
+    return [pl.BlockSpec(memory_space=pl.ANY)] * count
 
 
 def params(mib):
@@ -193,127 +204,202 @@
         ],
         out_specs=[tile] * 6,
         out_shape=[low, low, low, low, full, full],
-        compiler_params=params(40),
+        compiler_params=params(58),
         name="self_forward",
         cost_estimate=cost(27),
     )(x, weights, biases, gains, mask)
 
 
 def self_backward_kernel(
-    x_ref,
     w_ref,
     gain_ref,
     mask_ref,
     q_ref,
     k_ref,
     v_ref,
-    mix_ref,
     sum_ref,
     top_ref,
     low_ref,
-    dx_ref,
-    dw_ref,
+    grad_ref,
+    branch_ref,
+    down_ref,
     side_ref,
-    dq_all,
-    dk_all,
-    dv_all,
-    branch_all,
     dmix_all,
 ):
     step = pl.program_id(0)
     count = sum_ref.shape[0]
-    steps = x_ref.shape[0] // count
     low, high = half_lanes(SLOTS)
 
     @pl.when(step == 0)
     def _():
         side_ref[...] = jnp.zeros_like(side_ref)
 
-    @pl.when(step < steps)
-    def _():
-        base = pl.multiple_of(step * count, count)
-        here = pl.ds(base, count)
-        grad = jnp.concatenate([top_ref[...], low_ref[...]], 1).reshape(count, -1)
-        down, dgain, dshift = norm_grads(sum_ref[...], gain_ref[0:1], grad)
-        branch = down.astype(bf16)
-        branch_all[here] = branch
-        dmix_all[...] = dot_nt(branch, w_ref[3]).astype(bf16)
-
-        def one_row(r, carry):
-            local = pl.ds(pl.multiple_of(r * SLOTS, SLOTS), SLOTS)
-            rows = pl.ds(pl.multiple_of(base + r * SLOTS, SLOTS), SLOTS)
-            allowed = mask_ref[r] > 0.0
-            for g in range(GROUPS):
-                cols = slice(g * 256, (g + 1) * 256)
-                keys = k_ref[local, cols]
-                queries = spread_heads(q_ref[local, cols] * bf16(0.125), low, high)
-                outs = spread_heads(dmix_all[local, cols], low, high)
-                prob = columns_softmax(jnp.where(allowed, dot_nt(keys, queries), blocked))
-                dprob = dot_nt(v_ref[local, cols], outs)
-                dscore = (prob * (dprob - jnp.sum(dprob * prob, 0, keepdims=True))).astype(bf16)
-                dv_all[rows, cols] = dot_nn(prob.astype(bf16), outs).astype(bf16)
-                dk_all[rows, cols] = dot_nn(dscore, queries).astype(bf16)
-                dq_all[rows, cols] = (collect_heads(dot_tn(dscore, keys), SLOTS) * 0.125).astype(bf16)
-            return carry
-
-        lax.fori_loop(0, count // SLOTS, one_row, 0)
-        dq, dk, dv = dq_all[here], dk_all[here], dv_all[here]
-        dx_ref[...] = down + dot_nt(dq, w_ref[0]) + dot_nt(dk, w_ref[1]) + dot_nt(dv, w_ref[2])
-        side_ref[0:1] += dgain
-        side_ref[1:2] += dshift
-        for place, rows in enumerate((dq, dv, branch)):
-            side_ref[2 + place : 3 + place] += jnp.sum(rows.astype(f32), 0, keepdims=True)
-
-    for place, right in enumerate((dq_all, dk_all, dv_all, branch_all)):
-
-        @pl.when(step == steps + place)
-        def _():
-            left = mix_ref if place == 3 else x_ref
-            store_units(dw_ref.at[0], dot_tn(left[...], right[...]))
-
-
-def self_backward(x, weights, gains, mask, q, k, v, mix, total, top, text):
-    tokens, width = x.shape
+    grad = jnp.concatenate([top_ref[...], low_ref[...]], 1).reshape(count, -1)
+    down, dgain, dshift = norm_grads(sum_ref[...], gain_ref[0:1], grad)
+    branch = down.astype(bf16)
+    down_ref[...] = down
+    branch_ref[...] = branch
+    dmix_all[...] = dot_nt(branch, w_ref[0]).astype(bf16)
+
+    def one_row(r, carry):
+        rows = pl.ds(pl.multiple_of(r * SLOTS, SLOTS), SLOTS)
+        allowed = mask_ref[r] > 0.0
+        for g in range(GROUPS):
+            cols = slice(g * 256, (g + 1) * 256)
+            keys = k_ref[rows, cols]
+            queries = spread_heads(q_ref[rows, cols] * bf16(0.125), low, high)
+            outs = spread_heads(dmix_all[rows, cols], low, high)
+            prob = columns_softmax(jnp.where(allowed, dot_nt(keys, queries), blocked))
+            dprob = dot_nt(v_ref[rows, cols], outs)
+            dscore = (prob * (dprob - jnp.sum(dprob * prob, 0, keepdims=True))).astype(bf16)
+            grad_ref[2, rows, cols] = dot_nn(prob.astype(bf16), outs).astype(bf16)
+            grad_ref[1, rows, cols] = dot_nn(dscore, queries).astype(bf16)
+            turned = collect_heads(dot_tn(dscore, keys), SLOTS) * 0.125
+            grad_ref[0, rows, cols] = turned.astype(bf16)
+        return carry
+
+    lax.fori_loop(0, count // SLOTS, one_row, 0)
+    side_ref[0:1] += dgain
+    side_ref[1:2] += dshift
+    for place, rows in enumerate((grad_ref[0], grad_ref[2], branch)):
+        side_ref[2 + place : 3 + place] += jnp.sum(rows.astype(f32), 0, keepdims=True)
+
+
+def self_backward(weights, gains, mask, q, k, v, total, top, text, order):
+    tokens, width = q.shape
     count = 4 * SLOTS
-    steps = tokens // count
-
-    def near(i):
-        return jnp.minimum(i, steps - 1)
-
-    tile = pl.BlockSpec((count, width), lambda i: (near(i), 0))
-    part = pl.BlockSpec((4, QUERIES, width), lambda i: (near(i), 0, 0))
-    scratch = pltpu.VMEM((tokens, width), bf16)
+    tile = pl.BlockSpec((count, width), lambda i: (i, 0))
+    part = pl.BlockSpec((4, QUERIES, width), lambda i: (i, 0, 0))
     return pl.pallas_call(
-        self_backward_kernel,
-        grid=(steps + 4,),
+        ordered(self_backward_kernel, 9, len(order)),
+        grid=(tokens // count,),
         in_specs=[
-            held(x.shape, lambda i: (0, 0)),
-            held((4, width, width), lambda i: (0, 0, 0)),
+            held((1, width, width), lambda i: (3, 0, 0)),
             whole(gains.shape),
-            pl.BlockSpec((4,) + mask.shape[1:], lambda i: (near(i), 0, 0)),
+            pl.BlockSpec((4,) + mask.shape[1:], lambda i: (i, 0, 0)),
             tile,
             tile,
             tile,
-            held(x.shape, lambda i: (0, 0)),
             tile,
             part,
             part,
-        ],
+        ]
+        + unread(len(order)),
         out_specs=[
+            pl.BlockSpec((3, count, width), lambda i: (0, i, 0)),
             tile,
-            pl.BlockSpec((1, width // 128, width, 128), lambda i: (jnp.maximum(i - steps, 0), 0, 0, 0)),
+            tile,
             whole((8, width)),
         ],
         out_shape=[
-            jax.ShapeDtypeStruct(x.shape, f32),
-            jax.ShapeDtypeStruct((4, width // 128, width, 128), bf16),
+            jax.ShapeDtypeStruct((3, tokens, width), bf16),
+            jax.ShapeDtypeStruct((tokens, width), bf16),
+            jax.ShapeDtypeStruct((tokens, width), f32),
             jax.ShapeDtypeStruct((8, width), f32),
         ],
-        scratch_shapes=[scratch] * 4 + [pltpu.VMEM((count, width), bf16)],
-        compiler_params=params(48),
+        scratch_shapes=[pltpu.VMEM((count, width), bf16)],
+        compiler_params=params(58),
         name="self_backward",
-        cost_estimate=cost(37),
-    )(x, weights, gains, mask, q, k, v, mix, total, top, text)
+        cost_estimate=cost(25),
+    )(weights, gains, mask, q, k, v, total, top, text, *order)
+
+
+def input_grad_kernel(w_ref, grad_ref, down_ref, dx_ref):
+    dx_ref[...] = (
+        down_ref[...]
+        + dot_nt(grad_ref[0], w_ref[0])
+        + dot_nt(grad_ref[1], w_ref[1])
+        + dot_nt(grad_ref[2], w_ref[2])
+    )
+
+
+def input_gradient(weights, grads, down, order):
+    tokens, width = down.shape
+    count = 4 * SLOTS
+    tile = pl.BlockSpec((count, width), lambda i: (i, 0))
+
+    return pl.pallas_call(
+        ordered(input_grad_kernel, 3, len(order)),
+        grid=(tokens // count,),
+        in_specs=[
+            held((3, width, width), lambda i: (0, 0, 0)),
+            pl.BlockSpec((3, count, width), lambda i: (0, i, 0)),
+            tile,
+        ]
+        + unread(len(order)),
+        out_specs=tile,
+        out_shape=jax.ShapeDtypeStruct((tokens, width), f32),
+        compiler_params=params(58),
+        name="input_gradient",
+        cost_estimate=cost(7),
+    )(weights, grads, down, *order)
+
+
+def place_of(order, row_block, rep):
+    return tuple(rep if axis == "rep" else (row_block >> bit) & 1 for axis, bit in order)
+
+
+def slab_shape(order, units, rows):
+    return (2,) * (len(order) - 1) + (units, rows, 128)
+
+
+def store_halves(core_ref, keep_ref, send_ref, pieces):
+    for core in range(2):
+
+        @pl.when(core_ref[0] == core)
+        def _():
+            for places, block in pieces:
+                ref = keep_ref if places[0] == core else send_ref
+                ref[places[1:]] = block
+
+
+core_spec = pl.BlockSpec(memory_space=pltpu.SMEM)
+
+
+def attn_weight_kernel(fold, core_ref, left_ref, right_ref, left_two_ref, right_two_ref, *outs):
+    out_ref = outs[0]
+    pieces = []
+    for rep, (left, right) in enumerate(((left_ref, right_ref), (left_two_ref, right_two_ref))):
+        width = right.shape[-1]
+        lhs = left[...].reshape(-1, width).astype(bf16)
+        rhs = right[...].reshape(-1, width).astype(bf16)
+        grad = dot_tn(lhs, rhs).astype(bf16)
+        if fold is None:
+            store_units(out_ref.at[rep], grad)
+            continue
+        rows = out_ref.shape[-2]
+        for block in range(width // rows):
+            spot = place_of(fold, block, rep)
+            for unit in range(width // 128):
+                piece = grad[block * rows : (block + 1) * rows, unit * 128 : (unit + 1) * 128]
+                pieces.append((spot + (unit,), piece))
+    if fold is not None:
+        store_halves(core_ref, *outs, pieces)
+
+
+def attn_weight_grad(part, core, left, grads, left_two, left_two_spec, right_two, fold, rows, order):
+    tokens, width = left.shape
+    if fold is None:
+        shape = (2, width // 128, width, 128)
+    else:
+        shape = slab_shape(fold, width // 128, rows)
+    return pl.pallas_call(
+        ordered(functools.partial(attn_weight_kernel, fold), 5, len(order)),
+        grid=(1,),
+        in_specs=[
+            core_spec,
+            whole(left.shape),
+            pl.BlockSpec((1, tokens, width), lambda i: (part, 0, 0)),
+            left_two_spec,
+            whole(right_two.shape),
+        ]
+        + unread(len(order)),
+        out_specs=[whole(shape)] * (1 if fold is None else 2),
+        out_shape=[jax.ShapeDtypeStruct(shape, bf16)] * (1 if fold is None else 2),
+        compiler_params=params(58),
+        name="attn_weight_grad",
+        cost_estimate=cost(6),
+    )(core, left, grads, left_two, right_two, *order)
 
 
 TAIL = 16
@@ -346,14 +432,14 @@
     q_ref[...] = (dot_nn(residual.astype(bf16), w_ref[0]) + bias_ref[3:4]).astype(bf16)
     low, high = half_lanes(QUERIES)
     shown = lax.broadcasted_iota(jnp.int32, (main + TAIL, 128), 0) <= main
+    tokens = image_ref[:, :main].reshape(rows_here * main, -1)
+    key_ref[...] = dot_nt(tokens, kv_ref[0]).astype(bf16)
+    value_ref[...] = (dot_nt(tokens, kv_ref[1]) + bias_ref[4:5]).astype(bf16)
 
     def one_row(r, carry):
         span = pl.ds(pl.multiple_of(r * main, main), main)
         last = pl.ds(pl.multiple_of(r * TAIL, TAIL), TAIL)
         mine = pl.ds(pl.multiple_of(r * QUERIES, QUERIES), QUERIES)
-        tokens = image_ref[r, :main]
-        key_ref[span] = dot_nt(tokens, kv_ref[0]).astype(bf16)
-        value_ref[span] = (dot_nt(tokens, kv_ref[1]) + bias_ref[4:5]).astype(bf16)
         for g in range(GROUPS):
             cols = slice(g * 256, (g + 1) * 256)
             keys = jnp.concatenate([key_ref[span, cols], key_end_ref[last, cols]], 0)
@@ -405,54 +491,36 @@
             shape(QUERIES, f32),
             shape(QUERIES, f32),
         ],
-        compiler_params=params(48),
+        compiler_params=params(58),
         name="cross_forward",
         cost_estimate=cost(55),
     )(images, ends, kv, weights, biases, gains, norm)
 
 
 def cross_backward_kernel(
-    image_ref,
-    end_ref,
     w_ref,
-    norm_ref,
     key_ref,
     value_ref,
     key_end_ref,
     value_end_ref,
     q_ref,
-    mix_ref,
     down_ref,
-    order_ref,
     dnorm_ref,
-    dkey_w_ref,
-    dvalue_w_ref,
-    dw_ref,
+    dkv_ref,
+    dkv_end_ref,
+    dq_ref,
     side_ref,
-    key_sum,
-    value_sum,
-    w_sum,
-    dkey,
-    dvalue,
-    dkey_end,
-    dvalue_end,
-    dq_all,
     dmix_all,
 ):
-    del order_ref
     step = pl.program_id(0)
-    rows_here = image_ref.shape[0]
-    main = image_ref.shape[1] - 1
-    width = norm_ref.shape[-1]
+    rows_here, _, width = dnorm_ref.shape
+    main = key_ref.shape[0] // rows_here
     low, high = half_lanes(QUERIES)
     shown = lax.broadcasted_iota(jnp.int32, (main + TAIL, 128), 0) <= main
 
     @pl.when(step == 0)
     def _():
         side_ref[...] = jnp.zeros_like(side_ref)
-        key_sum[...] = jnp.zeros_like(key_sum)
-        value_sum[...] = jnp.zeros_like(value_sum)
-        w_sum[...] = jnp.zeros_like(w_sum)
 
     down = down_ref[...]
     branch = down.astype(bf16)
@@ -473,98 +541,128 @@
             dscore = (prob * (dprob - jnp.sum(dprob * prob, 0, keepdims=True))).astype(bf16)
             dv = dot_nn(prob.astype(bf16), outs).astype(bf16)
             dk = dot_nn(dscore, queries).astype(bf16)
-            dvalue[span, cols] = dv[:main]
-            dvalue_end[last, cols] = dv[main:]
-            dkey[span, cols] = dk[:main]
-            dkey_end[last, cols] = dk[main:]
-            dq_all[mine, cols] = (collect_heads(dot_tn(dscore, keys), QUERIES) * 0.125).astype(bf16)
+            dkv_ref[0, span, cols] = dk[:main]
+            dkv_end_ref[0, last, cols] = dk[main:]
+            dkv_ref[1, span, cols] = dv[:main]
+            dkv_end_ref[1, last, cols] = dv[main:]
+            dq_ref[mine, cols] = (collect_heads(dot_tn(dscore, keys), QUERIES) * 0.125).astype(bf16)
         return carry
 
     lax.fori_loop(0, rows_here, one_row, 0)
-    end = end_ref[...].reshape(rows_here * TAIL, -1)
-    for grads, grads_end, gathered in ((dkey, dkey_end, key_sum), (dvalue, dvalue_end, value_sum)):
-        gathered[...] += dot_tn(grads_end[...], end)
-
-        def add_row(r, carry):
-            span = pl.ds(pl.multiple_of(r * main, main), main)
-            gathered[...] += dot_tn(grads[span], image_ref[r, :main])
-            return carry
-
-        lax.fori_loop(0, rows_here, add_row, 0)
-    dq = dq_all[...]
+    dq = dq_ref[...]
     dnorm_ref[...] = (down + dot_nt(dq, w_ref[0])).reshape(rows_here, QUERIES, width)
-    low_norm = norm_ref[...].reshape(rows_here * QUERIES, width).astype(bf16)
-    w_sum[0] += dot_tn(low_norm, dq)
-    w_sum[1] += dot_tn(mix_ref[...], branch)
     side_ref[0:1] += jnp.sum(dq.astype(f32), 0, keepdims=True)
-    side_ref[1:2] += jnp.sum(dvalue[...].astype(f32), 0, keepdims=True) + jnp.sum(
-        dvalue_end[...].astype(f32), 0, keepdims=True
+    side_ref[1:2] += jnp.sum(dkv_ref[1].astype(f32), 0, keepdims=True) + jnp.sum(
+        dkv_end_ref[1].astype(f32), 0, keepdims=True
     )
     side_ref[2:3] += jnp.sum(branch.astype(f32), 0, keepdims=True)
 
-    @pl.when(step == pl.num_programs(0) - 1)
-    def _():
-        store_units(dkey_w_ref, key_sum[...])
-        store_units(dvalue_w_ref, value_sum[...])
-        store_units(dw_ref.at[0], w_sum[0])
-        store_units(dw_ref.at[1], w_sum[1])
-
-
-def cross_backward(images, ends, weights, norm, keys, values, key_ends, value_ends, q, mix, down, order):
-    rows, patches, vis = images.shape
-    main = patches - 1
-    width = norm.shape[-1]
-    take = 2
+
+def cross_backward(rows, weights, keys, values, key_ends, value_ends, q, down, order):
+    width = q.shape[1]
+    main = keys.shape[0] // rows
+    take = 4
     span = pl.BlockSpec((take * main, width), lambda i: (i, 0))
     tails = pl.BlockSpec((take * TAIL, width), lambda i: (i, 0))
     tile = pl.BlockSpec((take * QUERIES, width), lambda i: (i, 0))
-    part = pl.BlockSpec((take, QUERIES, width), lambda i: (i, 0, 0))
     return pl.pallas_call(
-        cross_backward_kernel,
+        ordered(cross_backward_kernel, 7, len(order)),
         grid=(rows // take,),
         in_specs=[
-            pl.BlockSpec((take, patches, vis), lambda i: (i, 0, 0)),
-            pl.BlockSpec((take, TAIL, vis), lambda i: (i, 0, 0)),
             held((2, width, width), lambda i: (2, 0, 0)),
-            part,
             span,
             span,
             tails,
             tails,
             tile,
             tile,
+        ]
+        + unread(len(order)),
+        out_specs=[
+            pl.BlockSpec((take, QUERIES, width), lambda i: (i, 0, 0)),
+            pl.BlockSpec((2, take * main, width), lambda i: (0, i, 0)),
+            pl.BlockSpec((2, take * TAIL, width), lambda i: (0, i, 0)),
             tile,
-            pl.BlockSpec(memory_space=pl.ANY),
-        ],
-        out_specs=[
-            part,
-            held((vis // 128, width, 128), lambda i: (0, 0, 0)),
-            held((vis // 128, width, 128), lambda i: (0, 0, 0)),
-            held((2, width // 128, width, 128), lambda i: (0, 0, 0, 0)),
             whole((8, width)),
         ],
         out_shape=[
             jax.ShapeDtypeStruct((rows, QUERIES, width), f32),
-            jax.ShapeDtypeStruct((vis // 128, width, 128), bf16),
-            jax.ShapeDtypeStruct((vis // 128, width, 128), bf16),
-            jax.ShapeDtypeStruct((2, width // 128, width, 128), bf16),
+            jax.ShapeDtypeStruct((2, rows * main, width), bf16),
+            jax.ShapeDtypeStruct((2, rows * TAIL, width), bf16),
+            jax.ShapeDtypeStruct((rows * QUERIES, width), bf16),
             jax.ShapeDtypeStruct((8, width), f32),
         ],
-        scratch_shapes=[
-            pltpu.VMEM((width, vis), f32),
-            pltpu.VMEM((width, vis), f32),
-            pltpu.VMEM((2, width, width), f32),
-            pltpu.VMEM((take * main, width), bf16),
-            pltpu.VMEM((take * main, width), bf16),
-            pltpu.VMEM((take * TAIL, width), bf16),
-            pltpu.VMEM((take * TAIL, width), bf16),
-            pltpu.VMEM((take * QUERIES, width), bf16),
-            pltpu.VMEM((take * QUERIES, width), bf16),
-        ],
-        compiler_params=params(52),
+        scratch_shapes=[pltpu.VMEM((take * QUERIES, width), bf16)],
+        compiler_params=params(58),
         name="cross_backward",
-        cost_estimate=cost(79),
-    )(images, ends, weights, norm, keys, values, key_ends, value_ends, q, mix, down, order)
+        cost_estimate=cost(40),
+    )(weights, keys, values, key_ends, value_ends, q, down, *order)
+
+
+def cross_weight_kernel(fold, core_ref, image_ref, end_ref, grad_ref, grad_end_ref, *rest):
+    outs, gathered = rest[:-1], rest[-1]
+    rows, patches, vis = image_ref.shape
+    main = patches - 1
+    take = 4
+    gathered[...] = dot_tn(grad_end_ref[0], end_ref[...].reshape(rows * TAIL, vis))
+
+    def add_rows(i, carry):
+        span = pl.ds(pl.multiple_of(i * take * main, take * main), take * main)
+        tokens = image_ref[pl.ds(i * take, take), :main].reshape(take * main, vis)
+        gathered[...] += dot_tn(grad_ref[0, span], tokens)
+        return carry
+
+    lax.fori_loop(0, rows // take, add_rows, 0)
+    if fold is None:
+        store_units(outs[0].at[0], gathered[...])
+        return
+    units, size = outs[0].shape[-3:-1]
+    pieces = []
+    for block in range(gathered.shape[0] // size):
+        spot = tuple(0 if axis == "rep" or bit == 3 else (block >> bit) & 1 for axis, bit in fold)
+        piece = gathered[block * size : (block + 1) * size].astype(bf16)
+        for unit in range(units):
+            pieces.append((spot + (unit,), piece[:, unit * 128 : (unit + 1) * 128]))
+    store_halves(core_ref, *outs, pieces)
+
+
+def cross_weight_grad(core, images, ends, grads, grads_end, fold, size, order):
+    rows, patches, vis = images.shape
+    width = grads.shape[2]
+    half = width // 2
+    units = vis // 128
+    if fold is None:
+        specs = [pl.BlockSpec((1, units, half, 128), lambda m, h: (m, 0, h, 0))]
+        shapes = [(2, units, width, 128)]
+    else:
+        shapes = [slab_shape(fold, units, size)] * 2
+        block = tuple(1 if axis == "rep" or bit == 3 else 2 for axis, bit in fold[1:])
+
+        def index(m, h):
+            spot = tuple(m if axis == "rep" else h if bit == 3 else 0 for axis, bit in fold[1:])
+            return spot + (0, 0, 0)
+
+        specs = [pl.BlockSpec(block + (units, size, 128), index)] * 2
+    return pl.pallas_call(
+        ordered(functools.partial(cross_weight_kernel, fold), 5, len(order)),
+        grid=(2, 2),
+        in_specs=[
+            core_spec,
+            held(images.shape, lambda m, h: (0, 0, 0)),
+            held(ends.shape, lambda m, h: (0, 0, 0)),
+            pl.BlockSpec((1, grads.shape[1], half), lambda m, h: (m, 0, h)),
+            pl.BlockSpec((1, grads_end.shape[1], half), lambda m, h: (m, 0, h)),
+        ]
+        + unread(len(order)),
+        out_specs=specs,
+        out_shape=[jax.ShapeDtypeStruct(shape, bf16) for shape in shapes],
+        scratch_shapes=[pltpu.VMEM((half, vis), f32)],
+        compiler_params=pltpu.CompilerParams(
+            vmem_limit_bytes=58 * MIB, dimension_semantics=("arbitrary", "arbitrary")
+        ),
+        name="cross_weight_grad",
+        cost_estimate=cost(30),
+    )(core, images, ends, grads, grads_end, *order)
 
 
 def ffn_forward_kernel(
@@ -607,7 +705,7 @@
         embed_ref[...] = (raw * size).astype(bf16)
 
 
-def ffn_forward(which, part, norm, ffn_in, ffn_bias, ffn_out, projections, proj_bias, biases, gains, layer):
+def ffn_forward(which, part, norm, ffn_in, ffn_bias, ffn_out, projections, proj_bias, biases, gains, layer, order=()):
     rows, width = norm.shape[0], norm.shape[-1]
     tokens = rows * QUERIES
     hidden = ffn_in.shape[2]
@@ -628,7 +726,7 @@
             whole(biases.shape),
             whole(gains.shape),
         ]
-        + [pl.BlockSpec(memory_space=pl.ANY)] * len(halves),
+        + unread(len(halves) + len(order)),
         out_specs=[
             cols,
             cols,
@@ -647,14 +745,16 @@
         ],
         scratch_shapes=[pltpu.VMEM((tokens, width), bf16)],
         input_output_aliases={8: 3} if halves else {},
-        compiler_params=params(48),
+        compiler_params=params(58),
         name="ffn_forward",
         cost_estimate=cost(15),
-    )(norm, ffn_in, ffn_bias, ffn_out, projections, proj_bias, biases, gains, *halves)
+    )(norm, ffn_in, ffn_bias, ffn_out, projections, proj_bias, biases, gains, *halves, *order)
 
 
 def ffn_backward_kernel(
     which,
+    folds,
+    core_ref,
     norm_ref,
     sum_ref,
     before_ref,
@@ -667,17 +767,12 @@
     out_ref,
     act_ref,
     slope_ref,
-    down_ref,
-    din_ref,
-    dout_ref,
-    dproj_ref,
-    side_ref,
-    dbias_ref,
-    dproj_bias_ref,
-    branch_all,
-    low_turned,
-    rest,
+    *rest,
 ):
+    count = 3 if folds is None else 6
+    down_ref, side_ref, dbias_ref, dproj_bias_ref = rest[-8 - count : -4 - count]
+    weight_refs = rest[-4 - count : -4]
+    branch_all, low_turned, left, dproj = rest[-4:]
     step = pl.program_id(0)
     tokens, width = sum_ref.shape
 
@@ -688,12 +783,12 @@
         down, dgain, dshift = norm_grads(sum_ref[...], gain_ref[2 + which : 3 + which], grad)
         branch = down.astype(bf16)
         branch_all[...] = branch
-        rest[...] = down
+        left[...] = down
         side_ref[...] = jnp.zeros_like(side_ref)
         side_ref[0:1] = dgain
         side_ref[1:2] = dshift
         side_ref[2:3] = jnp.sum(branch.astype(f32), 0, keepdims=True)
-        store_units(dproj_ref, dot_tn(layer_ref[...].reshape(tokens, width), raw))
+        dproj[...] = dot_tn(layer_ref[...].reshape(tokens, width), raw).astype(bf16)
         dproj_bias_ref[...] = jnp.broadcast_to(
             jnp.sum(raw.astype(f32), 0, keepdims=True), dproj_bias_ref.shape
         )
@@ -701,39 +796,112 @@
 
     branch = branch_all[...]
     du = (dot_nt(branch, out_ref[0]) * slope_ref[...].astype(f32)).astype(bf16)
-    rest[...] += dot_nt(du, in_ref[0])
-    store_units(dout_ref, dot_tn(act_ref[...], branch))
-    store_units(din_ref, dot_nn(low_turned[...], du))
+    left[...] += dot_nt(du, in_ref[0])
     dbias_ref[...] = jnp.broadcast_to(jnp.sum(du.astype(f32), 0, keepdims=True), dbias_ref.shape)
+    thin = width // 3
+    for part in range(3):
+
+        @pl.when(step == part)
+        def _():
+            din = dot_nn(low_turned[...], du).astype(bf16)
+            dout = dot_tn(act_ref[...], branch[:, part * thin : (part + 1) * thin]).astype(bf16)
+            if folds is None:
+                store_units(weight_refs[0], din)
+                store_units(weight_refs[1], dout)
+                if part == 0:
+                    store_units(weight_refs[2], dproj[...])
+                return
+            keep, send = weight_refs[2 * part : 2 * part + 2]
+            size = keep.shape[-2]
+            subs = dout.shape[0] // width
+            pieces = []
+            for block in range(width // size):
+                spot = place_of(folds[part], block, 0)
+                at = block * size
+                found = [
+                    din[at : at + size, unit * 128 : (unit + 1) * 128]
+                    for unit in range(din.shape[1] // 128)
+                ]
+                for sub in range(subs):
+                    row = at * subs + sub * size
+                    for unit in range(thin // 128):
+                        found.append(dout[row : row + size, unit * 128 : (unit + 1) * 128])
+                if part == 0:
+                    for unit in range(dproj.shape[1] // 128):
+                        found.append(dproj[at : at + size, unit * 128 : (unit + 1) * 128])
+                pieces += [(spot + (unit,), piece) for unit, piece in enumerate(found)]
+            store_halves(core_ref, keep, send, pieces)
 
     @pl.when(step == pl.num_programs(0) - 1)
     def _():
         if which == 0:
-            down, dgain, dshift = norm_grads(before_ref[...], gain_ref[1:2], rest[...])
+            down, dgain, dshift = norm_grads(before_ref[...], gain_ref[1:2], left[...])
             side_ref[3:4] = dgain
             side_ref[4:5] = dshift
             down_ref[...] = down.reshape(down_ref.shape)
         else:
-            down_ref[...] = rest[...].reshape(down_ref.shape)
+            down_ref[...] = left[...].reshape(down_ref.shape)
 
 
 def ffn_backward(
-    which, part, norm, total, before, layer, grad, raw, projections, gains, ffn_in, ffn_out, act, slope
+    which,
+    part,
+    core,
+    norm,
+    total,
+    before,
+    layer,
+    grad,
+    raw,
+    projections,
+    gains,
+    ffn_in,
+    ffn_out,
+    act,
+    slope,
+    slabs,
+    folds,
+    size,
 ):
     rows = layer.shape[0]
     tokens, width = total.shape
     hidden = ffn_in.shape[2]
     embed = projections.shape[2]
-    chunk = 512
-    cols = pl.BlockSpec((tokens, chunk), lambda j: (0, j))
-    before_spec = held(before.shape, lambda j: (0, 0))
+    chunk = hidden // 3
+    slabs = list(slabs)
+    if folds is None:
+        weight_specs = [
+            pl.BlockSpec((chunk // 128, width, 128), lambda j: (j, 0, 0)),
+            pl.BlockSpec((width // 384, hidden, 128), lambda j: (j, 0, 0)),
+            whole((embed // 128, width, 128)),
+        ]
+        weight_shapes = [
+            (hidden // 128, width, 128),
+            (width // 128, hidden, 128),
+            (embed // 128, width, 128),
+        ]
+    else:
+        units = chunk // 128 + (hidden // width) * (width // 384)
+        weight_shapes = [
+            slab_shape(fold, units + (embed // 128 if k == 0 else 0), size)
+            for k, fold in enumerate(folds)
+            for half in range(2)
+        ]
+
+        def spec(fold, shape):
+            block = tuple(1 if axis == "rep" else 2 for axis, bit in fold[1:])
+            spot = tuple(which if axis == "rep" else 0 for axis, bit in fold[1:])
+            return held(block + shape[-3:], lambda j: spot + (0, 0, 0))
+
+        weight_specs = [spec(folds[k // 2], shape) for k, shape in enumerate(weight_shapes)]
     return pl.pallas_call(
-        functools.partial(ffn_backward_kernel, which),
-        grid=(hidden // chunk,),
+        functools.partial(ffn_backward_kernel, which, folds),
+        grid=(3,),
         in_specs=[
+            core_spec,
             held((rows, QUERIES, width), lambda j: (0, part, 0)),
             held((tokens, width), lambda j: (0, 0)),
-            before_spec,
+            held(before.shape, lambda j: (0, 0)),
             held((rows, QUERIES, width), lambda j: (0, which, 0)),
             held((rows, QUERIES, width), lambda j: (0, which, 0)),
             held((tokens, embed), lambda j: (0, 0)),
@@ -741,36 +909,50 @@
             whole(gains.shape),
             pl.BlockSpec((1, width, chunk), lambda j: (which, 0, j)),
             pl.BlockSpec((1, chunk, width), lambda j: (which, j, 0)),
-            cols,
-            cols,
-        ],
+            held((tokens, hidden), lambda j: (0, 0)),
+            pl.BlockSpec((tokens, chunk), lambda j: (0, j)),
+        ]
+        + [pl.BlockSpec(memory_space=pl.ANY)] * len(slabs),
         out_specs=[
             whole((rows, QUERIES, width)),
-            pl.BlockSpec((chunk // 128, width, 128), lambda j: (j, 0, 0)),
-            pl.BlockSpec((width // 128, chunk, 128), lambda j: (0, j, 0)),
-            whole((embed // 128, width, 128)),
             whole((8, width)),
             pl.BlockSpec((8, chunk), lambda j: (0, j)),
             whole((8, embed)),
-        ],
+        ]
+        + weight_specs,
         out_shape=[
             jax.ShapeDtypeStruct((rows, QUERIES, width), f32),
-            jax.ShapeDtypeStruct((hidden // 128, width, 128), bf16),
-            jax.ShapeDtypeStruct((width // 128, hidden, 128), bf16),
-            jax.ShapeDtypeStruct((embed // 128, width, 128), bf16),
             jax.ShapeDtypeStruct((8, width), f32),
             jax.ShapeDtypeStruct((8, hidden), f32),
             jax.ShapeDtypeStruct((8, embed), f32),
-        ],
+        ]
+        + [jax.ShapeDtypeStruct(shape, bf16) for shape in weight_shapes],
         scratch_shapes=[
             pltpu.VMEM((tokens, width), bf16),
             pltpu.VMEM((width, tokens), bf16),
             pltpu.VMEM((tokens, width), f32),
+            pltpu.VMEM((width, embed), bf16),
         ],
-        compiler_params=params(52),
+        input_output_aliases={13 + k: 4 + k for k in range(len(slabs))},
+        compiler_params=params(60),
         name="ffn_backward",
         cost_estimate=cost(20),
-    )(norm, total, before, layer, grad, raw, projections, gains, ffn_in, ffn_out, act, slope)
+    )(
+        core,
+        norm,
+        total,
+        before,
+        layer,
+        grad,
+        raw,
+        projections,
+        gains,
+        ffn_in,
+        ffn_out,
+        act,
+        slope,
+        *slabs,
+    )
 
 
 def own_bit(stage):
@@ -783,85 +965,78 @@
     return lax.ppermute(values, axis, [(i, i ^ (1 << bit)) for i in range(sizes[axis])])
 
 
-def pick(term, places):
-    array, fixed = term
-    starts = [0] * array.ndim
-    extent = list(array.shape)
-    for dim, place in (fixed | places).items():
-        starts[dim] = place
-        extent[dim] = 1
-    return lax.dynamic_slice(array, starts, extent)
-
-
-def total(terms, places):
-    return sum(pick(term, places).astype(f32) for term in terms)
-
-
-def swap_all(pieces, stage, sizes):
-    flat = [piece.reshape(-1, 128) for piece in pieces]
-    sent = flat[0] if len(flat) == 1 else jnp.concatenate(flat, 0)
-    arrived = swap(sent, stage, sizes)
-    start, got = 0, []
-    for piece, rows in zip(pieces, flat):
-        got.append(arrived[start : start + rows.shape[0]].reshape(piece.shape))
-        start += rows.shape[0]
-    return got
-
-
-def scatter_pairs(pairs, order, sizes):
+def total(terms, ahead=()):
+    parts = []
+    for array, places in terms:
+        places = list(places) + list(ahead)
+        rest = array.shape[len(places) :]
+        if places:
+            at = sum(place << shift for shift, place in enumerate(reversed(places)))
+            flat = array.reshape((1 << len(places), -1, 128))
+            array = lax.dynamic_index_in_dim(flat, at, 0, keepdims=False).reshape(rest)
+        parts.append(array.astype(f32))
+    return sum(parts)
+
+
+def stage_order(part, sizes):
+    stages = [("dp", bit) for bit in range(sizes["dp"].bit_length() - 1)]
+    ring = stages[1:3] + [("rep", 0)]
+    return stages[:1] + ring[part:] + ring[:part] + stages[3:]
+
+
+def fold_pair(part, first, second, sizes):
     depth = sizes["dp"].bit_length() - 1
-
-    def spread(array):
-        units, rows, lanes = array.shape
-        return array.reshape((units,) + (2,) * depth + (rows // sizes["dp"], lanes))
-
-    streams = [[[(spread(array), {})] for array in pair] for pair in pairs]
-    for stage in order:
-        mine = own_bit(stage)
-        if stage[0] == "rep":
-            sums = [[total(terms, {}) for terms in pair] for pair in streams]
-            sent = [jnp.where(mine == 0, two, one).astype(bf16) for one, two in sums]
-            kept = [jnp.where(mine == 0, one, two).astype(bf16) for one, two in sums]
-            got = swap_all(sent, stage, sizes)
-            streams = [[[(keep, {}), (piece, {})]] for keep, piece in zip(kept, got)]
-        else:
-            dim = depth - stage[1]
-            sent = [total(terms, {dim: 1 - mine}).astype(bf16) for pair in streams for terms in pair]
-            got = iter(swap_all(sent, stage, sizes))
-            streams = [
-                [
-                    [(array, fixed | {dim: mine}) for array, fixed in terms] + [(next(got), {})]
-                    for terms in pair
-                ]
-                for pair in streams
-            ]
-    results = []
-    for (terms,) in streams:
-        result = total(terms, {})
-        results.append(result.reshape(result.shape[0], result.shape[-2], 128))
-    return results
-
-
-def orders(sizes):
-    stages = [("dp", bit) for bit in range(sizes["dp"].bit_length() - 1)]
-    head, mid, tail = stages[:1], stages[1:3], stages[3:]
-    ring = mid + [("rep", 0)]
-    return [head + ring[k:] + ring[:k] + tail for k in range(3)]
-
-
-def cut_units(array, part):
-    units = array.shape[0]
-    edges = [(units * k + 1) // 3 for k in range(4)]
-    return array[edges[part] : edges[part + 1]]
-
-
-def scatter_group(pairs, sizes):
-    parts = [
-        scatter_pairs([tuple(cut_units(array, part) for array in pair) for pair in pairs], order, sizes)
-        for part, order in enumerate(orders(sizes))
-    ]
-    joined = [jnp.concatenate(pieces, 0) for pieces in zip(*parts)]
-    return [array.transpose(1, 0, 2).reshape(array.shape[1], -1) for array in joined]
+    both = jnp.stack([first, second])
+    units, rows = first.shape[0], first.shape[1] // sizes["dp"]
+    both = both.reshape((2, units) + (2,) * depth + (rows, 128))
+    front = [0 if axis == "rep" else 1 + depth - bit for axis, bit in stage_order(part, sizes)]
+    return both.transpose(front + [1, 2 + depth, 3 + depth])
+
+
+def begin(part, keep, send, sizes):
+    return (1, [(keep, []), (swap(send, stage_order(part, sizes)[0], sizes), [])], send)
+
+
+def begin_folded(part, slab, sizes):
+    mine = own_bit(stage_order(part, sizes)[0])
+    halves = [lax.dynamic_index_in_dim(slab, place, 0, keepdims=False) for place in (mine, 1 - mine)]
+    return begin(part, *halves, sizes)
+
+
+def advance(part, state, sizes, after=None):
+    stage, terms = state[0], state[1]
+    if after is not None:
+        array, places = terms[-1]
+        terms = terms[:-1] + [(lax.optimization_barrier((array, after))[0], places)]
+    axis_bit = stage_order(part, sizes)[stage]
+    mine = own_bit(axis_bit)
+    sent = total(terms, [1 - mine]).astype(bf16)
+    arrived = swap(sent, axis_bit, sizes)
+    terms = [(array, places + [mine]) for array, places in terms] + [(arrived, [])]
+    return (stage + 1, terms, sent)
+
+
+def advance_all(states, sizes, after=None):
+    return [advance(part, state, sizes, after) for part, state in enumerate(states)]
+
+
+def finish(part, state, sizes, after=None):
+    while state[0] < len(stage_order(part, sizes)):
+        state = advance(part, state, sizes, after)
+        after = None
+    terms = state[1]
+    if after is not None:
+        array, places = terms[-1]
+        terms = terms[:-1] + [(lax.optimization_barrier((array, after))[0], places)]
+    return total(terms)
+
+
+def sends(states):
+    return [state[2] for state in states]
+
+
+def columns_of(units):
+    return units.transpose(1, 0, 2).reshape(units.shape[1], -1)
 
 
 def exchange(values, sizes):
@@ -907,8 +1082,20 @@
         inputs, attn_weights, biases, norm_gains, mask
     )
     first_norm = first_norm.reshape(row_count, slots, width)
+    image_ends = jnp.pad(image_features[:, -1:], ((0, 0), (0, TAIL - 1), (0, 0)))
     text_act, text_slope, fourth_sum, layer_half, caption_raw, caption_all = ffn_forward(
-        1, 1, first_norm, ffn_in, ffn_bias, ffn_out, projections, proj_bias, biases, norm_gains, None
+        1,
+        1,
+        first_norm,
+        ffn_in,
+        ffn_bias,
+        ffn_out,
+        projections,
+        proj_bias,
+        biases,
+        norm_gains,
+        None,
+        [image_ends],
     )
     caption_embed = (
         jnp.einsum(
@@ -921,7 +1108,6 @@
         .reshape(captions_here, -1)
     )
     every_caption = gather_rows(caption_embed, sizes)
-    image_ends = jnp.pad(image_features[:, -1:], ((0, 0), (0, TAIL - 1), (0, 0)))
     keys, values, key_ends, value_ends, cross_q, cross_mix, second_sum, second_norm = cross_forward(
         image_features, image_ends, cross_kv, attn_weights, biases, norm_gains, first_norm
     )
@@ -988,75 +1174,175 @@
     caption_raw_grad = jnp.einsum(
         "rkt,rkd->rtd", pick_low, head_raw_grad, preferred_element_type=f32
     ).astype(bf16)
-    grad_second, query_din, query_dout, query_dproj, query_side, query_dbias, query_dproj_bias = (
-        ffn_backward(
-            0,
-            0,
-            second_norm,
-            third_sum,
-            second_sum,
-            layer_out,
-            out_grad,
-            query_raw_grad.reshape(row_count * QUERIES, -1),
-            projections,
-            norm_gains,
-            ffn_in,
-            ffn_out,
-            query_act,
-            query_slope,
-        )
-    )
-    text_first, text_din, text_dout, text_dproj, text_side, text_dbias, text_dproj_bias = (
-        ffn_backward(
-            1,
-            1,
-            first_norm,
-            fourth_sum,
-            fourth_sum,
-            layer_out,
-            out_grad,
-            caption_raw_grad.reshape(row_count * TEXT, -1),
-            projections,
-            norm_gains,
-            ffn_in,
-            ffn_out,
-            text_act,
-            text_slope,
-        )
-    )
-    ffn_in_grad, ffn_out_grad, proj_grad = scatter_group(
-        [(query_din, text_din), (query_dout, text_dout), (query_dproj, text_dproj)], sizes
-    )
-    query_first, key_grad, value_grad, cross_dw, cross_side = cross_backward(
-        image_features,
-        image_ends,
+    fold = sizes["dp"] == 16 and sizes["rep"] == 2
+    stage_orders = [stage_order(part, sizes) for part in range(3)]
+    folds = stage_orders if fold else None
+    size = width // sizes["dp"]
+    core = (lax.axis_index("dp") & 1).astype(jnp.int32).reshape(1)
+    grad_second, query_side, query_dbias, query_dproj_bias, *query_slabs = ffn_backward(
+        0,
+        0,
+        core,
+        second_norm,
+        third_sum,
+        second_sum,
+        layer_out,
+        out_grad,
+        query_raw_grad.reshape(row_count * QUERIES, -1),
+        projections,
+        norm_gains,
+        ffn_in,
+        ffn_out,
+        query_act,
+        query_slope,
+        (),
+        folds,
+        size,
+    )
+    text_first, text_side, text_dbias, text_dproj_bias, *text_slabs = ffn_backward(
+        1,
+        1,
+        core,
+        first_norm,
+        fourth_sum,
+        fourth_sum,
+        layer_out,
+        out_grad,
+        caption_raw_grad.reshape(row_count * TEXT, -1),
+        projections,
+        norm_gains,
+        ffn_in,
+        ffn_out,
+        text_act,
+        text_slope,
+        query_slabs if fold else (),
+        folds,
+        size,
+    )
+    tall = ffn_out.shape[1] // width
+    if not fold:
+        text_slabs = [
+            fold_pair(
+                part,
+                *(
+                    jnp.concatenate(
+                        [
+                            din[part * 8 : part * 8 + 8],
+                            dout[2 * part : 2 * part + 2]
+                            .reshape(2, sizes["dp"], tall, size, 128)
+                            .transpose(2, 0, 1, 3, 4)
+                            .reshape(2 * tall, width, 128),
+                            dproj[: 2 if part == 0 else 0],
+                        ],
+                        0,
+                    )
+                    for din, dout, dproj in (query_slabs, text_slabs)
+                ),
+                sizes,
+            )
+            for part in range(3)
+        ]
+    if fold:
+        ffn_states = [
+            begin(part, *text_slabs[2 * part : 2 * part + 2], sizes) for part in range(3)
+        ]
+    else:
+        ffn_states = [begin_folded(part, slab, sizes) for part, slab in enumerate(text_slabs)]
+    cross_down = grad_second.reshape(row_count * QUERIES, width)
+    query_first, dkv, dkv_ends, cross_dq, cross_side = cross_backward(
+        row_count,
         attn_weights,
-        first_norm,
         keys,
         values,
         key_ends,
         value_ends,
         cross_q,
-        cross_mix,
-        grad_second.reshape(row_count * QUERIES, width),
-        text_first,
-    )
-    (cross_grad,) = scatter_group([(key_grad, value_grad)], sizes)
-    input_grad, self_dw, self_side = self_backward(
-        inputs,
+        cross_down,
+        [text_first] + sends(ffn_states),
+    )
+    ffn_states = advance_all(ffn_states, sizes, cross_side)
+    cross_slabs = cross_weight_grad(
+        core,
+        image_features,
+        image_ends,
+        dkv,
+        dkv_ends,
+        folds and folds[0],
+        size,
+        sends(ffn_states),
+    )
+    ffn_states = advance_all(ffn_states, sizes, cross_slabs[0])
+    if fold:
+        cross_states = [begin(0, *cross_slabs, sizes)]
+    else:
+        cross_states = [begin_folded(0, fold_pair(0, *cross_slabs[0], sizes), sizes)]
+    self_grads, self_branch, self_down, self_side = self_backward(
         attn_weights,
         norm_gains,
         mask,
         self_q,
         self_k,
         self_v,
-        self_mix,
         first_sum,
         query_first,
         text_first,
-    )
-    attn_pairs = ((self_dw[0], self_dw[3]), (self_dw[1], cross_dw[0]), (self_dw[2], cross_dw[1]))
-    attn_grad = jnp.stack(scatter_group(attn_pairs, sizes))
+        sends(ffn_states) + sends(cross_states),
+    )
+    ffn_states = advance_all(ffn_states, sizes, self_side)
+    cross_states = advance_all(cross_states, sizes, self_side)
+    query_half = pl.BlockSpec((row_count, QUERIES, width), lambda i: (0, 0, 0))
+    attn_states = []
+    order = sends(ffn_states) + sends(cross_states)
+    for part, (left_two, spec, right_two) in enumerate(
+        (
+            (self_mix, whole(self_mix.shape), self_branch),
+            (first_norm, query_half, cross_dq),
+            (cross_mix, whole(cross_mix.shape), cross_down),
+        )
+    ):
+        slabs = attn_weight_grad(
+            part,
+            core,
+            inputs,
+            self_grads,
+            left_two,
+            spec,
+            right_two,
+            folds and folds[part],
+            size,
+            order,
+        )
+        made = slabs[0]
+        if fold:
+            attn_states.append(begin(part, *slabs, sizes))
+        else:
+            attn_states.append(begin_folded(part, fold_pair(part, *made, sizes), sizes))
+        order = sends(attn_states[-1:])
+    ffn_states = advance_all(ffn_states, sizes, made)
+    cross_states = advance_all(cross_states, sizes, made)
+    input_grad = input_gradient(
+        attn_weights,
+        self_grads,
+        self_down,
+        order + sends(ffn_states) + sends(cross_states),
+    )
+    attn_grad = jnp.stack(
+        [
+            columns_of(finish(part, state, sizes, input_grad))
+            for part, state in enumerate(attn_states)
+        ]
+    )
+    ffn_sums = [finish(part, state, sizes, input_grad) for part, state in enumerate(ffn_states)]
+    ffn_in_grad = jnp.concatenate([columns_of(each[:8]) for each in ffn_sums], 1)
+    ffn_out_grad = jnp.concatenate(
+        [
+            each[8:16].reshape(tall, 2, size, 128).transpose(0, 2, 1, 3).reshape(tall * size, -1)
+            for each in ffn_sums
+        ],
+        1,
+    )
+    proj_grad = columns_of(ffn_sums[0][16:])
+    cross_grad = columns_of(finish(0, cross_states[0], sizes, input_grad))
     gain_grad = jnp.stack([self_side[0], query_side[3], query_side[0], text_side[0]])
     bias_grad = jnp.stack(
         [
@@ -1087,7 +1373,7 @@
         return cut.transpose(2, 0, 1, 3).reshape(world, -1)
 
     dealt = jnp.concatenate([deal(array) for array in vectors], 1)
-    arrived = jnp.sum(exchange(dealt, sizes), 0)
+    arrived = jnp.sum(lax.optimization_barrier((exchange(dealt, sizes), input_grad))[0], 0)
     small = []
     start = 0
     for array in vectors:

time: 693 us -> 523 us (0.75)
  local copies, waits for them, and re-layouts: 146 us -> 50.7 us
  waiting for transfers between devices: 119 us -> 49.2 us
  starting transfers between devices: 74.9 us -> 55.8 us
  Pallas kernels: 269 us -> 282 us
    ppermute x45 -> x35, waiting for transfers between devices: 111 us -> 35.9 us  [swap(): lax.ppermute(values, axis, [(i, i ^ 1 << bit) for i in range(sizes[axis])])]
    slice x56 -> x4, local copies, waits for them, and re-layouts: 39.9 us -> 1.64 us  [the longest x1 1.56 us: shards(): query_side[3]]
    unnamed x362 -> x50, local copies, waits for them, and re-layouts: 51.2 us -> 13.7 us
    dynamic_slice x50 -> x0, local copies, waits for them, and re-layouts: 30.4 us -> none  [pick(): return lax.dynamic_slice(array, starts, extent)]
    concatenate x26 -> x0, other arithmetic: 23.7 us -> none  [swap_all(): sent = flat[0] if len(flat) == 1 else jnp.concatenate(flat, 0)]
    ppermute x45 -> x35, starting transfers between devices: 51.7 us -> 36.1 us  [swap(): lax.ppermute(values, axis, [(i, i ^ 1 << bit) for i in range(sizes[axis])])]
    another operation x1 -> x8, other arithmetic: 0.8 us -> 12.4 us  [shards(): attn_grad = jnp.stack(scatter_group(attn_pairs, sizes))]
    pallas_call x4 -> x9, Pallas kernels: 157 us -> 168 us  [the longest x2 49.5 us: ffn_backward(): pl.pallas_call(functools.partial(ffn_backward_kernel, which, folds), grid...]
  transfers between devices with their start and end apart: 49 -> 39, of which waited for: 26 -> 15; matrix products, arithmetic and copies ran while one was open for 20% -> 19% of each run, Pallas kernels for 13% -> 41%
where the time goes in v4:
time: 523 us; the launch traced here: 515 us
  Pallas kernels  282 us (54%)
  other arithmetic  68.6 us (13%)
  starting transfers between devices  55.8 us (11%)
  local copies, waits for them, and re-layouts  50.7 us (10%)
  waiting for transfers between devices  49.2 us (9%)
  matrix products  7.03 us (1%)
    pallas_call x1, Pallas kernels, cross_forward(): pl.pallas_call(cross_forward_kernel, grid=(rows // take,), in_specs=[pl.B...  54.5 us
    pallas_call x2, Pallas kernels, ffn_backward(): pl.pallas_call(functools.partial(ffn_backward_kernel, which, folds), grid...  49.5 us
    ppermute x35, starting transfers between devices, swap(): lax.ppermute(values, axis, [(i, i ^ 1 << bit) for i in range(sizes[axis])])  36.1 us
    ppermute x35, waiting for transfers between devices, swap(): lax.ppermute(values, axis, [(i, i ^ 1 << bit) for i in range(sizes[axis])])  35.9 us
    convert_element_type x18, other arithmetic, advance(): sent = total(terms, [1 - mine]).astype(bf16)  34.9 us
    pallas_call x1, Pallas kernels, cross_weight_grad(): pl.pallas_call(ordered(functools.partial(cross_weight_kernel, fold), 5, l...  32.1 us
    pallas_call x2, Pallas kernels, ffn_forward(): pl.pallas_call(functools.partial(ffn_forward_kernel, which), grid=(hidden...  31.9 us
    pallas_call x1, Pallas kernels, cross_backward(): pl.pallas_call(ordered(cross_backward_kernel, 7, len(order)), grid=(rows...  31.5 us
  transfers between devices with their start and end apart: 39, of which 15 were waited for; matrix products, arithmetic and copies ran while one was open for 19% of the time, Pallas kernels for 41%

profile of v4, /device:TPU:0, one launch (start us, length us, event | category | flops | bytes accessed | tf_op | source)
XLA Modules:
  0.0 515.0 jit_solution(1250104125372794686)
XLA Ops:
  4.3 7.6 %copy.131.image_ref.refs_1_ = bf16[16,257,1408]{2,1,0:T(8,128)(2,1)S(1)} copy(bf16[16,257,1408]{2,0,1:T(8,128)(2,1)} %param.15) | data formatting | bytes 23158784 | tf_op args[1]
  11.9 4.3 copy-done
  17.3 27.8 %self_forward.1 = (bf16[1024,768]{1,0:T(8,128)(2,1)}, bf16[1024,768]{1,0:T(8,128)(2,1)}, bf16[1024,768]{1,0:T(8,128)(2,1)}, bf16[1024,768]{1,0:T(8,128)(2,1)}, f32[1024,768]{1,0:T(8,128)}, /*index=5*/f32[1024,768]{1,0:T(8,128)}) custom-call(bf16[1024,768]{1,0:T(8,128)(2,1)} %bitcast.337, bf16[6,768,768]{2,1,0:T(8,128)(2,1)} %refs_0_.5, f32[12,768]{1,0:T(8,128)} %bias_ref.7, ...), custom_call_target="tpu_custom_call" | custom-call | flops 29699999744 | tf_op jit(solution)/shard_map/self_forward/pallas_call | solution.py:195
  45.0 15.9 %ffn_forward.2 = (bf16[512,3072]{1,0:T(8,128)(2,1)}, bf16[512,3072]{1,0:T(8,128)(2,1)}, f32[512,768]{1,0:T(8,128)}, bf16[16,64,768]{2,1,0:T(8,128)(2,1)}, f32[512,256]{1,0:T(8,128)}, /*index=5*/bf16[512,256]{1,0:T(8,128)(2,1)}) custom-call(f32[16,64,768]{2,1,0:T(8,128)} %bitcast.341, bf16[2,768,3072]{2,1,0:T(8,128)(2,1)} %in_ref.7, f32[2,3072]{1,0:T(2,128)} %in_bias_ref.3, ...), custom_call_target="tpu_custom_call" | custom-call | flops 16499999744 | tf_op jit(solution)/shard_map/ffn_forward/pallas_call | solution.py:716
  63.0 7.5 %all-to-all-start = ((bf16[32,32,256]{2,1,0:T(8,128)(2,1)}), bf16[32,32,256]{2,1,0:T(8,128)(2,1)S(1)}, u32[]{:S(2)}, u32[]{:S(2)}) async-start(bf16[32,32,256]{2,1,0:T(8,128)(2,1)} %tile.20), calls=%async_computation | async-start | bytes 1048576 | tf_op jit(solution)/shard_map/all_to_all | solution.py:1043
  70.6 54.5 %cross_forward.1 = (bf16[4096,768]{1,0:T(8,128)(2,1)}, bf16[4096,768]{1,0:T(8,128)(2,1)}, bf16[256,768]{1,0:T(8,128)(2,1)}, bf16[256,768]{1,0:T(8,128)(2,1)}, bf...) custom-call(bf16[16,257,1408]{2,1,0:T(8,128)(2,1)} %copy-done, ...), custom_call_target="tpu_custom_call" | custom-call | flops 60500000768 | tf_op jit(solution)/shard_map/cross_forward/pallas_call | solution.py:471
  125.1 16.0 %ffn_forward.3 = (bf16[512,3072]{1,0:T(8,128)(2,1)}, bf16[512,3072]{1,0:T(8,128)(2,1)}, f32[512,768]{1,0:T(8,128)}, bf16[16,64,768]{2,1,0:T(8,128)(2,1)}, f32[512,256]{1,0:T(8,128)}, /*index=5*/bf16[512,256]{1,0:T(8,128)(2,1)}) custom-call(f32[16,32,768]{2,1,0:T(8,128)} %bitcast.346, bf16[2,768,3072]{2,1,0:T(8,128)(2,1)} %in_ref.7, ...), custom_call_target="tpu_custom_call", output_to_operand_aliasing={{3}: (8, {})} | custom-call | flops 16499999744 | tf_op jit(solution)/shard_map/ffn_forward/pallas_call | solution.py:716
  145.3 6.0 %all-to-all-start.1 = ((f32[32,1,1024]{2,1,0:T(1,128)}), f32[32,1,1024]{2,1,0:T(1,128)S(1)}, u32[]{:S(2)}, u32[]{:S(2)}) async-start(f32[32,1,1024]{2,1,0:T(1,128)} %broadcast_in_dim.10), calls=%async_computation.1 | async-start | bytes 262144 | tf_op jit(solution)/shard_map/all_to_all | solution.py:1043
  151.6 8.3 %all-to-all-done.1 = f32[32,1,1024]{2,1,0:T(1,128)S(1)} async-done(((f32[32,1,1024]{2,1,0:T(1,128)}), f32[32,1,1024]{2,1,0:T(1,128)S(1)}, u32[]{:S(2)}, u32[]{:S(2)}) %all-to-all-start.1) | async-done | bytes 131104 | tf_op jit(solution)/shard_map/all_to_all | solution.py:1043
  163.5 3.0 all-to-all-start.2
  168.5 24.7 %ffn_backward.2 = (f32[16,32,768]{2,1,0:T(8,128)}, f32[8,768]{1,0:T(8,128)}, f32[8,3072]{1,0:T(8,128)}, f32[8,256]{1,0:T(8,128)}, bf16[2,2,2,2,18,48,128]{6,5,4,...) custom-call(s32[1]{0:T(128)} %bitcast.11.core_ref.refs_0_, ...), custom_call_target="tpu_custom_call" | custom-call | flops 22000001024 | tf_op jit(solution)/shard_map/ffn_backward/pallas_call | solution.py:897
  197.1 24.8 %ffn_backward.3 = (f32[16,32,768]{2,1,0:T(8,128)}, f32[8,768]{1,0:T(8,128)}, f32[8,3072]{1,0:T(8,128)}, f32[8,256]{1,0:T(8,128)}, bf16[2,2,2,2,18,48,128]{6,5,4,...) custom-call(s32[1]{0:T(128)} %bitcast.11.core_ref.refs_0_, ...), custom_call_target="tpu_custom_call", output_to_operand_aliasing={{4}: (13, {}), {5}: (14, {}), {6}: (15, {}), {7}: (16, {}),... | custom-call | flops 22000001024 | tf_op jit(solution)/shard_map/ffn_backward/pallas_call | solution.py:897
  222.7 31.5 %cross_backward.1 = (f32[16,32,768]{2,1,0:T(8,128)}, bf16[2,4096,768]{2,1,0:T(8,128)(2,1)}, bf16[2,256,768]{2,1,0:T(8,128)(2,1)}, bf16[512,768]{1,0:T(8,128)(2,1)}, f32[8,768]{1,0:T(8,128)}) custom-call(bf16[6,768,768]{2,1,0:T(8,128)(2,1)} %refs_0_.5, bf16[4096,768]{1,0:T(8,128)(2,1)} %get-tuple-element.107.refs_1_, ...), custom_call_target="tpu_custom_call" | custom-call | flops 44000002048 | tf_op jit(solution)/shard_map/cross_backward/pallas_call | solution.py:568
  266.8 3.6 add_convert_fusion.2
  272.2 3.1 add_convert_fusion.1
  278.8 32.1 %cross_weight_grad.1 = (bf16[2,2,2,2,11,48,128]{6,5,4,3,2,1,0:T(8,128)(2,1)}, bf16[2,2,2,2,11,48,128]{6,5,4,3,2,1,0:T(8,128)(2,1)}) custom-call(s32[1]{0:T(128)} %bitcast.11.core_ref.refs_0_, bf16[16,257,1408]{2,1,0:T(8,128)(2,1)} %copy-done, bf16[16,16,1408]{2,1,0:T(8,128)(2,1)} %pad.6.end_ref.rest_0_.refs_2_, ...), custom_call_target="tpu_custom_call" | custom-call | flops 32999999488 | tf_op jit(solution)/shard_map/cross_weight_grad/pallas_call | solution.py:646
  312.0 2.9 add_convert_fusion.5
  316.3 2.8 add_convert_fusion.6
  320.6 2.7 add_convert_fusion.4
  323.3 25.9 %self_backward.1 = (bf16[3,1024,768]{2,1,0:T(8,128)(2,1)}, bf16[1024,768]{1,0:T(8,128)(2,1)}, f32[1024,768]{1,0:T(8,128)}, f32[8,768]{1,0:T(8,128)}) custom-call(bf16[6,768,768]{2,1,0:T(8,128)(2,1)} %refs_0_.5, f32[4,768]{1,0:T(4,128)} %refs_1_.2, f32[16,64,256]{2,1,0:T(8,128)} %tile.18.mask_ref.refs_2_, bf16[1024,768]{1,0:T(8,128)(2,1)} %get-tuple-element.103.refs_3_, ...), custom_call_target="tpu_custom_call" | custom-call | flops 27499999232 | tf_op jit(solution)/shard_map/self_backward/pallas_call | solution.py:273
  354.9 2.7 stack.18
  363.9 3.3 all-to-all-start.3
  370.0 5.0 all-to-all-done.3
  385.9 5.7 %collective-permute-done.6 = bf16[2,2,18,48,128]{4,3,2,1,0:T(8,128)(2,1)} collective-permute-done((bf16[2,2,18,48,128]{4,3,2,1,0:T(8,128)(2,1)}, bf16[2,2,18,48,128]{4,3,2,1,0:T(8,128)(2,1)}, u32[]{:S(2)}, u32[]{:S(2)}) %collective-permute-start.6) | collective-permute-done | bytes 884768 | tf_op jit(solution)/shard_map/ppermute | solution.py:965
  395.4 7.3 %attn_weight_grad.3 = (bf16[2,2,2,2,6,48,128]{6,5,4,3,2,1,0:T(8,128)(2,1)}, bf16[2,2,2,2,6,48,128]{6,5,4,3,2,1,0:T(8,128)(2,1)}) custom-call(s32[1]{0:T(128)} %bitcast.11.core_ref.refs_0_, bf16[1024,768]{1,0:T(8,128)(2,1)} %bitcast.338, bf16[3,1024,768]{2,1,0:T(8,128)(2,1)} %get-tuple-element.147.refs_2_.refs_1_, ...), custom_call_target="tpu_custom_call" | custom-call | flops 6600000000 | tf_op jit(solution)/shard_map/attn_weight_grad/pallas_call | solution.py:386
  402.7 6.2 %attn_weight_grad.4 = (bf16[2,2,2,2,6,48,128]{6,5,4,3,2,1,0:T(8,128)(2,1)}, bf16[2,2,2,2,6,48,128]{6,5,4,3,2,1,0:T(8,128)(2,1)}) custom-call(s32[1]{0:T(128)} %bitcast.11.core_ref.refs_0_, bf16[1024,768]{1,0:T(8,128)(2,1)} %bitcast.339, bf16[3,1024,768]{2,1,0:T(8,128)(2,1)} %get-tuple-element.147.refs_2_.refs_1_, f32[16,64,768]{2,1,0:T(8,128)} %bitcast.344, ...), custom_call_target="tpu_custom_call" | custom-call | flops 6600000000 | tf_op jit(solution)/shard_map/attn_weight_grad/pallas_call | solution.py:386
  408.9 6.3 %attn_weight_grad.5 = (bf16[2,2,2,2,6,48,128]{6,5,4,3,2,1,0:T(8,128)(2,1)}, bf16[2,2,2,2,6,48,128]{6,5,4,3,2,1,0:T(8,128)(2,1)}) custom-call(s32[1]{0:T(128)} %bitcast.11.core_ref.refs_0_, bf16[1024,768]{1,0:T(8,128)(2,1)} %bitcast.340, bf16[3,1024,768]{2,1,0:T(8,128)(2,1)} %get-tuple-element.147.refs_2_.refs_1_, ...), custom_call_target="tpu_custom_call" | custom-call | flops 6600000000 | tf_op jit(solution)/shard_map/attn_weight_grad/pallas_call | solution.py:386
  428.7 8.9 %input_gradient.1 = f32[1024,768]{1,0:T(8,128)} custom-call(bf16[6,768,768]{2,1,0:T(8,128)(2,1)} %refs_0_.5, bf16[3,1024,768]{2,1,0:T(8,128)(2,1)} %get-tuple-element.147.refs_2_.refs_1_, f32[1024,768]{1,0:T(8,128)} %get-tuple-element.148.refs_2_, bf16[2,2,2,2,6,48,128]{6,5,4,3,2,1,0:T(8,128)(2,1)} %get-tuple-element.160.refs_3_, ...), custom_call_target="tpu_custom_call" | custom-call | flops 7699999744 | tf_op jit(solution)/shard_map/input_gradient/pallas_call | solution.py:321
  447.0 4.8 collective-permute-done.32
  454.4 5.8 %collective-permute-done.29 = bf16[2,2,11,48,128]{4,3,2,1,0:T(8,128)(2,1)} collective-permute-done((bf16[2,2,11,48,128]{4,3,2,1,0:T(8,128)(2,1)}, bf16[2,2,11,48,128]{4,3,2,1,0:T(8,128)(2,1)}, u32[]{:S(2)}, u32[]{:S(2)}) %collective-permute-start.29) | collective-permute-done | bytes 540704 | tf_op jit(solution)/shard_map/ppermute | solution.py:965
  473.5 8.4 %collective-permute-done.25 = bf16[2,2,2,6,48,128]{5,4,3,2,1,0:T(8,128)(2,1)S(1)} collective-permute-done((bf16[2,2,2,6,48,128]{5,4,3,2,1,0:T(8,128)(2,1)S(1)}, bf16[2,2,2,6,48,128]{5,4,3,2,1,0:T(8,128)(2,1)S(1)}, u32[]{:S(2)}, u32[]{:S(2)}) %collective-permute-start.25) | collective-permute-done | bytes 589856 | tf_op jit(solution)/shard_map/ppermute | solution.py:965
  510.5 3.2 collective-permute-done.18
  (247 shorter events, 140.8 us)
Async XLA Ops:
  63.0 79.7 %all-to-all-start = ((bf16[32,32,256]{2,1,0:T(8,128)(2,1)}), bf16[32,32,256]{2,1,0:T(8,128)(2,1)S(1)}, u32[]{:S(2)}, u32[]{:S(2)}) async-start(bf16[32,32,256]{2,1,0:T(8,128)(2,1)} %tile.20), calls=%async_computation | async-start | bytes 1048576 | tf_op jit(solution)/shard_map/all_to_all | solution.py:1043
  145.3 14.6 %all-to-all-start.1 = ((f32[32,1,1024]{2,1,0:T(1,128)}), f32[32,1,1024]{2,1,0:T(1,128)S(1)}, u32[]{:S(2)}, u32[]{:S(2)}) async-start(f32[32,1,1024]{2,1,0:T(1,128)} %broadcast_in_dim.10), calls=%async_computation.1 | async-start | bytes 262144 | tf_op jit(solution)/shard_map/all_to_all | solution.py:1043
  163.5 32.2 %all-to-all-start.2 = ((bf16[32,32,256]{2,1,0:T(8,128)(2,1)}), bf16[32,32,256]{2,1,0:T(8,128)(2,1)S(1)}, u32[]{:S(2)}, u32[]{:S(2)}) async-start(bf16[32,32,256]{2,1,0:T(8,128)(2,1)} %bitcast.310), calls=%async_computation.2 | async-start | bytes 1048576 | tf_op jit(solution)/shard_map/all_to_all | solution.py:1043
  221.9 45.0 %collective-permute-start.2 = (bf16[2,2,2,2,16,48,128]{6,5,4,3,2,1,0:T(8,128)(2,1)}, bf16[2,2,2,2,16,48,128]{6,5,4,3,2,1,0:T(8,128)(2,1)}, u32[]{:S(2)}, u32[]{:S(2)}) collective-permute-start(bf16[2,2,2,2,16,48,128]{6,5,4,3,2,1,0:T(8,128)(2,1)} %get-tuple-element.130.refs_9_), channel_id=1, source_target_pairs={{0,2},{2,0},{4,6},{6,4},{8,10},{10,8},{12,14},{14,12},{16,18},{18,... | collective-permute-start | bytes 9437192 | tf_op jit(solution)/shard_map/ppermute | solution.py:965
  222.2 49.9 %collective-permute-start.3 = (bf16[2,2,2,2,16,48,128]{6,5,4,3,2,1,0:T(8,128)(2,1)}, bf16[2,2,2,2,16,48,128]{6,5,4,3,2,1,0:T(8,128)(2,1)}, u32[]{:S(2)}, u32[]{:S(2)}) collective-permute-start(bf16[2,2,2,2,16,48,128]{6,5,4,3,2,1,0:T(8,128)(2,1)} %get-tuple-element.131.refs_10_), channel_id=1, source_target_pairs={{0,2},{2,0},{4,6},{6,4},{8,10},{10,8},{12,14},{14,12},{16,18},{18,... | collective-permute-start | bytes 9437192 | tf_op jit(solution)/shard_map/ppermute | solution.py:965
  222.4 54.3 %collective-permute-start = (bf16[2,2,2,2,18,48,128]{6,5,4,3,2,1,0:T(8,128)(2,1)}, bf16[2,2,2,2,18,48,128]{6,5,4,3,2,1,0:T(8,128)(2,1)S(1)}, u32[]{:S(2)}, u32[]{:S(2)}) collective-permute-start(bf16[2,2,2,2,18,48,128]{6,5,4,3,2,1,0:T(8,128)(2,1)} %get-tuple-element.129.refs_8_), channel_id=1, source_target_pairs={{0,2},{2,0},{4,6},{6,4},{8,10},{10,8},{12,14},{14,12},{16,18},{18,... | collective-permute-start | bytes 10616840 | tf_op jit(solution)/shard_map/ppermute | solution.py:965
  270.4 41.5 %collective-permute-start.4 = (bf16[2,2,2,16,48,128]{5,4,3,2,1,0:T(8,128)(2,1)}, bf16[2,2,2,16,48,128]{5,4,3,2,1,0:T(8,128)(2,1)}, u32[]{:S(2)}, u32[]{:S(2)}) collective-permute-start(bf16[2,2,2,16,48,128]{5,4,3,2,1,0:T(8,128)(2,1)} %bitcast.28.refs_6_), channel_id=1, source_target_pairs={{0,8},{2,10},{4,12},{6,14},{8,0},{10,2},{12,4},{14,6},{16,24},{18,... | collective-permute-start | bytes 4718600 | tf_op jit(solution)/shard_map/ppermute | solution.py:965
  275.3 36.7 %collective-permute-start.5 = (bf16[2,2,2,16,48,128]{5,4,3,2,1,0:T(8,128)(2,1)}, bf16[2,2,2,16,48,128]{5,4,3,2,1,0:T(8,128)(2,1)}, u32[]{:S(2)}, u32[]{:S(2)}) collective-permute-start(bf16[2,2,2,16,48,128]{5,4,3,2,1,0:T(8,128)(2,1)} %bitcast.31.refs_7_), channel_id=1, source_target_pairs={{0,1},{1,0},{2,3},{3,2},{4,5},{5,4},{6,7},{7,6},{8,9},{9,8},{10,11... | collective-permute-start | bytes 4718600 | tf_op jit(solution)/shard_map/ppermute | solution.py:965
  277.3 43.3 %collective-permute-start.1 = (bf16[2,2,2,18,48,128]{5,4,3,2,1,0:T(8,128)(2,1)S(1)}, bf16[2,2,2,18,48,128]{5,4,3,2,1,0:T(8,128)(2,1)}, u32[]{:S(2)}, u32[]{:S(2)}) collective-permute-start(bf16[2,2,2,18,48,128]{5,4,3,2,1,0:T(8,128)(2,1)S(1)} %bitcast.266), channel_id=1, source_target_pairs={{0,4},{2,6},{4,0},{6,2},{8,12},{10,14},{12,8},{14,10},{16,20},{18,... | collective-permute-start | bytes 5308424 | tf_op jit(solution)/shard_map/ppermute | solution.py:965
  310.9 71.3 %collective-permute-start.9 = (bf16[2,2,2,2,11,48,128]{6,5,4,3,2,1,0:T(8,128)(2,1)}, bf16[2,2,2,2,11,48,128]{6,5,4,3,2,1,0:T(8,128)(2,1)}, u32[]{:S(2)}, u32[]{:S(2)}) collective-permute-start(bf16[2,2,2,2,11,48,128]{6,5,4,3,2,1,0:T(8,128)(2,1)} %get-tuple-element.146.refs_12_), channel_id=1, source_target_pairs={{0,2},{2,0},{4,6},{6,4},{8,10},{10,8},{12,14},{14,12},{16,18},{18,... | collective-permute-start | bytes 6488072 | tf_op jit(solution)/shard_map/ppermute | solution.py:965
  314.8 61.9 %collective-permute-start.8 = (bf16[2,2,16,48,128]{4,3,2,1,0:T(8,128)(2,1)}, bf16[2,2,16,48,128]{4,3,2,1,0:T(8,128)(2,1)}, u32[]{:S(2)}, u32[]{:S(2)}) collective-permute-start(bf16[2,2,16,48,128]{4,3,2,1,0:T(8,128)(2,1)} %bitcast.41.refs_11_), channel_id=1, source_target_pairs={{0,4},{2,6},{4,0},{6,2},{8,12},{10,14},{12,8},{14,10},{16,20},{18,... | collective-permute-start | bytes 2359304 | tf_op jit(solution)/shard_map/ppermute | solution.py:965
  319.1 59.9 %collective-permute-start.7 = (bf16[2,2,16,48,128]{4,3,2,1,0:T(8,128)(2,1)}, bf16[2,2,16,48,128]{4,3,2,1,0:T(8,128)(2,1)}, u32[]{:S(2)}, u32[]{:S(2)}) collective-permute-start(bf16[2,2,16,48,128]{4,3,2,1,0:T(8,128)(2,1)} %bitcast.37.refs_10_), channel_id=1, source_target_pairs={{0,1},{1,0},{2,3},{3,2},{4,5},{5,4},{6,7},{7,6},{8,9},{9,8},{10,11... | collective-permute-start | bytes 2359304 | tf_op jit(solution)/shard_map/ppermute | solution.py:965
  363.9 11.1 %all-to-all-start.3 = ((f32[32,1,592]{2,1,0:T(1,128)}), f32[32,1,592]{2,1,0:T(1,128)}, u32[]{:S(2)}, u32[]{:S(2)}) async-start(f32[32,1,592]{2,1,0:T(1,128)} %copy.153), calls=%async_computation.3 | async-start | bytes 163840 | tf_op jit(solution)/shard_map/all_to_all | solution.py:1043
  368.4 23.1 %collective-permute-start.6 = (bf16[2,2,18,48,128]{4,3,2,1,0:T(8,128)(2,1)}, bf16[2,2,18,48,128]{4,3,2,1,0:T(8,128)(2,1)}, u32[]{:S(2)}, u32[]{:S(2)}) collective-permute-start(bf16[2,2,18,48,128]{4,3,2,1,0:T(8,128)(2,1)} %bitcast.285), channel_id=1, source_target_pairs={{0,8},{2,10},{4,12},{6,14},{8,0},{10,2},{12,4},{14,6},{16,24},{18,... | collective-permute-start | bytes 2654216 | tf_op jit(solution)/shard_map/ppermute | solution.py:965
  379.0 36.1 %collective-permute-start.12 = (bf16[2,16,48,128]{3,2,1,0:T(8,128)(2,1)}, bf16[2,16,48,128]{3,2,1,0:T(8,128)(2,1)}, u32[]{:S(2)}, u32[]{:S(2)}) collective-permute-start(bf16[2,16,48,128]{3,2,1,0:T(8,128)(2,1)} %bitcast.56.refs_7_), channel_id=1, source_target_pairs={{0,8},{2,10},{4,12},{6,14},{8,0},{10,2},{12,4},{14,6},{16,24},{18,... | collective-permute-start | bytes 1179656 | tf_op jit(solution)/shard_map/ppermute | solution.py:965
  381.3 34.3 %collective-permute-start.11 = (bf16[2,16,48,128]{3,2,1,0:T(8,128)(2,1)}, bf16[2,16,48,128]{3,2,1,0:T(8,128)(2,1)}, u32[]{:S(2)}, u32[]{:S(2)}) collective-permute-start(bf16[2,16,48,128]{3,2,1,0:T(8,128)(2,1)} %bitcast.51.refs_6_), channel_id=1, source_target_pairs={{0,4},{2,6},{4,0},{6,2},{8,12},{10,14},{12,8},{14,10},{16,20},{18,... | collective-permute-start | bytes 1179656 | tf_op jit(solution)/shard_map/ppermute | solution.py:965
  384.7 41.7 %collective-permute-start.13 = (bf16[2,2,2,11,48,128]{5,4,3,2,1,0:T(8,128)(2,1)}, bf16[2,2,2,11,48,128]{5,4,3,2,1,0:T(8,128)(2,1)}, u32[]{:S(2)}, u32[]{:S(2)}) collective-permute-start(bf16[2,2,2,11,48,128]{5,4,3,2,1,0:T(8,128)(2,1)} %bitcast.59.refs_8_), channel_id=1, source_target_pairs={{0,4},{2,6},{4,0},{6,2},{8,12},{10,14},{12,8},{14,10},{16,20},{18,... | collective-permute-start | bytes 3244040 | tf_op jit(solution)/shard_map/ppermute | solution.py:965
  393.8 29.4 %collective-permute-start.10 = (bf16[2,18,48,128]{3,2,1,0:T(8,128)(2,1)}, bf16[2,18,48,128]{3,2,1,0:T(8,128)(2,1)S(1)}, u32[]{:S(2)}, u32[]{:S(2)}) collective-permute-start(bf16[2,18,48,128]{3,2,1,0:T(8,128)(2,1)} %bitcast.46.refs_5_), channel_id=1, source_target_pairs={{0,1},{1,0},{2,3},{3,2},{4,5},{5,4},{6,7},{7,6},{8,9},{9,8},{10,11... | collective-permute-start | bytes 1327112 | tf_op jit(solution)/shard_map/ppermute | solution.py:965
  408.9 56.1 %collective-permute-start.19 = (bf16[2,2,2,2,6,48,128]{6,5,4,3,2,1,0:T(8,128)(2,1)}, bf16[2,2,2,2,6,48,128]{6,5,4,3,2,1,0:T(8,128)(2,1)}, u32[]{:S(2)}, u32[]{:S(2)}) collective-permute-start(bf16[2,2,2,2,6,48,128]{6,5,4,3,2,1,0:T(8,128)(2,1)} %get-tuple-element.159.refs_5_), channel_id=1, source_target_pairs={{0,2},{2,0},{4,6},{6,4},{8,10},{10,8},{12,14},{14,12},{16,18},{18,... | collective-permute-start | bytes 3538952 | tf_op jit(solution)/shard_map/ppermute | solution.py:965
  415.2 51.1 %collective-permute-start.14 = (bf16[2,2,2,2,6,48,128]{6,5,4,3,2,1,0:T(8,128)(2,1)}, bf16[2,2,2,2,6,48,128]{6,5,4,3,2,1,0:T(8,128)(2,1)}, u32[]{:S(2)}, u32[]{:S(2)}) collective-permute-start(bf16[2,2,2,2,6,48,128]{6,5,4,3,2,1,0:T(8,128)(2,1)} %get-tuple-element.158.refs_5_), channel_id=1, source_target_pairs={{0,2},{2,0},{4,6},{6,4},{8,10},{10,8},{12,14},{14,12},{16,18},{18,... | collective-permute-start | bytes 3538952 | tf_op jit(solution)/shard_map/ppermute | solution.py:965
  418.3 23.3 %collective-permute-start.33 = (bf16[16,48,128]{2,1,0:T(8,128)(2,1)}, bf16[16,48,128]{2,1,0:T(8,128)(2,1)}, u32[]{:S(2)}, u32[]{:S(2)}) collective-permute-start(bf16[16,48,128]{2,1,0:T(8,128)(2,1)} %bitcast.71.refs_5_), channel_id=1, source_target_pairs={{0,16},{2,18},{4,20},{6,22},{8,24},{10,26},{12,28},{14,30},{16,0},... | collective-permute-start | bytes 589832 | tf_op jit(solution)/shard_map/ppermute | solution.py:965
  423.2 15.8 %collective-permute-start.34 = (bf16[16,48,128]{2,1,0:T(8,128)(2,1)}, bf16[16,48,128]{2,1,0:T(8,128)(2,1)}, u32[]{:S(2)}, u32[]{:S(2)}) collective-permute-start(bf16[16,48,128]{2,1,0:T(8,128)(2,1)} %bitcast.77.refs_6_), channel_id=1, source_target_pairs={{0,16},{2,18},{4,20},{6,22},{8,24},{10,26},{12,28},{14,30},{16,0},... | collective-permute-start | bytes 589832 | tf_op jit(solution)/shard_map/ppermute | solution.py:965
  426.4 35.7 %collective-permute-start.24 = (bf16[2,2,2,2,6,48,128]{6,5,4,3,2,1,0:T(8,128)(2,1)}, bf16[2,2,2,2,6,48,128]{6,5,4,3,2,1,0:T(8,128)(2,1)}, u32[]{:S(2)}, u32[]{:S(2)}) collective-permute-start(bf16[2,2,2,2,6,48,128]{6,5,4,3,2,1,0:T(8,128)(2,1)} %get-tuple-element.160.refs_3_), channel_id=1, source_target_pairs={{0,2},{2,0},{4,6},{6,4},{8,10},{10,8},{12,14},{14,12},{16,18},{18,... | collective-permute-start | bytes 3538952 | tf_op jit(solution)/shard_map/ppermute | solution.py:965
  439.0 12.8 %collective-permute-start.32 = (bf16[18,48,128]{2,1,0:T(8,128)(2,1)S(1)}, bf16[18,48,128]{2,1,0:T(8,128)(2,1)S(1)}, u32[]{:S(2)}, u32[]{:S(2)}) collective-permute-start(bf16[18,48,128]{2,1,0:T(8,128)(2,1)S(1)} %bitcast.320), channel_id=1, source_target_pairs={{0,16},{2,18},{4,20},{6,22},{8,24},{10,26},{12,28},{14,30},{16,0},... | collective-permute-start | bytes 663560 | tf_op jit(solution)/shard_map/ppermute | solution.py:965
  441.6 18.7 %collective-permute-start.29 = (bf16[2,2,11,48,128]{4,3,2,1,0:T(8,128)(2,1)}, bf16[2,2,11,48,128]{4,3,2,1,0:T(8,128)(2,1)}, u32[]{:S(2)}, u32[]{:S(2)}) collective-permute-start(bf16[2,2,11,48,128]{4,3,2,1,0:T(8,128)(2,1)} %bitcast.81.refs_7_), channel_id=1, source_target_pairs={{0,8},{2,10},{4,12},{6,14},{8,0},{10,2},{12,4},{14,6},{16,24},{18,... | collective-permute-start | bytes 1622024 | tf_op jit(solution)/shard_map/ppermute | solution.py:965
  461.6 9.5 %collective-permute-start.30 = (bf16[2,11,48,128]{3,2,1,0:T(8,128)(2,1)S(1)}, bf16[2,11,48,128]{3,2,1,0:T(8,128)(2,1)S(1)}, u32[]{:S(2)}, u32[]{:S(2)}) collective-permute-start(bf16[2,11,48,128]{3,2,1,0:T(8,128)(2,1)S(1)} %bitcast.315), channel_id=1, source_target_pairs={{0,1},{1,0},{2,3},{3,2},{4,5},{5,4},{6,7},{7,6},{8,9},{9,8},{10,11... | collective-permute-start | bytes 811016 | tf_op jit(solution)/shard_map/ppermute | solution.py:965
  463.4 18.5 %collective-permute-start.25 = (bf16[2,2,2,6,48,128]{5,4,3,2,1,0:T(8,128)(2,1)S(1)}, bf16[2,2,2,6,48,128]{5,4,3,2,1,0:T(8,128)(2,1)S(1)}, u32[]{:S(2)}, u32[]{:S(2)}) collective-permute-start(bf16[2,2,2,6,48,128]{5,4,3,2,1,0:T(8,128)(2,1)S(1)} %bitcast.303), channel_id=1, source_target_pairs={{0,1},{1,0},{2,3},{3,2},{4,5},{5,4},{6,7},{7,6},{8,9},{9,8},{10,11... | collective-permute-start | bytes 1769480 | tf_op jit(solution)/shard_map/ppermute | solution.py:965
  466.2 19.1 %collective-permute-start.20 = (bf16[2,2,2,6,48,128]{5,4,3,2,1,0:T(8,128)(2,1)S(1)}, bf16[2,2,2,6,48,128]{5,4,3,2,1,0:T(8,128)(2,1)S(1)}, u32[]{:S(2)}, u32[]{:S(2)}) collective-permute-start(bf16[2,2,2,6,48,128]{5,4,3,2,1,0:T(8,128)(2,1)S(1)} %bitcast.304), channel_id=1, source_target_pairs={{0,8},{2,10},{4,12},{6,14},{8,0},{10,2},{12,4},{14,6},{16,24},{18,... | collective-permute-start | bytes 1769480 | tf_op jit(solution)/shard_map/ppermute | solution.py:965
  467.5 20.3 %collective-permute-start.15 = (bf16[2,2,2,6,48,128]{5,4,3,2,1,0:T(8,128)(2,1)S(1)}, bf16[2,2,2,6,48,128]{5,4,3,2,1,0:T(8,128)(2,1)S(1)}, u32[]{:S(2)}, u32[]{:S(2)}) collective-permute-start(bf16[2,2,2,6,48,128]{5,4,3,2,1,0:T(8,128)(2,1)S(1)} %bitcast.305), channel_id=1, source_target_pairs={{0,4},{2,6},{4,0},{6,2},{8,12},{10,14},{12,8},{14,10},{16,20},{18,... | collective-permute-start | bytes 1769480 | tf_op jit(solution)/shard_map/ppermute | solution.py:965
  472.6 17.6 %collective-permute-start.31 = (bf16[11,48,128]{2,1,0:T(8,128)(2,1)S(1)}, bf16[11,48,128]{2,1,0:T(8,128)(2,1)S(1)}, u32[]{:S(2)}, u32[]{:S(2)}) collective-permute-start(bf16[11,48,128]{2,1,0:T(8,128)(2,1)S(1)} %bitcast.327), channel_id=1, source_target_pairs={{0,16},{2,18},{4,20},{6,22},{8,24},{10,26},{12,28},{14,30},{16,0},... | collective-permute-start | bytes 405512 | tf_op jit(solution)/shard_map/ppermute | solution.py:965
  489.9 8.5 %collective-permute-start.16 = (bf16[2,2,6,48,128]{4,3,2,1,0:T(8,128)(2,1)}, bf16[2,2,6,48,128]{4,3,2,1,0:T(8,128)(2,1)}, u32[]{:S(2)}, u32[]{:S(2)}) collective-permute-start(bf16[2,2,6,48,128]{4,3,2,1,0:T(8,128)(2,1)} %bitcast.92), channel_id=1, source_target_pairs={{0,8},{2,10},{4,12},{6,14},{8,0},{10,2},{12,4},{14,6},{16,24},{18,... | collective-permute-start | bytes 884744 | tf_op jit(solution)/shard_map/ppermute | solution.py:965
  492.5 8.5 %collective-permute-start.27 = (bf16[2,6,48,128]{3,2,1,0:T(8,128)(2,1)S(1)}, bf16[2,6,48,128]{3,2,1,0:T(8,128)(2,1)S(1)}, u32[]{:S(2)}, u32[]{:S(2)}) collective-permute-start(bf16[2,6,48,128]{3,2,1,0:T(8,128)(2,1)S(1)} %bitcast.323), channel_id=1, source_target_pairs={{0,8},{2,10},{4,12},{6,14},{8,0},{10,2},{12,4},{14,6},{16,24},{18,... | collective-permute-start | bytes 442376 | tf_op jit(solution)/shard_map/ppermute | solution.py:965
  (30 other events, 229.7 us)

commit v5 on v4

--- a/solution.py
+++ b/solution.py
@@ -157,6 +157,10 @@
 
 
 GROUPS = HEADS // 4
+SELF_ROWS = 4
+CROSS_ROWS = 4
+SELF_BACK_ROWS = 4
+CROSS_BACK_ROWS = 4
 
 
 def self_forward_kernel(
@@ -168,19 +172,28 @@
     v_ref[...] = (dot_nn(x, w_ref[2]) + bias_ref[1:2]).astype(bf16)
     low, high = half_lanes(SLOTS)
 
-    def one_row(r, carry):
-        rows = pl.ds(pl.multiple_of(r * SLOTS, SLOTS), SLOTS)
-        allowed = mask_ref[r] > 0.0
-        for g in range(GROUPS):
-            cols = slice(g * 256, (g + 1) * 256)
-            queries = spread_heads(q_ref[rows, cols] * bf16(0.125), low, high)
-            scores = jnp.where(allowed, dot_nt(k_ref[rows, cols], queries), blocked)
-            prob = columns_softmax(scores).astype(bf16)
-            mixed = dot_tn(prob, v_ref[rows, cols])
-            mix_ref[rows, cols] = collect_heads(mixed, SLOTS).astype(bf16)
+    def some_rows(step, carry):
+        spots = []
+        for near in range(SELF_ROWS):
+            r = step * SELF_ROWS + near
+            rows = pl.ds(pl.multiple_of(r * SLOTS, SLOTS), SLOTS)
+            spots += [(r, rows, slice(g * 256, (g + 1) * 256)) for g in range(GROUPS)]
+        scores = [
+            dot_nt(
+                k_ref[rows, cols], spread_heads(q_ref[rows, cols] * bf16(0.125), low, high)
+            )
+            for r, rows, cols in spots
+        ]
+        probs = [
+            columns_softmax(jnp.where(mask_ref[r] > 0.0, score, blocked)).astype(bf16)
+            for (r, rows, cols), score in zip(spots, scores)
+        ]
+        mixed = [dot_tn(prob, v_ref[rows, cols]) for (r, rows, cols), prob in zip(spots, probs)]
+        for (r, rows, cols), mix in zip(spots, mixed):
+            mix_ref[rows, cols] = collect_heads(mix, SLOTS).astype(bf16)
         return carry
 
-    lax.fori_loop(0, x_ref.shape[0] // SLOTS, one_row, 0)
+    lax.fori_loop(0, x_ref.shape[0] // (SELF_ROWS * SLOTS), some_rows, 0)
     total = x.astype(f32) + dot_nn(mix_ref[...], w_ref[3]) + bias_ref[2:3]
     sum_ref[...] = total
     unit, _ = norm_parts(total)
@@ -206,7 +219,7 @@
         out_shape=[low, low, low, low, full, full],
         compiler_params=params(58),
         name="self_forward",
-        cost_estimate=cost(27),
+        cost_estimate=cost(15),
     )(x, weights, biases, gains, mask)
 
 
@@ -241,24 +254,36 @@
     branch_ref[...] = branch
     dmix_all[...] = dot_nt(branch, w_ref[0]).astype(bf16)
 
-    def one_row(r, carry):
-        rows = pl.ds(pl.multiple_of(r * SLOTS, SLOTS), SLOTS)
-        allowed = mask_ref[r] > 0.0
-        for g in range(GROUPS):
-            cols = slice(g * 256, (g + 1) * 256)
-            keys = k_ref[rows, cols]
-            queries = spread_heads(q_ref[rows, cols] * bf16(0.125), low, high)
-            outs = spread_heads(dmix_all[rows, cols], low, high)
-            prob = columns_softmax(jnp.where(allowed, dot_nt(keys, queries), blocked))
-            dprob = dot_nt(v_ref[rows, cols], outs)
-            dscore = (prob * (dprob - jnp.sum(dprob * prob, 0, keepdims=True))).astype(bf16)
-            grad_ref[2, rows, cols] = dot_nn(prob.astype(bf16), outs).astype(bf16)
-            grad_ref[1, rows, cols] = dot_nn(dscore, queries).astype(bf16)
-            turned = collect_heads(dot_tn(dscore, keys), SLOTS) * 0.125
-            grad_ref[0, rows, cols] = turned.astype(bf16)
+    def some_rows(step, carry):
+        spots = []
+        for near in range(SELF_BACK_ROWS):
+            r = step * SELF_BACK_ROWS + near
+            rows = pl.ds(pl.multiple_of(r * SLOTS, SLOTS), SLOTS)
+            spots += [(r, rows, slice(g * 256, (g + 1) * 256)) for g in range(GROUPS)]
+        queries = [
+            spread_heads(q_ref[rows, cols] * bf16(0.125), low, high) for r, rows, cols in spots
+        ]
+        outs = [spread_heads(dmix_all[rows, cols], low, high) for r, rows, cols in spots]
+        scores = [dot_nt(k_ref[spot[1:]], turned) for spot, turned in zip(spots, queries)]
+        dprobs = [dot_nt(v_ref[spot[1:]], turned) for spot, turned in zip(spots, outs)]
+        probs = [
+            columns_softmax(jnp.where(mask_ref[spot[0]] > 0.0, score, blocked))
+            for spot, score in zip(spots, scores)
+        ]
+        for spot, prob, turned in zip(spots, probs, outs):
+            grad_ref[(2,) + spot[1:]] = dot_nn(prob.astype(bf16), turned).astype(bf16)
+        dscores = [
+            (prob * (dprob - jnp.sum(dprob * prob, 0, keepdims=True))).astype(bf16)
+            for prob, dprob in zip(probs, dprobs)
+        ]
+        for spot, dscore, turned in zip(spots, dscores, queries):
+            grad_ref[(1,) + spot[1:]] = dot_nn(dscore, turned).astype(bf16)
+        dqs = [dot_tn(dscore, k_ref[spot[1:]]) for spot, dscore in zip(spots, dscores)]
+        for spot, dq in zip(spots, dqs):
+            grad_ref[(0,) + spot[1:]] = (collect_heads(dq, SLOTS) * 0.125).astype(bf16)
         return carry
 
-    lax.fori_loop(0, count // SLOTS, one_row, 0)
+    lax.fori_loop(0, count // (SELF_BACK_ROWS * SLOTS), some_rows, 0)
     side_ref[0:1] += dgain
     side_ref[1:2] += dshift
     for place, rows in enumerate((grad_ref[0], grad_ref[2], branch)):
@@ -300,7 +325,7 @@
         scratch_shapes=[pltpu.VMEM((count, width), bf16)],
         compiler_params=params(58),
         name="self_backward",
-        cost_estimate=cost(25),
+        cost_estimate=cost(16),
     )(weights, gains, mask, q, k, v, total, top, text, *order)
 
 
@@ -331,7 +356,7 @@
         out_shape=jax.ShapeDtypeStruct((tokens, width), f32),
         compiler_params=params(58),
         name="input_gradient",
-        cost_estimate=cost(7),
+        cost_estimate=cost(9),
     )(weights, grads, down, *order)
 
 
@@ -398,11 +423,17 @@
         out_shape=[jax.ShapeDtypeStruct(shape, bf16)] * (1 if fold is None else 2),
         compiler_params=params(58),
         name="attn_weight_grad",
-        cost_estimate=cost(6),
+        cost_estimate=cost(7),
     )(core, left, grads, left_two, right_two, *order)
 
 
 TAIL = 16
+
+
+def hide_ends(scores, main):
+    end = scores[main:]
+    shown = lax.broadcasted_iota(jnp.int32, end.shape, 0) < 1
+    return jnp.concatenate([scores[:main], jnp.where(shown, end, blocked)], 0)
 
 
 def cross_forward_kernel(
@@ -431,25 +462,37 @@
     residual = norm_ref[...].reshape(rows_here * QUERIES, width)
     q_ref[...] = (dot_nn(residual.astype(bf16), w_ref[0]) + bias_ref[3:4]).astype(bf16)
     low, high = half_lanes(QUERIES)
-    shown = lax.broadcasted_iota(jnp.int32, (main + TAIL, 128), 0) <= main
     tokens = image_ref[:, :main].reshape(rows_here * main, -1)
     key_ref[...] = dot_nt(tokens, kv_ref[0]).astype(bf16)
     value_ref[...] = (dot_nt(tokens, kv_ref[1]) + bias_ref[4:5]).astype(bf16)
 
-    def one_row(r, carry):
-        span = pl.ds(pl.multiple_of(r * main, main), main)
-        last = pl.ds(pl.multiple_of(r * TAIL, TAIL), TAIL)
-        mine = pl.ds(pl.multiple_of(r * QUERIES, QUERIES), QUERIES)
-        for g in range(GROUPS):
-            cols = slice(g * 256, (g + 1) * 256)
-            keys = jnp.concatenate([key_ref[span, cols], key_end_ref[last, cols]], 0)
-            values = jnp.concatenate([value_ref[span, cols], value_end_ref[last, cols]], 0)
-            queries = spread_heads(q_ref[mine, cols] * bf16(0.125), low, high)
-            prob = columns_softmax(jnp.where(shown, dot_nt(keys, queries), blocked)).astype(bf16)
-            mix_ref[mine, cols] = collect_heads(dot_tn(prob, values), QUERIES).astype(bf16)
+    def some_rows(step, carry):
+        spots = []
+        for near in range(CROSS_ROWS):
+            r = step * CROSS_ROWS + near
+            span = pl.ds(pl.multiple_of(r * main, main), main)
+            last = pl.ds(pl.multiple_of(r * TAIL, TAIL), TAIL)
+            mine = pl.ds(pl.multiple_of(r * QUERIES, QUERIES), QUERIES)
+            spots += [(span, last, mine, slice(g * 256, (g + 1) * 256)) for g in range(GROUPS)]
+        scores = [
+            dot_nt(
+                jnp.concatenate([key_ref[span, cols], key_end_ref[last, cols]], 0),
+                spread_heads(q_ref[mine, cols] * bf16(0.125), low, high),
+            )
+            for span, last, mine, cols in spots
+        ]
+        probs = [columns_softmax(hide_ends(score, main)).astype(bf16) for score in scores]
+        mixed = [
+            dot_tn(
+                prob, jnp.concatenate([value_ref[span, cols], value_end_ref[last, cols]], 0)
+            )
+            for (span, last, mine, cols), prob in zip(spots, probs)
+        ]
+        for (span, last, mine, cols), mix in zip(spots, mixed):
+            mix_ref[mine, cols] = collect_heads(mix, QUERIES).astype(bf16)
         return carry
 
-    lax.fori_loop(0, rows_here, one_row, 0)
+    lax.fori_loop(0, rows_here // CROSS_ROWS, some_rows, 0)
     total = residual + dot_nn(mix_ref[...], w_ref[1]) + bias_ref[5:6]
     sum_ref[...] = total
     unit, _ = norm_parts(total)
@@ -493,7 +536,7 @@
         ],
         compiler_params=params(58),
         name="cross_forward",
-        cost_estimate=cost(55),
+        cost_estimate=cost(38),
     )(images, ends, kv, weights, biases, gains, norm)
 
 
@@ -516,7 +559,6 @@
     rows_here, _, width = dnorm_ref.shape
     main = key_ref.shape[0] // rows_here
     low, high = half_lanes(QUERIES)
-    shown = lax.broadcasted_iota(jnp.int32, (main + TAIL, 128), 0) <= main
 
     @pl.when(step == 0)
     def _():
@@ -526,29 +568,47 @@
     branch = down.astype(bf16)
     dmix_all[...] = dot_nt(branch, w_ref[1]).astype(bf16)
 
-    def one_row(r, carry):
-        span = pl.ds(pl.multiple_of(r * main, main), main)
-        last = pl.ds(pl.multiple_of(r * TAIL, TAIL), TAIL)
-        mine = pl.ds(pl.multiple_of(r * QUERIES, QUERIES), QUERIES)
-        for g in range(GROUPS):
-            cols = slice(g * 256, (g + 1) * 256)
-            keys = jnp.concatenate([key_ref[span, cols], key_end_ref[last, cols]], 0)
-            values = jnp.concatenate([value_ref[span, cols], value_end_ref[last, cols]], 0)
-            queries = spread_heads(q_ref[mine, cols] * bf16(0.125), low, high)
-            outs = spread_heads(dmix_all[mine, cols], low, high)
-            prob = columns_softmax(jnp.where(shown, dot_nt(keys, queries), blocked))
-            dprob = dot_nt(values, outs)
-            dscore = (prob * (dprob - jnp.sum(dprob * prob, 0, keepdims=True))).astype(bf16)
-            dv = dot_nn(prob.astype(bf16), outs).astype(bf16)
-            dk = dot_nn(dscore, queries).astype(bf16)
+    def some_rows(step, carry):
+        spots = []
+        for near in range(CROSS_BACK_ROWS):
+            r = step * CROSS_BACK_ROWS + near
+            span = pl.ds(pl.multiple_of(r * main, main), main)
+            last = pl.ds(pl.multiple_of(r * TAIL, TAIL), TAIL)
+            mine = pl.ds(pl.multiple_of(r * QUERIES, QUERIES), QUERIES)
+            spots += [(span, last, mine, slice(g * 256, (g + 1) * 256)) for g in range(GROUPS)]
+        keys = [
+            jnp.concatenate([key_ref[span, cols], key_end_ref[last, cols]], 0)
+            for span, last, mine, cols in spots
+        ]
+        queries = [
+            spread_heads(q_ref[mine, cols] * bf16(0.125), low, high)
+            for span, last, mine, cols in spots
+        ]
+        outs = [spread_heads(dmix_all[mine, cols], low, high) for span, last, mine, cols in spots]
+        scores = [dot_nt(rows, turned) for rows, turned in zip(keys, queries)]
+        dprobs = [
+            dot_nt(jnp.concatenate([value_ref[span, cols], value_end_ref[last, cols]], 0), turned)
+            for (span, last, mine, cols), turned in zip(spots, outs)
+        ]
+        probs = [columns_softmax(hide_ends(score, main)) for score in scores]
+        for (span, last, mine, cols), prob, turned in zip(spots, probs, outs):
+            dv = dot_nn(prob.astype(bf16), turned).astype(bf16)
+            dkv_ref[1, span, cols] = dv[:main]
+            dkv_end_ref[1, last, cols] = dv[main:]
+        dscores = [
+            (prob * (dprob - jnp.sum(dprob * prob, 0, keepdims=True))).astype(bf16)
+            for prob, dprob in zip(probs, dprobs)
+        ]
+        for (span, last, mine, cols), dscore, turned in zip(spots, dscores, queries):
+            dk = dot_nn(dscore, turned).astype(bf16)
             dkv_ref[0, span, cols] = dk[:main]
             dkv_end_ref[0, last, cols] = dk[main:]
-            dkv_ref[1, span, cols] = dv[:main]
-            dkv_end_ref[1, last, cols] = dv[main:]
-            dq_ref[mine, cols] = (collect_heads(dot_tn(dscore, keys), QUERIES) * 0.125).astype(bf16)
+        dqs = [dot_tn(dscore, rows) for dscore, rows in zip(dscores, keys)]
+        for (span, last, mine, cols), dq in zip(spots, dqs):
+            dq_ref[mine, cols] = (collect_heads(dq, QUERIES) * 0.125).astype(bf16)
         return carry
 
-    lax.fori_loop(0, rows_here, one_row, 0)
+    lax.fori_loop(0, rows_here // CROSS_BACK_ROWS, some_rows, 0)
     dq = dq_ref[...]
     dnorm_ref[...] = (down + dot_nt(dq, w_ref[0])).reshape(rows_here, QUERIES, width)
     side_ref[0:1] += jnp.sum(dq.astype(f32), 0, keepdims=True)
@@ -595,7 +655,7 @@
         scratch_shapes=[pltpu.VMEM((take * QUERIES, width), bf16)],
         compiler_params=params(58),
         name="cross_backward",
-        cost_estimate=cost(40),
+        cost_estimate=cost(19),
     )(weights, keys, values, key_ends, value_ends, q, down, *order)
 
 
@@ -661,7 +721,7 @@
             vmem_limit_bytes=58 * MIB, dimension_semantics=("arbitrary", "arbitrary")
         ),
         name="cross_weight_grad",
-        cost_estimate=cost(30),
+        cost_estimate=cost(32),
     )(core, images, ends, grads, grads_end, *order)
 
 
@@ -687,12 +747,26 @@
         rows_low[...] = full.astype(bf16)
         sum_ref[...] = full + bias_ref[6 + which : 7 + which]
 
-    u = dot_nn(rows_low[...], in_ref[0]) + in_bias_ref[which : which + 1]
-    act, slope = gate_parts(u)
-    act = act.astype(bf16)
-    act_ref[...] = act
-    slope_ref[...] = slope.astype(bf16)
-    sum_ref[...] += dot_nn(act, out_ref[0])
+    low = rows_low[...]
+    wide = 256
+    pieces = act_ref.shape[1] // wide
+
+    def before_gate(k):
+        cols = slice(k * wide, (k + 1) * wide)
+        return dot_nn(low, in_ref[0, :, cols]) + in_bias_ref[which : which + 1, cols]
+
+    ahead = [before_gate(k) for k in range(2)]
+    gathered = 0.0
+    for k in range(pieces):
+        if k + 2 < pieces:
+            ahead.append(before_gate(k + 2))
+        cols = slice(k * wide, (k + 1) * wide)
+        act, slope = gate_parts(ahead[k])
+        act = act.astype(bf16)
+        act_ref[:, cols] = act
+        slope_ref[:, cols] = slope.astype(bf16)
+        gathered += dot_nn(act, out_ref[0, cols])
+    sum_ref[...] += gathered
 
     @pl.when(step == pl.num_programs(0) - 1)
     def _():
@@ -710,7 +784,7 @@
     tokens = rows * QUERIES
     hidden = ffn_in.shape[2]
     embed = projections.shape[2]
-    chunk = 512
+    chunk = 1024
     cols = pl.BlockSpec((tokens, chunk), lambda j: (0, j))
     halves = [] if layer is None else [layer]
     return pl.pallas_call(
@@ -936,7 +1010,7 @@
         input_output_aliases={13 + k: 4 + k for k in range(len(slabs))},
         compiler_params=params(60),
         name="ffn_backward",
-        cost_estimate=cost(20),
+        cost_estimate=cost(25),
     )(
         core,
         norm,

time: 523 us -> 463 us (0.89)
  Pallas kernels: 282 us -> 227 us
    pallas_call x1, Pallas kernels: 54.5 us -> 37.5 us  [cross_forward(): pl.pallas_call(cross_forward_kernel, grid=(rows // take,), in_specs=[pl.B...]
    pallas_call x1, Pallas kernels: 27.8 us -> 14.7 us  [self_forward(): pl.pallas_call(self_forward_kernel, grid=(tokens // step,), in_specs=[til...]
    pallas_call x1, Pallas kernels: 31.5 us -> 18.9 us  [cross_backward(): pl.pallas_call(ordered(cross_backward_kernel, 7, len(order)), grid=(rows...]
    pallas_call x1, Pallas kernels: 25.9 us -> 15.7 us  [self_backward(): pl.pallas_call(ordered(self_backward_kernel, 9, len(order)), grid=(tokens...]
    unnamed x50 -> x52, local copies, waits for them, and re-layouts: 13.7 us -> 13.7 us
  transfers between devices with their start and end apart: 39 -> 39, of which waited for: 15 -> 15; matrix products, arithmetic and copies ran while one was open for 19% -> 20% of each run, Pallas kernels for 41% -> 38%
where the time goes in v5:
time: 463 us; the launch traced here: 454 us
  Pallas kernels  227 us (49%)
  other arithmetic  66.7 us (14%)
  starting transfers between devices  55.4 us (12%)
  waiting for transfers between devices  50.1 us (11%)
  local copies, waits for them, and re-layouts  46 us (10%)
  matrix products  7.01 us (2%)
    pallas_call x2, Pallas kernels, ffn_backward(): pl.pallas_call(functools.partial(ffn_backward_kernel, which, folds), grid...  49.7 us
    pallas_call x1, Pallas kernels, cross_forward(): pl.pallas_call(cross_forward_kernel, grid=(rows // take,), in_specs=[pl.B...  37.5 us
    ppermute x35, waiting for transfers between devices, swap(): lax.ppermute(values, axis, [(i, i ^ 1 << bit) for i in range(sizes[axis])])  36.9 us
    ppermute x35, starting transfers between devices, swap(): lax.ppermute(values, axis, [(i, i ^ 1 << bit) for i in range(sizes[axis])])  35.7 us
    convert_element_type x18, other arithmetic, advance(): sent = total(terms, [1 - mine]).astype(bf16)  34.8 us
    pallas_call x1, Pallas kernels, cross_weight_grad(): pl.pallas_call(ordered(functools.partial(cross_weight_kernel, fold), 5, l...  32 us
    pallas_call x2, Pallas kernels, ffn_forward(): pl.pallas_call(functools.partial(ffn_forward_kernel, which), grid=(hidden...  29.9 us
    all_to_all x4, starting transfers between devices, exchange(): return lax.all_to_all(values, ('dp', 'rep'), 0, 0, tiled=True)  19.7 us
  transfers between devices with their start and end apart: 39, of which 15 were waited for; matrix products, arithmetic and copies ran while one was open for 20% of the time, Pallas kernels for 38%

profile of v5, /device:TPU:0, one launch (start us, length us, event | category | flops | bytes accessed | tf_op | source)
XLA Modules:
  0.0 454.0 jit_solution(14186827004026352615)
XLA Ops:
  4.4 7.6 %copy.131.image_ref.refs_1_ = bf16[16,257,1408]{2,1,0:T(8,128)(2,1)S(1)} copy(bf16[16,257,1408]{2,0,1:T(8,128)(2,1)} %param.15) | data formatting | bytes 23158784 | tf_op args[1]
  11.9 4.3 copy-done
  17.3 14.7 %self_forward.1 = (bf16[1024,768]{1,0:T(8,128)(2,1)}, bf16[1024,768]{1,0:T(8,128)(2,1)}, bf16[1024,768]{1,0:T(8,128)(2,1)}, bf16[1024,768]{1,0:T(8,128)(2,1)}, f32[1024,768]{1,0:T(8,128)}, /*index=5*/f32[1024,768]{1,0:T(8,128)}) custom-call(bf16[1024,768]{1,0:T(8,128)(2,1)} %bitcast.337, bf16[6,768,768]{2,1,0:T(8,128)(2,1)} %refs_0_.5, f32[12,768]{1,0:T(8,128)} %bias_ref.7, ...), custom_call_target="tpu_custom_call" | custom-call | flops 16499999744 | tf_op jit(solution)/shard_map/self_forward/pallas_call | solution.py:208
  32.0 14.9 %ffn_forward.2 = (bf16[512,3072]{1,0:T(8,128)(2,1)}, bf16[512,3072]{1,0:T(8,128)(2,1)}, f32[512,768]{1,0:T(8,128)}, bf16[16,64,768]{2,1,0:T(8,128)(2,1)}, f32[512,256]{1,0:T(8,128)}, /*index=5*/bf16[512,256]{1,0:T(8,128)(2,1)}) custom-call(f32[16,64,768]{2,1,0:T(8,128)} %bitcast.341, bf16[2,768,3072]{2,1,0:T(8,128)(2,1)} %in_ref.7, f32[2,3072]{1,0:T(2,128)} %in_bias_ref.3, ...), custom_call_target="tpu_custom_call" | custom-call | flops 16499999744 | tf_op jit(solution)/shard_map/ffn_forward/pallas_call | solution.py:790
  48.9 7.5 %all-to-all-start = ((bf16[32,32,256]{2,1,0:T(8,128)(2,1)}), bf16[32,32,256]{2,1,0:T(8,128)(2,1)S(1)}, u32[]{:S(2)}, u32[]{:S(2)}) async-start(bf16[32,32,256]{2,1,0:T(8,128)(2,1)} %tile.20), calls=%async_computation | async-start | bytes 1048576 | tf_op jit(solution)/shard_map/all_to_all | solution.py:1117
  56.4 37.5 %cross_forward.1 = (bf16[4096,768]{1,0:T(8,128)(2,1)}, bf16[4096,768]{1,0:T(8,128)(2,1)}, bf16[256,768]{1,0:T(8,128)(2,1)}, bf16[256,768]{1,0:T(8,128)(2,1)}, bf...) custom-call(bf16[16,257,1408]{2,1,0:T(8,128)(2,1)} %copy-done, ...), custom_call_target="tpu_custom_call" | custom-call | flops 41799999488 | tf_op jit(solution)/shard_map/cross_forward/pallas_call | solution.py:514
  94.0 15.0 %ffn_forward.3 = (bf16[512,3072]{1,0:T(8,128)(2,1)}, bf16[512,3072]{1,0:T(8,128)(2,1)}, f32[512,768]{1,0:T(8,128)}, bf16[16,64,768]{2,1,0:T(8,128)(2,1)}, f32[512,256]{1,0:T(8,128)}, /*index=5*/bf16[512,256]{1,0:T(8,128)(2,1)}) custom-call(f32[16,32,768]{2,1,0:T(8,128)} %bitcast.348, bf16[2,768,3072]{2,1,0:T(8,128)(2,1)} %in_ref.7, ...), custom_call_target="tpu_custom_call", output_to_operand_aliasing={{3}: (8, {})} | custom-call | flops 16499999744 | tf_op jit(solution)/shard_map/ffn_forward/pallas_call | solution.py:790
  113.1 5.9 %all-to-all-start.1 = ((f32[32,1,1024]{2,1,0:T(1,128)}), f32[32,1,1024]{2,1,0:T(1,128)S(1)}, u32[]{:S(2)}, u32[]{:S(2)}) async-start(f32[32,1,1024]{2,1,0:T(1,128)} %broadcast_in_dim.10), calls=%async_computation.1 | async-start | bytes 262144 | tf_op jit(solution)/shard_map/all_to_all | solution.py:1117
  119.3 8.3 %all-to-all-done.1 = f32[32,1,1024]{2,1,0:T(1,128)S(1)} async-done(((f32[32,1,1024]{2,1,0:T(1,128)}), f32[32,1,1024]{2,1,0:T(1,128)S(1)}, u32[]{:S(2)}, u32[]{:S(2)}) %all-to-all-start.1) | async-done | bytes 131104 | tf_op jit(solution)/shard_map/all_to_all | solution.py:1117
  131.3 2.8 all-to-all-start.2
  136.0 24.6 %ffn_backward.2 = (f32[16,32,768]{2,1,0:T(8,128)}, f32[8,768]{1,0:T(8,128)}, f32[8,3072]{1,0:T(8,128)}, f32[8,256]{1,0:T(8,128)}, bf16[2,2,2,2,18,48,128]{6,5,4,...) custom-call(s32[1]{0:T(128)} %bitcast.11.core_ref.refs_0_, ...), custom_call_target="tpu_custom_call" | custom-call | flops 27499999232 | tf_op jit(solution)/shard_map/ffn_backward/pallas_call | solution.py:971
  162.1 25.1 %ffn_backward.3 = (f32[16,32,768]{2,1,0:T(8,128)}, f32[8,768]{1,0:T(8,128)}, f32[8,3072]{1,0:T(8,128)}, f32[8,256]{1,0:T(8,128)}, bf16[2,2,2,2,18,48,128]{6,5,4,...) custom-call(s32[1]{0:T(128)} %bitcast.11.core_ref.refs_0_, ...), custom_call_target="tpu_custom_call", output_to_operand_aliasing={{4}: (13, {}), {5}: (14, {}), {6}: (15, {}), {7}: (16, {}),... | custom-call | flops 27499999232 | tf_op jit(solution)/shard_map/ffn_backward/pallas_call | solution.py:971
  193.5 18.9 %cross_backward.1 = (f32[16,32,768]{2,1,0:T(8,128)}, bf16[2,4096,768]{2,1,0:T(8,128)(2,1)}, bf16[2,256,768]{2,1,0:T(8,128)(2,1)}, bf16[512,768]{1,0:T(8,128)(2,1)}, f32[8,768]{1,0:T(8,128)}) custom-call(bf16[6,768,768]{2,1,0:T(8,128)(2,1)} %refs_0_.5, bf16[4096,768]{1,0:T(8,128)(2,1)} %get-tuple-element.107.refs_1_, ...), custom_call_target="tpu_custom_call" | custom-call | flops 20899999744 | tf_op jit(solution)/shard_map/cross_backward/pallas_call | solution.py:628
  215.3 3.6 add_convert_fusion.2
  220.6 3.1 add_convert_fusion.1
  227.3 32.0 %cross_weight_grad.1 = (bf16[2,2,2,2,11,48,128]{6,5,4,3,2,1,0:T(8,128)(2,1)}, bf16[2,2,2,2,11,48,128]{6,5,4,3,2,1,0:T(8,128)(2,1)}) custom-call(s32[1]{0:T(128)} %bitcast.11.core_ref.refs_0_, bf16[16,257,1408]{2,1,0:T(8,128)(2,1)} %copy-done, bf16[16,16,1408]{2,1,0:T(8,128)(2,1)} %pad.6.end_ref.rest_0_.refs_2_, ...), custom_call_target="tpu_custom_call" | custom-call | flops 35200000000 | tf_op jit(solution)/shard_map/cross_weight_grad/pallas_call | solution.py:706
  260.4 2.9 add_convert_fusion.5
  264.8 2.8 add_convert_fusion.6
  269.1 2.7 add_convert_fusion.4
  271.8 15.7 %self_backward.1 = (bf16[3,1024,768]{2,1,0:T(8,128)(2,1)}, bf16[1024,768]{1,0:T(8,128)(2,1)}, f32[1024,768]{1,0:T(8,128)}, f32[8,768]{1,0:T(8,128)}) custom-call(bf16[6,768,768]{2,1,0:T(8,128)(2,1)} %refs_0_.5, f32[4,768]{1,0:T(4,128)} %refs_1_.2, f32[16,64,256]{2,1,0:T(8,128)} %tile.18.mask_ref.refs_2_, bf16[1024,768]{1,0:T(8,128)(2,1)} %get-tuple-element.103.refs_3_, ...), custom_call_target="tpu_custom_call" | custom-call | flops 17600000000 | tf_op jit(solution)/shard_map/self_backward/pallas_call | solution.py:298
  293.2 2.7 stack.18
  302.2 3.5 all-to-all-start.3
  308.8 4.8 %all-to-all-done.3 = f32[32,1,592]{2,1,0:T(1,128)} async-done(((f32[32,1,592]{2,1,0:T(1,128)}), f32[32,1,592]{2,1,0:T(1,128)}, u32[]{:S(2)}, u32[]{:S(2)}) %all-to-all-start.3) | async-done | bytes 75808 | tf_op jit(solution)/shard_map/all_to_all | solution.py:1117
  324.4 5.6 %collective-permute-done.6 = bf16[2,2,18,48,128]{4,3,2,1,0:T(8,128)(2,1)} collective-permute-done((bf16[2,2,18,48,128]{4,3,2,1,0:T(8,128)(2,1)}, bf16[2,2,18,48,128]{4,3,2,1,0:T(8,128)(2,1)}, u32[]{:S(2)}, u32[]{:S(2)}) %collective-permute-start.6) | collective-permute-done | bytes 884768 | tf_op jit(solution)/shard_map/ppermute | solution.py:1039
  334.0 7.1 %attn_weight_grad.3 = (bf16[2,2,2,2,6,48,128]{6,5,4,3,2,1,0:T(8,128)(2,1)}, bf16[2,2,2,2,6,48,128]{6,5,4,3,2,1,0:T(8,128)(2,1)}) custom-call(s32[1]{0:T(128)} %bitcast.11.core_ref.refs_0_, bf16[1024,768]{1,0:T(8,128)(2,1)} %bitcast.338, bf16[3,1024,768]{2,1,0:T(8,128)(2,1)} %get-tuple-element.147.refs_2_.refs_1_, ...), custom_call_target="tpu_custom_call" | custom-call | flops 7699999744 | tf_op jit(solution)/shard_map/attn_weight_grad/pallas_call | solution.py:411
  341.1 6.2 %attn_weight_grad.4 = (bf16[2,2,2,2,6,48,128]{6,5,4,3,2,1,0:T(8,128)(2,1)}, bf16[2,2,2,2,6,48,128]{6,5,4,3,2,1,0:T(8,128)(2,1)}) custom-call(s32[1]{0:T(128)} %bitcast.11.core_ref.refs_0_, bf16[1024,768]{1,0:T(8,128)(2,1)} %bitcast.339, bf16[3,1024,768]{2,1,0:T(8,128)(2,1)} %get-tuple-element.147.refs_2_.refs_1_, f32[16,64,768]{2,1,0:T(8,128)} %bitcast.344, ...), custom_call_target="tpu_custom_call" | custom-call | flops 7699999744 | tf_op jit(solution)/shard_map/attn_weight_grad/pallas_call | solution.py:411
  347.3 6.3 %attn_weight_grad.5 = (bf16[2,2,2,2,6,48,128]{6,5,4,3,2,1,0:T(8,128)(2,1)}, bf16[2,2,2,2,6,48,128]{6,5,4,3,2,1,0:T(8,128)(2,1)}) custom-call(s32[1]{0:T(128)} %bitcast.11.core_ref.refs_0_, bf16[1024,768]{1,0:T(8,128)(2,1)} %bitcast.340, bf16[3,1024,768]{2,1,0:T(8,128)(2,1)} %get-tuple-element.147.refs_2_.refs_1_, ...), custom_call_target="tpu_custom_call" | custom-call | flops 7699999744 | tf_op jit(solution)/shard_map/attn_weight_grad/pallas_call | solution.py:411
  354.1 2.6 convert_add_fusion.3
  367.1 9.1 %input_gradient.1 = f32[1024,768]{1,0:T(8,128)} custom-call(bf16[6,768,768]{2,1,0:T(8,128)(2,1)} %refs_0_.5, bf16[3,1024,768]{2,1,0:T(8,128)(2,1)} %get-tuple-element.147.refs_2_.refs_1_, f32[1024,768]{1,0:T(8,128)} %get-tuple-element.148.refs_2_, bf16[2,2,2,2,6,48,128]{6,5,4,3,2,1,0:T(8,128)(2,1)} %get-tuple-element.160.refs_3_, ...), custom_call_target="tpu_custom_call" | custom-call | flops 9900000256 | tf_op jit(solution)/shard_map/input_gradient/pallas_call | solution.py:346
  385.5 5.0 %collective-permute-done.32 = bf16[18,48,128]{2,1,0:T(8,128)(2,1)S(1)} collective-permute-done((bf16[18,48,128]{2,1,0:T(8,128)(2,1)S(1)}, bf16[18,48,128]{2,1,0:T(8,128)(2,1)S(1)}, u32[]{:S(2)}, u32[]{:S(2)}) %collective-permute-start.32) | collective-permute-done | bytes 221216 | tf_op jit(solution)/shard_map/ppermute | solution.py:1039
  393.1 5.8 %collective-permute-done.29 = bf16[2,2,11,48,128]{4,3,2,1,0:T(8,128)(2,1)} collective-permute-done((bf16[2,2,11,48,128]{4,3,2,1,0:T(8,128)(2,1)}, bf16[2,2,11,48,128]{4,3,2,1,0:T(8,128)(2,1)}, u32[]{:S(2)}, u32[]{:S(2)}) %collective-permute-start.29) | collective-permute-done | bytes 540704 | tf_op jit(solution)/shard_map/ppermute | solution.py:1039
  412.0 8.7 %collective-permute-done.25 = bf16[2,2,2,6,48,128]{5,4,3,2,1,0:T(8,128)(2,1)S(1)} collective-permute-done((bf16[2,2,2,6,48,128]{5,4,3,2,1,0:T(8,128)(2,1)S(1)}, bf16[2,2,2,6,48,128]{5,4,3,2,1,0:T(8,128)(2,1)S(1)}, u32[]{:S(2)}, u32[]{:S(2)}) %collective-permute-start.25) | collective-permute-done | bytes 589856 | tf_op jit(solution)/shard_map/ppermute | solution.py:1039
  (249 shorter events, 135.0 us)
Async XLA Ops:
  48.9 61.7 %all-to-all-start = ((bf16[32,32,256]{2,1,0:T(8,128)(2,1)}), bf16[32,32,256]{2,1,0:T(8,128)(2,1)S(1)}, u32[]{:S(2)}, u32[]{:S(2)}) async-start(bf16[32,32,256]{2,1,0:T(8,128)(2,1)} %tile.20), calls=%async_computation | async-start | bytes 1048576 | tf_op jit(solution)/shard_map/all_to_all | solution.py:1117
  113.1 14.6 %all-to-all-start.1 = ((f32[32,1,1024]{2,1,0:T(1,128)}), f32[32,1,1024]{2,1,0:T(1,128)S(1)}, u32[]{:S(2)}, u32[]{:S(2)}) async-start(f32[32,1,1024]{2,1,0:T(1,128)} %broadcast_in_dim.10), calls=%async_computation.1 | async-start | bytes 262144 | tf_op jit(solution)/shard_map/all_to_all | solution.py:1117
  131.3 29.4 %all-to-all-start.2 = ((bf16[32,32,256]{2,1,0:T(8,128)(2,1)}), bf16[32,32,256]{2,1,0:T(8,128)(2,1)S(1)}, u32[]{:S(2)}, u32[]{:S(2)}) async-start(bf16[32,32,256]{2,1,0:T(8,128)(2,1)} %bitcast.310), calls=%async_computation.2 | async-start | bytes 1048576 | tf_op jit(solution)/shard_map/all_to_all | solution.py:1117
  187.2 28.1 %collective-permute-start.2 = (bf16[2,2,2,2,16,48,128]{6,5,4,3,2,1,0:T(8,128)(2,1)}, bf16[2,2,2,2,16,48,128]{6,5,4,3,2,1,0:T(8,128)(2,1)}, u32[]{:S(2)}, u32[]{:S(2)}) collective-permute-start(bf16[2,2,2,2,16,48,128]{6,5,4,3,2,1,0:T(8,128)(2,1)} %get-tuple-element.130.refs_9_), channel_id=1, source_target_pairs={{0,2},{2,0},{4,6},{6,4},{8,10},{10,8},{12,14},{14,12},{16,18},{18,... | collective-permute-start | bytes 9437192 | tf_op jit(solution)/shard_map/ppermute | solution.py:1039
  190.8 29.8 %collective-permute-start.3 = (bf16[2,2,2,2,16,48,128]{6,5,4,3,2,1,0:T(8,128)(2,1)}, bf16[2,2,2,2,16,48,128]{6,5,4,3,2,1,0:T(8,128)(2,1)}, u32[]{:S(2)}, u32[]{:S(2)}) collective-permute-start(bf16[2,2,2,2,16,48,128]{6,5,4,3,2,1,0:T(8,128)(2,1)} %get-tuple-element.131.refs_10_), channel_id=1, source_target_pairs={{0,2},{2,0},{4,6},{6,4},{8,10},{10,8},{12,14},{14,12},{16,18},{18,... | collective-permute-start | bytes 9437192 | tf_op jit(solution)/shard_map/ppermute | solution.py:1039
  193.4 31.9 %collective-permute-start = (bf16[2,2,2,2,18,48,128]{6,5,4,3,2,1,0:T(8,128)(2,1)}, bf16[2,2,2,2,18,48,128]{6,5,4,3,2,1,0:T(8,128)(2,1)S(1)}, u32[]{:S(2)}, u32[]{:S(2)}) collective-permute-start(bf16[2,2,2,2,18,48,128]{6,5,4,3,2,1,0:T(8,128)(2,1)} %get-tuple-element.129.refs_8_), channel_id=1, source_target_pairs={{0,2},{2,0},{4,6},{6,4},{8,10},{10,8},{12,14},{14,12},{16,18},{18,... | collective-permute-start | bytes 10616840 | tf_op jit(solution)/shard_map/ppermute | solution.py:1039
  218.9 41.5 %collective-permute-start.4 = (bf16[2,2,2,16,48,128]{5,4,3,2,1,0:T(8,128)(2,1)}, bf16[2,2,2,16,48,128]{5,4,3,2,1,0:T(8,128)(2,1)}, u32[]{:S(2)}, u32[]{:S(2)}) collective-permute-start(bf16[2,2,2,16,48,128]{5,4,3,2,1,0:T(8,128)(2,1)} %bitcast.28.refs_6_), channel_id=1, source_target_pairs={{0,8},{2,10},{4,12},{6,14},{8,0},{10,2},{12,4},{14,6},{16,24},{18,... | collective-permute-start | bytes 4718600 | tf_op jit(solution)/shard_map/ppermute | solution.py:1039
  223.8 36.7 %collective-permute-start.5 = (bf16[2,2,2,16,48,128]{5,4,3,2,1,0:T(8,128)(2,1)}, bf16[2,2,2,16,48,128]{5,4,3,2,1,0:T(8,128)(2,1)}, u32[]{:S(2)}, u32[]{:S(2)}) collective-permute-start(bf16[2,2,2,16,48,128]{5,4,3,2,1,0:T(8,128)(2,1)} %bitcast.31.refs_7_), channel_id=1, source_target_pairs={{0,1},{1,0},{2,3},{3,2},{4,5},{5,4},{6,7},{7,6},{8,9},{9,8},{10,11... | collective-permute-start | bytes 4718600 | tf_op jit(solution)/shard_map/ppermute | solution.py:1039
  225.7 43.4 %collective-permute-start.1 = (bf16[2,2,2,18,48,128]{5,4,3,2,1,0:T(8,128)(2,1)S(1)}, bf16[2,2,2,18,48,128]{5,4,3,2,1,0:T(8,128)(2,1)}, u32[]{:S(2)}, u32[]{:S(2)}) collective-permute-start(bf16[2,2,2,18,48,128]{5,4,3,2,1,0:T(8,128)(2,1)S(1)} %bitcast.266), channel_id=1, source_target_pairs={{0,4},{2,6},{4,0},{6,2},{8,12},{10,14},{12,8},{14,10},{16,20},{18,... | collective-permute-start | bytes 5308424 | tf_op jit(solution)/shard_map/ppermute | solution.py:1039
  259.3 61.5 %collective-permute-start.9 = (bf16[2,2,2,2,11,48,128]{6,5,4,3,2,1,0:T(8,128)(2,1)}, bf16[2,2,2,2,11,48,128]{6,5,4,3,2,1,0:T(8,128)(2,1)}, u32[]{:S(2)}, u32[]{:S(2)}) collective-permute-start(bf16[2,2,2,2,11,48,128]{6,5,4,3,2,1,0:T(8,128)(2,1)} %get-tuple-element.146.refs_12_), channel_id=1, source_target_pairs={{0,2},{2,0},{4,6},{6,4},{8,10},{10,8},{12,14},{14,12},{16,18},{18,... | collective-permute-start | bytes 6488072 | tf_op jit(solution)/shard_map/ppermute | solution.py:1039
  263.3 52.0 %collective-permute-start.8 = (bf16[2,2,16,48,128]{4,3,2,1,0:T(8,128)(2,1)}, bf16[2,2,16,48,128]{4,3,2,1,0:T(8,128)(2,1)}, u32[]{:S(2)}, u32[]{:S(2)}) collective-permute-start(bf16[2,2,16,48,128]{4,3,2,1,0:T(8,128)(2,1)} %bitcast.41.refs_11_), channel_id=1, source_target_pairs={{0,4},{2,6},{4,0},{6,2},{8,12},{10,14},{12,8},{14,10},{16,20},{18,... | collective-permute-start | bytes 2359304 | tf_op jit(solution)/shard_map/ppermute | solution.py:1039
  267.6 50.0 %collective-permute-start.7 = (bf16[2,2,16,48,128]{4,3,2,1,0:T(8,128)(2,1)}, bf16[2,2,16,48,128]{4,3,2,1,0:T(8,128)(2,1)}, u32[]{:S(2)}, u32[]{:S(2)}) collective-permute-start(bf16[2,2,16,48,128]{4,3,2,1,0:T(8,128)(2,1)} %bitcast.37.refs_10_), channel_id=1, source_target_pairs={{0,1},{1,0},{2,3},{3,2},{4,5},{5,4},{6,7},{7,6},{8,9},{9,8},{10,11... | collective-permute-start | bytes 2359304 | tf_op jit(solution)/shard_map/ppermute | solution.py:1039
  302.2 11.3 %all-to-all-start.3 = ((f32[32,1,592]{2,1,0:T(1,128)}), f32[32,1,592]{2,1,0:T(1,128)}, u32[]{:S(2)}, u32[]{:S(2)}) async-start(f32[32,1,592]{2,1,0:T(1,128)} %copy.153), calls=%async_computation.3 | async-start | bytes 163840 | tf_op jit(solution)/shard_map/all_to_all | solution.py:1117
  307.0 23.1 %collective-permute-start.6 = (bf16[2,2,18,48,128]{4,3,2,1,0:T(8,128)(2,1)}, bf16[2,2,18,48,128]{4,3,2,1,0:T(8,128)(2,1)}, u32[]{:S(2)}, u32[]{:S(2)}) collective-permute-start(bf16[2,2,18,48,128]{4,3,2,1,0:T(8,128)(2,1)} %bitcast.285), channel_id=1, source_target_pairs={{0,8},{2,10},{4,12},{6,14},{8,0},{10,2},{12,4},{14,6},{16,24},{18,... | collective-permute-start | bytes 2654216 | tf_op jit(solution)/shard_map/ppermute | solution.py:1039
  317.6 36.0 %collective-permute-start.12 = (bf16[2,16,48,128]{3,2,1,0:T(8,128)(2,1)}, bf16[2,16,48,128]{3,2,1,0:T(8,128)(2,1)}, u32[]{:S(2)}, u32[]{:S(2)}) collective-permute-start(bf16[2,16,48,128]{3,2,1,0:T(8,128)(2,1)} %bitcast.56.refs_7_), channel_id=1, source_target_pairs={{0,8},{2,10},{4,12},{6,14},{8,0},{10,2},{12,4},{14,6},{16,24},{18,... | collective-permute-start | bytes 1179656 | tf_op jit(solution)/shard_map/ppermute | solution.py:1039
  319.9 34.2 %collective-permute-start.11 = (bf16[2,16,48,128]{3,2,1,0:T(8,128)(2,1)}, bf16[2,16,48,128]{3,2,1,0:T(8,128)(2,1)}, u32[]{:S(2)}, u32[]{:S(2)}) collective-permute-start(bf16[2,16,48,128]{3,2,1,0:T(8,128)(2,1)} %bitcast.51.refs_6_), channel_id=1, source_target_pairs={{0,4},{2,6},{4,0},{6,2},{8,12},{10,14},{12,8},{14,10},{16,20},{18,... | collective-permute-start | bytes 1179656 | tf_op jit(solution)/shard_map/ppermute | solution.py:1039
  323.3 41.6 %collective-permute-start.13 = (bf16[2,2,2,11,48,128]{5,4,3,2,1,0:T(8,128)(2,1)}, bf16[2,2,2,11,48,128]{5,4,3,2,1,0:T(8,128)(2,1)}, u32[]{:S(2)}, u32[]{:S(2)}) collective-permute-start(bf16[2,2,2,11,48,128]{5,4,3,2,1,0:T(8,128)(2,1)} %bitcast.59.refs_8_), channel_id=1, source_target_pairs={{0,4},{2,6},{4,0},{6,2},{8,12},{10,14},{12,8},{14,10},{16,20},{18,... | collective-permute-start | bytes 3244040 | tf_op jit(solution)/shard_map/ppermute | solution.py:1039
  332.3 29.3 %collective-permute-start.10 = (bf16[2,18,48,128]{3,2,1,0:T(8,128)(2,1)}, bf16[2,18,48,128]{3,2,1,0:T(8,128)(2,1)S(1)}, u32[]{:S(2)}, u32[]{:S(2)}) collective-permute-start(bf16[2,18,48,128]{3,2,1,0:T(8,128)(2,1)} %bitcast.46.refs_5_), channel_id=1, source_target_pairs={{0,1},{1,0},{2,3},{3,2},{4,5},{5,4},{6,7},{7,6},{8,9},{9,8},{10,11... | collective-permute-start | bytes 1327112 | tf_op jit(solution)/shard_map/ppermute | solution.py:1039
  347.3 56.3 %collective-permute-start.19 = (bf16[2,2,2,2,6,48,128]{6,5,4,3,2,1,0:T(8,128)(2,1)}, bf16[2,2,2,2,6,48,128]{6,5,4,3,2,1,0:T(8,128)(2,1)}, u32[]{:S(2)}, u32[]{:S(2)}) collective-permute-start(bf16[2,2,2,2,6,48,128]{6,5,4,3,2,1,0:T(8,128)(2,1)} %get-tuple-element.159.refs_5_), channel_id=1, source_target_pairs={{0,2},{2,0},{4,6},{6,4},{8,10},{10,8},{12,14},{14,12},{16,18},{18,... | collective-permute-start | bytes 3538952 | tf_op jit(solution)/shard_map/ppermute | solution.py:1039
  353.6 51.4 %collective-permute-start.14 = (bf16[2,2,2,2,6,48,128]{6,5,4,3,2,1,0:T(8,128)(2,1)}, bf16[2,2,2,2,6,48,128]{6,5,4,3,2,1,0:T(8,128)(2,1)}, u32[]{:S(2)}, u32[]{:S(2)}) collective-permute-start(bf16[2,2,2,2,6,48,128]{6,5,4,3,2,1,0:T(8,128)(2,1)} %get-tuple-element.158.refs_5_), channel_id=1, source_target_pairs={{0,2},{2,0},{4,6},{6,4},{8,10},{10,8},{12,14},{14,12},{16,18},{18,... | collective-permute-start | bytes 3538952 | tf_op jit(solution)/shard_map/ppermute | solution.py:1039
  356.8 23.5 %collective-permute-start.33 = (bf16[16,48,128]{2,1,0:T(8,128)(2,1)}, bf16[16,48,128]{2,1,0:T(8,128)(2,1)}, u32[]{:S(2)}, u32[]{:S(2)}) collective-permute-start(bf16[16,48,128]{2,1,0:T(8,128)(2,1)} %bitcast.71.refs_5_), channel_id=1, source_target_pairs={{0,16},{2,18},{4,20},{6,22},{8,24},{10,26},{12,28},{14,30},{16,0},... | collective-permute-start | bytes 589832 | tf_op jit(solution)/shard_map/ppermute | solution.py:1039
  361.7 15.8 %collective-permute-start.34 = (bf16[16,48,128]{2,1,0:T(8,128)(2,1)}, bf16[16,48,128]{2,1,0:T(8,128)(2,1)}, u32[]{:S(2)}, u32[]{:S(2)}) collective-permute-start(bf16[16,48,128]{2,1,0:T(8,128)(2,1)} %bitcast.77.refs_6_), channel_id=1, source_target_pairs={{0,16},{2,18},{4,20},{6,22},{8,24},{10,26},{12,28},{14,30},{16,0},... | collective-permute-start | bytes 589832 | tf_op jit(solution)/shard_map/ppermute | solution.py:1039
  364.9 35.8 %collective-permute-start.24 = (bf16[2,2,2,2,6,48,128]{6,5,4,3,2,1,0:T(8,128)(2,1)}, bf16[2,2,2,2,6,48,128]{6,5,4,3,2,1,0:T(8,128)(2,1)}, u32[]{:S(2)}, u32[]{:S(2)}) collective-permute-start(bf16[2,2,2,2,6,48,128]{6,5,4,3,2,1,0:T(8,128)(2,1)} %get-tuple-element.160.refs_3_), channel_id=1, source_target_pairs={{0,2},{2,0},{4,6},{6,4},{8,10},{10,8},{12,14},{14,12},{16,18},{18,... | collective-permute-start | bytes 3538952 | tf_op jit(solution)/shard_map/ppermute | solution.py:1039
  377.4 13.0 %collective-permute-start.32 = (bf16[18,48,128]{2,1,0:T(8,128)(2,1)S(1)}, bf16[18,48,128]{2,1,0:T(8,128)(2,1)S(1)}, u32[]{:S(2)}, u32[]{:S(2)}) collective-permute-start(bf16[18,48,128]{2,1,0:T(8,128)(2,1)S(1)} %bitcast.320), channel_id=1, source_target_pairs={{0,16},{2,18},{4,20},{6,22},{8,24},{10,26},{12,28},{14,30},{16,0},... | collective-permute-start | bytes 663560 | tf_op jit(solution)/shard_map/ppermute | solution.py:1039
  380.3 18.7 %collective-permute-start.29 = (bf16[2,2,11,48,128]{4,3,2,1,0:T(8,128)(2,1)}, bf16[2,2,11,48,128]{4,3,2,1,0:T(8,128)(2,1)}, u32[]{:S(2)}, u32[]{:S(2)}) collective-permute-start(bf16[2,2,11,48,128]{4,3,2,1,0:T(8,128)(2,1)} %bitcast.81.refs_7_), channel_id=1, source_target_pairs={{0,8},{2,10},{4,12},{6,14},{8,0},{10,2},{12,4},{14,6},{16,24},{18,... | collective-permute-start | bytes 1622024 | tf_op jit(solution)/shard_map/ppermute | solution.py:1039
  400.3 9.5 %collective-permute-start.30 = (bf16[2,11,48,128]{3,2,1,0:T(8,128)(2,1)S(1)}, bf16[2,11,48,128]{3,2,1,0:T(8,128)(2,1)S(1)}, u32[]{:S(2)}, u32[]{:S(2)}) collective-permute-start(bf16[2,11,48,128]{3,2,1,0:T(8,128)(2,1)S(1)} %bitcast.315), channel_id=1, source_target_pairs={{0,1},{1,0},{2,3},{3,2},{4,5},{5,4},{6,7},{7,6},{8,9},{9,8},{10,11... | collective-permute-start | bytes 811016 | tf_op jit(solution)/shard_map/ppermute | solution.py:1039
  401.9 18.8 %collective-permute-start.25 = (bf16[2,2,2,6,48,128]{5,4,3,2,1,0:T(8,128)(2,1)S(1)}, bf16[2,2,2,6,48,128]{5,4,3,2,1,0:T(8,128)(2,1)S(1)}, u32[]{:S(2)}, u32[]{:S(2)}) collective-permute-start(bf16[2,2,2,6,48,128]{5,4,3,2,1,0:T(8,128)(2,1)S(1)} %bitcast.303), channel_id=1, source_target_pairs={{0,1},{1,0},{2,3},{3,2},{4,5},{5,4},{6,7},{7,6},{8,9},{9,8},{10,11... | collective-permute-start | bytes 1769480 | tf_op jit(solution)/shard_map/ppermute | solution.py:1039
  404.9 19.3 %collective-permute-start.20 = (bf16[2,2,2,6,48,128]{5,4,3,2,1,0:T(8,128)(2,1)S(1)}, bf16[2,2,2,6,48,128]{5,4,3,2,1,0:T(8,128)(2,1)S(1)}, u32[]{:S(2)}, u32[]{:S(2)}) collective-permute-start(bf16[2,2,2,6,48,128]{5,4,3,2,1,0:T(8,128)(2,1)S(1)} %bitcast.304), channel_id=1, source_target_pairs={{0,8},{2,10},{4,12},{6,14},{8,0},{10,2},{12,4},{14,6},{16,24},{18,... | collective-permute-start | bytes 1769480 | tf_op jit(solution)/shard_map/ppermute | solution.py:1039
  406.2 20.5 %collective-permute-start.15 = (bf16[2,2,2,6,48,128]{5,4,3,2,1,0:T(8,128)(2,1)S(1)}, bf16[2,2,2,6,48,128]{5,4,3,2,1,0:T(8,128)(2,1)S(1)}, u32[]{:S(2)}, u32[]{:S(2)}) collective-permute-start(bf16[2,2,2,6,48,128]{5,4,3,2,1,0:T(8,128)(2,1)S(1)} %bitcast.305), channel_id=1, source_target_pairs={{0,4},{2,6},{4,0},{6,2},{8,12},{10,14},{12,8},{14,10},{16,20},{18,... | collective-permute-start | bytes 1769480 | tf_op jit(solution)/shard_map/ppermute | solution.py:1039
  411.2 17.6 %collective-permute-start.31 = (bf16[11,48,128]{2,1,0:T(8,128)(2,1)S(1)}, bf16[11,48,128]{2,1,0:T(8,128)(2,1)S(1)}, u32[]{:S(2)}, u32[]{:S(2)}) collective-permute-start(bf16[11,48,128]{2,1,0:T(8,128)(2,1)S(1)} %bitcast.327), channel_id=1, source_target_pairs={{0,16},{2,18},{4,20},{6,22},{8,24},{10,26},{12,28},{14,30},{16,0},... | collective-permute-start | bytes 405512 | tf_op jit(solution)/shard_map/ppermute | solution.py:1039
  428.7 8.7 %collective-permute-start.16 = (bf16[2,2,6,48,128]{4,3,2,1,0:T(8,128)(2,1)}, bf16[2,2,6,48,128]{4,3,2,1,0:T(8,128)(2,1)}, u32[]{:S(2)}, u32[]{:S(2)}) collective-permute-start(bf16[2,2,6,48,128]{4,3,2,1,0:T(8,128)(2,1)} %bitcast.92), channel_id=1, source_target_pairs={{0,8},{2,10},{4,12},{6,14},{8,0},{10,2},{12,4},{14,6},{16,24},{18,... | collective-permute-start | bytes 884744 | tf_op jit(solution)/shard_map/ppermute | solution.py:1039
  431.5 8.4 %collective-permute-start.27 = (bf16[2,6,48,128]{3,2,1,0:T(8,128)(2,1)S(1)}, bf16[2,6,48,128]{3,2,1,0:T(8,128)(2,1)S(1)}, u32[]{:S(2)}, u32[]{:S(2)}) collective-permute-start(bf16[2,6,48,128]{3,2,1,0:T(8,128)(2,1)S(1)} %bitcast.323), channel_id=1, source_target_pairs={{0,8},{2,10},{4,12},{6,14},{8,0},{10,2},{12,4},{14,6},{16,24},{18,... | collective-permute-start | bytes 442376 | tf_op jit(solution)/shard_map/ppermute | solution.py:1039
  (31 other events, 250.7 us)

commit v6 on v5

--- a/solution.py
+++ b/solution.py
@@ -72,6 +72,14 @@
 
 def cost(micros):
     return pl.CostEstimate(flops=int(micros * 1.1e9), bytes_accessed=0, transcendentals=0)
+
+
+def put_row(ref, place, row, add=False):
+    units = row.shape[1] // 128
+    for unit in range(units):
+        at = slice(place * units + unit, place * units + unit + 1)
+        piece = row[:, unit * 128 : (unit + 1) * 128]
+        ref[at] = ref[at] + piece if add else piece
 
 
 def store_units(ref, values):
@@ -284,10 +292,10 @@
         return carry
 
     lax.fori_loop(0, count // (SELF_BACK_ROWS * SLOTS), some_rows, 0)
-    side_ref[0:1] += dgain
-    side_ref[1:2] += dshift
+    put_row(side_ref, 0, dgain, True)
+    put_row(side_ref, 1, dshift, True)
     for place, rows in enumerate((grad_ref[0], grad_ref[2], branch)):
-        side_ref[2 + place : 3 + place] += jnp.sum(rows.astype(f32), 0, keepdims=True)
+        put_row(side_ref, 2 + place, jnp.sum(rows.astype(f32), 0, keepdims=True), True)
 
 
 def self_backward(weights, gains, mask, q, k, v, total, top, text, order):
@@ -314,13 +322,13 @@
             pl.BlockSpec((3, count, width), lambda i: (0, i, 0)),
             tile,
             tile,
-            whole((8, width)),
+            whole((width // 16, 128)),
         ],
         out_shape=[
             jax.ShapeDtypeStruct((3, tokens, width), bf16),
             jax.ShapeDtypeStruct((tokens, width), bf16),
             jax.ShapeDtypeStruct((tokens, width), f32),
-            jax.ShapeDtypeStruct((8, width), f32),
+            jax.ShapeDtypeStruct((width // 16, 128), f32),
         ],
         scratch_shapes=[pltpu.VMEM((count, width), bf16)],
         compiler_params=params(58),
@@ -381,50 +389,57 @@
 core_spec = pl.BlockSpec(memory_space=pltpu.SMEM)
 
 
-def attn_weight_kernel(fold, core_ref, left_ref, right_ref, left_two_ref, right_two_ref, *outs):
-    out_ref = outs[0]
-    pieces = []
-    for rep, (left, right) in enumerate(((left_ref, right_ref), (left_two_ref, right_two_ref))):
-        width = right.shape[-1]
-        lhs = left[...].reshape(-1, width).astype(bf16)
-        rhs = right[...].reshape(-1, width).astype(bf16)
-        grad = dot_tn(lhs, rhs).astype(bf16)
-        if fold is None:
-            store_units(out_ref.at[rep], grad)
-            continue
-        rows = out_ref.shape[-2]
-        for block in range(width // rows):
-            spot = place_of(fold, block, rep)
-            for unit in range(width // 128):
-                piece = grad[block * rows : (block + 1) * rows, unit * 128 : (unit + 1) * 128]
-                pieces.append((spot + (unit,), piece))
-    if fold is not None:
-        store_halves(core_ref, *outs, pieces)
-
-
-def attn_weight_grad(part, core, left, grads, left_two, left_two_spec, right_two, fold, rows, order):
+def attn_weight_kernel(folds, core_ref, left_ref, right_ref, *rest):
+    step = pl.program_id(0)
+    outs = rest[6:]
+    width = right_ref.shape[-1]
+    for part in range(3):
+
+        @pl.when(step == part)
+        def _():
+            pieces = []
+            pairs = ((left_ref, right_ref), rest[2 * part : 2 * part + 2])
+            for rep, (left, right) in enumerate(pairs):
+                lhs = left[...].reshape(-1, width).astype(bf16)
+                rhs = right[...].reshape(-1, width).astype(bf16)
+                grad = dot_tn(lhs, rhs).astype(bf16)
+                if folds is None:
+                    store_units(outs[part].at[rep], grad)
+                    continue
+                rows = outs[0].shape[-2]
+                for block in range(width // rows):
+                    spot = place_of(folds[part], block, rep)
+                    for unit in range(width // 128):
+                        piece = grad[
+                            block * rows : (block + 1) * rows, unit * 128 : (unit + 1) * 128
+                        ]
+                        pieces.append((spot + (unit,), piece))
+            if folds is not None:
+                store_halves(core_ref, *outs[2 * part : 2 * part + 2], pieces)
+
+
+def attn_weight_grad(core, left, grads, others, folds, rows, order):
     tokens, width = left.shape
-    if fold is None:
-        shape = (2, width // 128, width, 128)
+    if folds is None:
+        shapes = [(2, width // 128, width, 128)] * 3
     else:
-        shape = slab_shape(fold, width // 128, rows)
+        shapes = [slab_shape(fold, width // 128, rows) for fold in folds for half in range(2)]
     return pl.pallas_call(
-        ordered(functools.partial(attn_weight_kernel, fold), 5, len(order)),
-        grid=(1,),
+        ordered(functools.partial(attn_weight_kernel, folds), 9, len(order)),
+        grid=(3,),
         in_specs=[
             core_spec,
-            whole(left.shape),
-            pl.BlockSpec((1, tokens, width), lambda i: (part, 0, 0)),
-            left_two_spec,
-            whole(right_two.shape),
-        ]
+            held(left.shape, lambda i: (0, 0)),
+            pl.BlockSpec((1, tokens, width), lambda i: (i, 0, 0)),
+        ]
+        + [held(block, lambda i, zeros=(0,) * len(block): zeros) for _, block in others]
         + unread(len(order)),
-        out_specs=[whole(shape)] * (1 if fold is None else 2),
-        out_shape=[jax.ShapeDtypeStruct(shape, bf16)] * (1 if fold is None else 2),
+        out_specs=[held(shape, lambda i, zeros=(0,) * len(shape): zeros) for shape in shapes],
+        out_shape=[jax.ShapeDtypeStruct(shape, bf16) for shape in shapes],
         compiler_params=params(58),
         name="attn_weight_grad",
-        cost_estimate=cost(7),
-    )(core, left, grads, left_two, right_two, *order)
+        cost_estimate=cost(20),
+    )(core, left, grads, *(array for array, _ in others), *order)
 
 
 TAIL = 16
@@ -611,11 +626,11 @@
     lax.fori_loop(0, rows_here // CROSS_BACK_ROWS, some_rows, 0)
     dq = dq_ref[...]
     dnorm_ref[...] = (down + dot_nt(dq, w_ref[0])).reshape(rows_here, QUERIES, width)
-    side_ref[0:1] += jnp.sum(dq.astype(f32), 0, keepdims=True)
-    side_ref[1:2] += jnp.sum(dkv_ref[1].astype(f32), 0, keepdims=True) + jnp.sum(
-        dkv_end_ref[1].astype(f32), 0, keepdims=True
-    )
-    side_ref[2:3] += jnp.sum(branch.astype(f32), 0, keepdims=True)
+    put_row(side_ref, 0, jnp.sum(dq.astype(f32), 0, keepdims=True), True)
+    dvalue = jnp.sum(dkv_ref[1].astype(f32), 0, keepdims=True)
+    dvalue += jnp.sum(dkv_end_ref[1].astype(f32), 0, keepdims=True)
+    put_row(side_ref, 1, dvalue, True)
+    put_row(side_ref, 2, jnp.sum(branch.astype(f32), 0, keepdims=True), True)
 
 
 def cross_backward(rows, weights, keys, values, key_ends, value_ends, q, down, order):
@@ -643,14 +658,14 @@
             pl.BlockSpec((2, take * main, width), lambda i: (0, i, 0)),
             pl.BlockSpec((2, take * TAIL, width), lambda i: (0, i, 0)),
             tile,
-            whole((8, width)),
+            whole((width // 16, 128)),
         ],
         out_shape=[
             jax.ShapeDtypeStruct((rows, QUERIES, width), f32),
             jax.ShapeDtypeStruct((2, rows * main, width), bf16),
             jax.ShapeDtypeStruct((2, rows * TAIL, width), bf16),
             jax.ShapeDtypeStruct((rows * QUERIES, width), bf16),
-            jax.ShapeDtypeStruct((8, width), f32),
+            jax.ShapeDtypeStruct((width // 16, 128), f32),
         ],
         scratch_shapes=[pltpu.VMEM((take * QUERIES, width), bf16)],
         compiler_params=params(58),
@@ -659,7 +674,12 @@
     )(weights, keys, values, key_ends, value_ends, q, down, *order)
 
 
-def cross_weight_kernel(fold, core_ref, image_ref, end_ref, grad_ref, grad_end_ref, *rest):
+def third_units(units):
+    edges = [(units * k + 2) // 3 for k in range(4)]
+    return [edges[k + 1] - edges[k] for k in range(3)]
+
+
+def cross_weight_kernel(folds, core_ref, image_ref, end_ref, grad_ref, grad_end_ref, *rest):
     outs, gathered = rest[:-1], rest[-1]
     rows, patches, vis = image_ref.shape
     main = patches - 1
@@ -673,38 +693,49 @@
         return carry
 
     lax.fori_loop(0, rows // take, add_rows, 0)
-    if fold is None:
+    if folds is None:
         store_units(outs[0].at[0], gathered[...])
         return
-    units, size = outs[0].shape[-3:-1]
-    pieces = []
-    for block in range(gathered.shape[0] // size):
-        spot = tuple(0 if axis == "rep" or bit == 3 else (block >> bit) & 1 for axis, bit in fold)
-        piece = gathered[block * size : (block + 1) * size].astype(bf16)
-        for unit in range(units):
-            pieces.append((spot + (unit,), piece[:, unit * 128 : (unit + 1) * 128]))
-    store_halves(core_ref, *outs, pieces)
-
-
-def cross_weight_grad(core, images, ends, grads, grads_end, fold, size, order):
+    first = 0
+    for part, fold in enumerate(folds):
+        keep, send = outs[2 * part : 2 * part + 2]
+        units, size = keep.shape[-3:-1]
+        pieces = []
+        for block in range(gathered.shape[0] // size):
+            spot = tuple(
+                0 if axis == "rep" or bit == 3 else (block >> bit) & 1 for axis, bit in fold
+            )
+            piece = gathered[block * size : (block + 1) * size].astype(bf16)
+            for unit in range(units):
+                at = (first + unit) * 128
+                pieces.append((spot + (unit,), piece[:, at : at + 128]))
+        store_halves(core_ref, keep, send, pieces)
+        first += units
+
+
+def cross_weight_grad(core, images, ends, grads, grads_end, folds, size, order):
     rows, patches, vis = images.shape
     width = grads.shape[2]
     half = width // 2
     units = vis // 128
-    if fold is None:
+    if folds is None:
         specs = [pl.BlockSpec((1, units, half, 128), lambda m, h: (m, 0, h, 0))]
         shapes = [(2, units, width, 128)]
     else:
-        shapes = [slab_shape(fold, units, size)] * 2
-        block = tuple(1 if axis == "rep" or bit == 3 else 2 for axis, bit in fold[1:])
-
-        def index(m, h):
-            spot = tuple(m if axis == "rep" else h if bit == 3 else 0 for axis, bit in fold[1:])
-            return spot + (0, 0, 0)
-
-        specs = [pl.BlockSpec(block + (units, size, 128), index)] * 2
+        specs, shapes = [], []
+        for fold, count in zip(folds, third_units(units) if len(folds) == 3 else [units]):
+            block = tuple(1 if axis == "rep" or bit == 3 else 2 for axis, bit in fold[1:])
+
+            def index(m, h, fold=fold):
+                spot = tuple(
+                    m if axis == "rep" else h if bit == 3 else 0 for axis, bit in fold[1:]
+                )
+                return spot + (0, 0, 0)
+
+            specs += [pl.BlockSpec(block + (count, size, 128), index)] * 2
+            shapes += [slab_shape(fold, count, size)] * 2
     return pl.pallas_call(
-        ordered(functools.partial(cross_weight_kernel, fold), 5, len(order)),
+        ordered(functools.partial(cross_weight_kernel, folds), 5, len(order)),
         grid=(2, 2),
         in_specs=[
             core_spec,
@@ -859,19 +890,17 @@
         branch_all[...] = branch
         left[...] = down
         side_ref[...] = jnp.zeros_like(side_ref)
-        side_ref[0:1] = dgain
-        side_ref[1:2] = dshift
-        side_ref[2:3] = jnp.sum(branch.astype(f32), 0, keepdims=True)
+        put_row(side_ref, 0, dgain)
+        put_row(side_ref, 1, dshift)
+        put_row(side_ref, 2, jnp.sum(branch.astype(f32), 0, keepdims=True))
         dproj[...] = dot_tn(layer_ref[...].reshape(tokens, width), raw).astype(bf16)
-        dproj_bias_ref[...] = jnp.broadcast_to(
-            jnp.sum(raw.astype(f32), 0, keepdims=True), dproj_bias_ref.shape
-        )
+        put_row(dproj_bias_ref, 0, jnp.sum(raw.astype(f32), 0, keepdims=True))
         low_turned[...] = norm_ref[...].reshape(tokens, width).astype(bf16).T
 
     branch = branch_all[...]
     du = (dot_nt(branch, out_ref[0]) * slope_ref[...].astype(f32)).astype(bf16)
     left[...] += dot_nt(du, in_ref[0])
-    dbias_ref[...] = jnp.broadcast_to(jnp.sum(du.astype(f32), 0, keepdims=True), dbias_ref.shape)
+    put_row(dbias_ref, 0, jnp.sum(du.astype(f32), 0, keepdims=True))
     thin = width // 3
     for part in range(3):
 
@@ -910,8 +939,8 @@
     def _():
         if which == 0:
             down, dgain, dshift = norm_grads(before_ref[...], gain_ref[1:2], left[...])
-            side_ref[3:4] = dgain
-            side_ref[4:5] = dshift
+            put_row(side_ref, 3, dgain)
+            put_row(side_ref, 4, dshift)
             down_ref[...] = down.reshape(down_ref.shape)
         else:
             down_ref[...] = left[...].reshape(down_ref.shape)
@@ -989,16 +1018,16 @@
         + [pl.BlockSpec(memory_space=pl.ANY)] * len(slabs),
         out_specs=[
             whole((rows, QUERIES, width)),
-            whole((8, width)),
-            pl.BlockSpec((8, chunk), lambda j: (0, j)),
-            whole((8, embed)),
+            whole((width // 16, 128)),
+            pl.BlockSpec((chunk // 128, 128), lambda j: (j, 0)),
+            whole((embed // 128, 128)),
         ]
         + weight_specs,
         out_shape=[
             jax.ShapeDtypeStruct((rows, QUERIES, width), f32),
-            jax.ShapeDtypeStruct((8, width), f32),
-            jax.ShapeDtypeStruct((8, hidden), f32),
-            jax.ShapeDtypeStruct((8, embed), f32),
+            jax.ShapeDtypeStruct((width // 16, 128), f32),
+            jax.ShapeDtypeStruct((hidden // 128, 128), f32),
+            jax.ShapeDtypeStruct((embed // 128, 128), f32),
         ]
         + [jax.ShapeDtypeStruct(shape, bf16) for shape in weight_shapes],
         scratch_shapes=[
@@ -1029,32 +1058,16 @@
     )
 
 
-def own_bit(stage):
-    axis, bit = stage
-    return (lax.axis_index(axis) >> bit) & 1
-
-
 def swap(values, stage, sizes):
     axis, bit = stage
     return lax.ppermute(values, axis, [(i, i ^ (1 << bit)) for i in range(sizes[axis])])
 
 
-def total(terms, ahead=()):
-    parts = []
-    for array, places in terms:
-        places = list(places) + list(ahead)
-        rest = array.shape[len(places) :]
-        if places:
-            at = sum(place << shift for shift, place in enumerate(reversed(places)))
-            flat = array.reshape((1 << len(places), -1, 128))
-            array = lax.dynamic_index_in_dim(flat, at, 0, keepdims=False).reshape(rest)
-        parts.append(array.astype(f32))
-    return sum(parts)
-
-
 def stage_order(part, sizes):
     stages = [("dp", bit) for bit in range(sizes["dp"].bit_length() - 1)]
     ring = stages[1:3] + [("rep", 0)]
+    if part == 3:
+        return stages[:1] + ring[:2] + stages[3:] + ring[2:]
     return stages[:1] + ring[part:] + ring[:part] + stages[3:]
 
 
@@ -1067,46 +1080,186 @@
     return both.transpose(front + [1, 2 + depth, 3 + depth])
 
 
+def own_bits(sizes):
+    depth = sizes["dp"].bit_length() - 1
+    shifts = jnp.arange(depth + 1, dtype=jnp.int32)
+    both = lax.axis_index("dp") + (lax.axis_index("rep") << depth)
+    return ((both >> shifts) & 1).astype(jnp.int32)
+
+
+def bit_place(stage, sizes):
+    return sizes["dp"].bit_length() - 1 if stage[0] == "rep" else stage[1]
+
+
+def picked(place_bits, bits_ref):
+    at = 0
+    for bit, other in place_bits:
+        own = bits_ref[bit]
+        at = 2 * at + (1 - own if other else own)
+    return at
+
+
+def sum_kernel(plan, arrays, bits_ref, *refs):
+    sources, refs = refs[:arrays], refs[arrays:]
+    outs, refs = refs[: len(plan)], refs[len(plan) :]
+    count = sum(len(terms) for jobs in plan for _, terms in jobs)
+    held_terms, held_outs = refs[:count], refs[count : count + len(plan)]
+    in_sems, out_sems = refs[-2:]
+    fetches = []
+    for jobs in plan:
+        for rows, terms in jobs:
+            for source, start, place_bits in terms:
+                first = start + picked(place_bits, bits_ref) * rows
+                here = len(fetches)
+                fetches.append(
+                    pltpu.make_async_copy(
+                        sources[source].at[pl.ds(pl.multiple_of(first, 16), rows)],
+                        held_terms[here],
+                        in_sems.at[here],
+                    )
+                )
+    for fetch in fetches:
+        fetch.start()
+    here = 0
+    stores = []
+    for place, jobs in enumerate(plan):
+        at = 0
+        for rows, terms in jobs:
+            found = None
+            for _ in terms:
+                fetches[here].wait()
+                part = held_terms[here][...].astype(f32)
+                found = part if found is None else found + part
+                here += 1
+            held_outs[place][at : at + rows] = found.astype(held_outs[place].dtype)
+            at += rows
+        store = pltpu.make_async_copy(held_outs[place], outs[place], out_sems.at[place])
+        store.start()
+        stores.append(store)
+    for store in stores:
+        store.wait()
+
+
+def sum_jobs(outputs, bits):
+    arrays, plan, buffers = [], [], []
+
+    def number_of(array):
+        for number, known in enumerate(arrays):
+            if known is array:
+                return number
+        arrays.append(array)
+        return len(arrays) - 1
+
+    shapes, moved = [], 0
+    for dtype, jobs in outputs:
+        planned = []
+        for rows, terms in jobs:
+            planned.append((rows, [(number_of(array), start, bit) for array, start, bit in terms]))
+            buffers += [pltpu.VMEM((rows, 128), array.dtype) for array, _, _ in terms]
+            moved += rows * (1 + len(terms))
+        plan.append(planned)
+        shapes.append(jax.ShapeDtypeStruct((sum(rows for rows, _ in jobs), 128), dtype))
+    return pl.pallas_call(
+        functools.partial(sum_kernel, plan, len(arrays)),
+        in_specs=[core_spec] + unread(len(arrays)),
+        out_specs=unread(len(plan)),
+        out_shape=shapes,
+        scratch_shapes=buffers
+        + [pltpu.VMEM(shape.shape, shape.dtype) for shape in shapes]
+        + [pltpu.SemaphoreType.DMA((len(buffers),)), pltpu.SemaphoreType.DMA((len(plan),))],
+        compiler_params=pltpu.CompilerParams(vmem_limit_bytes=60 * MIB),
+        name="sum_terms",
+        cost_estimate=cost(3),
+    )(bits, *arrays)
+
+
+def sum_jobs_plain(outputs, bits):
+    results = []
+    for dtype, jobs in outputs:
+        pieces = []
+        for rows, terms in jobs:
+            found = [
+                lax.dynamic_slice_in_dim(array, start + picked(bit, bits) * rows, rows, 0)
+                for array, start, bit in terms
+            ]
+            pieces.append(sum(part.astype(f32) for part in found).astype(dtype))
+        results.append(pieces[0] if len(pieces) == 1 else jnp.concatenate(pieces, 0))
+    return results
+
+
 def begin(part, keep, send, sizes):
-    return (1, [(keep, []), (swap(send, stage_order(part, sizes)[0], sizes), [])], send)
+    keep, send = keep.reshape(-1, 128), send.reshape(-1, 128)
+    arrived = swap(send, stage_order(part, sizes)[0], sizes)
+    return (part, 1, [(keep, 0, keep.shape[0], []), (arrived, 0, send.shape[0], [])], send)
 
 
 def begin_folded(part, slab, sizes):
-    mine = own_bit(stage_order(part, sizes)[0])
-    halves = [lax.dynamic_index_in_dim(slab, place, 0, keepdims=False) for place in (mine, 1 - mine)]
+    own = lax.axis_index("dp") & 1
+    halves = [lax.dynamic_index_in_dim(slab, place, 0, keepdims=False) for place in (own, 1 - own)]
     return begin(part, *halves, sizes)
 
 
-def advance(part, state, sizes, after=None):
-    stage, terms = state[0], state[1]
-    if after is not None:
-        array, places = terms[-1]
-        terms = terms[:-1] + [(lax.optimization_barrier((array, after))[0], places)]
-    axis_bit = stage_order(part, sizes)[stage]
-    mine = own_bit(axis_bit)
-    sent = total(terms, [1 - mine]).astype(bf16)
-    arrived = swap(sent, axis_bit, sizes)
-    terms = [(array, places + [mine]) for array, places in terms] + [(arrived, [])]
-    return (stage + 1, terms, sent)
-
-
-def advance_all(states, sizes, after=None):
-    return [advance(part, state, sizes, after) for part, state in enumerate(states)]
-
-
-def finish(part, state, sizes, after=None):
-    while state[0] < len(stage_order(part, sizes)):
-        state = advance(part, state, sizes, after)
-        after = None
-    terms = state[1]
-    if after is not None:
-        array, places = terms[-1]
-        terms = terms[:-1] + [(lax.optimization_barrier((array, after))[0], places)]
-    return total(terms)
+def begin_whole(values, sizes):
+    send = values.astype(bf16)
+    arrived = swap(send, stage_order(0, sizes)[0], sizes)
+    return (None, 1, [(values, 0, len(values), []), (arrived, 0, len(values), [])], send)
+
+
+def advance(states, bits, sizes, plain, after=None):
+    last = len(stage_order(0, sizes))
+    changed = {}
+    fresh = []
+    for part, at, terms, sent in states:
+        array = terms[-1][0]
+        if after is not None:
+            if id(array) not in changed:
+                changed[id(array)] = (array, lax.optimization_barrier((array, after))[0])
+            array = changed[id(array)][1]
+        fresh.append((part, at, terms[:-1] + [(array,) + terms[-1][1:]], sent))
+    groups, finals = {}, []
+    for number, (part, at, terms, _) in enumerate(fresh):
+        if at == last:
+            finals.append(number)
+        else:
+            groups.setdefault(stage_order(part or 0, sizes)[at], []).append(number)
+
+    def job(number, ahead):
+        rows = fresh[number][2][0][2] >> (len(fresh[number][2][0][3]) + len(ahead))
+        return (
+            rows,
+            [(array, start, places + ahead) for array, start, _, places in fresh[number][2]],
+        )
+
+    outputs = []
+    for stage, members in groups.items():
+        jobs = []
+        for number in members:
+            ahead = [] if fresh[number][0] is None else [(bit_place(stage, sizes), True)]
+            jobs.append(job(number, ahead))
+        outputs.append((bf16, jobs))
+    outputs += [(f32, [job(number, [])]) for number in finals]
+    made = (sum_jobs_plain if plain else sum_jobs)(outputs, bits)
+    results = [None] * len(fresh)
+    for (stage, members), (_, jobs), sent in zip(groups.items(), outputs, made):
+        arrived = swap(sent, stage, sizes)
+        start = 0
+        for number, (rows, _) in zip(members, jobs):
+            part, at, terms, _ = fresh[number]
+            kept = [] if part is None else [(bit_place(stage, sizes), False)]
+            terms = [(array, first, size, places + kept) for array, first, size, places in terms]
+            results[number] = (part, at + 1, terms + [(arrived, start, rows, [])], sent)
+            start += rows
+    for number, found in zip(finals, made[len(groups) :]):
+        results[number] = found
+    return results
 
 
 def sends(states):
-    return [state[2] for state in states]
+    found = []
+    for state in states:
+        if not any(state[3] is known for known in found):
+            found.append(state[3])
+    return found
 
 
 def columns_of(units):
@@ -1251,8 +1404,11 @@
     fold = sizes["dp"] == 16 and sizes["rep"] == 2
     stage_orders = [stage_order(part, sizes) for part in range(3)]
     folds = stage_orders if fold else None
+    ffn_parts = (3, 1, 2)
+    ffn_folds = [stage_order(part, sizes) for part in ffn_parts] if fold else None
     size = width // sizes["dp"]
-    core = (lax.axis_index("dp") & 1).astype(jnp.int32).reshape(1)
+    bits = own_bits(sizes)
+    core = bits[:1]
     grad_second, query_side, query_dbias, query_dproj_bias, *query_slabs = ffn_backward(
         0,
         0,
@@ -1270,7 +1426,7 @@
         query_act,
         query_slope,
         (),
-        folds,
+        ffn_folds,
         size,
     )
     text_first, text_side, text_dbias, text_dproj_bias, *text_slabs = ffn_backward(
@@ -1290,14 +1446,14 @@
         text_act,
         text_slope,
         query_slabs if fold else (),
-        folds,
+        ffn_folds,
         size,
     )
     tall = ffn_out.shape[1] // width
     if not fold:
         text_slabs = [
             fold_pair(
-                part,
+                ffn_parts[part],
                 *(
                     jnp.concatenate(
                         [
@@ -1317,11 +1473,11 @@
             for part in range(3)
         ]
     if fold:
-        ffn_states = [
-            begin(part, *text_slabs[2 * part : 2 * part + 2], sizes) for part in range(3)
+        ffn = [
+            begin(ffn_parts[part], *text_slabs[2 * part : 2 * part + 2], sizes) for part in range(3)
         ]
     else:
-        ffn_states = [begin_folded(part, slab, sizes) for part, slab in enumerate(text_slabs)]
+        ffn = [begin_folded(part, slab, sizes) for part, slab in zip(ffn_parts, text_slabs)]
     cross_down = grad_second.reshape(row_count * QUERIES, width)
     query_first, dkv, dkv_ends, cross_dq, cross_side = cross_backward(
         row_count,
@@ -1332,24 +1488,26 @@
         value_ends,
         cross_q,
         cross_down,
-        [text_first] + sends(ffn_states),
-    )
-    ffn_states = advance_all(ffn_states, sizes, cross_side)
+        [text_first] + sends(ffn),
+    )
+    plain = not fold
+    ffn = advance(ffn, bits, sizes, plain, cross_side)
     cross_slabs = cross_weight_grad(
-        core,
-        image_features,
-        image_ends,
-        dkv,
-        dkv_ends,
-        folds and folds[0],
-        size,
-        sends(ffn_states),
-    )
-    ffn_states = advance_all(ffn_states, sizes, cross_slabs[0])
+        core, image_features, image_ends, dkv, dkv_ends, folds, size, sends(ffn)
+    )
     if fold:
-        cross_states = [begin(0, *cross_slabs, sizes)]
+        cross = [begin(part, *cross_slabs[2 * part : 2 * part + 2], sizes) for part in range(3)]
     else:
-        cross_states = [begin_folded(0, fold_pair(0, *cross_slabs[0], sizes), sizes)]
+        edges = [0, 4, 8, cross_slabs[0].shape[1]]
+        cross = [
+            begin_folded(
+                part,
+                fold_pair(part, *cross_slabs[0][:, edges[part] : edges[part + 1]], sizes),
+                sizes,
+            )
+            for part in range(3)
+        ]
+    ffn = advance(ffn, bits, sizes, plain, cross_slabs[0])
     self_grads, self_branch, self_down, self_side = self_backward(
         attn_weights,
         norm_gains,
@@ -1360,53 +1518,68 @@
         first_sum,
         query_first,
         text_first,
-        sends(ffn_states) + sends(cross_states),
-    )
-    ffn_states = advance_all(ffn_states, sizes, self_side)
-    cross_states = advance_all(cross_states, sizes, self_side)
-    query_half = pl.BlockSpec((row_count, QUERIES, width), lambda i: (0, 0, 0))
-    attn_states = []
-    order = sends(ffn_states) + sends(cross_states)
-    for part, (left_two, spec, right_two) in enumerate(
-        (
-            (self_mix, whole(self_mix.shape), self_branch),
-            (first_norm, query_half, cross_dq),
-            (cross_mix, whole(cross_mix.shape), cross_down),
-        )
-    ):
-        slabs = attn_weight_grad(
-            part,
-            core,
-            inputs,
-            self_grads,
-            left_two,
-            spec,
-            right_two,
-            folds and folds[part],
-            size,
-            order,
-        )
-        made = slabs[0]
-        if fold:
-            attn_states.append(begin(part, *slabs, sizes))
-        else:
-            attn_states.append(begin_folded(part, fold_pair(part, *made, sizes), sizes))
-        order = sends(attn_states[-1:])
-    ffn_states = advance_all(ffn_states, sizes, made)
-    cross_states = advance_all(cross_states, sizes, made)
-    input_grad = input_gradient(
-        attn_weights,
+        sends(ffn + cross),
+    )
+    rows = [
+        self_side,
+        cross_side,
+        query_side,
+        text_side,
+        query_dbias,
+        text_dbias,
+        query_dproj_bias,
+        text_dproj_bias,
+    ]
+    used = sum(array.shape[0] for array in rows)
+    packed = jnp.concatenate(rows + [jnp.zeros((-used % 64, 128), f32)], 0)
+    states = advance(ffn + cross, bits, sizes, plain, self_side)
+    vector = begin_whole(packed, sizes)
+    half = (row_count, QUERIES, width)
+    attn_slabs = attn_weight_grad(
+        core,
+        inputs,
         self_grads,
-        self_down,
-        order + sends(ffn_states) + sends(cross_states),
-    )
-    attn_grad = jnp.stack(
         [
-            columns_of(finish(part, state, sizes, input_grad))
-            for part, state in enumerate(attn_states)
-        ]
-    )
-    ffn_sums = [finish(part, state, sizes, input_grad) for part, state in enumerate(ffn_states)]
+            (self_mix, self_mix.shape),
+            (self_branch, self_branch.shape),
+            (first_norm, half),
+            (cross_dq, cross_dq.shape),
+            (cross_mix, cross_mix.shape),
+            (cross_down, cross_down.shape),
+        ],
+        folds,
+        size,
+        sends(states + [vector]),
+    )
+    if fold:
+        attn = [begin(part, *attn_slabs[2 * part : 2 * part + 2], sizes) for part in range(3)]
+    else:
+        attn = [
+            begin_folded(part, fold_pair(part, *slab, sizes), sizes)
+            for part, slab in enumerate(attn_slabs)
+        ]
+    states = advance(states + [vector], bits, sizes, plain, attn_slabs[0])
+    input_grad = input_gradient(attn_weights, self_grads, self_down, sends(states + attn))
+    ffn, cross, vector = states[:3], states[3:6], states[6]
+    last = len(stage_orders[0])
+    states = ffn + attn + cross + [vector]
+    done = [None] * len(states)
+    places = list(range(len(states)))
+    after = input_grad
+    while states:
+        ready = [state[1] == last for state in states]
+        states = advance(states, bits, sizes, plain, after)
+        after = None
+        for place, state, end in zip(places, states, ready):
+            if end:
+                done[place] = state
+        places = [place for place, end in zip(places, ready) if not end]
+        states = [state for state, end in zip(states, ready) if not end]
+    vector = done.pop()
+    shaped = [each.reshape(-1, size, 128) for each in done]
+    ffn_sums, attn_sums, cross_sums = shaped[:3], shaped[3:6], shaped[6:]
+    attn_grad = jnp.stack([columns_of(each) for each in attn_sums])
+    cross_grad = jnp.concatenate([columns_of(each) for each in cross_sums], 1)
     ffn_in_grad = jnp.concatenate([columns_of(each[:8]) for each in ffn_sums], 1)
     ffn_out_grad = jnp.concatenate(
         [
@@ -1416,44 +1589,39 @@
         1,
     )
     proj_grad = columns_of(ffn_sums[0][16:])
-    cross_grad = columns_of(finish(0, cross_states[0], sizes, input_grad))
-    gain_grad = jnp.stack([self_side[0], query_side[3], query_side[0], text_side[0]])
-    bias_grad = jnp.stack(
+    vectors = []
+    start = 0
+    for array, cols in zip(rows, (width,) * 4 + (ffn_in.shape[2],) * 2 + (projections.shape[2],) * 2):
+        piece = vector[start : start + array.shape[0]]
+        vectors.append(piece.reshape(-1, cols))
+        start += array.shape[0]
+    selfs, crosses, queries, texts = vectors[:4]
+    gain_grad = jnp.stack([selfs[0], queries[3], queries[0], texts[0]])
+    bias_grad = jnp.concatenate(
         [
-            self_side[2],
-            self_side[3],
-            self_side[4],
-            cross_side[0],
-            cross_side[1],
-            cross_side[2],
-            query_side[2],
-            text_side[2],
-            self_side[1],
-            query_side[4],
-            query_side[1],
-            text_side[1],
-        ]
-    )
-    vectors = (
-        gain_grad,
-        bias_grad,
-        jnp.stack([query_dbias[0], text_dbias[0]]),
-        jnp.stack([query_dproj_bias[0], text_dproj_bias[0]]),
-    )
-
-    def deal(array):
-        mats, cols = array.shape
-        cut = array.reshape(sizes["rep"], mats // sizes["rep"], sizes["dp"], cols // sizes["dp"])
-        return cut.transpose(2, 0, 1, 3).reshape(world, -1)
-
-    dealt = jnp.concatenate([deal(array) for array in vectors], 1)
-    arrived = jnp.sum(lax.optimization_barrier((exchange(dealt, sizes), input_grad))[0], 0)
-    small = []
-    start = 0
-    for array in vectors:
+            selfs[2:5],
+            crosses[0:3],
+            queries[2:3],
+            texts[2:3],
+            selfs[1:2],
+            queries[4:5],
+            queries[1:2],
+            texts[1:2],
+        ],
+        0,
+    )
+
+    def mine(array):
         mats, cols = array.shape[0] // sizes["rep"], array.shape[1] // sizes["dp"]
-        small.append(arrived[start : start + mats * cols].reshape(mats, cols))
-        start += mats * cols
+        starts = (lax.axis_index("rep") * mats, lax.axis_index("dp") * cols)
+        return lax.dynamic_slice(array, starts, (mats, cols))
+
+    small = [
+        mine(gain_grad),
+        mine(bias_grad),
+        mine(jnp.concatenate(vectors[4:6], 0)),
+        mine(jnp.concatenate(vectors[6:8], 0)),
+    ]
     return (
         layer_out,
         row_loss,

time: 463 us -> 445 us (0.961)
  other arithmetic: 66.7 us -> 11.3 us
  Pallas kernels: 227 us -> 265 us
  starting transfers between devices: 55.4 us -> 47.6 us
  waiting for transfers between devices: 50.1 us -> 57.8 us
    pallas_call x4 -> x11, Pallas kernels: 51.6 us -> 88.6 us  [the longest x9 40.5 us: sum_jobs(): pl.pallas_call(functools.partial(sum_kernel, plan, len(arrays)), in_specs...]
    convert_element_type x18 -> x1, other arithmetic: 34.8 us -> 0.01 us  [begin_whole(): send = values.astype(bf16)]
    ppermute x35 -> x36, waiting for transfers between devices: 36.9 us -> 50 us  [swap(): lax.ppermute(values, axis, [(i, i ^ 1 << bit) for i in range(sizes[axis])])]
    unnamed x52 -> x101, local copies, waits for them, and re-layouts: 13.7 us -> 25.8 us
    another operation x11 -> x2, other arithmetic: 12.5 us -> 1.45 us  [the longest x1 0.79 us: shards(): attn_grad = jnp.stack([columns_of(each) for each in attn_sums])]
    add x6 -> x0, other arithmetic: 9.74 us -> none  [total(): return sum(parts)]
    reshape x15 -> x4, local copies, waits for them, and re-layouts: 11 us -> 3.81 us  [shards(): shaped = [each.reshape(-1, size, 128) for each in done]]
    slice x11, local copies, waits for them, and re-layouts: 9.4 us -> 3.09 us  [the longest x2 1.49 us: shards(): piece = vector[start:start + array.shape[0]]]
  transfers between devices with their start and end apart: 39 -> 39, of which waited for: 15 -> 15; matrix products, arithmetic and copies ran while one was open for 20% -> 4% of each run, Pallas kernels for 38% -> 42%
where the time goes in v6:
time: 445 us; the launch traced here: 437 us
  Pallas kernels  265 us (60%)
  waiting for transfers between devices  57.8 us (13%)
  starting transfers between devices  47.6 us (11%)
  local copies, waits for them, and re-layouts  45.6 us (10%)
  other arithmetic  11.3 us (3%)
  matrix products  6.96 us (2%)
    pallas_call x2, Pallas kernels, ffn_backward(): pl.pallas_call(functools.partial(ffn_backward_kernel, which, folds), grid...  51 us
    ppermute x36, waiting for transfers between devices, swap(): lax.ppermute(values, axis, [(i, i ^ 1 << bit) for i in range(sizes[axis])])  50 us
    pallas_call x9, Pallas kernels, sum_jobs(): pl.pallas_call(functools.partial(sum_kernel, plan, len(arrays)), in_specs...  40.5 us
    pallas_call x1, Pallas kernels, cross_forward(): pl.pallas_call(cross_forward_kernel, grid=(rows // take,), in_specs=[pl.B...  37.5 us
    pallas_call x1, Pallas kernels, cross_weight_grad(): pl.pallas_call(ordered(functools.partial(cross_weight_kernel, folds), 5,...  32.7 us
    ppermute x36, starting transfers between devices, swap(): lax.ppermute(values, axis, [(i, i ^ 1 << bit) for i in range(sizes[axis])])  31.4 us
    pallas_call x2, Pallas kernels, ffn_forward(): pl.pallas_call(functools.partial(ffn_forward_kernel, which), grid=(hidden...  29.9 us
    unnamed x101, local copies, waits for them, and re-layouts  25.8 us
  transfers between devices with their start and end apart: 39, of which 15 were waited for; matrix products, arithmetic and copies ran while one was open for 4% of the time, Pallas kernels for 42%

profile of v6, /device:TPU:0, one launch (start us, length us, event | category | flops | bytes accessed | tf_op | source)
XLA Modules:
  0.0 436.5 jit_solution(10393835911867329978)
XLA Ops:
  0.7 7.6 %copy.109.image_ref.refs_1_ = bf16[16,257,1408]{2,1,0:T(8,128)(2,1)S(1)} copy(bf16[16,257,1408]{2,0,1:T(8,128)(2,1)} %param.15) | data formatting | bytes 23158784 | tf_op args[1]
  8.3 4.3 copy-done.5
  16.7 14.7 %self_forward.1 = (bf16[1024,768]{1,0:T(8,128)(2,1)}, bf16[1024,768]{1,0:T(8,128)(2,1)}, bf16[1024,768]{1,0:T(8,128)(2,1)}, bf16[1024,768]{1,0:T(8,128)(2,1)}, f32[1024,768]{1,0:T(8,128)}, /*index=5*/f32[1024,768]{1,0:T(8,128)}) custom-call(bf16[1024,768]{1,0:T(8,128)(2,1)} %bitcast.288, bf16[6,768,768]{2,1,0:T(8,128)(2,1)} %refs_0_.5, f32[12,768]{1,0:T(8,128)} %bias_ref.7, ...), custom_call_target="tpu_custom_call" | custom-call | flops 16499999744 | tf_op jit(solution)/shard_map/self_forward/pallas_call | solution.py:216
  31.3 14.9 %ffn_forward.2 = (bf16[512,3072]{1,0:T(8,128)(2,1)}, bf16[512,3072]{1,0:T(8,128)(2,1)}, f32[512,768]{1,0:T(8,128)}, bf16[16,64,768]{2,1,0:T(8,128)(2,1)}, f32[512,256]{1,0:T(8,128)}, /*index=5*/bf16[512,256]{1,0:T(8,128)(2,1)}) custom-call(f32[16,64,768]{2,1,0:T(8,128)} %bitcast.302, bf16[2,768,3072]{2,1,0:T(8,128)(2,1)} %in_ref.7, f32[2,3072]{1,0:T(2,128)} %in_bias_ref.3, ...), custom_call_target="tpu_custom_call" | custom-call | flops 16499999744 | tf_op jit(solution)/shard_map/ffn_forward/pallas_call | solution.py:821
  48.3 7.5 %all-to-all-start = ((bf16[32,32,256]{2,1,0:T(8,128)(2,1)}), bf16[32,32,256]{2,1,0:T(8,128)(2,1)S(1)}, u32[]{:S(2)}, u32[]{:S(2)}) async-start(bf16[32,32,256]{2,1,0:T(8,128)(2,1)} %tile.20), calls=%async_computation | async-start | bytes 1048576 | tf_op jit(solution)/shard_map/all_to_all | solution.py:1270
  55.7 37.5 %cross_forward.1 = (bf16[4096,768]{1,0:T(8,128)(2,1)}, bf16[4096,768]{1,0:T(8,128)(2,1)}, bf16[256,768]{1,0:T(8,128)(2,1)}, bf16[256,768]{1,0:T(8,128)(2,1)}, bf...) custom-call(bf16[16,257,1408]{2,1,0:T(8,128)(2,1)} %copy-done.5, ...), custom_call_target="tpu_custom_call" | custom-call | flops 41799999488 | tf_op jit(solution)/shard_map/cross_forward/pallas_call | solution.py:529
  93.3 15.0 %ffn_forward.3 = (bf16[512,3072]{1,0:T(8,128)(2,1)}, bf16[512,3072]{1,0:T(8,128)(2,1)}, f32[512,768]{1,0:T(8,128)}, bf16[16,64,768]{2,1,0:T(8,128)(2,1)}, f32[512,256]{1,0:T(8,128)}, /*index=5*/bf16[512,256]{1,0:T(8,128)(2,1)}) custom-call(f32[16,32,768]{2,1,0:T(8,128)} %bitcast.309, bf16[2,768,3072]{2,1,0:T(8,128)(2,1)} %in_ref.7, ...), custom_call_target="tpu_custom_call", output_to_operand_aliasing={{3}: (8, {})} | custom-call | flops 16499999744 | tf_op jit(solution)/shard_map/ffn_forward/pallas_call | solution.py:821
  112.4 5.9 %all-to-all-start.1 = ((f32[32,1,1024]{2,1,0:T(1,128)}), f32[32,1,1024]{2,1,0:T(1,128)S(1)}, u32[]{:S(2)}, u32[]{:S(2)}) async-start(f32[32,1,1024]{2,1,0:T(1,128)} %broadcast_in_dim.14), calls=%async_computation.1 | async-start | bytes 262144 | tf_op jit(solution)/shard_map/all_to_all | solution.py:1270
  119.2 7.8 %all-to-all-done.1 = f32[32,1,1024]{2,1,0:T(1,128)S(1)} async-done(((f32[32,1,1024]{2,1,0:T(1,128)}), f32[32,1,1024]{2,1,0:T(1,128)S(1)}, u32[]{:S(2)}, u32[]{:S(2)}) %all-to-all-start.1) | async-done | bytes 131104 | tf_op jit(solution)/shard_map/all_to_all | solution.py:1270
  131.5 2.8 all-to-all-start.2
  136.3 25.3 %ffn_backward.2 = (f32[16,32,768]{2,1,0:T(8,128)}, f32[48,128]{1,0:T(8,128)}, f32[24,128]{1,0:T(8,128)}, f32[2,128]{1,0:T(2,128)}, bf16[2,2,2,2,18,48,128]{6,5,4...) custom-call(s32[1]{0:T(128)} %bitcast.276, ...), custom_call_target="tpu_custom_call" | custom-call | flops 27499999232 | tf_op jit(solution)/shard_map/ffn_backward/pallas_call | solution.py:1000
  163.0 25.7 %ffn_backward.3 = (f32[16,32,768]{2,1,0:T(8,128)}, f32[48,128]{1,0:T(8,128)}, f32[24,128]{1,0:T(8,128)}, f32[2,128]{1,0:T(2,128)}, bf16[2,2,2,2,18,48,128]{6,5,4...) custom-call(s32[1]{0:T(128)} %bitcast.277, ...), custom_call_target="tpu_custom_call", output_to_operand_aliasing={{4}: (13, {}), {5}: (14, {}), {6}: (15, {}), {7}: (16, {}),... | custom-call | flops 27499999232 | tf_op jit(solution)/shard_map/ffn_backward/pallas_call | solution.py:1000
  189.6 18.9 %cross_backward.1 = (f32[16,32,768]{2,1,0:T(8,128)}, bf16[2,4096,768]{2,1,0:T(8,128)(2,1)}, bf16[2,256,768]{2,1,0:T(8,128)(2,1)}, bf16[512,768]{1,0:T(8,128)(2,1)}, f32[48,128]{1,0:T(8,128)}) custom-call(bf16[6,768,768]{2,1,0:T(8,128)(2,1)} %refs_0_.5, bf16[4096,768]{1,0:T(8,128)(2,1)} %get-tuple-element.149.refs_1_, ...), custom_call_target="tpu_custom_call" | custom-call | flops 20899999744 | tf_op jit(solution)/shard_map/cross_backward/pallas_call | solution.py:643
  210.3 7.2 %sum_terms.9 = (bf16[6912,128]{1,0:T(8,128)(2,1)}, bf16[6144,128]{1,0:T(8,128)(2,1)}, bf16[6144,128]{1,0:T(8,128)(2,1)}) custom-call(s32[5]{0:T(128)} %shift-right-arithmetic_and_fusion.bits_ref, bf16[13824,128]{1,0:T(8,128)(2,1)} %bitcast.192, bf16[13824,128]{1,0:T(8,128)(2,1)} %copy-done, bf16[12288,128]{1,0:T(8,128)(2,1)} %bitcast.197, ...), custom_call_target="tpu_custom_call" | custom-call | flops 3300000000 | tf_op jit(solution)/shard_map/sum_terms/pallas_call | solution.py:1162
  222.2 32.7 %cross_weight_grad.1 = (bf16[2,2,2,2,4,48,128]{6,5,4,3,2,1,0:T(8,128)(2,1)}, bf16[2,2,2,2,4,48,128]{6,5,4,3,2,1,0:T(8,128)(2,1)}, bf16[2,2,2,2,4,48,128]{6,5,4,3...) custom-call(s32[1]{0:T(128)} %bitcast.278, ...), custom_call_target="tpu_custom_call" | custom-call | flops 35200000000 | tf_op jit(solution)/shard_map/cross_weight_grad/pallas_call | solution.py:737
  259.8 5.3 %sum_terms.10 = (bf16[3456,128]{1,0:T(8,128)(2,1)}, bf16[3072,128]{1,0:T(8,128)(2,1)}, bf16[3072,128]{1,0:T(8,128)(2,1)}) custom-call(s32[5]{0:T(128)} %shift-right-arithmetic_and_fusion.bits_ref, bf16[13824,128]{1,0:T(8,128)(2,1)} %bitcast.193, bf16[13824,128]{1,0:T(8,128)(2,1)} %copy-done, bf16[6912,128]{1,0:T(8,128)(2,1)} %copy-done.1, ...), custom_call_target="tpu_custom_call" | custom-call | flops 3300000000 | tf_op jit(solution)/shard_map/sum_terms/pallas_call | solution.py:1162
  269.9 15.7 %self_backward.1 = (bf16[3,1024,768]{2,1,0:T(8,128)(2,1)}, bf16[1024,768]{1,0:T(8,128)(2,1)}, f32[1024,768]{1,0:T(8,128)}, f32[48,128]{1,0:T(8,128)}) custom-call(bf16[6,768,768]{2,1,0:T(8,128)(2,1)} %refs_0_.5, f32[4,768]{1,0:T(4,128)} %refs_1_.2, f32[16,64,256]{2,1,0:T(8,128)} %tile.18.mask_ref.refs_2_, bf16[1024,768]{1,0:T(8,128)(2,1)} %get-tuple-element.145.refs_3_, ...), custom_call_target="tpu_custom_call" | custom-call | flops 17600000000 | tf_op jit(solution)/shard_map/self_backward/pallas_call | solution.py:306
  288.4 4.9 %sum_terms.11 = (bf16[1728,128]{1,0:T(8,128)(2,1)}, bf16[3072,128]{1,0:T(8,128)(2,1)}, bf16[3072,128]{1,0:T(8,128)(2,1)}, bf16[1152,128]{1,0:T(8,128)(2,1)}) custom-call(s32[5]{0:T(128)} %shift-right-arithmetic_and_fusion.bits_ref, bf16[13824,128]{1,0:T(8,128)(2,1)} %bitcast.194, bf16[13824,128]{1,0:T(8,128)(2,1)} %copy-done, bf16[6912,128]{1,0:T(8,128)(2,1)} %copy-done.1, ...), custom_call_target="tpu_custom_call" | custom-call | flops 3300000000 | tf_op jit(solution)/shard_map/sum_terms/pallas_call | solution.py:1162
  299.6 15.3 %attn_weight_grad.1 = (bf16[2,2,2,2,6,48,128]{6,5,4,3,2,1,0:T(8,128)(2,1)}, bf16[2,2,2,2,6,48,128]{6,5,4,3,2,1,0:T(8,128)(2,1)}, bf16[2,2,2,2,6,48,128]{6,5,4,3,...) custom-call(s32[1]{0:T(128)} %bitcast.279, ...), custom_call_target="tpu_custom_call" | custom-call | flops 22000001024 | tf_op jit(solution)/shard_map/attn_weight_grad/pallas_call | solution.py:427
  316.6 8.5 %collective-permute-done.13.refs_7_.refs_4_.refs_18_.refs_22_ = bf16[3072,128]{1,0:T(8,128)(2,1)S(1)} collective-permute-done((bf16[3072,128]{1,0:T(8,128)(2,1)}, bf16[3072,128]{1,0:T(8,128)(2,1)S(1)}, u32[]{:S(2)}, u32[]{:S(2)}) %collective-permute-start.13) | collective-permute-done | bytes 786464 | tf_op jit(solution)/shard_map/ppermute | solution.py:1063
  327.0 4.1 sum_terms.12
  333.2 4.5 %collective-permute-done.22.refs_19_.refs_15_.refs_18_ = bf16[768,128]{1,0:T(8,128)(2,1)S(1)} collective-permute-done((bf16[768,128]{1,0:T(8,128)(2,1)}, bf16[768,128]{1,0:T(8,128)(2,1)S(1)}, u32[]{:S(2)}, u32[]{:S(2)}) %collective-permute-start.22) | collective-permute-done | bytes 196640 | tf_op jit(solution)/shard_map/ppermute | solution.py:1063
  338.1 9.1 %input_gradient.1 = f32[1024,768]{1,0:T(8,128)} custom-call(bf16[6,768,768]{2,1,0:T(8,128)(2,1)} %refs_0_.5, bf16[3,1024,768]{2,1,0:T(8,128)(2,1)} %get-tuple-element.197.refs_2_.refs_1_, f32[1024,768]{1,0:T(8,128)} %get-tuple-element.198.refs_2_, bf16[1632,128]{1,0:T(8,128)(2,1)} %get-tuple-element.228.refs_3_, ...), custom_call_target="tpu_custom_call" | custom-call | flops 9900000256 | tf_op jit(solution)/shard_map/input_gradient/pallas_call | solution.py:354
  347.2 9.7 %collective-permute-done.23.refs_29_ = bf16[1536,128]{1,0:T(8,128)(2,1)S(1)} collective-permute-done((bf16[1536,128]{1,0:T(8,128)(2,1)}, bf16[1536,128]{1,0:T(8,128)(2,1)S(1)}, u32[]{:S(2)}, u32[]{:S(2)}) %collective-permute-start.23) | collective-permute-done | bytes 393248 | tf_op jit(solution)/shard_map/ppermute | solution.py:1063
  357.9 6.2 %sum_terms.13 = (bf16[2688,128]{1,0:T(8,128)(2,1)}, bf16[2848,128]{1,0:T(8,128)(2,1)}, bf16[2688,128]{1,0:T(8,128)(2,1)}, f32[864,128]{1,0:T(8,128)}, f32[768,128]{1,0:T(8,128)}, /*index=5*/f32[768,128]{1,0:T(8,128)}) custom-call(s32[5]{0:T(128)} %shift-right-arithmetic_and_fusion.bits_ref, bf16[4608,128]{1,0:T(8,128)(2,1)} %bitcast.222, ...), custom_call_target="tpu_custom_call" | custom-call | flops 3300000000 | tf_op jit(solution)/shard_map/sum_terms/pallas_call | solution.py:1162
  370.0 11.2 %collective-permute-done.24.refs_2_ = bf16[2688,128]{1,0:T(8,128)(2,1)S(1)} collective-permute-done((bf16[2688,128]{1,0:T(8,128)(2,1)}, bf16[2688,128]{1,0:T(8,128)(2,1)S(1)}, u32[]{:S(2)}, u32[]{:S(2)}) %collective-permute-start.24) | collective-permute-done | bytes 688160 | tf_op jit(solution)/shard_map/ppermute | solution.py:1063
  383.8 3.5 sum_terms.14
  395.0 4.0 collective-permute-done.30.refs_19_
  400.6 3.4 sum_terms.15
  413.2 3.0 sum_terms.16
  423.5 5.2 %collective-permute-done.35.refs_5_ = bf16[864,128]{1,0:T(8,128)(2,1)S(1)} collective-permute-done((bf16[864,128]{1,0:T(8,128)(2,1)}, bf16[864,128]{1,0:T(8,128)(2,1)S(1)}, u32[]{:S(2)}, u32[]{:S(2)}) %collective-permute-start.35) | collective-permute-done | bytes 221216 | tf_op jit(solution)/shard_map/ppermute | solution.py:1063
  429.3 2.9 sum_terms.17
  (257 shorter events, 90.3 us)
Async XLA Ops:
  48.3 61.6 %all-to-all-start = ((bf16[32,32,256]{2,1,0:T(8,128)(2,1)}), bf16[32,32,256]{2,1,0:T(8,128)(2,1)S(1)}, u32[]{:S(2)}, u32[]{:S(2)}) async-start(bf16[32,32,256]{2,1,0:T(8,128)(2,1)} %tile.20), calls=%async_computation | async-start | bytes 1048576 | tf_op jit(solution)/shard_map/all_to_all | solution.py:1270
  112.4 14.6 %all-to-all-start.1 = ((f32[32,1,1024]{2,1,0:T(1,128)}), f32[32,1,1024]{2,1,0:T(1,128)S(1)}, u32[]{:S(2)}, u32[]{:S(2)}) async-start(f32[32,1,1024]{2,1,0:T(1,128)} %broadcast_in_dim.14), calls=%async_computation.1 | async-start | bytes 262144 | tf_op jit(solution)/shard_map/all_to_all | solution.py:1270
  131.5 30.1 %all-to-all-start.2 = ((bf16[32,32,256]{2,1,0:T(8,128)(2,1)}), bf16[32,32,256]{2,1,0:T(8,128)(2,1)S(1)}, u32[]{:S(2)}, u32[]{:S(2)}) async-start(bf16[32,32,256]{2,1,0:T(8,128)(2,1)} %bitcast.259), calls=%async_computation.2 | async-start | bytes 1048576 | tf_op jit(solution)/shard_map/all_to_all | solution.py:1270
  188.8 19.7 %collective-permute-start = (bf16[13824,128]{1,0:T(8,128)(2,1)}, bf16[13824,128]{1,0:T(8,128)(2,1)S(1)}, u32[]{:S(2)}, u32[]{:S(2)}) collective-permute-start(bf16[13824,128]{1,0:T(8,128)(2,1)} %bitcast.282), channel_id=1, source_target_pairs={{0,2},{2,0},{4,6},{6,4},{8,10},{10,8},{12,14},{14,12},{16,18},{18,... | collective-permute-start | bytes 10616840 | tf_op jit(solution)/shard_map/ppermute | solution.py:1063
  189.1 19.4 %collective-permute-start.1 = (bf16[12288,128]{1,0:T(8,128)(2,1)}, bf16[12288,128]{1,0:T(8,128)(2,1)}, u32[]{:S(2)}, u32[]{:S(2)}) collective-permute-start(bf16[12288,128]{1,0:T(8,128)(2,1)} %bitcast.284), channel_id=1, source_target_pairs={{0,2},{2,0},{4,6},{6,4},{8,10},{10,8},{12,14},{14,12},{16,18},{18,... | collective-permute-start | bytes 9437192 | tf_op jit(solution)/shard_map/ppermute | solution.py:1063
  189.4 19.1 %collective-permute-start.2 = (bf16[12288,128]{1,0:T(8,128)(2,1)}, bf16[12288,128]{1,0:T(8,128)(2,1)}, u32[]{:S(2)}, u32[]{:S(2)}) collective-permute-start(bf16[12288,128]{1,0:T(8,128)(2,1)} %bitcast.286), channel_id=1, source_target_pairs={{0,2},{2,0},{4,6},{6,4},{8,10},{10,8},{12,14},{14,12},{16,18},{18,... | collective-permute-start | bytes 9437192 | tf_op jit(solution)/shard_map/ppermute | solution.py:1063
  217.5 41.0 %collective-permute-start.3 = (bf16[6912,128]{1,0:T(8,128)(2,1)}, bf16[6912,128]{1,0:T(8,128)(2,1)S(1)}, u32[]{:S(2)}, u32[]{:S(2)}) collective-permute-start(bf16[6912,128]{1,0:T(8,128)(2,1)} %get-tuple-element.182.refs_5_), channel_id=1, source_target_pairs={{0,4},{2,6},{4,0},{6,2},{8,12},{10,14},{12,8},{14,10},{16,20},{18,... | collective-permute-start | bytes 5308424 | tf_op jit(solution)/shard_map/ppermute | solution.py:1063
  219.2 36.6 %collective-permute-start.4 = (bf16[6144,128]{1,0:T(8,128)(2,1)}, bf16[6144,128]{1,0:T(8,128)(2,1)S(1)}, u32[]{:S(2)}, u32[]{:S(2)}) collective-permute-start(bf16[6144,128]{1,0:T(8,128)(2,1)} %get-tuple-element.185.refs_6_), channel_id=1, source_target_pairs={{0,8},{2,10},{4,12},{6,14},{8,0},{10,2},{12,4},{14,6},{16,24},{18,... | collective-permute-start | bytes 4718600 | tf_op jit(solution)/shard_map/ppermute | solution.py:1063
  220.7 36.4 %collective-permute-start.5 = (bf16[6144,128]{1,0:T(8,128)(2,1)}, bf16[6144,128]{1,0:T(8,128)(2,1)}, u32[]{:S(2)}, u32[]{:S(2)}) collective-permute-start(bf16[6144,128]{1,0:T(8,128)(2,1)} %get-tuple-element.186.refs_7_), channel_id=1, source_target_pairs={{0,1},{1,0},{2,3},{3,2},{4,5},{5,4},{6,7},{7,6},{8,9},{9,8},{10,11... | collective-permute-start | bytes 4718600 | tf_op jit(solution)/shard_map/ppermute | solution.py:1063
  255.0 13.4 %collective-permute-start.8 = (bf16[3072,128]{1,0:T(8,128)(2,1)}, bf16[3072,128]{1,0:T(8,128)(2,1)}, u32[]{:S(2)}, u32[]{:S(2)}) collective-permute-start(bf16[3072,128]{1,0:T(8,128)(2,1)} %bitcast.296), channel_id=1, source_target_pairs={{0,2},{2,0},{4,6},{6,4},{8,10},{10,8},{12,14},{14,12},{16,18},{18,... | collective-permute-start | bytes 2359304 | tf_op jit(solution)/shard_map/ppermute | solution.py:1063
  255.0 30.5 %collective-permute-start.10 = (bf16[3072,128]{1,0:T(8,128)(2,1)}, bf16[3072,128]{1,0:T(8,128)(2,1)}, u32[]{:S(2)}, u32[]{:S(2)}) collective-permute-start(bf16[3072,128]{1,0:T(8,128)(2,1)} %bitcast.298), channel_id=1, source_target_pairs={{0,2},{2,0},{4,6},{6,4},{8,10},{10,8},{12,14},{14,12},{16,18},{18,... | collective-permute-start | bytes 2359304 | tf_op jit(solution)/shard_map/ppermute | solution.py:1063
  255.8 29.8 %collective-permute-start.11 = (bf16[2304,128]{1,0:T(8,128)(2,1)}, bf16[2304,128]{1,0:T(8,128)(2,1)}, u32[]{:S(2)}, u32[]{:S(2)}) collective-permute-start(bf16[2304,128]{1,0:T(8,128)(2,1)} %bitcast.300), channel_id=1, source_target_pairs={{0,2},{2,0},{4,6},{6,4},{8,10},{10,8},{12,14},{14,12},{16,18},{18,... | collective-permute-start | bytes 1769480 | tf_op jit(solution)/shard_map/ppermute | solution.py:1063
  265.0 22.0 %collective-permute-start.6 = (bf16[3456,128]{1,0:T(8,128)(2,1)}, bf16[3456,128]{1,0:T(8,128)(2,1)S(1)}, u32[]{:S(2)}, u32[]{:S(2)}) collective-permute-start(bf16[3456,128]{1,0:T(8,128)(2,1)} %get-tuple-element.191.refs_9_), channel_id=1, source_target_pairs={{0,8},{2,10},{4,12},{6,14},{8,0},{10,2},{12,4},{14,6},{16,24},{18,... | collective-permute-start | bytes 2654216 | tf_op jit(solution)/shard_map/ppermute | solution.py:1063
  266.9 20.0 %collective-permute-start.7 = (bf16[3072,128]{1,0:T(8,128)(2,1)}, bf16[3072,128]{1,0:T(8,128)(2,1)S(1)}, u32[]{:S(2)}, u32[]{:S(2)}) collective-permute-start(bf16[3072,128]{1,0:T(8,128)(2,1)} %get-tuple-element.192.refs_10_), channel_id=1, source_target_pairs={{0,1},{1,0},{2,3},{3,2},{4,5},{5,4},{6,7},{7,6},{8,9},{9,8},{10,11... | collective-permute-start | bytes 2359304 | tf_op jit(solution)/shard_map/ppermute | solution.py:1063
  268.4 18.6 %collective-permute-start.9 = (bf16[3072,128]{1,0:T(8,128)(2,1)}, bf16[3072,128]{1,0:T(8,128)(2,1)S(1)}, u32[]{:S(2)}, u32[]{:S(2)}) collective-permute-start(bf16[3072,128]{1,0:T(8,128)(2,1)} %get-tuple-element.193.refs_11_), channel_id=1, source_target_pairs={{0,4},{2,6},{4,0},{6,2},{8,12},{10,14},{12,8},{14,10},{16,20},{18,... | collective-permute-start | bytes 2359304 | tf_op jit(solution)/shard_map/ppermute | solution.py:1063
  286.8 28.1 %collective-permute-start.16 = (bf16[256,128]{1,0:T(8,128)(2,1)S(1)}, bf16[256,128]{1,0:T(8,128)(2,1)S(1)}, u32[]{:S(2)}, u32[]{:S(2)}) collective-permute-start(bf16[256,128]{1,0:T(8,128)(2,1)S(1)} %convert_element_type.67.refs_13_), channel_id=1, source_target_pairs={{0,2},{2,0},{4,6},{6,4},{8,10},{10,8},{12,14},{14,12},{16,18},{18,... | collective-permute-start | bytes 196616 | tf_op jit(solution)/shard_map/ppermute | solution.py:1063
  293.4 23.2 %collective-permute-start.12 = (bf16[1728,128]{1,0:T(8,128)(2,1)}, bf16[1728,128]{1,0:T(8,128)(2,1)S(1)}, u32[]{:S(2)}, u32[]{:S(2)}) collective-permute-start(bf16[1728,128]{1,0:T(8,128)(2,1)} %get-tuple-element.208.refs_9_), channel_id=1, source_target_pairs={{0,16},{2,18},{4,20},{6,22},{8,24},{10,26},{12,28},{14,30},{16,0},... | collective-permute-start | bytes 1327112 | tf_op jit(solution)/shard_map/ppermute | solution.py:1063
  295.9 29.2 %collective-permute-start.13 = (bf16[3072,128]{1,0:T(8,128)(2,1)}, bf16[3072,128]{1,0:T(8,128)(2,1)S(1)}, u32[]{:S(2)}, u32[]{:S(2)}) collective-permute-start(bf16[3072,128]{1,0:T(8,128)(2,1)} %get-tuple-element.214.refs_11_), channel_id=1, source_target_pairs={{0,8},{2,10},{4,12},{6,14},{8,0},{10,2},{12,4},{14,6},{16,24},{18,... | collective-permute-start | bytes 2359304 | tf_op jit(solution)/shard_map/ppermute | solution.py:1063
  296.6 28.5 %collective-permute-start.14 = (bf16[3072,128]{1,0:T(8,128)(2,1)}, bf16[3072,128]{1,0:T(8,128)(2,1)S(1)}, u32[]{:S(2)}, u32[]{:S(2)}) collective-permute-start(bf16[3072,128]{1,0:T(8,128)(2,1)} %get-tuple-element.213.refs_10_), channel_id=1, source_target_pairs={{0,4},{2,6},{4,0},{6,2},{8,12},{10,14},{12,8},{14,10},{16,20},{18,... | collective-permute-start | bytes 2359304 | tf_op jit(solution)/shard_map/ppermute | solution.py:1063
  298.1 16.9 %collective-permute-start.15 = (bf16[1152,128]{1,0:T(8,128)(2,1)}, bf16[1152,128]{1,0:T(8,128)(2,1)S(1)}, u32[]{:S(2)}, u32[]{:S(2)}) collective-permute-start(bf16[1152,128]{1,0:T(8,128)(2,1)} %get-tuple-element.215.refs_12_), channel_id=1, source_target_pairs={{0,1},{1,0},{2,3},{3,2},{4,5},{5,4},{6,7},{7,6},{8,9},{9,8},{10,11... | collective-permute-start | bytes 884744 | tf_op jit(solution)/shard_map/ppermute | solution.py:1063
  314.9 32.3 %collective-permute-start.17 = (bf16[4608,128]{1,0:T(8,128)(2,1)}, bf16[4608,128]{1,0:T(8,128)(2,1)S(1)}, u32[]{:S(2)}, u32[]{:S(2)}) collective-permute-start(bf16[4608,128]{1,0:T(8,128)(2,1)} %bitcast.294), channel_id=1, source_target_pairs={{0,2},{2,0},{4,6},{6,4},{8,10},{10,8},{12,14},{14,12},{16,18},{18,... | collective-permute-start | bytes 3538952 | tf_op jit(solution)/shard_map/ppermute | solution.py:1063
  315.0 32.2 %collective-permute-start.19 = (bf16[4608,128]{1,0:T(8,128)(2,1)}, bf16[4608,128]{1,0:T(8,128)(2,1)}, u32[]{:S(2)}, u32[]{:S(2)}) collective-permute-start(bf16[4608,128]{1,0:T(8,128)(2,1)} %bitcast.292), channel_id=1, source_target_pairs={{0,2},{2,0},{4,6},{6,4},{8,10},{10,8},{12,14},{14,12},{16,18},{18,... | collective-permute-start | bytes 3538952 | tf_op jit(solution)/shard_map/ppermute | solution.py:1063
  316.6 30.6 %collective-permute-start.21 = (bf16[4608,128]{1,0:T(8,128)(2,1)}, bf16[4608,128]{1,0:T(8,128)(2,1)}, u32[]{:S(2)}, u32[]{:S(2)}) collective-permute-start(bf16[4608,128]{1,0:T(8,128)(2,1)} %bitcast.290), channel_id=1, source_target_pairs={{0,2},{2,0},{4,6},{6,4},{8,10},{10,8},{12,14},{14,12},{16,18},{18,... | collective-permute-start | bytes 3538952 | tf_op jit(solution)/shard_map/ppermute | solution.py:1063
  337.7 19.3 %collective-permute-start.18 = (bf16[1632,128]{1,0:T(8,128)(2,1)}, bf16[1632,128]{1,0:T(8,128)(2,1)S(1)}, u32[]{:S(2)}, u32[]{:S(2)}) collective-permute-start(bf16[1632,128]{1,0:T(8,128)(2,1)} %get-tuple-element.228.refs_3_), channel_id=1, source_target_pairs={{0,1},{1,0},{2,3},{3,2},{4,5},{5,4},{6,7},{7,6},{8,9},{9,8},{10,11... | collective-permute-start | bytes 1253384 | tf_op jit(solution)/shard_map/ppermute | solution.py:1063
  338.1 18.9 %collective-permute-start.23 = (bf16[1536,128]{1,0:T(8,128)(2,1)}, bf16[1536,128]{1,0:T(8,128)(2,1)S(1)}, u32[]{:S(2)}, u32[]{:S(2)}) collective-permute-start(bf16[1536,128]{1,0:T(8,128)(2,1)} %get-tuple-element.229.refs_4_), channel_id=1, source_target_pairs={{0,16},{2,18},{4,20},{6,22},{8,24},{10,26},{12,28},{14,30},{16,0},... | collective-permute-start | bytes 1179656 | tf_op jit(solution)/shard_map/ppermute | solution.py:1063
  364.1 18.1 %collective-permute-start.25 = (bf16[2848,128]{1,0:T(8,128)(2,1)}, bf16[2848,128]{1,0:T(8,128)(2,1)S(1)}, u32[]{:S(2)}, u32[]{:S(2)}) collective-permute-start(bf16[2848,128]{1,0:T(8,128)(2,1)} %get-tuple-element.245), channel_id=1, source_target_pairs={{0,8},{2,10},{4,12},{6,14},{8,0},{10,2},{12,4},{14,6},{16,24},{18,... | collective-permute-start | bytes 2187272 | tf_op jit(solution)/shard_map/ppermute | solution.py:1063
  364.2 17.0 %collective-permute-start.24 = (bf16[2688,128]{1,0:T(8,128)(2,1)}, bf16[2688,128]{1,0:T(8,128)(2,1)S(1)}, u32[]{:S(2)}, u32[]{:S(2)}) collective-permute-start(bf16[2688,128]{1,0:T(8,128)(2,1)} %get-tuple-element.244), channel_id=1, source_target_pairs={{0,4},{2,6},{4,0},{6,2},{8,12},{10,14},{12,8},{14,10},{16,20},{18,... | collective-permute-start | bytes 2064392 | tf_op jit(solution)/shard_map/ppermute | solution.py:1063
  365.4 16.7 %collective-permute-start.26 = (bf16[2688,128]{1,0:T(8,128)(2,1)}, bf16[2688,128]{1,0:T(8,128)(2,1)S(1)}, u32[]{:S(2)}, u32[]{:S(2)}) collective-permute-start(bf16[2688,128]{1,0:T(8,128)(2,1)} %get-tuple-element.246), channel_id=1, source_target_pairs={{0,1},{1,0},{2,3},{3,2},{4,5},{5,4},{6,7},{7,6},{8,9},{9,8},{10,11... | collective-permute-start | bytes 2064392 | tf_op jit(solution)/shard_map/ppermute | solution.py:1063
  387.4 11.6 %collective-permute-start.27 = (bf16[1152,128]{1,0:T(8,128)(2,1)}, bf16[1152,128]{1,0:T(8,128)(2,1)S(1)}, u32[]{:S(2)}, u32[]{:S(2)}) collective-permute-start(bf16[1152,128]{1,0:T(8,128)(2,1)} %get-tuple-element.247), channel_id=1, source_target_pairs={{0,8},{2,10},{4,12},{6,14},{8,0},{10,2},{12,4},{14,6},{16,24},{18,... | collective-permute-start | bytes 884744 | tf_op jit(solution)/shard_map/ppermute | solution.py:1063
  389.2 9.8 %collective-permute-start.28 = (bf16[1408,128]{1,0:T(8,128)(2,1)}, bf16[1408,128]{1,0:T(8,128)(2,1)S(1)}, u32[]{:S(2)}, u32[]{:S(2)}) collective-permute-start(bf16[1408,128]{1,0:T(8,128)(2,1)} %get-tuple-element.248), channel_id=1, source_target_pairs={{0,1},{1,0},{2,3},{3,2},{4,5},{5,4},{6,7},{7,6},{8,9},{9,8},{10,11... | collective-permute-start | bytes 1081352 | tf_op jit(solution)/shard_map/ppermute | solution.py:1063
  390.9 8.1 %collective-permute-start.29 = (bf16[1152,128]{1,0:T(8,128)(2,1)}, bf16[1152,128]{1,0:T(8,128)(2,1)S(1)}, u32[]{:S(2)}, u32[]{:S(2)}) collective-permute-start(bf16[1152,128]{1,0:T(8,128)(2,1)} %get-tuple-element.249), channel_id=1, source_target_pairs={{0,4},{2,6},{4,0},{6,2},{8,12},{10,14},{12,8},{14,10},{16,20},{18,... | collective-permute-start | bytes 884744 | tf_op jit(solution)/shard_map/ppermute | solution.py:1063
  419.2 9.4 %collective-permute-start.35 = (bf16[864,128]{1,0:T(8,128)(2,1)}, bf16[864,128]{1,0:T(8,128)(2,1)S(1)}, u32[]{:S(2)}, u32[]{:S(2)}) collective-permute-start(bf16[864,128]{1,0:T(8,128)(2,1)} %get-tuple-element.255), channel_id=1, source_target_pairs={{0,16},{2,18},{4,20},{6,22},{8,24},{10,26},{12,28},{14,30},{16,0},... | collective-permute-start | bytes 663560 | tf_op jit(solution)/shard_map/ppermute | solution.py:1063
  (54 other events, 354.0 us)

commit v7 on v6

--- a/solution.py
+++ b/solution.py
@@ -95,7 +95,7 @@
 
 
 def unread(count):
-    return [pl.BlockSpec(memory_space=pl.ANY)] * count
+    return [pl.BlockSpec(memory_space=pltpu.HBM)] * count
 
 
 def params(mib):
@@ -346,25 +346,26 @@
     )
 
 
-def input_gradient(weights, grads, down, order):
+def input_gradient(weights, grads, down, order, first, last, prior=()):
     tokens, width = down.shape
     count = 4 * SLOTS
-    tile = pl.BlockSpec((count, width), lambda i: (i, 0))
-
+    tile = pl.BlockSpec((count, width), lambda i: (first + i, 0))
+    order = list(prior) + list(order)
     return pl.pallas_call(
         ordered(input_grad_kernel, 3, len(order)),
-        grid=(tokens // count,),
+        grid=(last - first,),
         in_specs=[
             held((3, width, width), lambda i: (0, 0, 0)),
-            pl.BlockSpec((3, count, width), lambda i: (0, i, 0)),
+            pl.BlockSpec((3, count, width), lambda i: (0, first + i, 0)),
             tile,
         ]
         + unread(len(order)),
         out_specs=tile,
         out_shape=jax.ShapeDtypeStruct((tokens, width), f32),
+        input_output_aliases={3: 0} if prior else {},
         compiler_params=params(58),
         name="input_gradient",
-        cost_estimate=cost(9),
+        cost_estimate=cost(5),
     )(weights, grads, down, *order)
 
 
@@ -1015,7 +1016,7 @@
             held((tokens, hidden), lambda j: (0, 0)),
             pl.BlockSpec((tokens, chunk), lambda j: (0, j)),
         ]
-        + [pl.BlockSpec(memory_space=pl.ANY)] * len(slabs),
+        + unread(len(slabs)),
         out_specs=[
             whole((rows, QUERIES, width)),
             whole((width // 16, 128)),
@@ -1131,7 +1132,12 @@
                 part = held_terms[here][...].astype(f32)
                 found = part if found is None else found + part
                 here += 1
-            held_outs[place][at : at + rows] = found.astype(held_outs[place].dtype)
+            size, cols = held_outs[place].shape
+            for unit in range(cols // 128 if cols > 128 else 0):
+                lanes = slice(unit * 128, (unit + 1) * 128)
+                held_outs[place][:, lanes] = found[unit * size : (unit + 1) * size]
+            if cols == 128:
+                held_outs[place][at : at + rows] = found.astype(held_outs[place].dtype)
             at += rows
         store = pltpu.make_async_copy(held_outs[place], outs[place], out_sems.at[place])
         store.start()
@@ -1151,14 +1157,16 @@
         return len(arrays) - 1
 
     shapes, moved = [], 0
-    for dtype, jobs in outputs:
+    for dtype, jobs, tall in outputs:
         planned = []
         for rows, terms in jobs:
             planned.append((rows, [(number_of(array), start, bit) for array, start, bit in terms]))
             buffers += [pltpu.VMEM((rows, 128), array.dtype) for array, _, _ in terms]
             moved += rows * (1 + len(terms))
         plan.append(planned)
-        shapes.append(jax.ShapeDtypeStruct((sum(rows for rows, _ in jobs), 128), dtype))
+        total = sum(rows for rows, _ in jobs)
+        shape = (tall, total // tall * 128) if tall else (total, 128)
+        shapes.append(jax.ShapeDtypeStruct(shape, dtype))
     return pl.pallas_call(
         functools.partial(sum_kernel, plan, len(arrays)),
         in_specs=[core_spec] + unread(len(arrays)),
@@ -1167,7 +1175,7 @@
         scratch_shapes=buffers
         + [pltpu.VMEM(shape.shape, shape.dtype) for shape in shapes]
         + [pltpu.SemaphoreType.DMA((len(buffers),)), pltpu.SemaphoreType.DMA((len(plan),))],
-        compiler_params=pltpu.CompilerParams(vmem_limit_bytes=60 * MIB),
+        compiler_params=pltpu.CompilerParams(vmem_limit_bytes=121 * MIB // 2),
         name="sum_terms",
         cost_estimate=cost(3),
     )(bits, *arrays)
@@ -1175,7 +1183,7 @@
 
 def sum_jobs_plain(outputs, bits):
     results = []
-    for dtype, jobs in outputs:
+    for dtype, jobs, tall in outputs:
         pieces = []
         for rows, terms in jobs:
             found = [
@@ -1183,7 +1191,8 @@
                 for array, start, bit in terms
             ]
             pieces.append(sum(part.astype(f32) for part in found).astype(dtype))
-        results.append(pieces[0] if len(pieces) == 1 else jnp.concatenate(pieces, 0))
+        made = pieces[0] if len(pieces) == 1 else jnp.concatenate(pieces, 0)
+        results.append(columns_of(made.reshape(-1, tall, 128)) if tall else made)
     return results
 
 
@@ -1193,6 +1202,17 @@
     return (part, 1, [(keep, 0, keep.shape[0], []), (arrived, 0, send.shape[0], [])], send)
 
 
+def begin_together(parts, keep, send, sizes):
+    count = len(parts)
+    keep, send = keep.reshape(-1, 128), send.reshape(-1, 128)
+    rows = keep.shape[0] // count
+    arrived = swap(send, stage_order(0, sizes)[0], sizes)
+    return [
+        (part, 1, [(keep, at * rows, rows, []), (arrived, at * rows, rows, [])], send)
+        for at, part in enumerate(parts)
+    ]
+
+
 def begin_folded(part, slab, sizes):
     own = lax.axis_index("dp") & 1
     halves = [lax.dynamic_index_in_dim(slab, place, 0, keepdims=False) for place in (own, 1 - own)]
@@ -1205,7 +1225,7 @@
     return (None, 1, [(values, 0, len(values), []), (arrived, 0, len(values), [])], send)
 
 
-def advance(states, bits, sizes, plain, after=None):
+def advance(states, bits, sizes, plain, tall, after=None):
     last = len(stage_order(0, sizes))
     changed = {}
     fresh = []
@@ -1236,11 +1256,13 @@
         for number in members:
             ahead = [] if fresh[number][0] is None else [(bit_place(stage, sizes), True)]
             jobs.append(job(number, ahead))
-        outputs.append((bf16, jobs))
-    outputs += [(f32, [job(number, [])]) for number in finals]
+        outputs.append((bf16, jobs, 0))
+    outputs += [
+        (f32, [job(number, [])], 0 if fresh[number][0] is None else tall) for number in finals
+    ]
     made = (sum_jobs_plain if plain else sum_jobs)(outputs, bits)
     results = [None] * len(fresh)
-    for (stage, members), (_, jobs), sent in zip(groups.items(), outputs, made):
+    for (stage, members), (_, jobs, _), sent in zip(groups.items(), outputs, made):
         arrived = swap(sent, stage, sizes)
         start = 0
         for number, (rows, _) in zip(members, jobs):
@@ -1303,7 +1325,7 @@
     allowed, pick_mask = caption_layout(caption_lengths)
     pick_low = pick_mask.astype(bf16)
     pick_full = pick_mask.astype(f32)
-    mask = jnp.tile(allowed.astype(f32), (1, 1, 4))
+    mask = jnp.tile(allowed, (1, 1, 4)).astype(f32)
     inputs = hidden_states.reshape(row_count * slots, width)
     self_q, self_k, self_v, self_mix, first_sum, first_norm = self_forward(
         inputs, attn_weights, biases, norm_gains, mask
@@ -1491,7 +1513,7 @@
         [text_first] + sends(ffn),
     )
     plain = not fold
-    ffn = advance(ffn, bits, sizes, plain, cross_side)
+    ffn = advance(ffn, bits, sizes, plain, size, cross_side)
     cross_slabs = cross_weight_grad(
         core, image_features, image_ends, dkv, dkv_ends, folds, size, sends(ffn)
     )
@@ -1507,7 +1529,7 @@
             )
             for part in range(3)
         ]
-    ffn = advance(ffn, bits, sizes, plain, cross_slabs[0])
+    ffn = advance(ffn, bits, sizes, plain, size, cross_slabs[0])
     self_grads, self_branch, self_down, self_side = self_backward(
         attn_weights,
         norm_gains,
@@ -1532,7 +1554,7 @@
     ]
     used = sum(array.shape[0] for array in rows)
     packed = jnp.concatenate(rows + [jnp.zeros((-used % 64, 128), f32)], 0)
-    states = advance(ffn + cross, bits, sizes, plain, self_side)
+    states = advance(ffn + cross, bits, sizes, plain, size, self_side)
     vector = begin_whole(packed, sizes)
     half = (row_count, QUERIES, width)
     attn_slabs = attn_weight_grad(
@@ -1558,17 +1580,22 @@
             begin_folded(part, fold_pair(part, *slab, sizes), sizes)
             for part, slab in enumerate(attn_slabs)
         ]
-    states = advance(states + [vector], bits, sizes, plain, attn_slabs[0])
-    input_grad = input_gradient(attn_weights, self_grads, self_down, sends(states + attn))
-    ffn, cross, vector = states[:3], states[3:6], states[6]
+    ffn, cross = states[:3], states[3:6]
+    states = advance(ffn + cross + [vector], bits, sizes, plain, size, attn_slabs[0])
+    blocks = row_count // 4
+    begun = input_gradient(attn_weights, self_grads, self_down, sends(states), 0, 1)
+    *attn, vector = advance(attn + states[6:], bits, sizes, plain, size, begun)
+    input_grad = input_gradient(
+        attn_weights, self_grads, self_down, sends(attn), 1, blocks, [begun]
+    )
+    states = states[:3] + attn + states[3:6] + [vector]
     last = len(stage_orders[0])
-    states = ffn + attn + cross + [vector]
     done = [None] * len(states)
     places = list(range(len(states)))
     after = input_grad
-    while states:
+    while len(states) > 3:
         ready = [state[1] == last for state in states]
-        states = advance(states, bits, sizes, plain, after)
+        states = advance(states, bits, sizes, plain, size, after)
         after = None
         for place, state, end in zip(places, states, ready):
             if end:
@@ -1576,19 +1603,21 @@
         places = [place for place, end in zip(places, ready) if not end]
         states = [state for state, end in zip(states, ready) if not end]
     vector = done.pop()
-    shaped = [each.reshape(-1, size, 128) for each in done]
-    ffn_sums, attn_sums, cross_sums = shaped[:3], shaped[3:6], shaped[6:]
-    attn_grad = jnp.stack([columns_of(each) for each in attn_sums])
-    cross_grad = jnp.concatenate([columns_of(each) for each in cross_sums], 1)
-    ffn_in_grad = jnp.concatenate([columns_of(each[:8]) for each in ffn_sums], 1)
+    ffn_sums, cross_sums = done[:3], done[6:]
+    cross_grad = jnp.concatenate(cross_sums, 1)
+    chunk = ffn_in.shape[2] // 3
+    ffn_in_grad = jnp.concatenate([each[:, :chunk] for each in ffn_sums], 1)
     ffn_out_grad = jnp.concatenate(
         [
-            each[8:16].reshape(tall, 2, size, 128).transpose(0, 2, 1, 3).reshape(tall * size, -1)
+            each[:, chunk : 2 * chunk]
+            .reshape(size, tall, -1)
+            .transpose(1, 0, 2)
+            .reshape(tall * size, -1)
             for each in ffn_sums
         ],
         1,
     )
-    proj_grad = columns_of(ffn_sums[0][16:])
+    proj_grad = ffn_sums[0][:, 2 * chunk :]
     vectors = []
     start = 0
     for array, cols in zip(rows, (width,) * 4 + (ffn_in.shape[2],) * 2 + (projections.shape[2],) * 2):
@@ -1622,6 +1651,10 @@
         mine(jnp.concatenate(vectors[4:6], 0)),
         mine(jnp.concatenate(vectors[6:8], 0)),
     ]
+    attn_sums = advance(
+        states, bits, sizes, plain, size, (small, cross_grad, ffn_in_grad, ffn_out_grad, proj_grad)
+    )
+    attn_grad = jnp.stack(attn_sums)
     return (
         layer_out,
         row_loss,

time: 445 us -> 432 us (0.971)
  waiting for transfers between devices: 57.8 us -> 43.7 us
    ppermute x36 -> x35, waiting for transfers between devices: 50 us -> 35.9 us  [swap(): lax.ppermute(values, axis, [(i, i ^ 1 << bit) for i in range(sizes[axis])])]
    reshape x8 -> x3, local copies, waits for them, and re-layouts: 4.81 us -> 0.28 us  [shards(): ffn_out_grad = jnp.concatenate([each[:, chunk:2 * chunk].reshape(size, ta...]
    pallas_call x1 -> x2, Pallas kernels: 9.1 us -> 12.1 us  [input_gradient(): pl.pallas_call(ordered(input_grad_kernel, 3, len(order)), grid=(last - fi...]
    unnamed x101 -> x97, local copies, waits for them, and re-layouts: 25.8 us -> 26.7 us
    ppermute x36 -> x35, starting transfers between devices: 31.4 us -> 30.6 us  [swap(): lax.ppermute(values, axis, [(i, i ^ 1 << bit) for i in range(sizes[axis])])]
  transfers between devices with their start and end apart: 39 -> 38, of which waited for: 15 -> 14; matrix products, arithmetic and copies ran while one was open for 4% -> 5% of each run, Pallas kernels for 42% -> 45%
where the time goes in v7:
time: 432 us; the launch traced here: 424 us
  Pallas kernels  269 us (62%)
  starting transfers between devices  46.9 us (11%)
  waiting for transfers between devices  43.7 us (10%)
  local copies, waits for them, and re-layouts  43.3 us (10%)
  other arithmetic  12.3 us (3%)
  matrix products  6.99 us (2%)
    pallas_call x2, Pallas kernels, ffn_backward(): pl.pallas_call(functools.partial(ffn_backward_kernel, which, folds), grid...  51.1 us
    pallas_call x9, Pallas kernels, sum_jobs(): pl.pallas_call(functools.partial(sum_kernel, plan, len(arrays)), in_specs...  40.6 us
    pallas_call x1, Pallas kernels, cross_forward(): pl.pallas_call(cross_forward_kernel, grid=(rows // take,), in_specs=[pl.B...  37.5 us
    ppermute x35, waiting for transfers between devices, swap(): lax.ppermute(values, axis, [(i, i ^ 1 << bit) for i in range(sizes[axis])])  35.9 us
    pallas_call x1, Pallas kernels, cross_weight_grad(): pl.pallas_call(ordered(functools.partial(cross_weight_kernel, folds), 5,...  32.8 us
    ppermute x35, starting transfers between devices, swap(): lax.ppermute(values, axis, [(i, i ^ 1 << bit) for i in range(sizes[axis])])  30.6 us
    pallas_call x2, Pallas kernels, ffn_forward(): pl.pallas_call(functools.partial(ffn_forward_kernel, which), grid=(hidden...  29.9 us
    unnamed x97, local copies, waits for them, and re-layouts  26.7 us
  transfers between devices with their start and end apart: 38, of which 14 were waited for; matrix products, arithmetic and copies ran while one was open for 5% of the time, Pallas kernels for 45%

profile of v7, /device:TPU:0, one launch (start us, length us, event | category | flops | bytes accessed | tf_op | source)
XLA Modules:
  0.0 424.0 jit_solution(13778034073833241443)
XLA Ops:
  0.7 7.6 %copy.70.image_ref.refs_1_ = bf16[16,257,1408]{2,1,0:T(8,128)(2,1)S(1)} copy(bf16[16,257,1408]{2,0,1:T(8,128)(2,1)} %param.15) | data formatting | bytes 23158784 | tf_op args[1]
  8.3 4.3 %copy-done.5 = bf16[16,257,1408]{2,1,0:T(8,128)(2,1)} copy-done((bf16[16,257,1408]{2,1,0:T(8,128)(2,1)}, bf16[16,257,1408]{2,1,0:T(8,128)(2,1)S(1)}, u32[]{:S(2)}) %copy-start.5) | copy-done | bytes 11579416
  16.6 14.7 %self_forward.1 = (bf16[1024,768]{1,0:T(8,128)(2,1)}, bf16[1024,768]{1,0:T(8,128)(2,1)}, bf16[1024,768]{1,0:T(8,128)(2,1)}, bf16[1024,768]{1,0:T(8,128)(2,1)}, f32[1024,768]{1,0:T(8,128)}, /*index=5*/f32[1024,768]{1,0:T(8,128)}) custom-call(bf16[1024,768]{1,0:T(8,128)(2,1)} %bitcast.204, bf16[6,768,768]{2,1,0:T(8,128)(2,1)} %refs_0_.7, f32[12,768]{1,0:T(8,128)} %bias_ref.7, ...), custom_call_target="tpu_custom_call" | custom-call | flops 16499999744 | tf_op jit(solution)/shard_map/self_forward/pallas_call | solution.py:216
  31.3 14.9 %ffn_forward.2 = (bf16[512,3072]{1,0:T(8,128)(2,1)}, bf16[512,3072]{1,0:T(8,128)(2,1)}, f32[512,768]{1,0:T(8,128)}, bf16[16,64,768]{2,1,0:T(8,128)(2,1)}, f32[512,256]{1,0:T(8,128)}, /*index=5*/bf16[512,256]{1,0:T(8,128)(2,1)}) custom-call(f32[16,64,768]{2,1,0:T(8,128)} %bitcast.215, bf16[2,768,3072]{2,1,0:T(8,128)(2,1)} %in_ref.7, f32[2,3072]{1,0:T(2,128)} %in_bias_ref.3, ...), custom_call_target="tpu_custom_call" | custom-call | flops 16499999744 | tf_op jit(solution)/shard_map/ffn_forward/pallas_call | solution.py:822
  48.2 7.5 %all-to-all-start = ((bf16[32,32,256]{2,1,0:T(8,128)(2,1)}), bf16[32,32,256]{2,1,0:T(8,128)(2,1)S(1)}, u32[]{:S(2)}, u32[]{:S(2)}) async-start(bf16[32,32,256]{2,1,0:T(8,128)(2,1)} %tile.8), calls=%async_computation | async-start | bytes 1048576 | tf_op jit(solution)/shard_map/all_to_all | solution.py:1292
  55.7 37.5 %cross_forward.1 = (bf16[4096,768]{1,0:T(8,128)(2,1)}, bf16[4096,768]{1,0:T(8,128)(2,1)}, bf16[256,768]{1,0:T(8,128)(2,1)}, bf16[256,768]{1,0:T(8,128)(2,1)}, bf...) custom-call(bf16[16,257,1408]{2,1,0:T(8,128)(2,1)} %copy-done.5, ...), custom_call_target="tpu_custom_call" | custom-call | flops 41799999488 | tf_op jit(solution)/shard_map/cross_forward/pallas_call | solution.py:530
  93.2 15.0 %ffn_forward.3 = (bf16[512,3072]{1,0:T(8,128)(2,1)}, bf16[512,3072]{1,0:T(8,128)(2,1)}, f32[512,768]{1,0:T(8,128)}, bf16[16,64,768]{2,1,0:T(8,128)(2,1)}, f32[512,256]{1,0:T(8,128)}, /*index=5*/bf16[512,256]{1,0:T(8,128)(2,1)}) custom-call(f32[16,32,768]{2,1,0:T(8,128)} %bitcast.221, bf16[2,768,3072]{2,1,0:T(8,128)(2,1)} %in_ref.7, ...), custom_call_target="tpu_custom_call", output_to_operand_aliasing={{3}: (8, {})} | custom-call | flops 16499999744 | tf_op jit(solution)/shard_map/ffn_forward/pallas_call | solution.py:822
  112.4 5.9 %all-to-all-start.1 = ((f32[32,1,1024]{2,1,0:T(1,128)}), f32[32,1,1024]{2,1,0:T(1,128)S(1)}, u32[]{:S(2)}, u32[]{:S(2)}) async-start(f32[32,1,1024]{2,1,0:T(1,128)} %broadcast_in_dim.16), calls=%async_computation.1 | async-start | bytes 262144 | tf_op jit(solution)/shard_map/all_to_all | solution.py:1292
  119.2 7.8 %all-to-all-done.1 = f32[32,1,1024]{2,1,0:T(1,128)S(1)} async-done(((f32[32,1,1024]{2,1,0:T(1,128)}), f32[32,1,1024]{2,1,0:T(1,128)S(1)}, u32[]{:S(2)}, u32[]{:S(2)}) %all-to-all-start.1) | async-done | bytes 131104 | tf_op jit(solution)/shard_map/all_to_all | solution.py:1292
  131.0 2.8 all-to-all-start.2
  135.8 25.3 %ffn_backward.2 = (f32[16,32,768]{2,1,0:T(8,128)}, f32[48,128]{1,0:T(8,128)}, f32[24,128]{1,0:T(8,128)}, f32[2,128]{1,0:T(2,128)}, bf16[2,2,2,2,18,48,128]{6,5,4...) custom-call(s32[1]{0:T(128)} %bitcast.192, ...), custom_call_target="tpu_custom_call" | custom-call | flops 27499999232 | tf_op jit(solution)/shard_map/ffn_backward/pallas_call | solution.py:1001
  162.6 25.8 %ffn_backward.3 = (f32[16,32,768]{2,1,0:T(8,128)}, f32[48,128]{1,0:T(8,128)}, f32[24,128]{1,0:T(8,128)}, f32[2,128]{1,0:T(2,128)}, bf16[2,2,2,2,18,48,128]{6,5,4...) custom-call(s32[1]{0:T(128)} %bitcast.193, ...), custom_call_target="tpu_custom_call", output_to_operand_aliasing={{4}: (13, {}), {5}: (14, {}), {6}: (15, {}), {7}: (16, {}),... | custom-call | flops 27499999232 | tf_op jit(solution)/shard_map/ffn_backward/pallas_call | solution.py:1001
  189.2 18.9 %cross_backward.1 = (f32[16,32,768]{2,1,0:T(8,128)}, bf16[2,4096,768]{2,1,0:T(8,128)(2,1)}, bf16[2,256,768]{2,1,0:T(8,128)(2,1)}, bf16[512,768]{1,0:T(8,128)(2,1)}, f32[48,128]{1,0:T(8,128)}) custom-call(bf16[6,768,768]{2,1,0:T(8,128)(2,1)} %refs_0_.7, bf16[4096,768]{1,0:T(8,128)(2,1)} %get-tuple-element.153.refs_1_, ...), custom_call_target="tpu_custom_call" | custom-call | flops 20899999744 | tf_op jit(solution)/shard_map/cross_backward/pallas_call | solution.py:644
  209.9 7.2 %sum_terms.9 = (bf16[6912,128]{1,0:T(8,128)(2,1)}, bf16[6144,128]{1,0:T(8,128)(2,1)}, bf16[6144,128]{1,0:T(8,128)(2,1)}) custom-call(s32[5]{0:T(128)} %shift-right-arithmetic_and_fusion.bits_ref, bf16[13824,128]{1,0:T(8,128)(2,1)} %bitcast.124, bf16[13824,128]{1,0:T(8,128)(2,1)} %copy-done, bf16[12288,128]{1,0:T(8,128)(2,1)} %bitcast.129, ...), custom_call_target="tpu_custom_call" | custom-call | flops 3300000000 | tf_op jit(solution)/shard_map/sum_terms/pallas_call | solution.py:1170
  221.9 32.8 %cross_weight_grad.1 = (bf16[2,2,2,2,4,48,128]{6,5,4,3,2,1,0:T(8,128)(2,1)}, bf16[2,2,2,2,4,48,128]{6,5,4,3,2,1,0:T(8,128)(2,1)}, bf16[2,2,2,2,4,48,128]{6,5,4,3...) custom-call(s32[1]{0:T(128)} %bitcast.194, ...), custom_call_target="tpu_custom_call" | custom-call | flops 35200000000 | tf_op jit(solution)/shard_map/cross_weight_grad/pallas_call | solution.py:738
  259.4 5.2 %sum_terms.10 = (bf16[3456,128]{1,0:T(8,128)(2,1)}, bf16[3072,128]{1,0:T(8,128)(2,1)}, bf16[3072,128]{1,0:T(8,128)(2,1)}) custom-call(s32[5]{0:T(128)} %shift-right-arithmetic_and_fusion.bits_ref, bf16[13824,128]{1,0:T(8,128)(2,1)} %bitcast.125, bf16[13824,128]{1,0:T(8,128)(2,1)} %copy-done, bf16[6912,128]{1,0:T(8,128)(2,1)} %copy-done.1, ...), custom_call_target="tpu_custom_call" | custom-call | flops 3300000000 | tf_op jit(solution)/shard_map/sum_terms/pallas_call | solution.py:1170
  269.5 15.6 %self_backward.1 = (bf16[3,1024,768]{2,1,0:T(8,128)(2,1)}, bf16[1024,768]{1,0:T(8,128)(2,1)}, f32[1024,768]{1,0:T(8,128)}, f32[48,128]{1,0:T(8,128)}) custom-call(bf16[6,768,768]{2,1,0:T(8,128)(2,1)} %refs_0_.7, f32[4,768]{1,0:T(4,128)} %refs_1_.2, f32[16,64,256]{2,1,0:T(8,128)} %convert_element_type.56.mask_ref.refs_2_, ...), custom_call_target="tpu_custom_call" | custom-call | flops 17600000000 | tf_op jit(solution)/shard_map/self_backward/pallas_call | solution.py:306
  288.5 4.9 %sum_terms.11 = (bf16[1728,128]{1,0:T(8,128)(2,1)}, bf16[3072,128]{1,0:T(8,128)(2,1)}, bf16[3072,128]{1,0:T(8,128)(2,1)}, bf16[1152,128]{1,0:T(8,128)(2,1)}) custom-call(s32[5]{0:T(128)} %shift-right-arithmetic_and_fusion.bits_ref, bf16[13824,128]{1,0:T(8,128)(2,1)} %bitcast.126, bf16[13824,128]{1,0:T(8,128)(2,1)} %copy-done, bf16[6912,128]{1,0:T(8,128)(2,1)} %copy-done.1, ...), custom_call_target="tpu_custom_call" | custom-call | flops 3300000000 | tf_op jit(solution)/shard_map/sum_terms/pallas_call | solution.py:1170
  293.5 2.5 collective-permute-start.12
  299.2 15.7 %attn_weight_grad.1 = (bf16[2,2,2,2,6,48,128]{6,5,4,3,2,1,0:T(8,128)(2,1)}, bf16[2,2,2,2,6,48,128]{6,5,4,3,2,1,0:T(8,128)(2,1)}, bf16[2,2,2,2,6,48,128]{6,5,4,3,...) custom-call(s32[1]{0:T(128)} %bitcast.195, ...), custom_call_target="tpu_custom_call" | custom-call | flops 22000001024 | tf_op jit(solution)/shard_map/attn_weight_grad/pallas_call | solution.py:428
  318.6 6.7 %collective-permute-done.13.refs_7_.refs_22_.refs_18_ = bf16[3072,128]{1,0:T(8,128)(2,1)S(1)} collective-permute-done((bf16[3072,128]{1,0:T(8,128)(2,1)}, bf16[3072,128]{1,0:T(8,128)(2,1)S(1)}, u32[]{:S(2)}, u32[]{:S(2)}) %collective-permute-start.13) | collective-permute-done | bytes 786464 | tf_op jit(solution)/shard_map/ppermute | solution.py:1064
  327.1 4.1 sum_terms.12
  332.3 4.5 %input_gradient.2.refs_3_ = f32[1024,768]{1,0:T(8,128)} custom-call(bf16[6,768,768]{2,1,0:T(8,128)(2,1)} %refs_0_.7, bf16[3,1024,768]{2,1,0:T(8,128)(2,1)} %get-tuple-element.201.refs_2_.refs_1_, f32[1024,768]{1,0:T(8,128)} %get-tuple-element.202.refs_2_, bf16[1632,128]{1,0:T(8,128)(2,1)} %get-tuple-element.232.refs_3_, ...), custom_call_target="tpu_custom_call" | custom-call | flops 5500000256 | tf_op jit(solution)/shard_map/input_gradient/pallas_call | solution.py:354
  339.2 3.8 sum_terms.13
  347.5 7.6 %input_gradient.3 = f32[1024,768]{1,0:T(8,128)} custom-call(bf16[6,768,768]{2,1,0:T(8,128)(2,1)} %refs_0_.7, bf16[3,1024,768]{2,1,0:T(8,128)(2,1)} %get-tuple-element.201.refs_2_.refs_1_, f32[1024,768]{1,0:T(8,128)} %get-tuple-element.202.refs_2_, f32[1024,768]{1,0:T(8,128)} %input_gradient.2.refs_3_, ...), custom_call_target="tpu_custom_call", output_to_operand_aliasing={{}: (3, {})} | custom-call | flops 5500000256 | tf_op jit(solution)/shard_map/input_gradient/pallas_call | solution.py:354
  355.1 11.3 %collective-permute-done.26.refs_33_ = bf16[1536,128]{1,0:T(8,128)(2,1)S(1)} collective-permute-done((bf16[1536,128]{1,0:T(8,128)(2,1)}, bf16[1536,128]{1,0:T(8,128)(2,1)S(1)}, u32[]{:S(2)}, u32[]{:S(2)}) %collective-permute-start.26) | collective-permute-done | bytes 393248 | tf_op jit(solution)/shard_map/ppermute | solution.py:1064
  369.6 5.5 %sum_terms.14 = (bf16[1440,128]{1,0:T(8,128)(2,1)}, bf16[1792,128]{1,0:T(8,128)(2,1)}, bf16[1536,128]{1,0:T(8,128)(2,1)}, f32[48,2304]{1,0:T(8,128)}, f32[48,2048]{1,0:T(8,128)}, /*index=5*/f32[48,2048]{1,0:T(8,128)}) custom-call(s32[5]{0:T(128)} %shift-right-arithmetic_and_fusion.bits_ref, bf16[4608,128]{1,0:T(8,128)(2,1)} %bitcast.155, ...), custom_call_target="tpu_custom_call" | custom-call | flops 3300000000 | tf_op jit(solution)/shard_map/sum_terms/pallas_call | solution.py:1170
  386.6 3.5 sum_terms.15
  398.5 3.8 collective-permute-done.33.refs_19_
  402.9 3.4 sum_terms.16
  415.2 3.0 collective-permute-done.34.refs_5_
  418.8 2.9 sum_terms.17
  (242 shorter events, 90.0 us)
Async XLA Ops:
  48.2 61.7 %all-to-all-start = ((bf16[32,32,256]{2,1,0:T(8,128)(2,1)}), bf16[32,32,256]{2,1,0:T(8,128)(2,1)S(1)}, u32[]{:S(2)}, u32[]{:S(2)}) async-start(bf16[32,32,256]{2,1,0:T(8,128)(2,1)} %tile.8), calls=%async_computation | async-start | bytes 1048576 | tf_op jit(solution)/shard_map/all_to_all | solution.py:1292
  112.4 14.6 %all-to-all-start.1 = ((f32[32,1,1024]{2,1,0:T(1,128)}), f32[32,1,1024]{2,1,0:T(1,128)S(1)}, u32[]{:S(2)}, u32[]{:S(2)}) async-start(f32[32,1,1024]{2,1,0:T(1,128)} %broadcast_in_dim.16), calls=%async_computation.1 | async-start | bytes 262144 | tf_op jit(solution)/shard_map/all_to_all | solution.py:1292
  131.0 30.1 %all-to-all-start.2 = ((bf16[32,32,256]{2,1,0:T(8,128)(2,1)}), bf16[32,32,256]{2,1,0:T(8,128)(2,1)S(1)}, u32[]{:S(2)}, u32[]{:S(2)}) async-start(bf16[32,32,256]{2,1,0:T(8,128)(2,1)} %bitcast.180), calls=%async_computation.2 | async-start | bytes 1048576 | tf_op jit(solution)/shard_map/all_to_all | solution.py:1292
  188.4 19.7 %collective-permute-start = (bf16[13824,128]{1,0:T(8,128)(2,1)}, bf16[13824,128]{1,0:T(8,128)(2,1)S(1)}, u32[]{:S(2)}, u32[]{:S(2)}) collective-permute-start(bf16[13824,128]{1,0:T(8,128)(2,1)} %bitcast.198), channel_id=1, source_target_pairs={{0,2},{2,0},{4,6},{6,4},{8,10},{10,8},{12,14},{14,12},{16,18},{18,... | collective-permute-start | bytes 10616840 | tf_op jit(solution)/shard_map/ppermute | solution.py:1064
  188.7 19.4 %collective-permute-start.1 = (bf16[12288,128]{1,0:T(8,128)(2,1)}, bf16[12288,128]{1,0:T(8,128)(2,1)}, u32[]{:S(2)}, u32[]{:S(2)}) collective-permute-start(bf16[12288,128]{1,0:T(8,128)(2,1)} %bitcast.200), channel_id=1, source_target_pairs={{0,2},{2,0},{4,6},{6,4},{8,10},{10,8},{12,14},{14,12},{16,18},{18,... | collective-permute-start | bytes 9437192 | tf_op jit(solution)/shard_map/ppermute | solution.py:1064
  188.9 19.1 %collective-permute-start.2 = (bf16[12288,128]{1,0:T(8,128)(2,1)}, bf16[12288,128]{1,0:T(8,128)(2,1)}, u32[]{:S(2)}, u32[]{:S(2)}) collective-permute-start(bf16[12288,128]{1,0:T(8,128)(2,1)} %bitcast.202), channel_id=1, source_target_pairs={{0,2},{2,0},{4,6},{6,4},{8,10},{10,8},{12,14},{14,12},{16,18},{18,... | collective-permute-start | bytes 9437192 | tf_op jit(solution)/shard_map/ppermute | solution.py:1064
  217.1 41.1 %collective-permute-start.3 = (bf16[6912,128]{1,0:T(8,128)(2,1)}, bf16[6912,128]{1,0:T(8,128)(2,1)S(1)}, u32[]{:S(2)}, u32[]{:S(2)}) collective-permute-start(bf16[6912,128]{1,0:T(8,128)(2,1)} %get-tuple-element.186.refs_5_), channel_id=1, source_target_pairs={{0,4},{2,6},{4,0},{6,2},{8,12},{10,14},{12,8},{14,10},{16,20},{18,... | collective-permute-start | bytes 5308424 | tf_op jit(solution)/shard_map/ppermute | solution.py:1064
  218.8 36.5 %collective-permute-start.4 = (bf16[6144,128]{1,0:T(8,128)(2,1)}, bf16[6144,128]{1,0:T(8,128)(2,1)S(1)}, u32[]{:S(2)}, u32[]{:S(2)}) collective-permute-start(bf16[6144,128]{1,0:T(8,128)(2,1)} %get-tuple-element.189.refs_6_), channel_id=1, source_target_pairs={{0,8},{2,10},{4,12},{6,14},{8,0},{10,2},{12,4},{14,6},{16,24},{18,... | collective-permute-start | bytes 4718600 | tf_op jit(solution)/shard_map/ppermute | solution.py:1064
  220.3 36.4 %collective-permute-start.5 = (bf16[6144,128]{1,0:T(8,128)(2,1)}, bf16[6144,128]{1,0:T(8,128)(2,1)}, u32[]{:S(2)}, u32[]{:S(2)}) collective-permute-start(bf16[6144,128]{1,0:T(8,128)(2,1)} %get-tuple-element.190.refs_7_), channel_id=1, source_target_pairs={{0,1},{1,0},{2,3},{3,2},{4,5},{5,4},{6,7},{7,6},{8,9},{9,8},{10,11... | collective-permute-start | bytes 4718600 | tf_op jit(solution)/shard_map/ppermute | solution.py:1064
  254.7 13.3 %collective-permute-start.8 = (bf16[3072,128]{1,0:T(8,128)(2,1)}, bf16[3072,128]{1,0:T(8,128)(2,1)}, u32[]{:S(2)}, u32[]{:S(2)}) collective-permute-start(bf16[3072,128]{1,0:T(8,128)(2,1)} %bitcast.209), channel_id=1, source_target_pairs={{0,2},{2,0},{4,6},{6,4},{8,10},{10,8},{12,14},{14,12},{16,18},{18,... | collective-permute-start | bytes 2359304 | tf_op jit(solution)/shard_map/ppermute | solution.py:1064
  254.8 30.4 %collective-permute-start.10 = (bf16[3072,128]{1,0:T(8,128)(2,1)}, bf16[3072,128]{1,0:T(8,128)(2,1)}, u32[]{:S(2)}, u32[]{:S(2)}) collective-permute-start(bf16[3072,128]{1,0:T(8,128)(2,1)} %bitcast.211), channel_id=1, source_target_pairs={{0,2},{2,0},{4,6},{6,4},{8,10},{10,8},{12,14},{14,12},{16,18},{18,... | collective-permute-start | bytes 2359304 | tf_op jit(solution)/shard_map/ppermute | solution.py:1064
  255.4 29.8 %collective-permute-start.11 = (bf16[2304,128]{1,0:T(8,128)(2,1)}, bf16[2304,128]{1,0:T(8,128)(2,1)}, u32[]{:S(2)}, u32[]{:S(2)}) collective-permute-start(bf16[2304,128]{1,0:T(8,128)(2,1)} %bitcast.213), channel_id=1, source_target_pairs={{0,2},{2,0},{4,6},{6,4},{8,10},{10,8},{12,14},{14,12},{16,18},{18,... | collective-permute-start | bytes 1769480 | tf_op jit(solution)/shard_map/ppermute | solution.py:1064
  264.6 22.4 %collective-permute-start.6 = (bf16[3456,128]{1,0:T(8,128)(2,1)}, bf16[3456,128]{1,0:T(8,128)(2,1)S(1)}, u32[]{:S(2)}, u32[]{:S(2)}) collective-permute-start(bf16[3456,128]{1,0:T(8,128)(2,1)} %get-tuple-element.195.refs_9_), channel_id=1, source_target_pairs={{0,8},{2,10},{4,12},{6,14},{8,0},{10,2},{12,4},{14,6},{16,24},{18,... | collective-permute-start | bytes 2654216 | tf_op jit(solution)/shard_map/ppermute | solution.py:1064
  266.5 20.6 %collective-permute-start.7 = (bf16[3072,128]{1,0:T(8,128)(2,1)}, bf16[3072,128]{1,0:T(8,128)(2,1)S(1)}, u32[]{:S(2)}, u32[]{:S(2)}) collective-permute-start(bf16[3072,128]{1,0:T(8,128)(2,1)} %get-tuple-element.196.refs_10_), channel_id=1, source_target_pairs={{0,1},{1,0},{2,3},{3,2},{4,5},{5,4},{6,7},{7,6},{8,9},{9,8},{10,11... | collective-permute-start | bytes 2359304 | tf_op jit(solution)/shard_map/ppermute | solution.py:1064
  268.0 19.1 %collective-permute-start.9 = (bf16[3072,128]{1,0:T(8,128)(2,1)}, bf16[3072,128]{1,0:T(8,128)(2,1)S(1)}, u32[]{:S(2)}, u32[]{:S(2)}) collective-permute-start(bf16[3072,128]{1,0:T(8,128)(2,1)} %get-tuple-element.197.refs_11_), channel_id=1, source_target_pairs={{0,4},{2,6},{4,0},{6,2},{8,12},{10,14},{12,8},{14,10},{16,20},{18,... | collective-permute-start | bytes 2359304 | tf_op jit(solution)/shard_map/ppermute | solution.py:1064
  287.0 27.8 %collective-permute-start.16 = (bf16[256,128]{1,0:T(8,128)(2,1)}, bf16[256,128]{1,0:T(8,128)(2,1)S(1)}, u32[]{:S(2)}, u32[]{:S(2)}) collective-permute-start(bf16[256,128]{1,0:T(8,128)(2,1)} %convert_element_type.66.refs_13_), channel_id=1, source_target_pairs={{0,2},{2,0},{4,6},{6,4},{8,10},{10,8},{12,14},{14,12},{16,18},{18,... | collective-permute-start | bytes 196616 | tf_op jit(solution)/shard_map/ppermute | solution.py:1064
  293.5 23.3 %collective-permute-start.12 = (bf16[1728,128]{1,0:T(8,128)(2,1)}, bf16[1728,128]{1,0:T(8,128)(2,1)S(1)}, u32[]{:S(2)}, u32[]{:S(2)}) collective-permute-start(bf16[1728,128]{1,0:T(8,128)(2,1)} %get-tuple-element.212.refs_9_), channel_id=1, source_target_pairs={{0,16},{2,18},{4,20},{6,22},{8,24},{10,26},{12,28},{14,30},{16,0},... | collective-permute-start | bytes 1327112 | tf_op jit(solution)/shard_map/ppermute | solution.py:1064
  296.0 29.3 %collective-permute-start.13 = (bf16[3072,128]{1,0:T(8,128)(2,1)}, bf16[3072,128]{1,0:T(8,128)(2,1)S(1)}, u32[]{:S(2)}, u32[]{:S(2)}) collective-permute-start(bf16[3072,128]{1,0:T(8,128)(2,1)} %get-tuple-element.218.refs_11_), channel_id=1, source_target_pairs={{0,8},{2,10},{4,12},{6,14},{8,0},{10,2},{12,4},{14,6},{16,24},{18,... | collective-permute-start | bytes 2359304 | tf_op jit(solution)/shard_map/ppermute | solution.py:1064
  296.5 28.8 %collective-permute-start.14 = (bf16[3072,128]{1,0:T(8,128)(2,1)}, bf16[3072,128]{1,0:T(8,128)(2,1)S(1)}, u32[]{:S(2)}, u32[]{:S(2)}) collective-permute-start(bf16[3072,128]{1,0:T(8,128)(2,1)} %get-tuple-element.217.refs_10_), channel_id=1, source_target_pairs={{0,4},{2,6},{4,0},{6,2},{8,12},{10,14},{12,8},{14,10},{16,20},{18,... | collective-permute-start | bytes 2359304 | tf_op jit(solution)/shard_map/ppermute | solution.py:1064
  297.6 17.9 %collective-permute-start.15 = (bf16[1152,128]{1,0:T(8,128)(2,1)}, bf16[1152,128]{1,0:T(8,128)(2,1)S(1)}, u32[]{:S(2)}, u32[]{:S(2)}) collective-permute-start(bf16[1152,128]{1,0:T(8,128)(2,1)} %get-tuple-element.219.refs_12_), channel_id=1, source_target_pairs={{0,1},{1,0},{2,3},{3,2},{4,5},{5,4},{6,7},{7,6},{8,9},{9,8},{10,11... | collective-permute-start | bytes 884744 | tf_op jit(solution)/shard_map/ppermute | solution.py:1064
  315.5 22.6 %collective-permute-start.17 = (bf16[4608,128]{1,0:T(8,128)(2,1)}, bf16[4608,128]{1,0:T(8,128)(2,1)S(1)}, u32[]{:S(2)}, u32[]{:S(2)}) collective-permute-start(bf16[4608,128]{1,0:T(8,128)(2,1)} %bitcast.208), channel_id=1, source_target_pairs={{0,2},{2,0},{4,6},{6,4},{8,10},{10,8},{12,14},{14,12},{16,18},{18,... | collective-permute-start | bytes 3538952 | tf_op jit(solution)/shard_map/ppermute | solution.py:1064
  315.5 22.6 %collective-permute-start.18 = (bf16[4608,128]{1,0:T(8,128)(2,1)}, bf16[4608,128]{1,0:T(8,128)(2,1)}, u32[]{:S(2)}, u32[]{:S(2)}) collective-permute-start(bf16[4608,128]{1,0:T(8,128)(2,1)} %bitcast.207), channel_id=1, source_target_pairs={{0,2},{2,0},{4,6},{6,4},{8,10},{10,8},{12,14},{14,12},{16,18},{18,... | collective-permute-start | bytes 3538952 | tf_op jit(solution)/shard_map/ppermute | solution.py:1064
  316.8 21.4 %collective-permute-start.20 = (bf16[4608,128]{1,0:T(8,128)(2,1)}, bf16[4608,128]{1,0:T(8,128)(2,1)}, u32[]{:S(2)}, u32[]{:S(2)}) collective-permute-start(bf16[4608,128]{1,0:T(8,128)(2,1)} %bitcast.206), channel_id=1, source_target_pairs={{0,2},{2,0},{4,6},{6,4},{8,10},{10,8},{12,14},{14,12},{16,18},{18,... | collective-permute-start | bytes 3538952 | tf_op jit(solution)/shard_map/ppermute | solution.py:1064
  331.9 15.6 %collective-permute-start.23 = (bf16[768,128]{1,0:T(8,128)(2,1)}, bf16[768,128]{1,0:T(8,128)(2,1)S(1)}, u32[]{:S(2)}, u32[]{:S(2)}) collective-permute-start(bf16[768,128]{1,0:T(8,128)(2,1)} %get-tuple-element.234.refs_5_), channel_id=1, source_target_pairs={{0,8},{2,10},{4,12},{6,14},{8,0},{10,2},{12,4},{14,6},{16,24},{18,... | collective-permute-start | bytes 589832 | tf_op jit(solution)/shard_map/ppermute | solution.py:1064
  343.1 24.6 %collective-permute-start.21 = (bf16[2304,128]{1,0:T(8,128)(2,1)}, bf16[2304,128]{1,0:T(8,128)(2,1)S(1)}, u32[]{:S(2)}, u32[]{:S(2)}) collective-permute-start(bf16[2304,128]{1,0:T(8,128)(2,1)} %get-tuple-element.245.refs_4_), channel_id=1, source_target_pairs={{0,4},{2,6},{4,0},{6,2},{8,12},{10,14},{12,8},{14,10},{16,20},{18,... | collective-permute-start | bytes 1769480 | tf_op jit(solution)/shard_map/ppermute | solution.py:1064
  343.4 24.2 %collective-permute-start.22 = (bf16[2560,128]{1,0:T(8,128)(2,1)}, bf16[2560,128]{1,0:T(8,128)(2,1)S(1)}, u32[]{:S(2)}, u32[]{:S(2)}) collective-permute-start(bf16[2560,128]{1,0:T(8,128)(2,1)} %get-tuple-element.246.refs_5_), channel_id=1, source_target_pairs={{0,8},{2,10},{4,12},{6,14},{8,0},{10,2},{12,4},{14,6},{16,24},{18,... | collective-permute-start | bytes 1966088 | tf_op jit(solution)/shard_map/ppermute | solution.py:1064
  345.0 22.7 %collective-permute-start.24 = (bf16[2304,128]{1,0:T(8,128)(2,1)}, bf16[2304,128]{1,0:T(8,128)(2,1)S(1)}, u32[]{:S(2)}, u32[]{:S(2)}) collective-permute-start(bf16[2304,128]{1,0:T(8,128)(2,1)} %get-tuple-element.247.refs_6_), channel_id=1, source_target_pairs={{0,1},{1,0},{2,3},{3,2},{4,5},{5,4},{6,7},{7,6},{8,9},{9,8},{10,11... | collective-permute-start | bytes 1769480 | tf_op jit(solution)/shard_map/ppermute | solution.py:1064
  346.0 21.6 %collective-permute-start.25 = (bf16[1632,128]{1,0:T(8,128)(2,1)S(1)}, bf16[1632,128]{1,0:T(8,128)(2,1)S(1)}, u32[]{:S(2)}, u32[]{:S(2)}) collective-permute-start(bf16[1632,128]{1,0:T(8,128)(2,1)S(1)} %copy-done.44), channel_id=1, source_target_pairs={{0,1},{1,0},{2,3},{3,2},{4,5},{5,4},{6,7},{7,6},{8,9},{9,8},{10,11... | collective-permute-start | bytes 1253384 | tf_op jit(solution)/shard_map/ppermute | solution.py:1064
  347.5 18.9 %collective-permute-start.26 = (bf16[1536,128]{1,0:T(8,128)(2,1)}, bf16[1536,128]{1,0:T(8,128)(2,1)S(1)}, u32[]{:S(2)}, u32[]{:S(2)}) collective-permute-start(bf16[1536,128]{1,0:T(8,128)(2,1)} %get-tuple-element.233.refs_4_), channel_id=1, source_target_pairs={{0,16},{2,18},{4,20},{6,22},{8,24},{10,26},{12,28},{14,30},{16,0},... | collective-permute-start | bytes 1179656 | tf_op jit(solution)/shard_map/ppermute | solution.py:1064
  375.9 9.9 %collective-permute-start.28 = (bf16[1792,128]{1,0:T(8,128)(2,1)}, bf16[1792,128]{1,0:T(8,128)(2,1)S(1)}, u32[]{:S(2)}, u32[]{:S(2)}) collective-permute-start(bf16[1792,128]{1,0:T(8,128)(2,1)} %get-tuple-element.256), channel_id=1, source_target_pairs={{0,1},{1,0},{2,3},{3,2},{4,5},{5,4},{6,7},{7,6},{8,9},{9,8},{10,11... | collective-permute-start | bytes 1376264 | tf_op jit(solution)/shard_map/ppermute | solution.py:1064
  393.3 9.0 %collective-permute-start.33 = (bf16[784,128]{1,0:T(8,128)(2,1)}, bf16[784,128]{1,0:T(8,128)(2,1)S(1)}, u32[]{:S(2)}, u32[]{:S(2)}) collective-permute-start(bf16[784,128]{1,0:T(8,128)(2,1)} %get-tuple-element.261), channel_id=1, source_target_pairs={{0,16},{2,18},{4,20},{6,22},{8,24},{10,26},{12,28},{14,30},{16,0},... | collective-permute-start | bytes 602120 | tf_op jit(solution)/shard_map/ppermute | solution.py:1064
  409.4 8.8 %collective-permute-start.34 = (bf16[864,128]{1,0:T(8,128)(2,1)}, bf16[864,128]{1,0:T(8,128)(2,1)S(1)}, u32[]{:S(2)}, u32[]{:S(2)}) collective-permute-start(bf16[864,128]{1,0:T(8,128)(2,1)} %get-tuple-element.262), channel_id=1, source_target_pairs={{0,16},{2,18},{4,20},{6,22},{8,24},{10,26},{12,28},{14,30},{16,0},... | collective-permute-start | bytes 663560 | tf_op jit(solution)/shard_map/ppermute | solution.py:1064
  (52 other events, 323.1 us)

commit v8 on v7

--- a/solution.py
+++ b/solution.py
@@ -166,7 +166,7 @@
 
 GROUPS = HEADS // 4
 SELF_ROWS = 4
-CROSS_ROWS = 4
+CROSS_ROWS = 8
 SELF_BACK_ROWS = 4
 CROSS_BACK_ROWS = 4
 
@@ -193,7 +193,7 @@
             for r, rows, cols in spots
         ]
         probs = [
-            columns_softmax(jnp.where(mask_ref[r] > 0.0, score, blocked)).astype(bf16)
+            columns_softmax(jnp.where(mask_ref[r].astype(f32) > 0.0, score, blocked)).astype(bf16)
             for (r, rows, cols), score in zip(spots, scores)
         ]
         mixed = [dot_tn(prob, v_ref[rows, cols]) for (r, rows, cols), prob in zip(spots, probs)]
@@ -275,7 +275,7 @@
         scores = [dot_nt(k_ref[spot[1:]], turned) for spot, turned in zip(spots, queries)]
         dprobs = [dot_nt(v_ref[spot[1:]], turned) for spot, turned in zip(spots, outs)]
         probs = [
-            columns_softmax(jnp.where(mask_ref[spot[0]] > 0.0, score, blocked))
+            columns_softmax(jnp.where(mask_ref[spot[0]].astype(f32) > 0.0, score, blocked))
             for spot, score in zip(spots, scores)
         ]
         for spot, prob, turned in zip(spots, probs, outs):
@@ -519,7 +519,7 @@
     rows, patches, vis = images.shape
     main = patches - 1
     width = norm.shape[-1]
-    take = 4
+    take = 8
     keys = pl.BlockSpec((take * main, width), lambda i: (i, 0))
     tails = pl.BlockSpec((take * TAIL, width), lambda i: (i, 0))
     tile = pl.BlockSpec((take * QUERIES, width), lambda i: (i, 0))
@@ -973,6 +973,7 @@
     embed = projections.shape[2]
     chunk = hidden // 3
     slabs = list(slabs)
+    before_spec = held(before.shape, lambda j: (0, 0))
     if folds is None:
         weight_specs = [
             pl.BlockSpec((chunk // 128, width, 128), lambda j: (j, 0, 0)),
@@ -1005,7 +1006,7 @@
             core_spec,
             held((rows, QUERIES, width), lambda j: (0, part, 0)),
             held((tokens, width), lambda j: (0, 0)),
-            held(before.shape, lambda j: (0, 0)),
+            before_spec,
             held((rows, QUERIES, width), lambda j: (0, which, 0)),
             held((rows, QUERIES, width), lambda j: (0, which, 0)),
             held((tokens, embed), lambda j: (0, 0)),
@@ -1325,7 +1326,7 @@
     allowed, pick_mask = caption_layout(caption_lengths)
     pick_low = pick_mask.astype(bf16)
     pick_full = pick_mask.astype(f32)
-    mask = jnp.tile(allowed, (1, 1, 4)).astype(f32)
+    mask = jnp.tile(allowed.astype(bf16), (1, 1, 4))
     inputs = hidden_states.reshape(row_count * slots, width)
     self_q, self_k, self_v, self_mix, first_sum, first_norm = self_forward(
         inputs, attn_weights, biases, norm_gains, mask
@@ -1457,7 +1458,7 @@
         core,
         first_norm,
         fourth_sum,
-        fourth_sum,
+        norm_gains,
         layer_out,
         out_grad,
         caption_raw_grad.reshape(row_count * TEXT, -1),

time: 432 us -> 430 us (level)
  no operation moved by 1% of the time
where the time goes in v8:
time: 430 us; the launch traced here: 422 us
  Pallas kernels  268 us (62%)
  starting transfers between devices  46.5 us (11%)
  waiting for transfers between devices  44.2 us (10%)
  local copies, waits for them, and re-layouts  42.7 us (10%)
  other arithmetic  12.2 us (3%)
  matrix products  6.96 us (2%)
    pallas_call x2, Pallas kernels, ffn_backward(): pl.pallas_call(functools.partial(ffn_backward_kernel, which, folds), grid...  50.4 us
    pallas_call x9, Pallas kernels, sum_jobs(): pl.pallas_call(functools.partial(sum_kernel, plan, len(arrays)), in_specs...  40.6 us
    pallas_call x1, Pallas kernels, cross_forward(): pl.pallas_call(cross_forward_kernel, grid=(rows // take,), in_specs=[pl.B...  37.3 us
    ppermute x35, waiting for transfers between devices, swap(): lax.ppermute(values, axis, [(i, i ^ 1 << bit) for i in range(sizes[axis])])  36.3 us
    pallas_call x1, Pallas kernels, cross_weight_grad(): pl.pallas_call(ordered(functools.partial(cross_weight_kernel, folds), 5,...  32.7 us
    ppermute x35, starting transfers between devices, swap(): lax.ppermute(values, axis, [(i, i ^ 1 << bit) for i in range(sizes[axis])])  30.6 us
    pallas_call x2, Pallas kernels, ffn_forward(): pl.pallas_call(functools.partial(ffn_forward_kernel, which), grid=(hidden...  29.9 us
    unnamed x97, local copies, waits for them, and re-layouts  26.7 us
  transfers between devices with their start and end apart: 38, of which 14 were waited for; matrix products, arithmetic and copies ran while one was open for 5% of the time, Pallas kernels for 45%

profile of v8, /device:TPU:0, one launch (start us, length us, event | category | flops | bytes accessed | tf_op | source)
XLA Modules:
  0.0 422.2 jit_solution(15158608220937463482)
XLA Ops:
  0.7 7.6 %copy.70.image_ref.refs_1_ = bf16[16,257,1408]{2,1,0:T(8,128)(2,1)S(1)} copy(bf16[16,257,1408]{2,0,1:T(8,128)(2,1)} %param.15) | data formatting | bytes 23158784 | tf_op args[1]
  8.3 4.3 %copy-done.5 = bf16[16,257,1408]{2,1,0:T(8,128)(2,1)} copy-done((bf16[16,257,1408]{2,1,0:T(8,128)(2,1)}, bf16[16,257,1408]{2,1,0:T(8,128)(2,1)S(1)}, u32[]{:S(2)}) %copy-start.5) | copy-done | bytes 11579416
  16.0 14.7 %self_forward.1 = (bf16[1024,768]{1,0:T(8,128)(2,1)}, bf16[1024,768]{1,0:T(8,128)(2,1)}, bf16[1024,768]{1,0:T(8,128)(2,1)}, bf16[1024,768]{1,0:T(8,128)(2,1)}, f32[1024,768]{1,0:T(8,128)}, /*index=5*/f32[1024,768]{1,0:T(8,128)}) custom-call(bf16[1024,768]{1,0:T(8,128)(2,1)} %bitcast.204, bf16[6,768,768]{2,1,0:T(8,128)(2,1)} %refs_0_.7, f32[12,768]{1,0:T(8,128)} %bias_ref.7, ...), custom_call_target="tpu_custom_call" | custom-call | flops 16499999744 | tf_op jit(solution)/shard_map/self_forward/pallas_call | solution.py:216
  30.7 14.9 %ffn_forward.2 = (bf16[512,3072]{1,0:T(8,128)(2,1)}, bf16[512,3072]{1,0:T(8,128)(2,1)}, f32[512,768]{1,0:T(8,128)}, bf16[16,64,768]{2,1,0:T(8,128)(2,1)}, f32[512,256]{1,0:T(8,128)}, /*index=5*/bf16[512,256]{1,0:T(8,128)(2,1)}) custom-call(f32[16,64,768]{2,1,0:T(8,128)} %bitcast.215, bf16[2,768,3072]{2,1,0:T(8,128)(2,1)} %in_ref.7, f32[2,3072]{1,0:T(2,128)} %in_bias_ref.3, ...), custom_call_target="tpu_custom_call" | custom-call | flops 16499999744 | tf_op jit(solution)/shard_map/ffn_forward/pallas_call | solution.py:822
  47.6 7.3 %all-to-all-start = ((bf16[32,32,256]{2,1,0:T(8,128)(2,1)}), bf16[32,32,256]{2,1,0:T(8,128)(2,1)S(1)}, u32[]{:S(2)}, u32[]{:S(2)}) async-start(bf16[32,32,256]{2,1,0:T(8,128)(2,1)} %tile.20), calls=%async_computation | async-start | bytes 1048576 | tf_op jit(solution)/shard_map/all_to_all | solution.py:1293
  54.9 37.3 %cross_forward.1 = (bf16[4096,768]{1,0:T(8,128)(2,1)}, bf16[4096,768]{1,0:T(8,128)(2,1)}, bf16[256,768]{1,0:T(8,128)(2,1)}, bf16[256,768]{1,0:T(8,128)(2,1)}, bf...) custom-call(bf16[16,257,1408]{2,1,0:T(8,128)(2,1)} %copy-done.5, ...), custom_call_target="tpu_custom_call" | custom-call | flops 41799999488 | tf_op jit(solution)/shard_map/cross_forward/pallas_call | solution.py:530
  92.3 15.0 %ffn_forward.3 = (bf16[512,3072]{1,0:T(8,128)(2,1)}, bf16[512,3072]{1,0:T(8,128)(2,1)}, f32[512,768]{1,0:T(8,128)}, bf16[16,64,768]{2,1,0:T(8,128)(2,1)}, f32[512,256]{1,0:T(8,128)}, /*index=5*/bf16[512,256]{1,0:T(8,128)(2,1)}) custom-call(f32[16,32,768]{2,1,0:T(8,128)} %bitcast.221, bf16[2,768,3072]{2,1,0:T(8,128)(2,1)} %in_ref.7, ...), custom_call_target="tpu_custom_call", output_to_operand_aliasing={{3}: (8, {})} | custom-call | flops 16499999744 | tf_op jit(solution)/shard_map/ffn_forward/pallas_call | solution.py:822
  111.4 5.8 %all-to-all-start.1 = ((f32[32,1,1024]{2,1,0:T(1,128)}), f32[32,1,1024]{2,1,0:T(1,128)S(1)}, u32[]{:S(2)}, u32[]{:S(2)}) async-start(f32[32,1,1024]{2,1,0:T(1,128)} %broadcast_in_dim.16), calls=%async_computation.1 | async-start | bytes 262144 | tf_op jit(solution)/shard_map/all_to_all | solution.py:1293
  118.0 7.9 %all-to-all-done.1 = f32[32,1,1024]{2,1,0:T(1,128)S(1)} async-done(((f32[32,1,1024]{2,1,0:T(1,128)}), f32[32,1,1024]{2,1,0:T(1,128)S(1)}, u32[]{:S(2)}, u32[]{:S(2)}) %all-to-all-start.1) | async-done | bytes 131104 | tf_op jit(solution)/shard_map/all_to_all | solution.py:1293
  129.9 2.8 all-to-all-start.2
  134.7 25.2 %ffn_backward.2 = (f32[16,32,768]{2,1,0:T(8,128)}, f32[48,128]{1,0:T(8,128)}, f32[24,128]{1,0:T(8,128)}, f32[2,128]{1,0:T(2,128)}, bf16[2,2,2,2,18,48,128]{6,5,4...) custom-call(s32[1]{0:T(128)} %bitcast.192, ...), custom_call_target="tpu_custom_call" | custom-call | flops 27499999232 | tf_op jit(solution)/shard_map/ffn_backward/pallas_call | solution.py:1002
  161.4 25.2 %ffn_backward.3 = (f32[16,32,768]{2,1,0:T(8,128)}, f32[48,128]{1,0:T(8,128)}, f32[24,128]{1,0:T(8,128)}, f32[2,128]{1,0:T(2,128)}, bf16[2,2,2,2,18,48,128]{6,5,4...) custom-call(s32[1]{0:T(128)} %bitcast.193, ...), custom_call_target="tpu_custom_call", output_to_operand_aliasing={{4}: (13, {}), {5}: (14, {}), {6}: (15, {}), {7}: (16, {}),... | custom-call | flops 27499999232 | tf_op jit(solution)/shard_map/ffn_backward/pallas_call | solution.py:1002
  187.4 18.9 %cross_backward.1 = (f32[16,32,768]{2,1,0:T(8,128)}, bf16[2,4096,768]{2,1,0:T(8,128)(2,1)}, bf16[2,256,768]{2,1,0:T(8,128)(2,1)}, bf16[512,768]{1,0:T(8,128)(2,1)}, f32[48,128]{1,0:T(8,128)}) custom-call(bf16[6,768,768]{2,1,0:T(8,128)(2,1)} %refs_0_.7, bf16[4096,768]{1,0:T(8,128)(2,1)} %get-tuple-element.153.refs_1_, ...), custom_call_target="tpu_custom_call" | custom-call | flops 20899999744 | tf_op jit(solution)/shard_map/cross_backward/pallas_call | solution.py:644
  208.1 7.2 %sum_terms.9 = (bf16[6912,128]{1,0:T(8,128)(2,1)}, bf16[6144,128]{1,0:T(8,128)(2,1)}, bf16[6144,128]{1,0:T(8,128)(2,1)}) custom-call(s32[5]{0:T(128)} %shift-right-arithmetic_and_fusion.bits_ref, bf16[13824,128]{1,0:T(8,128)(2,1)} %bitcast.124, bf16[13824,128]{1,0:T(8,128)(2,1)} %copy-done, bf16[12288,128]{1,0:T(8,128)(2,1)} %bitcast.129, ...), custom_call_target="tpu_custom_call" | custom-call | flops 3300000000 | tf_op jit(solution)/shard_map/sum_terms/pallas_call | solution.py:1171
  220.0 32.7 %cross_weight_grad.1 = (bf16[2,2,2,2,4,48,128]{6,5,4,3,2,1,0:T(8,128)(2,1)}, bf16[2,2,2,2,4,48,128]{6,5,4,3,2,1,0:T(8,128)(2,1)}, bf16[2,2,2,2,4,48,128]{6,5,4,3...) custom-call(s32[1]{0:T(128)} %bitcast.194, ...), custom_call_target="tpu_custom_call" | custom-call | flops 35200000000 | tf_op jit(solution)/shard_map/cross_weight_grad/pallas_call | solution.py:738
  257.6 5.2 %sum_terms.10 = (bf16[3456,128]{1,0:T(8,128)(2,1)}, bf16[3072,128]{1,0:T(8,128)(2,1)}, bf16[3072,128]{1,0:T(8,128)(2,1)}) custom-call(s32[5]{0:T(128)} %shift-right-arithmetic_and_fusion.bits_ref, bf16[13824,128]{1,0:T(8,128)(2,1)} %bitcast.125, bf16[13824,128]{1,0:T(8,128)(2,1)} %copy-done, bf16[6912,128]{1,0:T(8,128)(2,1)} %copy-done.1, ...), custom_call_target="tpu_custom_call" | custom-call | flops 3300000000 | tf_op jit(solution)/shard_map/sum_terms/pallas_call | solution.py:1171
  267.7 15.6 %self_backward.1 = (bf16[3,1024,768]{2,1,0:T(8,128)(2,1)}, bf16[1024,768]{1,0:T(8,128)(2,1)}, f32[1024,768]{1,0:T(8,128)}, f32[48,128]{1,0:T(8,128)}) custom-call(bf16[6,768,768]{2,1,0:T(8,128)(2,1)} %refs_0_.7, f32[4,768]{1,0:T(4,128)} %refs_1_.2, bf16[16,64,256]{2,1,0:T(8,128)(2,1)} %tile.18.mask_ref.refs_2_, ...), custom_call_target="tpu_custom_call" | custom-call | flops 17600000000 | tf_op jit(solution)/shard_map/self_backward/pallas_call | solution.py:306
  286.7 4.9 %sum_terms.11 = (bf16[1728,128]{1,0:T(8,128)(2,1)}, bf16[3072,128]{1,0:T(8,128)(2,1)}, bf16[3072,128]{1,0:T(8,128)(2,1)}, bf16[1152,128]{1,0:T(8,128)(2,1)}) custom-call(s32[5]{0:T(128)} %shift-right-arithmetic_and_fusion.bits_ref, bf16[13824,128]{1,0:T(8,128)(2,1)} %bitcast.126, bf16[13824,128]{1,0:T(8,128)(2,1)} %copy-done, bf16[6912,128]{1,0:T(8,128)(2,1)} %copy-done.1, ...), custom_call_target="tpu_custom_call" | custom-call | flops 3300000000 | tf_op jit(solution)/shard_map/sum_terms/pallas_call | solution.py:1171
  291.6 2.6 collective-permute-start.12
  297.4 15.5 %attn_weight_grad.1 = (bf16[2,2,2,2,6,48,128]{6,5,4,3,2,1,0:T(8,128)(2,1)}, bf16[2,2,2,2,6,48,128]{6,5,4,3,2,1,0:T(8,128)(2,1)}, bf16[2,2,2,2,6,48,128]{6,5,4,3,...) custom-call(s32[1]{0:T(128)} %bitcast.195, ...), custom_call_target="tpu_custom_call" | custom-call | flops 22000001024 | tf_op jit(solution)/shard_map/attn_weight_grad/pallas_call | solution.py:428
  316.8 6.7 %collective-permute-done.13.refs_7_.refs_22_.refs_18_ = bf16[3072,128]{1,0:T(8,128)(2,1)S(1)} collective-permute-done((bf16[3072,128]{1,0:T(8,128)(2,1)}, bf16[3072,128]{1,0:T(8,128)(2,1)S(1)}, u32[]{:S(2)}, u32[]{:S(2)}) %collective-permute-start.13) | collective-permute-done | bytes 786464 | tf_op jit(solution)/shard_map/ppermute | solution.py:1065
  325.3 4.1 sum_terms.12
  330.5 4.5 %input_gradient.2.refs_3_ = f32[1024,768]{1,0:T(8,128)} custom-call(bf16[6,768,768]{2,1,0:T(8,128)(2,1)} %refs_0_.7, bf16[3,1024,768]{2,1,0:T(8,128)(2,1)} %get-tuple-element.201.refs_2_.refs_1_, f32[1024,768]{1,0:T(8,128)} %get-tuple-element.202.refs_2_, bf16[1632,128]{1,0:T(8,128)(2,1)} %get-tuple-element.232.refs_3_, ...), custom_call_target="tpu_custom_call" | custom-call | flops 5500000256 | tf_op jit(solution)/shard_map/input_gradient/pallas_call | solution.py:354
  337.4 3.8 sum_terms.13
  345.7 7.6 %input_gradient.3 = f32[1024,768]{1,0:T(8,128)} custom-call(bf16[6,768,768]{2,1,0:T(8,128)(2,1)} %refs_0_.7, bf16[3,1024,768]{2,1,0:T(8,128)(2,1)} %get-tuple-element.201.refs_2_.refs_1_, f32[1024,768]{1,0:T(8,128)} %get-tuple-element.202.refs_2_, f32[1024,768]{1,0:T(8,128)} %input_gradient.2.refs_3_, ...), custom_call_target="tpu_custom_call", output_to_operand_aliasing={{}: (3, {})} | custom-call | flops 5500000256 | tf_op jit(solution)/shard_map/input_gradient/pallas_call | solution.py:354
  353.3 11.3 %collective-permute-done.26.refs_33_ = bf16[1536,128]{1,0:T(8,128)(2,1)S(1)} collective-permute-done((bf16[1536,128]{1,0:T(8,128)(2,1)}, bf16[1536,128]{1,0:T(8,128)(2,1)S(1)}, u32[]{:S(2)}, u32[]{:S(2)}) %collective-permute-start.26) | collective-permute-done | bytes 393248 | tf_op jit(solution)/shard_map/ppermute | solution.py:1065
  367.8 5.5 %sum_terms.14 = (bf16[1440,128]{1,0:T(8,128)(2,1)}, bf16[1792,128]{1,0:T(8,128)(2,1)}, bf16[1536,128]{1,0:T(8,128)(2,1)}, f32[48,2304]{1,0:T(8,128)}, f32[48,2048]{1,0:T(8,128)}, /*index=5*/f32[48,2048]{1,0:T(8,128)}) custom-call(s32[5]{0:T(128)} %shift-right-arithmetic_and_fusion.bits_ref, bf16[4608,128]{1,0:T(8,128)(2,1)} %bitcast.155, ...), custom_call_target="tpu_custom_call" | custom-call | flops 3300000000 | tf_op jit(solution)/shard_map/sum_terms/pallas_call | solution.py:1171
  384.9 3.5 sum_terms.15
  396.7 3.8 collective-permute-done.33.refs_19_
  401.1 3.4 sum_terms.16
  413.4 3.0 collective-permute-done.34.refs_5_
  417.0 2.9 sum_terms.17
  (242 shorter events, 89.5 us)
Async XLA Ops:
  47.6 61.3 %all-to-all-start = ((bf16[32,32,256]{2,1,0:T(8,128)(2,1)}), bf16[32,32,256]{2,1,0:T(8,128)(2,1)S(1)}, u32[]{:S(2)}, u32[]{:S(2)}) async-start(bf16[32,32,256]{2,1,0:T(8,128)(2,1)} %tile.20), calls=%async_computation | async-start | bytes 1048576 | tf_op jit(solution)/shard_map/all_to_all | solution.py:1293
  111.4 14.5 %all-to-all-start.1 = ((f32[32,1,1024]{2,1,0:T(1,128)}), f32[32,1,1024]{2,1,0:T(1,128)S(1)}, u32[]{:S(2)}, u32[]{:S(2)}) async-start(f32[32,1,1024]{2,1,0:T(1,128)} %broadcast_in_dim.16), calls=%async_computation.1 | async-start | bytes 262144 | tf_op jit(solution)/shard_map/all_to_all | solution.py:1293
  129.9 30.0 %all-to-all-start.2 = ((bf16[32,32,256]{2,1,0:T(8,128)(2,1)}), bf16[32,32,256]{2,1,0:T(8,128)(2,1)S(1)}, u32[]{:S(2)}, u32[]{:S(2)}) async-start(bf16[32,32,256]{2,1,0:T(8,128)(2,1)} %bitcast.180), calls=%async_computation.2 | async-start | bytes 1048576 | tf_op jit(solution)/shard_map/all_to_all | solution.py:1293
  186.6 19.7 %collective-permute-start = (bf16[13824,128]{1,0:T(8,128)(2,1)}, bf16[13824,128]{1,0:T(8,128)(2,1)S(1)}, u32[]{:S(2)}, u32[]{:S(2)}) collective-permute-start(bf16[13824,128]{1,0:T(8,128)(2,1)} %bitcast.198), channel_id=1, source_target_pairs={{0,2},{2,0},{4,6},{6,4},{8,10},{10,8},{12,14},{14,12},{16,18},{18,... | collective-permute-start | bytes 10616840 | tf_op jit(solution)/shard_map/ppermute | solution.py:1065
  186.9 19.4 %collective-permute-start.1 = (bf16[12288,128]{1,0:T(8,128)(2,1)}, bf16[12288,128]{1,0:T(8,128)(2,1)}, u32[]{:S(2)}, u32[]{:S(2)}) collective-permute-start(bf16[12288,128]{1,0:T(8,128)(2,1)} %bitcast.200), channel_id=1, source_target_pairs={{0,2},{2,0},{4,6},{6,4},{8,10},{10,8},{12,14},{14,12},{16,18},{18,... | collective-permute-start | bytes 9437192 | tf_op jit(solution)/shard_map/ppermute | solution.py:1065
  187.2 19.1 %collective-permute-start.2 = (bf16[12288,128]{1,0:T(8,128)(2,1)}, bf16[12288,128]{1,0:T(8,128)(2,1)}, u32[]{:S(2)}, u32[]{:S(2)}) collective-permute-start(bf16[12288,128]{1,0:T(8,128)(2,1)} %bitcast.202), channel_id=1, source_target_pairs={{0,2},{2,0},{4,6},{6,4},{8,10},{10,8},{12,14},{14,12},{16,18},{18,... | collective-permute-start | bytes 9437192 | tf_op jit(solution)/shard_map/ppermute | solution.py:1065
  215.3 41.0 %collective-permute-start.3 = (bf16[6912,128]{1,0:T(8,128)(2,1)}, bf16[6912,128]{1,0:T(8,128)(2,1)S(1)}, u32[]{:S(2)}, u32[]{:S(2)}) collective-permute-start(bf16[6912,128]{1,0:T(8,128)(2,1)} %get-tuple-element.186.refs_5_), channel_id=1, source_target_pairs={{0,4},{2,6},{4,0},{6,2},{8,12},{10,14},{12,8},{14,10},{16,20},{18,... | collective-permute-start | bytes 5308424 | tf_op jit(solution)/shard_map/ppermute | solution.py:1065
  217.0 36.6 %collective-permute-start.4 = (bf16[6144,128]{1,0:T(8,128)(2,1)}, bf16[6144,128]{1,0:T(8,128)(2,1)S(1)}, u32[]{:S(2)}, u32[]{:S(2)}) collective-permute-start(bf16[6144,128]{1,0:T(8,128)(2,1)} %get-tuple-element.189.refs_6_), channel_id=1, source_target_pairs={{0,8},{2,10},{4,12},{6,14},{8,0},{10,2},{12,4},{14,6},{16,24},{18,... | collective-permute-start | bytes 4718600 | tf_op jit(solution)/shard_map/ppermute | solution.py:1065
  218.5 36.4 %collective-permute-start.5 = (bf16[6144,128]{1,0:T(8,128)(2,1)}, bf16[6144,128]{1,0:T(8,128)(2,1)}, u32[]{:S(2)}, u32[]{:S(2)}) collective-permute-start(bf16[6144,128]{1,0:T(8,128)(2,1)} %get-tuple-element.190.refs_7_), channel_id=1, source_target_pairs={{0,1},{1,0},{2,3},{3,2},{4,5},{5,4},{6,7},{7,6},{8,9},{9,8},{10,11... | collective-permute-start | bytes 4718600 | tf_op jit(solution)/shard_map/ppermute | solution.py:1065
  252.7 13.4 %collective-permute-start.8 = (bf16[3072,128]{1,0:T(8,128)(2,1)}, bf16[3072,128]{1,0:T(8,128)(2,1)}, u32[]{:S(2)}, u32[]{:S(2)}) collective-permute-start(bf16[3072,128]{1,0:T(8,128)(2,1)} %bitcast.209), channel_id=1, source_target_pairs={{0,2},{2,0},{4,6},{6,4},{8,10},{10,8},{12,14},{14,12},{16,18},{18,... | collective-permute-start | bytes 2359304 | tf_op jit(solution)/shard_map/ppermute | solution.py:1065
  252.8 30.5 %collective-permute-start.10 = (bf16[3072,128]{1,0:T(8,128)(2,1)}, bf16[3072,128]{1,0:T(8,128)(2,1)}, u32[]{:S(2)}, u32[]{:S(2)}) collective-permute-start(bf16[3072,128]{1,0:T(8,128)(2,1)} %bitcast.211), channel_id=1, source_target_pairs={{0,2},{2,0},{4,6},{6,4},{8,10},{10,8},{12,14},{14,12},{16,18},{18,... | collective-permute-start | bytes 2359304 | tf_op jit(solution)/shard_map/ppermute | solution.py:1065
  253.6 29.8 %collective-permute-start.11 = (bf16[2304,128]{1,0:T(8,128)(2,1)}, bf16[2304,128]{1,0:T(8,128)(2,1)}, u32[]{:S(2)}, u32[]{:S(2)}) collective-permute-start(bf16[2304,128]{1,0:T(8,128)(2,1)} %bitcast.213), channel_id=1, source_target_pairs={{0,2},{2,0},{4,6},{6,4},{8,10},{10,8},{12,14},{14,12},{16,18},{18,... | collective-permute-start | bytes 1769480 | tf_op jit(solution)/shard_map/ppermute | solution.py:1065
  262.8 22.4 %collective-permute-start.6 = (bf16[3456,128]{1,0:T(8,128)(2,1)}, bf16[3456,128]{1,0:T(8,128)(2,1)S(1)}, u32[]{:S(2)}, u32[]{:S(2)}) collective-permute-start(bf16[3456,128]{1,0:T(8,128)(2,1)} %get-tuple-element.195.refs_9_), channel_id=1, source_target_pairs={{0,8},{2,10},{4,12},{6,14},{8,0},{10,2},{12,4},{14,6},{16,24},{18,... | collective-permute-start | bytes 2654216 | tf_op jit(solution)/shard_map/ppermute | solution.py:1065
  264.7 20.5 %collective-permute-start.7 = (bf16[3072,128]{1,0:T(8,128)(2,1)}, bf16[3072,128]{1,0:T(8,128)(2,1)S(1)}, u32[]{:S(2)}, u32[]{:S(2)}) collective-permute-start(bf16[3072,128]{1,0:T(8,128)(2,1)} %get-tuple-element.196.refs_10_), channel_id=1, source_target_pairs={{0,1},{1,0},{2,3},{3,2},{4,5},{5,4},{6,7},{7,6},{8,9},{9,8},{10,11... | collective-permute-start | bytes 2359304 | tf_op jit(solution)/shard_map/ppermute | solution.py:1065
  266.2 19.1 %collective-permute-start.9 = (bf16[3072,128]{1,0:T(8,128)(2,1)}, bf16[3072,128]{1,0:T(8,128)(2,1)S(1)}, u32[]{:S(2)}, u32[]{:S(2)}) collective-permute-start(bf16[3072,128]{1,0:T(8,128)(2,1)} %get-tuple-element.197.refs_11_), channel_id=1, source_target_pairs={{0,4},{2,6},{4,0},{6,2},{8,12},{10,14},{12,8},{14,10},{16,20},{18,... | collective-permute-start | bytes 2359304 | tf_op jit(solution)/shard_map/ppermute | solution.py:1065
  285.2 27.7 %collective-permute-start.16 = (bf16[256,128]{1,0:T(8,128)(2,1)}, bf16[256,128]{1,0:T(8,128)(2,1)S(1)}, u32[]{:S(2)}, u32[]{:S(2)}) collective-permute-start(bf16[256,128]{1,0:T(8,128)(2,1)} %convert_element_type.67.refs_13_), channel_id=1, source_target_pairs={{0,2},{2,0},{4,6},{6,4},{8,10},{10,8},{12,14},{14,12},{16,18},{18,... | collective-permute-start | bytes 196616 | tf_op jit(solution)/shard_map/ppermute | solution.py:1065
  291.6 23.3 %collective-permute-start.12 = (bf16[1728,128]{1,0:T(8,128)(2,1)}, bf16[1728,128]{1,0:T(8,128)(2,1)S(1)}, u32[]{:S(2)}, u32[]{:S(2)}) collective-permute-start(bf16[1728,128]{1,0:T(8,128)(2,1)} %get-tuple-element.212.refs_9_), channel_id=1, source_target_pairs={{0,16},{2,18},{4,20},{6,22},{8,24},{10,26},{12,28},{14,30},{16,0},... | collective-permute-start | bytes 1327112 | tf_op jit(solution)/shard_map/ppermute | solution.py:1065
  294.2 29.3 %collective-permute-start.13 = (bf16[3072,128]{1,0:T(8,128)(2,1)}, bf16[3072,128]{1,0:T(8,128)(2,1)S(1)}, u32[]{:S(2)}, u32[]{:S(2)}) collective-permute-start(bf16[3072,128]{1,0:T(8,128)(2,1)} %get-tuple-element.218.refs_11_), channel_id=1, source_target_pairs={{0,8},{2,10},{4,12},{6,14},{8,0},{10,2},{12,4},{14,6},{16,24},{18,... | collective-permute-start | bytes 2359304 | tf_op jit(solution)/shard_map/ppermute | solution.py:1065
  294.7 28.8 %collective-permute-start.14 = (bf16[3072,128]{1,0:T(8,128)(2,1)}, bf16[3072,128]{1,0:T(8,128)(2,1)S(1)}, u32[]{:S(2)}, u32[]{:S(2)}) collective-permute-start(bf16[3072,128]{1,0:T(8,128)(2,1)} %get-tuple-element.217.refs_10_), channel_id=1, source_target_pairs={{0,4},{2,6},{4,0},{6,2},{8,12},{10,14},{12,8},{14,10},{16,20},{18,... | collective-permute-start | bytes 2359304 | tf_op jit(solution)/shard_map/ppermute | solution.py:1065
  295.8 17.7 %collective-permute-start.15 = (bf16[1152,128]{1,0:T(8,128)(2,1)}, bf16[1152,128]{1,0:T(8,128)(2,1)S(1)}, u32[]{:S(2)}, u32[]{:S(2)}) collective-permute-start(bf16[1152,128]{1,0:T(8,128)(2,1)} %get-tuple-element.219.refs_12_), channel_id=1, source_target_pairs={{0,1},{1,0},{2,3},{3,2},{4,5},{5,4},{6,7},{7,6},{8,9},{9,8},{10,11... | collective-permute-start | bytes 884744 | tf_op jit(solution)/shard_map/ppermute | solution.py:1065
  313.5 22.8 %collective-permute-start.17 = (bf16[4608,128]{1,0:T(8,128)(2,1)}, bf16[4608,128]{1,0:T(8,128)(2,1)S(1)}, u32[]{:S(2)}, u32[]{:S(2)}) collective-permute-start(bf16[4608,128]{1,0:T(8,128)(2,1)} %bitcast.208), channel_id=1, source_target_pairs={{0,2},{2,0},{4,6},{6,4},{8,10},{10,8},{12,14},{14,12},{16,18},{18,... | collective-permute-start | bytes 3538952 | tf_op jit(solution)/shard_map/ppermute | solution.py:1065
  313.6 22.7 %collective-permute-start.18 = (bf16[4608,128]{1,0:T(8,128)(2,1)}, bf16[4608,128]{1,0:T(8,128)(2,1)}, u32[]{:S(2)}, u32[]{:S(2)}) collective-permute-start(bf16[4608,128]{1,0:T(8,128)(2,1)} %bitcast.207), channel_id=1, source_target_pairs={{0,2},{2,0},{4,6},{6,4},{8,10},{10,8},{12,14},{14,12},{16,18},{18,... | collective-permute-start | bytes 3538952 | tf_op jit(solution)/shard_map/ppermute | solution.py:1065
  314.9 21.4 %collective-permute-start.20 = (bf16[4608,128]{1,0:T(8,128)(2,1)}, bf16[4608,128]{1,0:T(8,128)(2,1)}, u32[]{:S(2)}, u32[]{:S(2)}) collective-permute-start(bf16[4608,128]{1,0:T(8,128)(2,1)} %bitcast.206), channel_id=1, source_target_pairs={{0,2},{2,0},{4,6},{6,4},{8,10},{10,8},{12,14},{14,12},{16,18},{18,... | collective-permute-start | bytes 3538952 | tf_op jit(solution)/shard_map/ppermute | solution.py:1065
  330.0 15.7 %collective-permute-start.23 = (bf16[768,128]{1,0:T(8,128)(2,1)}, bf16[768,128]{1,0:T(8,128)(2,1)S(1)}, u32[]{:S(2)}, u32[]{:S(2)}) collective-permute-start(bf16[768,128]{1,0:T(8,128)(2,1)} %get-tuple-element.234.refs_5_), channel_id=1, source_target_pairs={{0,8},{2,10},{4,12},{6,14},{8,0},{10,2},{12,4},{14,6},{16,24},{18,... | collective-permute-start | bytes 589832 | tf_op jit(solution)/shard_map/ppermute | solution.py:1065
  341.3 24.6 %collective-permute-start.21 = (bf16[2304,128]{1,0:T(8,128)(2,1)}, bf16[2304,128]{1,0:T(8,128)(2,1)S(1)}, u32[]{:S(2)}, u32[]{:S(2)}) collective-permute-start(bf16[2304,128]{1,0:T(8,128)(2,1)} %get-tuple-element.245.refs_4_), channel_id=1, source_target_pairs={{0,4},{2,6},{4,0},{6,2},{8,12},{10,14},{12,8},{14,10},{16,20},{18,... | collective-permute-start | bytes 1769480 | tf_op jit(solution)/shard_map/ppermute | solution.py:1065
  341.6 24.3 %collective-permute-start.22 = (bf16[2560,128]{1,0:T(8,128)(2,1)}, bf16[2560,128]{1,0:T(8,128)(2,1)S(1)}, u32[]{:S(2)}, u32[]{:S(2)}) collective-permute-start(bf16[2560,128]{1,0:T(8,128)(2,1)} %get-tuple-element.246.refs_5_), channel_id=1, source_target_pairs={{0,8},{2,10},{4,12},{6,14},{8,0},{10,2},{12,4},{14,6},{16,24},{18,... | collective-permute-start | bytes 1966088 | tf_op jit(solution)/shard_map/ppermute | solution.py:1065
  343.2 22.7 %collective-permute-start.24 = (bf16[2304,128]{1,0:T(8,128)(2,1)}, bf16[2304,128]{1,0:T(8,128)(2,1)S(1)}, u32[]{:S(2)}, u32[]{:S(2)}) collective-permute-start(bf16[2304,128]{1,0:T(8,128)(2,1)} %get-tuple-element.247.refs_6_), channel_id=1, source_target_pairs={{0,1},{1,0},{2,3},{3,2},{4,5},{5,4},{6,7},{7,6},{8,9},{9,8},{10,11... | collective-permute-start | bytes 1769480 | tf_op jit(solution)/shard_map/ppermute | solution.py:1065
  344.2 21.7 %collective-permute-start.25 = (bf16[1632,128]{1,0:T(8,128)(2,1)S(1)}, bf16[1632,128]{1,0:T(8,128)(2,1)S(1)}, u32[]{:S(2)}, u32[]{:S(2)}) collective-permute-start(bf16[1632,128]{1,0:T(8,128)(2,1)S(1)} %copy-done.44), channel_id=1, source_target_pairs={{0,1},{1,0},{2,3},{3,2},{4,5},{5,4},{6,7},{7,6},{8,9},{9,8},{10,11... | collective-permute-start | bytes 1253384 | tf_op jit(solution)/shard_map/ppermute | solution.py:1065
  345.7 18.9 %collective-permute-start.26 = (bf16[1536,128]{1,0:T(8,128)(2,1)}, bf16[1536,128]{1,0:T(8,128)(2,1)S(1)}, u32[]{:S(2)}, u32[]{:S(2)}) collective-permute-start(bf16[1536,128]{1,0:T(8,128)(2,1)} %get-tuple-element.233.refs_4_), channel_id=1, source_target_pairs={{0,16},{2,18},{4,20},{6,22},{8,24},{10,26},{12,28},{14,30},{16,0},... | collective-permute-start | bytes 1179656 | tf_op jit(solution)/shard_map/ppermute | solution.py:1065
  374.1 10.0 %collective-permute-start.28 = (bf16[1792,128]{1,0:T(8,128)(2,1)}, bf16[1792,128]{1,0:T(8,128)(2,1)S(1)}, u32[]{:S(2)}, u32[]{:S(2)}) collective-permute-start(bf16[1792,128]{1,0:T(8,128)(2,1)} %get-tuple-element.256), channel_id=1, source_target_pairs={{0,1},{1,0},{2,3},{3,2},{4,5},{5,4},{6,7},{7,6},{8,9},{9,8},{10,11... | collective-permute-start | bytes 1376264 | tf_op jit(solution)/shard_map/ppermute | solution.py:1065
  391.5 9.0 %collective-permute-start.33 = (bf16[784,128]{1,0:T(8,128)(2,1)}, bf16[784,128]{1,0:T(8,128)(2,1)S(1)}, u32[]{:S(2)}, u32[]{:S(2)}) collective-permute-start(bf16[784,128]{1,0:T(8,128)(2,1)} %get-tuple-element.261), channel_id=1, source_target_pairs={{0,16},{2,18},{4,20},{6,22},{8,24},{10,26},{12,28},{14,30},{16,0},... | collective-permute-start | bytes 602120 | tf_op jit(solution)/shard_map/ppermute | solution.py:1065
  407.6 8.8 %collective-permute-start.34 = (bf16[864,128]{1,0:T(8,128)(2,1)}, bf16[864,128]{1,0:T(8,128)(2,1)S(1)}, u32[]{:S(2)}, u32[]{:S(2)}) collective-permute-start(bf16[864,128]{1,0:T(8,128)(2,1)} %get-tuple-element.262), channel_id=1, source_target_pairs={{0,16},{2,18},{4,20},{6,22},{8,24},{10,26},{12,28},{14,30},{16,0},... | collective-permute-start | bytes 663560 | tf_op jit(solution)/shard_map/ppermute | solution.py:1065
  (52 other events, 322.8 us)
